TPU v7x, 32 devices: a whole 2x2x4 slice. The times are simulated.
32 devices in a mesh: expert: 8 (over z, x), head: 4 (over y, core).
Axes of the slice: x: 2, y: 2, z: 4, core: 2. Of those that a mesh axis runs over, the one named last changes fastest.
Arguments:
- inputs: bfloat16 [1024, 768], P('expert', 'head'), may hold values from -6 to 6
- out_grad: bfloat16 [1024, 768], P('expert', 'head'), may hold values from -6 to 6
- lengths: int32 [8], P('expert'), may hold values from 1 to 128, 768 in all
- routes: int32 [1024, 1], P('expert'), may hold values from 0 to 7; in each aligned block of 128 rows (0 to 127, 128 to 255, ...) at most 22 rows name the same one
- buckets: int32 [255], replicated, may hold values from 0 to 31
- gain_attn: bfloat16 [768], P('head'), may hold values from 0.25 to 1.75
- w_query: bfloat16 [768, 768], P(None, 'head'), may hold values from -0.21875 to 0.21875
- w_key: bfloat16 [768, 768], P(None, 'head'), may hold values from -0.21875 to 0.21875
- w_value: bfloat16 [768, 768], P(None, 'head'), may hold values from -0.21875 to 0.21875
- w_output: bfloat16 [768, 768], P('head'), may hold values from -1.75 to 1.75
- bias_table: float32 [32, 12], P(None, 'head'), may hold values from -6 to 6
- gain_ffn: bfloat16 [768], P('head'), may hold values from 0.25 to 1.75
- w_router: bfloat16 [768, 8], replicated, may hold values from -0.15625 to 0.15625
- w_in: bfloat16 [8, 768, 3072], P('expert', None, 'head'), may hold values from -0.21875 to 0.21875
- w_out: bfloat16 [8, 3072, 768], P('expert', 'head'), may hold values from -0.875 to 0.875
Outputs:
- block_out: bfloat16 [1024, 768], P('expert', 'head')
- input_grad: float32 [1024, 768], P('expert', 'head')
- aux_loss: float32 [], replicated
- gain_attn_grad: float32 [768], P('head')
- query_weight_grad: float32 [768, 768], P(None, 'head')
- key_weight_grad: float32 [768, 768], P(None, 'head')
- value_weight_grad: float32 [768, 768], P(None, 'head')
- output_weight_grad: float32 [768, 768], P('head')
- table_grad: float32 [32, 12], P(None, 'head')
- gain_ffn_grad: float32 [768], P('head')
- router_grad: float32 [768, 8], replicated
- in_weight_grad: float32 [8, 768, 3072], P('expert', None, 'head')
- out_weight_grad: float32 [8, 3072, 768], P('expert', 'head')
Inputs may be any that keep to these rules, and one draw needn't show every extreme that they name: Entry b is the length of the one sequence that starts at row b * 128; the lengths sum to 768, and the largest is 128. `routes`: among the 128 rows of one device no expert is named by more than 22 rows, a bound that some block reaches. `buckets`: entry r is the bucket of relative position r - 127.
All inputs are finite; a program needn't handle non-finite values. No bound on the sum of `lengths` on one device may be relied on, other than what follows from the above.
Results may differ from a plain program's by a relative error of at most 0.017.
Values may be sent and summed in bfloat16 or wider, within the bound.
No kernel may reach another device: no remote copies, remote signals or barrier semaphores. Data moves between devices by JAX's collectives and lax.ppermute only.
A program may use at most 64 MiB of HBM per device.

v0:
```python
import jax
import jax.numpy as jnp
from jax import lax
from jax.sharding import PartitionSpec as P

eps = 1e-06
aux_weight = 0.01


def rms_scale(values):
    return lax.rsqrt(jnp.mean(values * values, axis=-1, keepdims=True) + eps)


def smooth(values):
    return jax.nn.gelu(values, approximate=True)


def own_columns(matrix, col_width):
    return lax.dynamic_slice_in_dim(
        matrix, lax.axis_index("head") * col_width, col_width, matrix.ndim - 1
    )


def to_owner(buffer):
    arrived = lax.all_to_all(buffer, "expert", split_axis=0, concat_axis=0, tiled=True)
    return arrived


def from_owner(partial_rows):
    shared = lax.psum_scatter(partial_rows, "head", scatter_dimension=2, tiled=True)
    return lax.all_to_all(
        shared.astype(jnp.bfloat16), "expert", split_axis=0, concat_axis=0, tiled=True
    )


def attention_scores(query_heads, key_heads, bias_full, key_mask, score_scale):
    scores = (
        jnp.einsum("qhd,khd->hqk", query_heads, key_heads, preferred_element_type=jnp.float32)
        * score_scale
        + bias_full
    )
    return jnp.where(key_mask, scores, -1000000000.0)


def diagonal_spread(offsets, tok_rows):
    heads_here = offsets.shape[1]
    reversed_rows = jnp.transpose(offsets[::-1], (1, 0))
    tiled = jnp.broadcast_to(reversed_rows[:, None, :], (heads_here, tok_rows, 2 * tok_rows - 1))
    flat = tiled.reshape(heads_here, tok_rows * (2 * tok_rows - 1))
    flat = jnp.pad(flat, ((0, 0), (0, tok_rows)))
    skewed = flat.reshape(heads_here, tok_rows, 2 * tok_rows)[:, :, :tok_rows]
    return skewed[:, :, ::-1]


def shards(
    inputs,
    out_grad,
    lengths,
    routes,
    buckets,
    gain_attn,
    w_query,
    w_key,
    w_value,
    w_output,
    bias_table,
    gain_ffn,
    w_router,
    w_in,
    w_out,
):
    tok_rows, col_width = inputs.shape
    heads_here = bias_table.shape[1]
    head_size = w_query.shape[1] // heads_here
    model_width = w_query.shape[0]
    experts = w_router.shape[1]
    bucket_count = bias_table.shape[0]
    capacity = max(2, (4 * tok_rows + 3 * experts - 1) // (3 * experts))
    valid_total = 3 * tok_rows * lax.axis_size("expert") // 4
    score_scale = head_size ** (-0.5)
    full_in, full_grad, gain_one, gain_two = (
        lax.all_gather(inputs, "head", axis=1, tiled=True),
        lax.all_gather(out_grad, "head", axis=1, tiled=True),
        lax.all_gather(gain_attn, "head", axis=0, tiled=True),
        lax.all_gather(gain_ffn, "head", axis=0, tiled=True),
    )
    gain_one = gain_one.astype(jnp.float32)
    gain_two = gain_two.astype(jnp.float32)
    inputs_wide = full_in.astype(jnp.float32)
    scale_one = rms_scale(inputs_wide)
    unit_one = inputs_wide * scale_one
    normed_one = (unit_one * gain_one).astype(jnp.bfloat16)
    query_rows = jnp.dot(normed_one, w_query, preferred_element_type=jnp.float32).astype(
        jnp.bfloat16
    )
    key_rows = jnp.dot(normed_one, w_key, preferred_element_type=jnp.float32).astype(jnp.bfloat16)
    value_rows = jnp.dot(normed_one, w_value, preferred_element_type=jnp.float32).astype(
        jnp.bfloat16
    )
    query_heads = query_rows.reshape(tok_rows, heads_here, head_size)
    key_heads = key_rows.reshape(tok_rows, heads_here, head_size)
    value_heads = value_rows.reshape(tok_rows, heads_here, head_size)
    bucket_hot = (buckets[:, None] == jnp.arange(bucket_count)[None, :]).astype(jnp.float32)
    offset_bias = jnp.dot(bucket_hot, bias_table, precision=lax.Precision.HIGHEST)
    positions = jnp.arange(tok_rows)

    def expand(offsets):
        return diagonal_spread(offsets, tok_rows)

    bias_full, expand_back = jax.vjp(expand, offset_bias)
    key_mask = (positions < lengths[0])[None, None, :]
    scores = attention_scores(query_heads, key_heads, bias_full, key_mask, score_scale)
    row_max = jnp.max(scores, axis=-1, keepdims=True)
    log_total = row_max + jnp.log(jnp.sum(jnp.exp(scores - row_max), axis=-1, keepdims=True))
    attention_weights = jnp.exp(scores - log_total)
    attended = jnp.einsum(
        "hqk,khd->qhd",
        attention_weights.astype(jnp.bfloat16),
        value_heads,
        preferred_element_type=jnp.float32,
    )
    attended = attended.reshape(tok_rows, col_width).astype(jnp.bfloat16)
    attn_part = jnp.dot(attended, w_output, preferred_element_type=jnp.float32)
    residual = inputs_wide + lax.psum(attn_part, "head")
    scale_two = rms_scale(residual)
    unit_two = residual * scale_two
    normed_two = (unit_two * gain_two).astype(jnp.bfloat16)
    logits = jnp.dot(normed_two, w_router, preferred_element_type=jnp.float32)
    router_weights = jax.nn.softmax(logits, axis=-1)
    route_hot = (routes == jnp.arange(experts)[None, :]).astype(jnp.float32)
    gate_value = jnp.sum(router_weights * route_hot, axis=1)
    valid_rows = (positions < lengths[0]).astype(jnp.float32)
    counts, prob_sums = lax.psum(
        (
            jnp.sum(route_hot * valid_rows[:, None], axis=0),
            jnp.sum(router_weights * valid_rows[:, None], axis=0),
        ),
        "expert",
    )
    fraction = counts / valid_total
    aux_loss = experts * jnp.sum(fraction * (prob_sums / valid_total))
    route_int = (routes == jnp.arange(experts)[None, :]).astype(jnp.int32)
    earlier = jnp.cumsum(route_int, axis=0, dtype=jnp.int32) - route_int
    slot_index = routes[:, 0] * capacity + jnp.sum(earlier * route_int, axis=1)

    def dispatch(rows):
        placed = jnp.zeros((experts * capacity, rows.shape[1]), rows.dtype).at[slot_index].set(rows)
        return placed.reshape(experts, capacity, rows.shape[1])

    arrived = to_owner(dispatch(normed_two))
    expert_rows = arrived.reshape(-1, model_width)
    before_act = jnp.dot(expert_rows, w_in[0], preferred_element_type=jnp.float32)
    hidden = smooth(before_act).astype(jnp.bfloat16)
    expert_part = jnp.dot(hidden, w_out[0], preferred_element_type=jnp.float32)
    returned = from_owner(expert_part.reshape(arrived.shape)).reshape(
        experts * capacity, col_width
    )[slot_index]
    returned_wide = returned.astype(jnp.float32)
    block_out = (own_columns(residual, col_width) + gate_value[:, None] * returned_wide).astype(
        jnp.bfloat16
    )
    grad_own = out_grad.astype(jnp.float32)
    grad_wide = full_grad.astype(jnp.float32)
    gate_grad = lax.psum(jnp.sum(grad_own * returned_wide, axis=1), "head")
    back_rows = to_owner(dispatch((gate_value[:, None] * grad_wide).astype(jnp.bfloat16))).reshape(
        -1, model_width
    )
    hidden_grad = jnp.einsum("rd,fd->rf", back_rows, w_out[0], preferred_element_type=jnp.float32)
    out_weight_grad = jnp.einsum(
        "rf,rd->fd", hidden, back_rows, preferred_element_type=jnp.float32
    )[None]
    act_back = jax.vjp(smooth, before_act)[1]
    before_grad = act_back(hidden_grad)[0].astype(jnp.bfloat16)
    in_weight_grad = jnp.einsum(
        "rd,rf->df", expert_rows, before_grad, preferred_element_type=jnp.float32
    )[None]
    rows_grad = jnp.einsum("rf,df->rd", before_grad, w_in[0], preferred_element_type=jnp.float32)
    came_back = from_owner(rows_grad.reshape(arrived.shape))
    expert_grad = lax.all_gather(came_back, "head", axis=2, tiled=True).reshape(
        experts * capacity, model_width
    )[slot_index]
    prob_grad = (
        route_hot * gate_grad[:, None]
        + aux_weight * experts * fraction[None, :] * valid_rows[:, None] / valid_total
    )
    logit_grad = (
        router_weights * (prob_grad - jnp.sum(router_weights * prob_grad, axis=1, keepdims=True))
    ).astype(jnp.bfloat16)
    router_grad = jnp.einsum(
        "td,te->de", normed_two, logit_grad, preferred_element_type=jnp.float32
    )
    normed_grad = jnp.einsum(
        "te,de->td", logit_grad, w_router, preferred_element_type=jnp.float32
    ) + expert_grad.astype(jnp.float32)
    gain_two_grad = own_columns(jnp.sum(normed_grad * unit_two, axis=0), col_width)
    unit_grad = normed_grad * gain_two
    residual_grad = grad_wide + scale_two * (
        unit_grad - unit_two * jnp.mean(unit_grad * unit_two, axis=-1, keepdims=True)
    )
    branch_grad = residual_grad.astype(jnp.bfloat16)
    output_grad = jnp.einsum("tc,td->cd", attended, branch_grad, preferred_element_type=jnp.float32)
    attended_grad = jnp.einsum(
        "td,cd->tc", branch_grad, w_output, preferred_element_type=jnp.float32
    ).astype(jnp.bfloat16)
    attended_grad = attended_grad.reshape(tok_rows, heads_here, head_size)
    scores = attention_scores(query_heads, key_heads, bias_full, key_mask, score_scale)
    attention_weights = jnp.exp(scores - log_total)
    mass_grad = jnp.einsum(
        "qhd,khd->hqk", attended_grad, value_heads, preferred_element_type=jnp.float32
    )
    value_grad = jnp.einsum(
        "hqk,qhd->khd",
        attention_weights.astype(jnp.bfloat16),
        attended_grad,
        preferred_element_type=jnp.float32,
    ).astype(jnp.bfloat16)
    score_grad = (
        attention_weights
        * (mass_grad - jnp.sum(attention_weights * mass_grad, axis=-1, keepdims=True))
    ).astype(jnp.bfloat16)
    query_grad = (
        jnp.einsum("hqk,khd->qhd", score_grad, key_heads, preferred_element_type=jnp.float32)
        * score_scale
    ).astype(jnp.bfloat16)
    key_grad = (
        jnp.einsum("hqk,qhd->khd", score_grad, query_heads, preferred_element_type=jnp.float32)
        * score_scale
    ).astype(jnp.bfloat16)
    offset_grad = expand_back(score_grad.astype(jnp.float32))[0]
    table_grad = jnp.dot(bucket_hot.T, offset_grad, precision=lax.Precision.HIGHEST)
    query_flat = query_grad.reshape(tok_rows, col_width)
    key_flat = key_grad.reshape(tok_rows, col_width)
    value_flat = value_grad.reshape(tok_rows, col_width)
    w_query_grad = jnp.einsum(
        "td,tc->dc", normed_one, query_flat, preferred_element_type=jnp.float32
    )
    w_key_grad = jnp.einsum("td,tc->dc", normed_one, key_flat, preferred_element_type=jnp.float32)
    w_value_grad = jnp.einsum(
        "td,tc->dc", normed_one, value_flat, preferred_element_type=jnp.float32
    )
    first_grad = jnp.einsum("tc,dc->td", query_flat, w_query, preferred_element_type=jnp.float32)
    first_grad = first_grad + jnp.einsum(
        "tc,dc->td", key_flat, w_key, preferred_element_type=jnp.float32
    )
    first_grad = first_grad + jnp.einsum(
        "tc,dc->td", value_flat, w_value, preferred_element_type=jnp.float32
    )
    first_grad = lax.psum(first_grad.astype(jnp.bfloat16), "head").astype(jnp.float32)
    gain_one_grad = own_columns(jnp.sum(first_grad * unit_one, axis=0), col_width)
    unit_one_grad = first_grad * gain_one
    input_full = residual_grad + scale_one * (
        unit_one_grad - unit_one * jnp.mean(unit_one_grad * unit_one, axis=-1, keepdims=True)
    )
    input_grad = own_columns(input_full, col_width)
    summed = lax.psum(
        (
            w_query_grad,
            w_key_grad,
            w_value_grad,
            output_grad,
            table_grad,
            gain_one_grad,
            gain_two_grad,
            router_grad,
        ),
        "expert",
    )
    return (
        block_out,
        input_grad,
        aux_loss,
        summed[5],
        summed[0],
        summed[1],
        summed[2],
        summed[3],
        summed[4],
        summed[6],
        summed[7],
        in_weight_grad,
        out_weight_grad,
    )


def solution(mesh):
    return jax.shard_map(
        shards,
        mesh=mesh,
        in_specs=(
            P("expert", "head"),
            P("expert", "head"),
            P("expert"),
            P("expert", None),
            P(),
            P("head"),
            P(None, "head"),
            P(None, "head"),
            P(None, "head"),
            P("head", None),
            P(None, "head"),
            P("head"),
            P(),
            P("expert", None, "head"),
            P("expert", "head", None),
        ),
        out_specs=(
            P("expert", "head"),
            P("expert", "head"),
            P(),
            P("head"),
            P(None, "head"),
            P(None, "head"),
            P(None, "head"),
            P("head", None),
            P(None, "head"),
            P("head"),
            P(),
            P("expert", None, "head"),
            P("expert", "head", None),
        ),
        check_vma=False,
    )
```

profile of v0, /device:TPU:0, one launch (start us, length us, event | category | flops | bytes accessed | tf_op | source)
XLA Modules:
  0.0 374.8 jit_solution(72936010742185421)
XLA Ops:
  7.2 7.2 %all_gather.15 = bf16[128,768]{0,1:T(8,128)(2,1)S(1)} all-gather(bf16[128,192]{0,1:T(8,128)(2,1)} %param.15), channel_id=1, replica_groups=mesh['expert'=8,'head'=4] {'head'}, dimensions={1}, use_global_device_ids=true | all-gather | bytes 245760 | tf_op jit(solution)/shard_map/all_gather | solution.py:82
  14.6 1.2 dynamic-slice
  16.5 0.8 dynamic-update-slice
  17.4 0.8 dynamic-update-slice.1
  18.2 7.3 %all-reduce.6 = (bf16[768]{0:T(1024)(128)(2,1)S(1)}, bf16[768]{0:T(1024)(128)(2,1)S(1)}) all-reduce(bf16[768]{0:T(1024)(128)(2,1)S(1)} %dynamic-update-slice, bf16[768]{0:T(1024)(128)(2,1)S(1)} %dynamic-update-slice.1), channel_id=1, replica_groups=mesh['expert'=8,'head'=4] {'head'}, use_global_device_ids=true, to_apply=%add.2 | all-reduce | flops 1536 | bytes 6144
  25.6 0.9 fusion.37
  30.8 1.0 fusion.57
  32.2 32.6 %all-reduce.11.cloned.1.call-done = f32[128,768]{1,0:T(8,128)} async-done(((f32[128,768]{1,0:T(8,128)}), f32[128,768]{1,0:T(8,128)}) %all-reduce.11.cloned.1.call-update) | async-done | bytes 393232 | tf_op jit(solution)/shard_map/psum | solution.py:124
  64.8 1.1 multiply_reduce_fusion.3
  66.0 1.2 scatter_custom_fusion
  67.3 14.6 %all_to_all.20 = bf16[8,22,768]{2,1,0:T(8,128)(2,1)S(1)} all-to-all(bf16[8,22,768]{2,1,0:T(8,128)(2,1)S(1)} %reshape.145), channel_id=1, replica_groups=mesh['expert'=8,'head'=4] {'expert'}, dimensions={0} | all-to-all | bytes 540672 | tf_op jit(solution)/shard_map/all_to_all | solution.py:25
  83.5 1.7 fusion.2
  85.2 2.2 copy.71
  87.4 3.1 reshape.201
  90.7 18.7 %psum.93 = f32[8]{0:T(128)S(1)} all-reduce(f32[8]{0:T(128)S(1)} %select_reduce_fusion), channel_id=1, replica_groups=mesh['expert'=8,'head'=4] {'expert'}, use_global_device_ids=true, to_apply=%region_15.16 | all-reduce | flops 8 | bytes 64 | tf_op jit(solution)/shard_map/psum | solution.py:133
  109.5 5.6 %all_gather.18 = bf16[128,768]{0,1:T(8,128)(2,1)S(1)} all-gather(bf16[128,192]{0,1:T(8,128)(2,1)S(1)} %copy-done.32), channel_id=1, replica_groups=mesh['expert'=8,'head'=4] {'head'}, dimensions={1}, use_global_device_ids=true | all-gather | bytes 245760 | tf_op jit(solution)/shard_map/all_gather | solution.py:83
  115.4 1.3 reshape.202
  116.7 0.9 copy.72
  117.7 3.4 all-to-all-start.1
  121.3 6.9 %all-to-all-done.1 = bf16[8,22,192]{2,1,0:T(8,128)(2,1)S(1)} async-done(((bf16[8,22,192]{2,1,0:T(8,128)(2,1)}), bf16[8,22,192]{2,1,0:T(8,128)(2,1)S(1)}, u32[]{:S(2)}, u32[]{:S(2)}) %all-to-all-start.1) | async-done | bytes 67616 | tf_op jit(solution)/shard_map/all_to_all | solution.py:31
  128.3 0.8 gather_fusion
  129.3 5.7 %psum.92 = f32[128]{0:T(128)S(1)} all-reduce(f32[128]{0:T(128)S(1)} %fusion.34), channel_id=1, replica_groups=mesh['expert'=8,'head'=4] {'head'}, use_global_device_ids=true, to_apply=%region_13.14 | all-reduce | flops 128 | bytes 1024 | tf_op jit(solution)/shard_map/psum | solution.py:164
  135.7 1.2 scatter_custom_fusion.1
  137.0 13.0 %all_to_all.21 = bf16[8,22,768]{2,1,0:T(8,128)(2,1)S(1)} all-to-all(bf16[8,22,768]{2,1,0:T(8,128)(2,1)S(1)} %reshape.148), channel_id=1, replica_groups=mesh['expert'=8,'head'=4] {'expert'}, dimensions={0} | all-to-all | bytes 540672 | tf_op jit(solution)/shard_map/all_to_all | solution.py:25
  150.1 2.0 fusion.19
  153.5 2.2 copy.73
  155.8 3.1 reshape.203
  158.9 21.2 %reduce-scatter.9.cloned.1.call-done = f32[192,176]{1,0:T(8,128)} async-done(((f32[768,176]{1,0:T(8,128)}), f32[192,176]{1,0:T(8,128)}) %reduce-scatter.9.cloned.1.call-update) | async-done | bytes 135184
  180.2 1.2 reshape.204
  181.7 12.4 %all_to_all.22 = bf16[8,22,192]{2,1,0:T(8,128)(2,1)S(1)} all-to-all(bf16[8,22,192]{2,1,0:T(8,128)(2,1)S(1)} %copy.74), channel_id=1, replica_groups=mesh['expert'=8,'head'=4] {'expert'}, dimensions={0} | all-to-all | bytes 135168 | tf_op jit(solution)/shard_map/all_to_all | solution.py:31
  194.1 1.0 copy.59
  195.1 12.1 %all_gather.19 = bf16[8,22,768]{1,0,2:T(8,128)(2,1)S(1)} all-gather(bf16[8,22,192]{1,0,2:T(8,128)(2,1)} %copy.59), channel_id=1, replica_groups=mesh['expert'=8,'head'=4] {'head'}, dimensions={2}, use_global_device_ids=true | all-gather | bytes 337920 | tf_op jit(solution)/shard_map/all_gather | solution.py:179
  207.3 1.7 copy.60
  209.0 1.1 reshape.150
  210.1 1.1 gather_fusion.1
  213.9 1.1 fusion.51
  215.0 1.0 fusion.38
  216.0 1.1 fusion.52
  217.4 0.9 fusion.8
  218.4 1.1 fusion.53
  221.4 1.9 convolution_bitcast_fusion.1
  223.3 1.9 convolution_bitcast_fusion
  227.1 20.9 %all-reduce.13.cloned.1.call-done = bf16[128,768]{1,0:T(8,128)(2,1)} async-done(((bf16[128,768]{1,0:T(8,128)(2,1)}), bf16[128,768]{1,0:T(8,128)(2,1)}) %all-reduce.13.cloned.1.call-update) | async-done | bytes 196624 | tf_op jit(solution)/shard_map/psum | solution.py:248
  247.9 1.2 fusion.23
  249.2 39.6 %all-reduce.4 = (f32[8]{0:T(128)S(1)}, f32[192]{0:T(256)}, f32[32,3]{0,1:T(4,128)}, f32[192]{0:T(256)}, f32[768,8]{0,1:T(8,128)}) all-reduce(f32[8]{0:T(128)S(1)} %copy-done.57, f32[192]{0:T(256)S(1)} %dynamic_slice.14, f32[32,3]{0,1:T(4,128)S(1)} %fusion.36, ...), channel_id=1, replica_groups=mesh['expert'=8,'head'=4] {'expert'}, use_global_device_ids=true, to_apply=%region_24.25 | all-reduce | flops 6632 | bytes 53056 | tf_op jit(solution)/shard_map/psum | solution.py:133
  291.0 71.7 %all-reduce.15.cloned.1.call-done = (f32[768,192]{0,1:T(8,128)}, f32[768,192]{0,1:T(8,128)}, f32[768,192]{0,1:T(8,128)}, f32[192,768]{1,0:T(8,128)}) async-done(((f32[768,192]{0,1:T(8,128)}, f32[768,192]{0,1:T(8,128)}, f32[768,192]{0,1:T(8,128)}, f32[192,768]{1,0:T(8,128)}), (f32[768,192]{0,1:T(8,128)}, f32[768,192]{0,1:T(8,128)}, f32[768,192]{0,1:T(8,128)}, ...) | async-done | bytes 2359312 | tf_op jit(solution)/shard_map/psum | solution.py:255
  362.7 2.0 copy.92
  365.5 0.8 copy.94
  (216 shorter events, 18.9 us)
Async XLA Ops:
  7.2 74.8 %copy-start = (bf16[1,768,768]{2,1,0:T(8,128)(2,1)S(1)}, bf16[1,768,768]{2,1,0:T(8,128)(2,1)}, u32[]{:S(2)}) copy-start(bf16[1,768,768]{2,1,0:T(8,128)(2,1)} %param.28) | copy-start | bytes 3538948
  7.2 57.6 %all-reduce.11.cloned.1.call-start = ((), (), s32[]{:S(2)}) async-start(), calls=%async_computation.6 | async-start | bytes 786432 | tf_op jit(solution)/shard_map/psum | solution.py:124
  25.6 3.5 copy-start.37
  28.8 1.8 copy-start.33
  28.8 1.9 copy-start.3
  29.5 2.6 copy-start.30
  29.5 2.3 copy-start.41
  31.8 83.7 %reduce-scatter.7.cloned.1.call-start = ((), (), s32[]{:S(2)}) async-start(), calls=%async_computation.8 | async-start | bytes 983040
  65.9 49.3 %copy-start.43 = (f32[128]{0:T(128)}, f32[128]{0:T(128)S(1)}, u32[]{:S(2)}) copy-start(f32[128]{0:T(128)S(1)} %add_rsqrt_fusion) | copy-start | bytes 1540
  87.4 22.0 %copy-start.32 = (bf16[128,192]{0,1:T(8,128)(2,1)S(1)}, bf16[128,192]{0,1:T(8,128)(2,1)}, u32[]{:S(2)}) copy-start(bf16[128,192]{0,1:T(8,128)(2,1)} %param.16) | copy-start | bytes 147460
  90.5 44.4 %copy-start.50 = (f32[128]{0:T(128)}, f32[128]{0:T(128)S(1)}, u32[]{:S(2)}) copy-start(f32[128]{0:T(128)S(1)} %fusion.49) | copy-start | bytes 1540
  109.3 8.3 %copy-start.59 = (f32[8]{0:T(128)}, f32[8]{0:T(128)S(1)}, u32[]{:S(2)}) copy-start(f32[8]{0:T(128)S(1)} %psum.93) | copy-start | bytes 100
  115.1 6.0 %copy-start.35 = (bf16[768,8]{0,1:T(8,128)(2,1)S(1)}, bf16[768,8]{0,1:T(8,128)(2,1)}, u32[]{:S(2)}) copy-start(bf16[768,8]{0,1:T(8,128)(2,1)} %param.27) | copy-start | bytes 36868
  115.2 20.4 %copy-start.1 = (bf16[128,768]{1,0:T(8,128)(2,1)}, bf16[128,768]{1,0:T(8,128)(2,1)S(1)}, u32[]{:S(2)}) copy-start(bf16[128,768]{1,0:T(8,128)(2,1)S(1)} %copy.57) | copy-start | bytes 589828
  115.2 13.9 %copy-start.45 = (s32[1024]{0:T(1024)}, s32[1024]{0:T(1024)S(1)}, u32[]{:S(2)}) copy-start(s32[1024]{0:T(1024)S(1)} %pad_clamp_fusion) | copy-start | bytes 12292
  115.3 19.7 %copy-start.52 = (f32[8]{0:T(128)}, f32[8]{0:T(128)S(1)}, u32[]{:S(2)}) copy-start(f32[8]{0:T(128)S(1)} %broadcast_multiply_fusion) | copy-start | bytes 100
  115.4 13.9 %copy-start.13 = (bf16[128,768]{1,0:T(8,128)(2,1)}, bf16[128,768]{1,0:T(8,128)(2,1)S(1)}, u32[]{:S(2)}) copy-start(bf16[128,768]{1,0:T(8,128)(2,1)S(1)} %multiply_convert_fusion.1) | copy-start | bytes 589828
  117.7 10.6 %all-to-all-start.1 = ((bf16[8,22,192]{2,1,0:T(8,128)(2,1)}), bf16[8,22,192]{2,1,0:T(8,128)(2,1)S(1)}, u32[]{:S(2)}, u32[]{:S(2)}) async-start(bf16[8,22,192]{2,1,0:T(8,128)(2,1)} %copy.72), calls=%async_computation.1 | async-start | bytes 196608 | tf_op jit(solution)/shard_map/all_to_all | solution.py:31
  121.0 59.1 %reduce-scatter.9.cloned.1.call-start = ((), (), s32[]{:S(2)}) async-start(), calls=%async_computation.9 | async-start | bytes 983040
  121.2 14.4 %copy-start.39 = (f32[128]{0:T(128)}, f32[128]{0:T(128)S(1)}, u32[]{:S(2)}) copy-start(f32[128]{0:T(128)S(1)} %get-tuple-element.78) | copy-start | bytes 1540
  121.3 28.7 %copy-start.46 = (f32[128]{0:T(128)}, f32[128]{0:T(128)S(1)}, u32[]{:S(2)}) copy-start(f32[128]{0:T(128)S(1)} %fusion.47) | copy-start | bytes 1540
  129.2 6.5 %copy-start.18 = (bf16[128,192]{1,0:T(8,128)(2,1)}, bf16[128,192]{1,0:T(8,128)(2,1)S(1)}, u32[]{:S(2)}) copy-start(bf16[128,192]{1,0:T(8,128)(2,1)S(1)} %gather_fusion) | copy-start | bytes 147460
  135.0 15.1 %copy-start.54 = (f32[128]{0:T(128)}, f32[128]{0:T(128)S(1)}, u32[]{:S(2)}) copy-start(f32[128]{0:T(128)S(1)} %psum.92) | copy-start | bytes 1540
  135.7 14.5 %copy-start.48 = (f32[128]{0:T(128)}, f32[128]{0:T(128)S(1)}, u32[]{:S(2)}) copy-start(f32[128]{0:T(128)S(1)} %get-tuple-element.58) | copy-start | bytes 1540
  150.1 2.1 copy-start.9
  158.9 89.0 %all-reduce.13.cloned.1.call-start = ((), (), s32[]{:S(2)}) async-start(), calls=%async_computation.7 | async-start | bytes 393216 | tf_op jit(solution)/shard_map/psum | solution.py:248
  208.9 2.3 copy-start.36
  208.9 2.3 copy-start.40
  208.9 2.3 copy-start.42
  208.9 2.3 copy-start.44
  208.9 2.3 copy-start.47
  208.9 2.3 copy-start.51
  209.0 2.3 copy-start.53
  209.0 2.3 copy-start.55
  209.0 2.3 copy-start.56
  210.0 1.7 copy-start.2
  213.0 2.0 copy-start.21
  213.9 3.3 copy-start.27
  218.3 144.4 %all-reduce.15.cloned.1.call-start = ((), (), s32[]{:S(2)}) async-start(), calls=%async_computation.10 | async-start | bytes 4718592 | tf_op jit(solution)/shard_map/psum | solution.py:255
  219.5 1.7 copy-start.14
  219.5 1.9 copy-start.6
  219.5 1.9 copy-start.12
  221.4 1.9 copy-start.8
  221.4 1.9 copy-start.10
  225.9 23.2 %copy-start.57 = (f32[8]{0:T(128)S(1)}, f32[8]{0:T(128)}, u32[]{:S(2)}) copy-start(f32[8]{0:T(128)} %get-tuple-element.56) | copy-start | bytes 100
  226.5 63.3 %copy-start.60 = (f32[8]{0:T(128)S(1)}, f32[8]{0:T(128)}, u32[]{:S(2)}) copy-start(f32[8]{0:T(128)} %copy-done.59) | copy-start | bytes 100
  362.7 2.0 copy-start.17
  362.7 2.8 copy-start.16
  (19 other events, 20.7 us)
Sparse Core Ops, SparseCore 0:
  31.9 32.8 all-reduce.10
  90.6 21.1 reduce-scatter.6
  159.0 21.1 reduce-scatter.8
  218.5 29.3 all-reduce.12
  252.3 110.3 all-reduce.14
where the time goes:
time: 376 us; the launch traced here: 375 us
  waiting for transfers between devices  153 us (41%)
  blocking collectives  136 us (36%)
  local copies, waits for them, and re-layouts  36.7 us (10%)
  matrix products  19.6 us (5%)
  between operations  17.9 us (5%)
  other arithmetic  7.46 us (2%)
    psum x1, waiting for transfers between devices, shards(): lax.psum((w_query_grad, w_key_grad, w_value_grad, output_grad, table_grad...  71.7 us
    psum x2, blocking collectives, shards(): lax.psum((jnp.sum(route_hot * valid_rows[:, None], axis=0), jnp.sum(route...  58.3 us
    psum x1, waiting for transfers between devices, shards(): residual = inputs_wide + lax.psum(attn_part, 'head')  32.6 us
    unnamed x149, local copies, waits for them, and re-layouts  28.3 us
    all_to_all x2, blocking collectives, to_owner(): lax.all_to_all(buffer, 'expert', split_axis=0, concat_axis=0, tiled=True)  27.6 us
    unnamed x7, waiting for transfers between devices  21.3 us
    psum x1, waiting for transfers between devices, shards(): lax.psum(first_grad.astype(jnp.bfloat16), 'head').astype(jnp.float32)  20.9 us
    all_to_all x1, blocking collectives, from_owner(): lax.all_to_all(shared.astype(jnp.bfloat16), 'expert', split_axis=0, conca...  12.4 us
  transfers between devices with their start and end apart: 6, of which 5 were waited for; matrix products, arithmetic and copies ran while one was open for 3% of the time, Pallas kernels for 0%

commit v1 on v0

v1 whole, which is shorter than its diff:
```python
import jax
import jax.numpy as jnp
from jax import lax
from jax.sharding import PartitionSpec as P

eps = 1e-06
aux_weight = 0.01
f32 = jnp.float32
bf16 = jnp.bfloat16


def swap(block, axis, offset):
    size = lax.axis_size(axis)
    return lax.ppermute(block, axis, [(i, i ^ offset) for i in range(size)])


def mm(left, right, dims=((1,), (0,))):
    return lax.dot_general(left, right, (dims, ((), ())), preferred_element_type=f32)


def rms_scale(values):
    return lax.rsqrt(jnp.mean(values * values, axis=-1, keepdims=True) + eps)


def smooth(values):
    return jax.nn.gelu(values, approximate=True)


def gather_head(block):
    size = lax.axis_size("head")
    parts = jnp.stack([block] + [swap(block, "head", k) for k in range(1, size)])
    return parts[jnp.arange(size) ^ lax.axis_index("head")]


def widen(parts):
    count, rows, cols = parts.shape
    return jnp.transpose(parts, (1, 0, 2)).reshape(rows, count * cols)


def column_parts(matrix, count):
    rows, cols = matrix.shape
    return jnp.transpose(matrix.reshape(rows, count, cols // count), (1, 0, 2))


def sum_scatter_head(parts):
    size, me = lax.axis_size("head"), lax.axis_index("head")
    total = parts[me].astype(f32)
    for k in range(1, size):
        total = total + swap(parts[me ^ k].astype(bf16), "head", k).astype(f32)
    return total


def few_experts():
    return lax.axis_size("expert") <= 8


def exchange(blocks):
    if few_experts():
        return jnp.stack([blocks[0]] + [swap(blocks[k], "expert", k) for k in range(1, blocks.shape[0])])
    return lax.all_to_all(blocks, "expert", split_axis=0, concat_axis=0, tiled=True)


def gather_expert(block):
    if few_experts():
        return jnp.stack([block] + [swap(block, "expert", k) for k in range(1, lax.axis_size("expert"))])
    return lax.all_gather(block, "expert", axis=0)


def sum_expert(block):
    if few_experts():
        return jnp.sum(gather_expert(block).astype(f32), axis=0)
    return lax.psum(block.astype(f32), "expert")


def diagonal_spread(offsets, tok_rows):
    heads_here = offsets.shape[1]
    reversed_rows = jnp.transpose(offsets[::-1], (1, 0))
    tiled = jnp.broadcast_to(reversed_rows[:, None, :], (heads_here, tok_rows, 2 * tok_rows - 1))
    flat = tiled.reshape(heads_here, tok_rows * (2 * tok_rows - 1))
    flat = jnp.pad(flat, ((0, 0), (0, tok_rows)))
    skewed = flat.reshape(heads_here, tok_rows, 2 * tok_rows)[:, :, :tok_rows]
    return skewed[:, :, ::-1]


def shards(
    inputs,
    out_grad,
    lengths,
    routes,
    buckets,
    gain_attn,
    w_query,
    w_key,
    w_value,
    w_output,
    bias_table,
    gain_ffn,
    w_router,
    w_in,
    w_out,
):
    tok_rows, col_width = inputs.shape
    heads_here = bias_table.shape[1]
    head_size = w_query.shape[1] // heads_here
    model_width = w_query.shape[0]
    experts = w_router.shape[1]
    bucket_count = bias_table.shape[0]
    head_count = model_width // col_width
    me_head, me_expert = lax.axis_index("head"), lax.axis_index("expert")
    capacity = max(2, (4 * tok_rows + 3 * experts - 1) // (3 * experts))
    slots = -(-capacity // 8) * 8
    valid_total = 3 * tok_rows * lax.axis_size("expert") // 4
    score_scale = head_size ** (-0.5)
    positions = jnp.arange(tok_rows)
    w_in, w_out = w_in[0], w_out[0]

    valid_rows = (positions < lengths[0]).astype(f32)
    expert_ids = jnp.arange(experts)[None, :]
    route_hot = (routes == expert_ids).astype(f32)
    counts = jnp.sum(route_hot * valid_rows[:, None], axis=0)
    fraction = sum_expert(counts) / valid_total
    route_int = (routes == expert_ids).astype(jnp.int32)
    earlier = jnp.cumsum(route_int, axis=0, dtype=jnp.int32) - route_int
    slot = jnp.sum(earlier * route_int, axis=1)
    place = (routes[:, 0] ^ me_expert) if few_experts() else routes[:, 0]
    spots = place * slots + slot
    spot_hot = (spots[:, None] == jnp.arange(experts * slots)[None, :]).astype(bf16)

    packed = jnp.concatenate([inputs, out_grad, gain_attn[None], gain_ffn[None]], axis=0)
    packed = gather_head(packed)
    full_in = widen(packed[:, :tok_rows])
    full_grad = widen(packed[:, tok_rows : 2 * tok_rows])
    gain_one = packed[:, 2 * tok_rows].reshape(1, model_width).astype(f32)
    gain_two = packed[:, 2 * tok_rows + 1].reshape(1, model_width).astype(f32)
    w_output_full = gather_head(w_output).reshape(model_width, model_width)
    all_in = lax.all_gather(inputs, ("expert", "head"), axis=0) if few_experts() else None

    inputs_wide = full_in.astype(f32)
    scale_one = rms_scale(inputs_wide)
    unit_one = inputs_wide * scale_one
    normed_one = (unit_one * gain_one).astype(bf16)
    w_qkv = jnp.concatenate([w_query, w_key, w_value], axis=1)
    qkv = mm(normed_one, w_qkv).astype(bf16)
    query_heads, key_heads, value_heads = (
        qkv[:, i * col_width : (i + 1) * col_width].reshape(tok_rows, heads_here, head_size)
        for i in range(3)
    )
    bucket_hot = (buckets[:, None] == jnp.arange(bucket_count)[None, :]).astype(f32)
    offset_bias = jnp.dot(bucket_hot, bias_table, precision=lax.Precision.HIGHEST)
    bias_full, expand_back = jax.vjp(lambda o: diagonal_spread(o, tok_rows), offset_bias)
    key_mask = (positions < lengths[0])[None, None, :]
    scores = (
        jnp.einsum("qhd,khd->hqk", query_heads, key_heads, preferred_element_type=f32)
        * score_scale
        + bias_full
    )
    scores = jnp.where(key_mask, scores, -1000000000.0)
    raised = jnp.exp(scores - jnp.max(scores, axis=-1, keepdims=True))
    attention_weights = raised / jnp.sum(raised, axis=-1, keepdims=True)
    weights_low = attention_weights.astype(bf16)
    attended = jnp.einsum("hqk,khd->qhd", weights_low, value_heads, preferred_element_type=f32)
    attended = attended.reshape(tok_rows, col_width).astype(bf16)

    attended_parts = gather_head(attended)
    if few_experts():
        all_attended = lax.all_gather(attended, ("expert", "head"), axis=0)
    residual = inputs_wide + mm(widen(attended_parts), w_output_full)
    scale_two = rms_scale(residual)
    unit_two = residual * scale_two
    normed_two = (unit_two * gain_two).astype(bf16)
    logits = mm(normed_two, w_router)
    router_weights = jax.nn.softmax(logits, axis=-1)
    gate_value = jnp.sum(router_weights * route_hot, axis=1)
    prob_sums = jnp.sum(router_weights * valid_rows[:, None], axis=0)

    def dispatch(rows):
        placed = mm(spot_hot, rows, ((0,), (0,))).astype(bf16)
        return exchange(placed.reshape(experts, slots, model_width)).reshape(-1, model_width)

    grad_rows = dispatch(full_grad)
    expert_rows = dispatch(normed_two)
    before_act = mm(expert_rows, w_in)
    act, act_back = jax.vjp(smooth, before_act)
    hidden = act.astype(bf16)
    expert_part = mm(hidden, w_out)
    row_probs = jax.nn.softmax(mm(expert_rows, w_router), axis=-1)
    row_gate = lax.dynamic_slice_in_dim(row_probs, me_expert, 1, 1)
    grad_rows_wide = grad_rows.astype(f32)
    back_rows = (row_gate * grad_rows_wide).astype(bf16)
    gate_part = jnp.sum(grad_rows_wide * expert_part, axis=1, keepdims=True)
    hidden_grad = mm(back_rows, w_out, ((1,), (1,)))
    before_grad = act_back(hidden_grad)[0].astype(bf16)
    rows_part = mm(before_grad, w_in, ((1,), (1,)))
    out_weight_grad = mm(hidden, back_rows, ((0,), (0,)))[None]
    in_weight_grad = mm(expert_rows, before_grad, ((0,), (0,)))[None]

    gate_high = gate_part.astype(bf16).astype(f32)
    gate_low = gate_part - gate_high
    pad = jnp.zeros((experts * slots, 62), f32)
    extra = jnp.concatenate([gate_high, gate_low, pad], axis=1)
    extra = jnp.broadcast_to(extra[None], (head_count,) + extra.shape)
    parts = jnp.concatenate(
        [column_parts(rows_part, head_count), column_parts(expert_part, head_count), extra], axis=2
    )
    own_sum = sum_scatter_head(parts)
    gate_sum = own_sum[:, 2 * col_width : 2 * col_width + 1] + own_sum[:, 2 * col_width + 1 : 2 * col_width + 2]
    gate_high = gate_sum.astype(bf16)
    gate_low = (gate_sum - gate_high.astype(f32)).astype(bf16)
    message = jnp.concatenate(
        [own_sum[:, : 2 * col_width].astype(bf16), gate_high, gate_low, pad.astype(bf16)], axis=1
    )
    came = exchange(message.reshape(experts, slots, -1)).reshape(experts * slots, -1)
    came = mm(spot_hot, came)
    expert_grad_own = came[:, :col_width].astype(bf16)
    returned = came[:, col_width : 2 * col_width]
    gate_grad = came[:, 2 * col_width] + came[:, 2 * col_width + 1]
    expert_grad = widen(gather_head(expert_grad_own)).astype(f32)
    residual_own = lax.dynamic_index_in_dim(column_parts(residual, head_count), me_head, 0, False)
    block_out = (residual_own + gate_value[:, None] * returned).astype(bf16)

    prob_grad = (
        route_hot * gate_grad[:, None]
        + aux_weight * experts * fraction[None, :] * valid_rows[:, None] / valid_total
    )
    logit_grad = (
        router_weights * (prob_grad - jnp.sum(router_weights * prob_grad, axis=1, keepdims=True))
    ).astype(bf16)
    router_grad = mm(logit_grad, normed_two, ((0,), (0,)))
    normed_grad = mm(logit_grad, w_router, ((1,), (1,))) + expert_grad
    gain_two_grad = jnp.sum(normed_grad * unit_two, axis=0)
    unit_grad = normed_grad * gain_two
    residual_grad = full_grad.astype(f32) + scale_two * (
        unit_grad - unit_two * jnp.mean(unit_grad * unit_two, axis=-1, keepdims=True)
    )
    branch_grad = residual_grad.astype(bf16)
    branch_own = lax.dynamic_index_in_dim(column_parts(branch_grad, head_count), me_head, 0, False)

    attended_grad = mm(branch_grad, w_output, ((1,), (1,))).astype(bf16)
    attended_grad = attended_grad.reshape(tok_rows, heads_here, head_size)
    mass_grad = jnp.einsum("qhd,khd->hqk", attended_grad, value_heads, preferred_element_type=f32)
    value_grad = jnp.einsum("hqk,qhd->khd", weights_low, attended_grad, preferred_element_type=f32)
    score_grad = (
        attention_weights
        * (mass_grad - jnp.sum(attention_weights * mass_grad, axis=-1, keepdims=True))
    ).astype(bf16)
    query_grad = (
        jnp.einsum("hqk,khd->qhd", score_grad, key_heads, preferred_element_type=f32) * score_scale
    )
    key_grad = (
        jnp.einsum("hqk,qhd->khd", score_grad, query_heads, preferred_element_type=f32)
        * score_scale
    )
    qkv_grad = jnp.concatenate(
        [g.reshape(tok_rows, col_width).astype(bf16) for g in (query_grad, key_grad, value_grad)],
        axis=1,
    )
    offset_grad = expand_back(score_grad.astype(f32))[0]
    table_part = jnp.dot(bucket_hot.T, offset_grad, precision=lax.Precision.HIGHEST)

    def in_arrival_order(blocks):
        blocks = blocks.reshape((lax.axis_size("expert"), head_count, tok_rows, col_width))
        blocks = blocks[jnp.arange(blocks.shape[0]) ^ me_expert]
        return jnp.transpose(blocks, (0, 2, 1, 3)).reshape(-1, model_width)

    if few_experts():
        all_late = gather_expert(jnp.concatenate([qkv_grad, branch_own], axis=1))
        all_in = in_arrival_order(all_in).astype(f32)
        all_normed = (all_in * rms_scale(all_in) * gain_one).astype(bf16)
        all_late = all_late.reshape(-1, 4 * col_width)
        qkv_weight_grad = mm(all_normed, all_late[:, : 3 * col_width], ((0,), (0,)))
        output_cols = mm(in_arrival_order(all_attended), all_late[:, 3 * col_width :], ((0,), (0,)))
        output_parts = output_cols.astype(bf16).reshape(head_count, col_width, col_width)
        traded = jnp.stack(
            [output_parts[me_head]]
            + [swap(output_parts[me_head ^ k], "head", k) for k in range(1, head_count)]
        )[jnp.arange(head_count) ^ me_head]
        output_grad = widen(traded).astype(f32)
    else:
        qkv_weight_grad = sum_expert(mm(normed_one, qkv_grad, ((0,), (0,))))
        output_grad = sum_expert(mm(attended, branch_grad, ((0,), (0,))))

    first_part = mm(qkv_grad, w_qkv, ((1,), (1,)))
    row_part = jnp.sum(qkv_grad.astype(f32) * qkv.astype(f32), axis=1, keepdims=True)
    row_high = row_part.astype(bf16).astype(f32)
    extra = jnp.concatenate([row_high, row_part - row_high, jnp.zeros((tok_rows, 62), f32)], axis=1)
    extra = jnp.broadcast_to(extra[None], (head_count,) + extra.shape)
    own_first = sum_scatter_head(
        jnp.concatenate([column_parts(first_part, head_count), extra], axis=2)
    )
    first_own = own_first[:, :col_width]
    row_mean = (own_first[:, col_width] + own_first[:, col_width + 1])[:, None] / model_width
    unit_own = inputs.astype(f32) * scale_one
    gain_one_part = jnp.sum(first_own * unit_own, axis=0)
    residual_grad_own = lax.dynamic_index_in_dim(
        column_parts(residual_grad, head_count), me_head, 0, False
    )
    input_grad = residual_grad_own + scale_one * (
        first_own * gain_attn.astype(f32)[None, :] - unit_own * row_mean
    )

    gain_two_own = lax.dynamic_slice_in_dim(gain_two_grad, me_head * col_width, col_width)
    small = jnp.concatenate(
        [prob_sums, gain_two_own, table_part.reshape(-1), router_grad.reshape(-1)]
    )
    small = sum_expert(small)
    prob_sums = small[:experts]
    gain_two_grad = small[experts : experts + col_width]
    at = experts + col_width
    table_grad = small[at : at + table_part.size].reshape(table_part.shape)
    router_grad = small[at + table_part.size :].reshape(experts, model_width).T
    gain_one_grad = sum_expert(gain_one_part)
    aux_loss = experts * jnp.sum(fraction * (prob_sums / valid_total))
    return (
        block_out,
        input_grad,
        aux_loss,
        gain_one_grad,
        qkv_weight_grad[:, :col_width],
        qkv_weight_grad[:, col_width : 2 * col_width],
        qkv_weight_grad[:, 2 * col_width :],
        output_grad,
        table_grad,
        gain_two_grad,
        router_grad,
        in_weight_grad,
        out_weight_grad,
    )


def solution(mesh):
    return jax.shard_map(
        shards,
        mesh=mesh,
        in_specs=(
            P("expert", "head"),
            P("expert", "head"),
            P("expert"),
            P("expert", None),
            P(),
            P("head"),
            P(None, "head"),
            P(None, "head"),
            P(None, "head"),
            P("head", None),
            P(None, "head"),
            P("head"),
            P(),
            P("expert", None, "head"),
            P("expert", "head", None),
        ),
        out_specs=(
            P("expert", "head"),
            P("expert", "head"),
            P(),
            P("head"),
            P(None, "head"),
            P(None, "head"),
            P(None, "head"),
            P("head", None),
            P(None, "head"),
            P("head"),
            P(),
            P("expert", None, "head"),
            P("expert", "head", None),
        ),
        check_vma=False,
    )
```

time: 376 us -> 300 us (0.80)
  blocking collectives: 136 us -> 0 us
  starting transfers between devices: 3.57 us -> 101 us
  waiting for transfers between devices: 153 us -> 79.8 us
  other arithmetic: 7.46 us -> 28.1 us
  local copies, waits for them, and re-layouts: 36.7 us -> 43.3 us
  matrix products: 19.6 us -> 25.3 us
    psum x3 -> x0, waiting for transfers between devices: 125 us -> none  [the longest x1 71.7 us: shards(): lax.psum((w_query_grad, w_key_grad, w_value_grad, output_grad, table_grad...]
    ppermute x0 -> x70, starting transfers between devices: none -> 101 us  [swap(): return lax.ppermute(block, axis, [(i, i ^ offset) for i in range(size)])]
    ppermute x0 -> x70, waiting for transfers between devices: none -> 79.7 us  [swap(): return lax.ppermute(block, axis, [(i, i ^ offset) for i in range(size)])]
    psum x3 -> x0, blocking collectives: 64 us -> none  [the longest x2 58.3 us: shards(): lax.psum((jnp.sum(route_hot * valid_rows[:, None], axis=0), jnp.sum(route...]
    all_to_all x3 -> x0, blocking collectives: 40.1 us -> none  [the longest x2 27.6 us: to_owner(): lax.all_to_all(buffer, 'expert', split_axis=0, concat_axis=0, tiled=True)]
    all_gather x3 -> x0, blocking collectives: 24.9 us -> none  [the longest x1 12.1 us: shards(): lax.all_gather(came_back, 'head', axis=2, tiled=True)]
    unnamed x7 -> x2, waiting for transfers between devices: 21.3 us -> 0.03 us
    unnamed x149, local copies, waits for them, and re-layouts: 28.3 us -> 7.09 us
  transfers between devices with their start and end apart: 6 -> 72, of which waited for: 5 -> 28; matrix products, arithmetic and copies ran while one was open for 3% -> 28% of each run, Pallas kernels for 0% -> 0%
where the time goes in v1:
time: 300 us; the launch traced here: 295 us
  starting transfers between devices  101 us (34%)
  waiting for transfers between devices  79.8 us (27%)
  local copies, waits for them, and re-layouts  43.3 us (14%)
  other arithmetic  28.1 us (9%)
  matrix products  25.3 us (8%)
  between operations  18 us (6%)
    ppermute x70, starting transfers between devices, swap(): return lax.ppermute(block, axis, [(i, i ^ offset) for i in range(size)])  101 us
    ppermute x70, waiting for transfers between devices, swap(): return lax.ppermute(block, axis, [(i, i ^ offset) for i in range(size)])  79.7 us
    dot_general x19, matrix products, mm(): lax.dot_general(left, right, (dims, ((), ())), preferred_element_type=f32)  21.9 us
    unnamed x149, local copies, waits for them, and re-layouts  7.09 us
    another operation x5, other arithmetic, gather_head(): jnp.stack([block] + [swap(block, 'head', k) for k in range(1, size)])  6.17 us
    gather x4, local copies, waits for them, and re-layouts, gather_head(): return parts[jnp.arange(size) ^ lax.axis_index('head')]  6.09 us
  transfers between devices with their start and end apart: 72, of which 28 were waited for; matrix products, arithmetic and copies ran while one was open for 28% of the time, Pallas kernels for 0%

profile of v1, /device:TPU:0, one launch (start us, length us, event | category | flops | bytes accessed | tf_op | source)
XLA Modules:
  0.0 295.1 jit_solution(17475970344833646082)
XLA Ops:
  10.4 2.4 collective-permute-start.2
  15.5 4.8 %collective-permute-start.39 = (f32[8]{0:T(128)S(1)}, f32[8]{0:T(128)S(1)}, u32[]{:S(2)}, u32[]{:S(2)}) collective-permute-start(f32[8]{0:T(128)S(1)} %select_reduce_fusion), channel_id=1, source_target_pairs={{0,28},{4,24},{8,20},{12,16},{16,12},{20,8},{24,4},{28,0},{1,29},{... | collective-permute-start | bytes 104 | tf_op jit(solution)/shard_map/ppermute | solution.py:14
  30.7 2.0 collective-permute-start.36
  32.7 2.6 collective-permute-done.37
  40.2 3.1 %collective-permute-done.33 = f32[8]{0:T(128)S(1)} collective-permute-done((f32[8]{0:T(128)S(1)}, f32[8]{0:T(128)S(1)}, u32[]{:S(2)}, u32[]{:S(2)}) %collective-permute-start.33) | collective-permute-done | bytes 64 | tf_op jit(solution)/shard_map/ppermute | solution.py:14
  45.4 2.0 pad_maximum_fusion.2
  57.6 2.0 collective-permute-done.17
  61.0 3.8 %collective-permute-done.18 = bf16[24,768]{1,0:T(8,128)(2,1)S(1)} collective-permute-done((bf16[24,768]{1,0:T(8,128)(2,1)}, bf16[24,768]{1,0:T(8,128)(2,1)S(1)}, u32[]{:S(2)}, u32[]{:S(2)}) %collective-permute-start.18) | collective-permute-done | bytes 36896 | tf_op jit(solution)/shard_map/ppermute | solution.py:14
  64.8 4.3 %collective-permute-start.19 = (bf16[24,768]{1,0:T(8,128)(2,1)}, bf16[24,768]{1,0:T(8,128)(2,1)S(1)}, u32[]{:S(2)}, u32[]{:S(2)}) collective-permute-start(bf16[24,768]{1,0:T(8,128)(2,1)} %get-tuple-element.154), channel_id=1, source_target_pairs={{0,16},{4,20},{8,24},{12,28},{16,0},{20,4},{24,8},{28,12},{1,17},{... | collective-permute-start | bytes 110600 | tf_op jit(solution)/shard_map/ppermute | solution.py:14
  69.0 2.6 collective-permute-done.19
  71.6 2.7 collective-permute-start.20
  74.3 3.6 %collective-permute-done.20 = bf16[24,768]{1,0:T(8,128)(2,1)S(1)} collective-permute-done((bf16[24,768]{1,0:T(8,128)(2,1)}, bf16[24,768]{1,0:T(8,128)(2,1)S(1)}, u32[]{:S(2)}, u32[]{:S(2)}) %collective-permute-start.20) | collective-permute-done | bytes 36896 | tf_op jit(solution)/shard_map/ppermute | solution.py:14
  77.9 4.8 %collective-permute-start.21 = (bf16[24,768]{1,0:T(8,128)(2,1)}, bf16[24,768]{1,0:T(8,128)(2,1)S(1)}, u32[]{:S(2)}, u32[]{:S(2)}) collective-permute-start(bf16[24,768]{1,0:T(8,128)(2,1)} %get-tuple-element.152), channel_id=1, source_target_pairs={{0,24},{4,28},{8,16},{12,20},{16,8},{20,12},{24,0},{28,4},{1,25},{... | collective-permute-start | bytes 110600 | tf_op jit(solution)/shard_map/ppermute | solution.py:14
  82.7 2.5 collective-permute-done.21
  85.2 3.6 %collective-permute-start.22 = (bf16[24,768]{1,0:T(8,128)(2,1)}, bf16[24,768]{1,0:T(8,128)(2,1)S(1)}, u32[]{:S(2)}, u32[]{:S(2)}) collective-permute-start(bf16[24,768]{1,0:T(8,128)(2,1)} %get-tuple-element.151), channel_id=1, source_target_pairs={{0,28},{4,24},{8,20},{12,16},{16,12},{20,8},{24,4},{28,0},{1,29},{... | collective-permute-start | bytes 110600 | tf_op jit(solution)/shard_map/ppermute | solution.py:14
  88.8 3.3 %collective-permute-done.22 = bf16[24,768]{1,0:T(8,128)(2,1)S(1)} collective-permute-done((bf16[24,768]{1,0:T(8,128)(2,1)}, bf16[24,768]{1,0:T(8,128)(2,1)S(1)}, u32[]{:S(2)}, u32[]{:S(2)}) %collective-permute-start.22) | collective-permute-done | bytes 36896 | tf_op jit(solution)/shard_map/ppermute | solution.py:14
  93.4 3.0 %collective-permute-done.4 = bf16[128,192]{0,1:T(8,128)(2,1)S(1)} collective-permute-done((bf16[128,192]{0,1:T(8,128)(2,1)}, bf16[128,192]{0,1:T(8,128)(2,1)S(1)}, u32[]{:S(2)}, u32[]{:S(2)}) %collective-permute-start.4) | collective-permute-done | bytes 49184 | tf_op jit(solution)/shard_map/ppermute | solution.py:14
  97.8 2.4 pad_maximum_fusion.1
  100.2 2.9 gather_fusion.2
  108.3 2.8 collective-permute-start.11
  111.2 2.1 collective-permute-start.12
  114.2 3.5 %collective-permute-start.14 = (bf16[24,768]{1,0:T(8,128)(2,1)S(1)}, bf16[24,768]{1,0:T(8,128)(2,1)S(1)}, u32[]{:S(2)}, u32[]{:S(2)}) collective-permute-start(bf16[24,768]{1,0:T(8,128)(2,1)S(1)} %get-tuple-element.159), channel_id=1, source_target_pairs={{0,24},{4,28},{8,16},{12,20},{16,8},{20,12},{24,0},{28,4},{1,25},{... | collective-permute-start | bytes 110600 | tf_op jit(solution)/shard_map/ppermute | solution.py:14
  120.3 4.3 %collective-permute-done.15 = bf16[24,768]{1,0:T(8,128)(2,1)S(1)} collective-permute-done((bf16[24,768]{1,0:T(8,128)(2,1)S(1)}, bf16[24,768]{1,0:T(8,128)(2,1)S(1)}, u32[]{:S(2)}, u32[]{:S(2)}) %collective-permute-start.15) | collective-permute-done | bytes 36896 | tf_op jit(solution)/shard_map/ppermute | solution.py:14
  127.2 2.4 fusion.18
  130.9 2.0 multiply_reduce_fusion
  135.9 2.5 fusion.98
  140.8 2.1 fusion.34
  145.9 3.1 %convolution_bitcast_fusion = f32[1,768,768]{2,1,0:T(8,128)} fusion(f32[192,768]{1,0:T(8,128)S(1)} %copy-done.2, f32[192]{0:T(256)S(1)} %bitcast.374, f32[192,768]{1,0:T(8,128)} %fusion.16), kind=kOutput, calls=%fused_computation.15 | convolution fusion | flops 228114432 | bytes 3539712 | tf_op jit(solution)/shard_map/dot_general | solution.py:18
  149.1 2.8 collective-permute-done.25
  151.8 5.1 %collective-permute-done.24 = bf16[192,448]{0,1:T(8,128)(2,1)S(1)} collective-permute-done((bf16[192,448]{0,1:T(8,128)(2,1)S(1)}, bf16[192,448]{0,1:T(8,128)(2,1)S(1)}, u32[]{:S(2)}, u32[]{:S(2)}) %collective-permute-start.24) | collective-permute-done | bytes 172064 | tf_op jit(solution)/shard_map/ppermute | solution.py:14
  160.3 2.8 collective-permute-start.28
  163.1 3.1 %collective-permute-start.30 = (bf16[24,448]{0,1:T(8,128)(2,1)S(1)}, bf16[24,448]{0,1:T(8,128)(2,1)S(1)}, u32[]{:S(2)}, u32[]{:S(2)}) collective-permute-start(bf16[24,448]{0,1:T(8,128)(2,1)S(1)} %get-tuple-element.167), channel_id=1, source_target_pairs={{0,20},{4,16},{8,28},{12,24},{16,4},{20,0},{24,12},{28,8},{1,21},{... | collective-permute-start | bytes 64520 | tf_op jit(solution)/shard_map/ppermute | solution.py:14
  166.7 4.1 %collective-permute-start.32 = (bf16[24,448]{0,1:T(8,128)(2,1)S(1)}, bf16[24,448]{0,1:T(8,128)(2,1)S(1)}, u32[]{:S(2)}, u32[]{:S(2)}) collective-permute-start(bf16[24,448]{0,1:T(8,128)(2,1)S(1)} %get-tuple-element.165), channel_id=1, source_target_pairs={{0,28},{4,24},{8,20},{12,16},{16,12},{20,8},{24,4},{28,0},{1,29},{... | collective-permute-start | bytes 64520 | tf_op jit(solution)/shard_map/ppermute | solution.py:14
  171.1 7.6 %collective-permute-done.29 = bf16[24,448]{0,1:T(8,128)(2,1)S(1)} collective-permute-done((bf16[24,448]{0,1:T(8,128)(2,1)S(1)}, bf16[24,448]{0,1:T(8,128)(2,1)S(1)}, u32[]{:S(2)}, u32[]{:S(2)}) %collective-permute-start.29) | collective-permute-done | bytes 21536 | tf_op jit(solution)/shard_map/ppermute | solution.py:14
  178.8 2.7 collective-permute-done.30
  196.5 2.6 collective-permute-start.51
  199.1 2.7 collective-permute-start.50
  202.4 3.2 %collective-permute-start.48 = (f32[6440]{0:T(1024)S(1)}, f32[6440]{0:T(1024)}, u32[]{:S(2)}, u32[]{:S(2)}) collective-permute-start(f32[6440]{0:T(1024)S(1)} %concatenate.39), channel_id=1, source_target_pairs={{0,12},{4,8},{8,4},{12,0},{16,28},{20,24},{24,20},{28,16},{1,13},{... | collective-permute-start | bytes 77288 | tf_op jit(solution)/shard_map/ppermute | solution.py:14
  215.3 2.3 collective-permute-start.58
  218.6 3.3 %collective-permute-start.56 = (f32[192]{0:T(256)S(1)}, f32[192]{0:T(256)S(1)}, u32[]{:S(2)}, u32[]{:S(2)}) collective-permute-start(f32[192]{0:T(256)S(1)} %get-tuple-element.173), channel_id=1, source_target_pairs={{0,16},{4,20},{8,24},{12,28},{16,0},{20,4},{24,8},{28,12},{1,17},{... | collective-permute-start | bytes 2312 | tf_op jit(solution)/shard_map/ppermute | solution.py:14
  229.1 2.7 collective-permute-start.62
  232.1 2.8 collective-permute-start.64
  237.0 4.1 %collective-permute-done.61 = bf16[128,768]{0,1:T(8,128)(2,1)S(1)} collective-permute-done((bf16[128,768]{0,1:T(8,128)(2,1)S(1)}, bf16[128,768]{0,1:T(8,128)(2,1)S(1)}, u32[]{:S(2)}, u32[]{:S(2)}) %collective-permute-start.61) | collective-permute-done | bytes 196640 | tf_op jit(solution)/shard_map/ppermute | solution.py:14
  241.1 2.7 collective-permute-start.66
  244.4 12.5 %collective-permute-done.63 = bf16[128,768]{0,1:T(8,128)(2,1)S(1)} collective-permute-done((bf16[128,768]{0,1:T(8,128)(2,1)S(1)}, bf16[128,768]{0,1:T(8,128)(2,1)S(1)}, u32[]{:S(2)}, u32[]{:S(2)}) %collective-permute-start.63) | collective-permute-done | bytes 196640 | tf_op jit(solution)/shard_map/ppermute | solution.py:14
  256.9 4.4 %collective-permute-done.64 = bf16[128,768]{0,1:T(8,128)(2,1)S(1)} collective-permute-done((bf16[128,768]{0,1:T(8,128)(2,1)S(1)}, bf16[128,768]{0,1:T(8,128)(2,1)S(1)}, u32[]{:S(2)}, u32[]{:S(2)}) %collective-permute-start.64) | collective-permute-done | bytes 196640 | tf_op jit(solution)/shard_map/ppermute | solution.py:14
  263.1 2.8 reshape.454
  272.6 2.4 gather_fusion.5
  (415 shorter events, 117.2 us)
Async XLA Ops:
  7.2 255.9 %all-gather.6.cloned.1.call-start = ((), (), s32[]{:S(2)}) async-start(), calls=%async_computation.1 | async-start | bytes 1622016 | tf_op jit(solution)/shard_map/all_gather | solution.py:136
  10.4 35.0 %collective-permute-start.2 = (bf16[258,192]{0,1:T(8,128)(2,1)}, bf16[258,192]{0,1:T(8,128)(2,1)}, u32[]{:S(2)}, u32[]{:S(2)}) collective-permute-start(bf16[258,192]{0,1:T(8,128)(2,1)} %pad_maximum_fusion.7), channel_id=1, source_target_pairs={{0,3},{1,2},{2,1},{3,0},{4,7},{5,6},{6,5},{7,4},{8,11},{9,10},{10,... | collective-permute-start | bytes 297224 | tf_op jit(solution)/shard_map/ppermute | solution.py:14
  12.8 32.6 %collective-permute-start.1 = (bf16[258,192]{0,1:T(8,128)(2,1)}, bf16[258,192]{0,1:T(8,128)(2,1)}, u32[]{:S(2)}, u32[]{:S(2)}) collective-permute-start(bf16[258,192]{0,1:T(8,128)(2,1)} %pad_maximum_fusion.7), channel_id=1, source_target_pairs={{0,2},{1,3},{2,0},{3,1},{4,6},{5,7},{6,4},{7,5},{8,10},{9,11},{10,... | collective-permute-start | bytes 297224 | tf_op jit(solution)/shard_map/ppermute | solution.py:14
  13.4 32.0 %collective-permute-start = (bf16[258,192]{0,1:T(8,128)(2,1)}, bf16[258,192]{0,1:T(8,128)(2,1)}, u32[]{:S(2)}, u32[]{:S(2)}) collective-permute-start(bf16[258,192]{0,1:T(8,128)(2,1)} %pad_maximum_fusion.7), channel_id=1, source_target_pairs={{0,1},{1,0},{2,3},{3,2},{4,5},{5,4},{6,7},{7,6},{8,9},{9,8},{10,11... | collective-permute-start | bytes 297224 | tf_op jit(solution)/shard_map/ppermute | solution.py:14
  15.5 14.4 %collective-permute-start.39 = (f32[8]{0:T(128)S(1)}, f32[8]{0:T(128)S(1)}, u32[]{:S(2)}, u32[]{:S(2)}) collective-permute-start(f32[8]{0:T(128)S(1)} %select_reduce_fusion), channel_id=1, source_target_pairs={{0,28},{4,24},{8,20},{12,16},{16,12},{20,8},{24,4},{28,0},{1,29},{... | collective-permute-start | bytes 104 | tf_op jit(solution)/shard_map/ppermute | solution.py:14
  20.3 10.5 %collective-permute-start.38 = (f32[8]{0:T(128)S(1)}, f32[8]{0:T(128)S(1)}, u32[]{:S(2)}, u32[]{:S(2)}) collective-permute-start(f32[8]{0:T(128)S(1)} %select_reduce_fusion), channel_id=1, source_target_pairs={{0,24},{4,28},{8,16},{12,20},{16,8},{20,12},{24,0},{28,4},{1,25},{... | collective-permute-start | bytes 104 | tf_op jit(solution)/shard_map/ppermute | solution.py:14
  20.5 252.1 %all-gather.4.cloned.1.call-start = ((), (), s32[]{:S(2)}) async-start(), calls=%async_computation | async-start | bytes 1622016 | tf_op jit(solution)/shard_map/all_gather | solution.py:166
  40.2 57.6 %collective-permute-start.8 = (bf16[192,768]{1,0:T(8,128)(2,1)}, bf16[192,768]{1,0:T(8,128)(2,1)}, u32[]{:S(2)}, u32[]{:S(2)}) collective-permute-start(bf16[192,768]{1,0:T(8,128)(2,1)} %param.24), channel_id=1, source_target_pairs={{0,3},{1,2},{2,1},{3,0},{4,7},{5,6},{6,5},{7,4},{8,11},{9,10},{10,... | collective-permute-start | bytes 884744 | tf_op jit(solution)/shard_map/ppermute | solution.py:14
  43.3 54.5 %collective-permute-start.7 = (bf16[192,768]{1,0:T(8,128)(2,1)}, bf16[192,768]{1,0:T(8,128)(2,1)}, u32[]{:S(2)}, u32[]{:S(2)}) collective-permute-start(bf16[192,768]{1,0:T(8,128)(2,1)} %param.24), channel_id=1, source_target_pairs={{0,2},{1,3},{2,0},{3,1},{4,6},{5,7},{6,4},{7,5},{8,10},{9,11},{10,... | collective-permute-start | bytes 884744 | tf_op jit(solution)/shard_map/ppermute | solution.py:14
  45.4 52.4 %collective-permute-start.6 = (bf16[192,768]{1,0:T(8,128)(2,1)}, bf16[192,768]{1,0:T(8,128)(2,1)}, u32[]{:S(2)}, u32[]{:S(2)}) collective-permute-start(bf16[192,768]{1,0:T(8,128)(2,1)} %param.24), channel_id=1, source_target_pairs={{0,1},{1,0},{2,3},{3,2},{4,5},{5,4},{6,7},{7,6},{8,9},{9,8},{10,11... | collective-permute-start | bytes 884744 | tf_op jit(solution)/shard_map/ppermute | solution.py:14
  55.0 38.4 %collective-permute-start.5 = (bf16[128,192]{0,1:T(8,128)(2,1)S(1)}, bf16[128,192]{0,1:T(8,128)(2,1)S(1)}, u32[]{:S(2)}, u32[]{:S(2)}) collective-permute-start(bf16[128,192]{0,1:T(8,128)(2,1)S(1)} %bitcast.339), channel_id=1, source_target_pairs={{0,3},{1,2},{2,1},{3,0},{4,7},{5,6},{6,5},{7,4},{8,11},{9,10},{10,... | collective-permute-start | bytes 147464 | tf_op jit(solution)/shard_map/ppermute | solution.py:14
  64.8 6.8 %collective-permute-start.19 = (bf16[24,768]{1,0:T(8,128)(2,1)}, bf16[24,768]{1,0:T(8,128)(2,1)S(1)}, u32[]{:S(2)}, u32[]{:S(2)}) collective-permute-start(bf16[24,768]{1,0:T(8,128)(2,1)} %get-tuple-element.154), channel_id=1, source_target_pairs={{0,16},{4,20},{8,24},{12,28},{16,0},{20,4},{24,8},{28,12},{1,17},{... | collective-permute-start | bytes 110600 | tf_op jit(solution)/shard_map/ppermute | solution.py:14
  71.6 6.3 %collective-permute-start.20 = (bf16[24,768]{1,0:T(8,128)(2,1)}, bf16[24,768]{1,0:T(8,128)(2,1)S(1)}, u32[]{:S(2)}, u32[]{:S(2)}) collective-permute-start(bf16[24,768]{1,0:T(8,128)(2,1)} %get-tuple-element.153), channel_id=1, source_target_pairs={{0,20},{4,16},{8,28},{12,24},{16,4},{20,0},{24,12},{28,8},{1,21},{... | collective-permute-start | bytes 110600 | tf_op jit(solution)/shard_map/ppermute | solution.py:14
  77.9 7.3 %collective-permute-start.21 = (bf16[24,768]{1,0:T(8,128)(2,1)}, bf16[24,768]{1,0:T(8,128)(2,1)S(1)}, u32[]{:S(2)}, u32[]{:S(2)}) collective-permute-start(bf16[24,768]{1,0:T(8,128)(2,1)} %get-tuple-element.152), channel_id=1, source_target_pairs={{0,24},{4,28},{8,16},{12,20},{16,8},{20,12},{24,0},{28,4},{1,25},{... | collective-permute-start | bytes 110600 | tf_op jit(solution)/shard_map/ppermute | solution.py:14
  85.2 6.9 %collective-permute-start.22 = (bf16[24,768]{1,0:T(8,128)(2,1)}, bf16[24,768]{1,0:T(8,128)(2,1)S(1)}, u32[]{:S(2)}, u32[]{:S(2)}) collective-permute-start(bf16[24,768]{1,0:T(8,128)(2,1)} %get-tuple-element.151), channel_id=1, source_target_pairs={{0,28},{4,24},{8,20},{12,16},{16,12},{20,8},{24,4},{28,0},{1,29},{... | collective-permute-start | bytes 110600 | tf_op jit(solution)/shard_map/ppermute | solution.py:14
  106.0 8.2 %collective-permute-start.9 = (bf16[24,768]{1,0:T(8,128)(2,1)S(1)}, bf16[24,768]{1,0:T(8,128)(2,1)S(1)}, u32[]{:S(2)}, u32[]{:S(2)}) collective-permute-start(bf16[24,768]{1,0:T(8,128)(2,1)S(1)} %get-tuple-element.164), channel_id=1, source_target_pairs={{0,4},{4,0},{8,12},{12,8},{16,20},{20,16},{24,28},{28,24},{1,5},{5... | collective-permute-start | bytes 110600 | tf_op jit(solution)/shard_map/ppermute | solution.py:14
  108.3 9.4 %collective-permute-start.10 = (bf16[24,768]{1,0:T(8,128)(2,1)S(1)}, bf16[24,768]{1,0:T(8,128)(2,1)S(1)}, u32[]{:S(2)}, u32[]{:S(2)}) collective-permute-start(bf16[24,768]{1,0:T(8,128)(2,1)S(1)} %get-tuple-element.163), channel_id=1, source_target_pairs={{0,8},{4,12},{8,0},{12,4},{16,24},{20,28},{24,16},{28,20},{1,9},{5... | collective-permute-start | bytes 110600 | tf_op jit(solution)/shard_map/ppermute | solution.py:14
  108.3 10.5 %collective-permute-start.11 = (bf16[24,768]{1,0:T(8,128)(2,1)S(1)}, bf16[24,768]{1,0:T(8,128)(2,1)S(1)}, u32[]{:S(2)}, u32[]{:S(2)}) collective-permute-start(bf16[24,768]{1,0:T(8,128)(2,1)S(1)} %get-tuple-element.162), channel_id=1, source_target_pairs={{0,12},{4,8},{8,4},{12,0},{16,28},{20,24},{24,20},{28,16},{1,13},{... | collective-permute-start | bytes 110600 | tf_op jit(solution)/shard_map/ppermute | solution.py:14
  111.2 7.7 %collective-permute-start.12 = (bf16[24,768]{1,0:T(8,128)(2,1)S(1)}, bf16[24,768]{1,0:T(8,128)(2,1)S(1)}, u32[]{:S(2)}, u32[]{:S(2)}) collective-permute-start(bf16[24,768]{1,0:T(8,128)(2,1)S(1)} %get-tuple-element.161), channel_id=1, source_target_pairs={{0,16},{4,20},{8,24},{12,28},{16,0},{20,4},{24,8},{28,12},{1,17},{... | collective-permute-start | bytes 110600 | tf_op jit(solution)/shard_map/ppermute | solution.py:14
  117.7 6.9 %collective-permute-start.15 = (bf16[24,768]{1,0:T(8,128)(2,1)S(1)}, bf16[24,768]{1,0:T(8,128)(2,1)S(1)}, u32[]{:S(2)}, u32[]{:S(2)}) collective-permute-start(bf16[24,768]{1,0:T(8,128)(2,1)S(1)} %get-tuple-element.158), channel_id=1, source_target_pairs={{0,28},{4,24},{8,20},{12,16},{16,12},{20,8},{24,4},{28,0},{1,29},{... | collective-permute-start | bytes 110600 | tf_op jit(solution)/shard_map/ppermute | solution.py:14
  144.0 7.8 %collective-permute-start.25 = (bf16[192,448]{0,1:T(8,128)(2,1)S(1)}, bf16[192,448]{0,1:T(8,128)(2,1)S(1)}, u32[]{:S(2)}, u32[]{:S(2)}) collective-permute-start(bf16[192,448]{0,1:T(8,128)(2,1)S(1)} %get-tuple-element.135), channel_id=1, source_target_pairs={{0,3},{1,2},{2,1},{3,0},{4,7},{5,6},{6,5},{7,4},{8,11},{9,10},{10,... | collective-permute-start | bytes 516104 | tf_op jit(solution)/shard_map/ppermute | solution.py:14
  144.1 12.8 %collective-permute-start.24 = (bf16[192,448]{0,1:T(8,128)(2,1)S(1)}, bf16[192,448]{0,1:T(8,128)(2,1)S(1)}, u32[]{:S(2)}, u32[]{:S(2)}) collective-permute-start(bf16[192,448]{0,1:T(8,128)(2,1)S(1)} %get-tuple-element.136), channel_id=1, source_target_pairs={{0,2},{1,3},{2,0},{3,1},{4,6},{5,7},{6,4},{7,5},{8,10},{9,11},{10,... | collective-permute-start | bytes 516104 | tf_op jit(solution)/shard_map/ppermute | solution.py:14
  145.7 11.2 %collective-permute-start.23 = (bf16[192,448]{0,1:T(8,128)(2,1)S(1)}, bf16[192,448]{0,1:T(8,128)(2,1)S(1)}, u32[]{:S(2)}, u32[]{:S(2)}) collective-permute-start(bf16[192,448]{0,1:T(8,128)(2,1)S(1)} %get-tuple-element.134), channel_id=1, source_target_pairs={{0,1},{1,0},{2,3},{3,2},{4,5},{5,4},{6,7},{7,6},{8,9},{9,8},{10,11... | collective-permute-start | bytes 516104 | tf_op jit(solution)/shard_map/ppermute | solution.py:14
  157.5 8.7 %collective-permute-start.26 = (bf16[24,448]{0,1:T(8,128)(2,1)S(1)}, bf16[24,448]{0,1:T(8,128)(2,1)S(1)}, u32[]{:S(2)}, u32[]{:S(2)}) collective-permute-start(bf16[24,448]{0,1:T(8,128)(2,1)S(1)} %get-tuple-element.171), channel_id=1, source_target_pairs={{0,4},{4,0},{8,12},{12,8},{16,20},{20,16},{24,28},{28,24},{1,5},{5... | collective-permute-start | bytes 64520 | tf_op jit(solution)/shard_map/ppermute | solution.py:14
  158.3 8.4 %collective-permute-start.27 = (bf16[24,448]{0,1:T(8,128)(2,1)S(1)}, bf16[24,448]{0,1:T(8,128)(2,1)S(1)}, u32[]{:S(2)}, u32[]{:S(2)}) collective-permute-start(bf16[24,448]{0,1:T(8,128)(2,1)S(1)} %get-tuple-element.170), channel_id=1, source_target_pairs={{0,8},{4,12},{8,0},{12,4},{16,24},{20,28},{24,16},{28,20},{1,9},{5... | collective-permute-start | bytes 64520 | tf_op jit(solution)/shard_map/ppermute | solution.py:14
  160.3 10.6 %collective-permute-start.28 = (bf16[24,448]{0,1:T(8,128)(2,1)S(1)}, bf16[24,448]{0,1:T(8,128)(2,1)S(1)}, u32[]{:S(2)}, u32[]{:S(2)}) collective-permute-start(bf16[24,448]{0,1:T(8,128)(2,1)S(1)} %get-tuple-element.169), channel_id=1, source_target_pairs={{0,12},{4,8},{8,4},{12,0},{16,28},{20,24},{24,20},{28,16},{1,13},{... | collective-permute-start | bytes 64520 | tf_op jit(solution)/shard_map/ppermute | solution.py:14
  163.1 15.6 %collective-permute-start.29 = (bf16[24,448]{0,1:T(8,128)(2,1)S(1)}, bf16[24,448]{0,1:T(8,128)(2,1)S(1)}, u32[]{:S(2)}, u32[]{:S(2)}) collective-permute-start(bf16[24,448]{0,1:T(8,128)(2,1)S(1)} %get-tuple-element.168), channel_id=1, source_target_pairs={{0,16},{4,20},{8,24},{12,28},{16,0},{20,4},{24,8},{28,12},{1,17},{... | collective-permute-start | bytes 64520 | tf_op jit(solution)/shard_map/ppermute | solution.py:14
  163.1 18.3 %collective-permute-start.30 = (bf16[24,448]{0,1:T(8,128)(2,1)S(1)}, bf16[24,448]{0,1:T(8,128)(2,1)S(1)}, u32[]{:S(2)}, u32[]{:S(2)}) collective-permute-start(bf16[24,448]{0,1:T(8,128)(2,1)S(1)} %get-tuple-element.167), channel_id=1, source_target_pairs={{0,20},{4,16},{8,28},{12,24},{16,4},{20,0},{24,12},{28,8},{1,21},{... | collective-permute-start | bytes 64520 | tf_op jit(solution)/shard_map/ppermute | solution.py:14
  166.2 15.3 %collective-permute-start.31 = (bf16[24,448]{0,1:T(8,128)(2,1)S(1)}, bf16[24,448]{0,1:T(8,128)(2,1)S(1)}, u32[]{:S(2)}, u32[]{:S(2)}) collective-permute-start(bf16[24,448]{0,1:T(8,128)(2,1)S(1)} %get-tuple-element.166), channel_id=1, source_target_pairs={{0,24},{4,28},{8,16},{12,20},{16,8},{20,12},{24,0},{28,4},{1,25},{... | collective-permute-start | bytes 64520 | tf_op jit(solution)/shard_map/ppermute | solution.py:14
  166.7 14.9 %collective-permute-start.32 = (bf16[24,448]{0,1:T(8,128)(2,1)S(1)}, bf16[24,448]{0,1:T(8,128)(2,1)S(1)}, u32[]{:S(2)}, u32[]{:S(2)}) collective-permute-start(bf16[24,448]{0,1:T(8,128)(2,1)S(1)} %get-tuple-element.165), channel_id=1, source_target_pairs={{0,28},{4,24},{8,20},{12,16},{16,12},{20,8},{24,4},{28,0},{1,29},{... | collective-permute-start | bytes 64520 | tf_op jit(solution)/shard_map/ppermute | solution.py:14
  194.7 11.3 %collective-permute-start.52 = (f32[6440]{0:T(1024)S(1)}, f32[6440]{0:T(1024)S(1)}, u32[]{:S(2)}, u32[]{:S(2)}) collective-permute-start(f32[6440]{0:T(1024)S(1)} %concatenate.39), channel_id=1, source_target_pairs={{0,28},{4,24},{8,20},{12,16},{16,12},{20,8},{24,4},{28,0},{1,29},{... | collective-permute-start | bytes 77288 | tf_op jit(solution)/shard_map/ppermute | solution.py:14
  196.5 9.5 %collective-permute-start.51 = (f32[6440]{0:T(1024)S(1)}, f32[6440]{0:T(1024)S(1)}, u32[]{:S(2)}, u32[]{:S(2)}) collective-permute-start(f32[6440]{0:T(1024)S(1)} %concatenate.39), channel_id=1, source_target_pairs={{0,24},{4,28},{8,16},{12,20},{16,8},{20,12},{24,0},{28,4},{1,25},{... | collective-permute-start | bytes 77288 | tf_op jit(solution)/shard_map/ppermute | solution.py:14
  199.1 8.2 %collective-permute-start.50 = (f32[6440]{0:T(1024)S(1)}, f32[6440]{0:T(1024)S(1)}, u32[]{:S(2)}, u32[]{:S(2)}) collective-permute-start(f32[6440]{0:T(1024)S(1)} %concatenate.39), channel_id=1, source_target_pairs={{0,20},{4,16},{8,28},{12,24},{16,4},{20,0},{24,12},{28,8},{1,21},{... | collective-permute-start | bytes 77288 | tf_op jit(solution)/shard_map/ppermute | solution.py:14
  202.4 6.4 %collective-permute-start.48 = (f32[6440]{0:T(1024)S(1)}, f32[6440]{0:T(1024)}, u32[]{:S(2)}, u32[]{:S(2)}) collective-permute-start(f32[6440]{0:T(1024)S(1)} %concatenate.39), channel_id=1, source_target_pairs={{0,12},{4,8},{8,4},{12,0},{16,28},{20,24},{24,20},{28,16},{1,13},{... | collective-permute-start | bytes 77288 | tf_op jit(solution)/shard_map/ppermute | solution.py:14
  213.7 8.5 %collective-permute-start.59 = (f32[192]{0:T(256)S(1)}, f32[192]{0:T(256)S(1)}, u32[]{:S(2)}, u32[]{:S(2)}) collective-permute-start(f32[192]{0:T(256)S(1)} %get-tuple-element.173), channel_id=1, source_target_pairs={{0,28},{4,24},{8,20},{12,16},{16,12},{20,8},{24,4},{28,0},{1,29},{... | collective-permute-start | bytes 2312 | tf_op jit(solution)/shard_map/ppermute | solution.py:14
  215.3 8.8 %collective-permute-start.58 = (f32[192]{0:T(256)S(1)}, f32[192]{0:T(256)S(1)}, u32[]{:S(2)}, u32[]{:S(2)}) collective-permute-start(f32[192]{0:T(256)S(1)} %get-tuple-element.173), channel_id=1, source_target_pairs={{0,24},{4,28},{8,16},{12,20},{16,8},{20,12},{24,0},{28,4},{1,25},{... | collective-permute-start | bytes 2312 | tf_op jit(solution)/shard_map/ppermute | solution.py:14
  217.6 10.7 %collective-permute-start.57 = (f32[192]{0:T(256)S(1)}, f32[192]{0:T(256)S(1)}, u32[]{:S(2)}, u32[]{:S(2)}) collective-permute-start(f32[192]{0:T(256)S(1)} %get-tuple-element.173), channel_id=1, source_target_pairs={{0,20},{4,16},{8,28},{12,24},{16,4},{20,0},{24,12},{28,8},{1,21},{... | collective-permute-start | bytes 2312 | tf_op jit(solution)/shard_map/ppermute | solution.py:14
  218.6 10.3 %collective-permute-start.56 = (f32[192]{0:T(256)S(1)}, f32[192]{0:T(256)S(1)}, u32[]{:S(2)}, u32[]{:S(2)}) collective-permute-start(f32[192]{0:T(256)S(1)} %get-tuple-element.173), channel_id=1, source_target_pairs={{0,16},{4,20},{8,24},{12,28},{16,0},{20,4},{24,8},{28,12},{1,17},{... | collective-permute-start | bytes 2312 | tf_op jit(solution)/shard_map/ppermute | solution.py:14
  222.1 7.1 %collective-permute-start.55 = (f32[192]{0:T(256)S(1)}, f32[192]{0:T(256)S(1)}, u32[]{:S(2)}, u32[]{:S(2)}) collective-permute-start(f32[192]{0:T(256)S(1)} %get-tuple-element.173), channel_id=1, source_target_pairs={{0,12},{4,8},{8,4},{12,0},{16,28},{20,24},{24,20},{28,16},{1,13},{... | collective-permute-start | bytes 2312 | tf_op jit(solution)/shard_map/ppermute | solution.py:14
  222.3 9.6 %collective-permute-start.54 = (f32[192]{0:T(256)S(1)}, f32[192]{0:T(256)S(1)}, u32[]{:S(2)}, u32[]{:S(2)}) collective-permute-start(f32[192]{0:T(256)S(1)} %get-tuple-element.173), channel_id=1, source_target_pairs={{0,8},{4,12},{8,0},{12,4},{16,24},{20,28},{24,16},{28,20},{1,9},{5... | collective-permute-start | bytes 2312 | tf_op jit(solution)/shard_map/ppermute | solution.py:14
  224.2 7.9 %collective-permute-start.53 = (f32[192]{0:T(256)S(1)}, f32[192]{0:T(256)S(1)}, u32[]{:S(2)}, u32[]{:S(2)}) collective-permute-start(f32[192]{0:T(256)S(1)} %get-tuple-element.173), channel_id=1, source_target_pairs={{0,4},{4,0},{8,12},{12,8},{16,20},{20,16},{24,28},{28,24},{1,5},{5... | collective-permute-start | bytes 2312 | tf_op jit(solution)/shard_map/ppermute | solution.py:14
  228.3 7.1 %collective-permute-start.60 = (bf16[128,768]{0,1:T(8,128)(2,1)S(1)}, bf16[128,768]{0,1:T(8,128)(2,1)S(1)}, u32[]{:S(2)}, u32[]{:S(2)}) collective-permute-start(bf16[128,768]{0,1:T(8,128)(2,1)S(1)} %pad_maximum_fusion.6), channel_id=1, source_target_pairs={{0,4},{4,0},{8,12},{12,8},{16,20},{20,16},{24,28},{28,24},{1,5},{5... | collective-permute-start | bytes 589832 | tf_op jit(solution)/shard_map/ppermute | solution.py:14
  229.0 12.1 %collective-permute-start.61 = (bf16[128,768]{0,1:T(8,128)(2,1)S(1)}, bf16[128,768]{0,1:T(8,128)(2,1)S(1)}, u32[]{:S(2)}, u32[]{:S(2)}) collective-permute-start(bf16[128,768]{0,1:T(8,128)(2,1)S(1)} %pad_maximum_fusion.6), channel_id=1, source_target_pairs={{0,8},{4,12},{8,0},{12,4},{16,24},{20,28},{24,16},{28,20},{1,9},{5... | collective-permute-start | bytes 589832 | tf_op jit(solution)/shard_map/ppermute | solution.py:14
  229.1 15.2 %collective-permute-start.62 = (bf16[128,768]{0,1:T(8,128)(2,1)S(1)}, bf16[128,768]{0,1:T(8,128)(2,1)S(1)}, u32[]{:S(2)}, u32[]{:S(2)}) collective-permute-start(bf16[128,768]{0,1:T(8,128)(2,1)S(1)} %pad_maximum_fusion.6), channel_id=1, source_target_pairs={{0,12},{4,8},{8,4},{12,0},{16,28},{20,24},{24,20},{28,16},{1,13},{... | collective-permute-start | bytes 589832 | tf_op jit(solution)/shard_map/ppermute | solution.py:14
  231.9 25.0 %collective-permute-start.63 = (bf16[128,768]{0,1:T(8,128)(2,1)S(1)}, bf16[128,768]{0,1:T(8,128)(2,1)S(1)}, u32[]{:S(2)}, u32[]{:S(2)}) collective-permute-start(bf16[128,768]{0,1:T(8,128)(2,1)S(1)} %pad_maximum_fusion.6), channel_id=1, source_target_pairs={{0,16},{4,20},{8,24},{12,28},{16,0},{20,4},{24,8},{28,12},{1,17},{... | collective-permute-start | bytes 589832 | tf_op jit(solution)/shard_map/ppermute | solution.py:14
  232.1 29.3 %collective-permute-start.64 = (bf16[128,768]{0,1:T(8,128)(2,1)S(1)}, bf16[128,768]{0,1:T(8,128)(2,1)S(1)}, u32[]{:S(2)}, u32[]{:S(2)}) collective-permute-start(bf16[128,768]{0,1:T(8,128)(2,1)S(1)} %pad_maximum_fusion.6), channel_id=1, source_target_pairs={{0,20},{4,16},{8,28},{12,24},{16,4},{20,0},{24,12},{28,8},{1,21},{... | collective-permute-start | bytes 589832 | tf_op jit(solution)/shard_map/ppermute | solution.py:14
  235.4 25.9 %collective-permute-start.65 = (bf16[128,768]{0,1:T(8,128)(2,1)S(1)}, bf16[128,768]{0,1:T(8,128)(2,1)S(1)}, u32[]{:S(2)}, u32[]{:S(2)}) collective-permute-start(bf16[128,768]{0,1:T(8,128)(2,1)S(1)} %pad_maximum_fusion.6), channel_id=1, source_target_pairs={{0,24},{4,28},{8,16},{12,20},{16,8},{20,12},{24,0},{28,4},{1,25},{... | collective-permute-start | bytes 589832 | tf_op jit(solution)/shard_map/ppermute | solution.py:14
  241.1 20.4 %collective-permute-start.66 = (bf16[128,768]{0,1:T(8,128)(2,1)S(1)}, bf16[128,768]{0,1:T(8,128)(2,1)S(1)}, u32[]{:S(2)}, u32[]{:S(2)}) collective-permute-start(bf16[128,768]{0,1:T(8,128)(2,1)S(1)} %pad_maximum_fusion.6), channel_id=1, source_target_pairs={{0,28},{4,24},{8,20},{12,16},{16,12},{20,8},{24,4},{28,0},{1,29},{... | collective-permute-start | bytes 589832 | tf_op jit(solution)/shard_map/ppermute | solution.py:14
  (80 other events, 720.3 us)
Sparse Core Ops, SparseCore 0:
  20.6 53.9 all-gather.5
  77.5 54.3 all-gather.3

commit v2 on v1

v2 whole, which is shorter than its diff:
```python
import functools

import jax
import jax.numpy as jnp
from jax import lax
from jax.experimental import pallas as pl
from jax.experimental.pallas import tpu as pltpu
from jax.sharding import PartitionSpec as P

eps = 1e-06
aux_weight = 0.01
f32 = jnp.float32
bf16 = jnp.bfloat16
gelu_scale = 0.7978845608028654
gelu_cube = 0.044715
scalar_memory = pl.BlockSpec(memory_space=pltpu.SMEM)


def mm(left, right, dims=((1,), (0,)), precision=None):
    return lax.dot_general(left, right, (dims, ((), ())), precision=precision, preferred_element_type=f32)


nt = ((1,), (1,))
tn = ((0,), (0,))


def call(body, outs, *args, scratch=()):
    in_specs = [scalar_memory if a.dtype == jnp.int32 and a.ndim == 1 else pl.BlockSpec() for a in args]
    return pl.pallas_call(
        body,
        out_shape=[jax.ShapeDtypeStruct(shape, kind) for shape, kind in outs],
        in_specs=in_specs,
        scratch_shapes=list(scratch),
        compiler_params=pltpu.CompilerParams(vmem_limit_bytes=40 * 1024 * 1024),
    )(*args)


def wide(ref, first, rows):
    return jnp.concatenate(
        [ref[i, first : first + rows, :].astype(f32) for i in range(ref.shape[0])], axis=1
    )


def row_scale(values):
    return lax.rsqrt(jnp.sum(values * values, axis=1, keepdims=True) * (1.0 / values.shape[1]) + eps)


def lanes(shape):
    return lax.broadcasted_iota(jnp.int32, shape, len(shape) - 1)


def sublanes(shape):
    return lax.broadcasted_iota(jnp.int32, shape, len(shape) - 2)


def side_lanes(rows, width, columns):
    spot = lanes((rows, width))
    out = jnp.zeros((rows, width), f32)
    for i, column in enumerate(columns):
        out = jnp.where(spot == i, column, out)
    return out


def high_low(values, count=2):
    pieces = []
    for _ in range(count):
        piece = values.astype(bf16).astype(f32)
        pieces.append(piece)
        values = values - piece
    return pieces


def softmax(values):
    raised = jnp.exp(values - jnp.max(values, axis=1, keepdims=True))
    return raised / jnp.sum(raised, axis=1, keepdims=True)


def gelu_parts(u):
    t = jnp.tanh(gelu_scale * (u + gelu_cube * u * u * u))
    value = 0.5 * u * (1.0 + t)
    slope = 0.5 * (1.0 + t) + 0.5 * u * (1.0 - t * t) * gelu_scale * (1.0 + 3.0 * gelu_cube * u * u)
    return value, slope


def bucket_hot(buckets_ref, count):
    span = buckets_ref.shape[1]
    return (sublanes((count, span)) == buckets_ref[...]).astype(f32)


def attend_kernel(scale, scalars, packed, wq, wk, wv, buckets, table, qkv_ref, weights_ref, attended_ref, scale_ref):
    tok = weights_ref.shape[1]
    heads = weights_ref.shape[0]
    col = wq.shape[1]
    size = col // heads
    x = wide(packed, 0, tok)
    gain = wide(packed, 2 * tok, 16)[0:1]
    scale_one = row_scale(x)
    scale_ref[...] = scale_one
    normed = (x * scale_one * gain).astype(bf16)
    projected = []
    for i, w in enumerate((wq, wk, wv)):
        rows = mm(normed, w[...]).astype(bf16)
        qkv_ref[:, i * col : (i + 1) * col] = rows
        projected.append(rows)
    query, key, value = projected
    offsets = mm(table[...], bucket_hot(buckets, table.shape[0]), tn, lax.Precision.HIGHEST)
    open_keys = lanes((tok, tok)) < scalars[0]
    outs = []
    for h in range(heads):
        at = slice(h * size, (h + 1) * size)
        spread = jnp.broadcast_to(offsets[h : h + 1, :], (tok, 2 * tok))
        bias = pltpu.roll(spread, tok + 1, 1, stride=1, stride_axis=0)[:, :tok]
        scores = mm(query[:, at], key[:, at], nt) * scale + bias
        weights = softmax(jnp.where(open_keys, scores, -1000000000.0))
        weights_ref[h] = weights
        outs.append(mm(weights.astype(bf16), value[:, at]))
    attended_ref[...] = jnp.concatenate(outs, axis=1).astype(bf16)


def route_kernel(
    capacity, scalars, packed, attended, w_output, routes, w_router,
    residual_ref, own_ref, scale_ref, normed_ref, router_ref, gate_ref, spots_ref, send_ref, parts,
):
    tok = routes.shape[0]
    width = w_router.shape[0]
    experts, slots, _ = send_ref.shape
    heads, _, col = packed.shape
    residual = wide(packed, 0, tok)
    for i in range(heads):
        residual = residual + mm(attended[i], w_output[i])
    residual_ref[...] = residual
    for i in range(heads):
        parts[i] = residual[:, i * col : (i + 1) * col]
    own_ref[...] = parts[scalars[1]]
    gain = wide(packed, 2 * tok, 16)[1:2]
    scale_two = row_scale(residual)
    scale_ref[...] = scale_two
    normed = (residual * scale_two * gain).astype(bf16)
    normed_ref[...] = normed
    router = softmax(mm(normed, w_router[...]))
    router_ref[...] = router
    route_hot = (lanes((tok, experts)) == routes[...]).astype(f32)
    gate_ref[...] = jnp.sum(router * route_hot, axis=1, keepdims=True)
    before = (lanes((tok, tok)) < sublanes((tok, tok))).astype(bf16)
    slot = jnp.sum(mm(before, route_hot.astype(bf16)) * route_hot, axis=1, keepdims=True).astype(jnp.int32)
    spots_ref[...] = routes[...] * slots + slot
    valid = (sublanes((tok, 1)) < scalars[0]).astype(f32)
    counts = jnp.sum(route_hot * valid, axis=0, keepdims=True)
    probs = jnp.sum(router * valid, axis=0, keepdims=True)
    grads = wide(packed, tok, tok).astype(bf16)
    both = jnp.concatenate([normed, grads], axis=1)
    for e in range(experts):
        pick = ((slot == lanes((tok, slots))) & (routes[...] == e)).astype(bf16)
        rows = mm(pick, both, tn)
        send_ref[e, :, :width] = rows[:, :width].astype(bf16)
        stats = side_lanes(1, width, [counts[:, e : e + 1]] + high_low(probs[:, e : e + 1], 3))
        tail = jnp.where(sublanes((slots, width)) == capacity, stats, rows[:, width:])
        send_ref[e, :, width:] = tail.astype(bf16)


def expert_kernel(
    capacity, scalars, rows_ref, w_in, w_out, w_router,
    back_ref, part_ref, hidden_ref, before_ref, grads_ref,
):
    total = rows_ref.shape[0]
    width, experts = w_router.shape
    heads, _, col = part_ref.shape
    slots = total // experts
    rows = rows_ref[:, :width]
    grads = rows_ref[:, width:].astype(f32)
    hidden, slope = gelu_parts(mm(rows, w_in[...]))
    hidden = hidden.astype(bf16)
    hidden_ref[...] = hidden
    produced = mm(hidden, w_out[...])
    for i in range(heads):
        part_ref[i] = produced[:, i * col : (i + 1) * col]
    probs = softmax(mm(rows, w_router[...]))
    gate = jnp.sum(jnp.where(lanes((total, experts)) == scalars[2], probs, 0.0), axis=1, keepdims=True)
    back = (gate * grads).astype(bf16)
    grads_ref[...] = back
    before = (mm(back, w_out[...], nt) * slope).astype(bf16)
    before_ref[...] = before
    rows_grad = mm(before, w_in[...], nt)
    gate_grad = jnp.sum(grads * produced, axis=1, keepdims=True)
    stats = jnp.zeros((1, 128), f32)
    for b in range(experts):
        stats = stats + grads[b * slots + capacity : b * slots + capacity + 1, :128]
    count = stats[:, 0:1]
    prob = stats[:, 1:2] + stats[:, 2:3] + stats[:, 3:4]
    side = side_lanes(
        total, 256 - col, high_low(gate_grad) + high_low(count) + high_low(prob, 3)
    ).astype(bf16)
    rows_grad = rows_grad.astype(bf16).astype(f32)
    for b in range(experts):
        at = slice(b * slots, (b + 1) * slots)
        for i in range(heads):
            back_ref[b * heads + i] = jnp.concatenate(
                [rows_grad[at, i * col : (i + 1) * col], side[at].astype(f32)], axis=1
            ).astype(bf16)


def weights_kernel(rows_ref, hidden, before, grads, in_ref, out_ref):
    width = in_ref.shape[0]
    in_ref[...] = mm(rows_ref[:, :width], before[...], tn)
    out_ref[...] = mm(hidden[...], grads[...], tn)


def collect_kernel(came, spots, grad_ref, gate_ref, stats_ref):
    tok, col = grad_ref.shape
    sources, slots, _ = came.shape
    experts = stats_ref.shape[1]
    heads = sources // experts
    sums = []
    for e in range(experts):
        total = came[e * heads].astype(f32)
        for i in range(1, heads):
            total = total + came[e * heads + i].astype(f32)
        sums.append(total)
    stats = jnp.concatenate([total[0:1, col:] for total in sums], axis=0) * (1.0 / heads)
    sums = jnp.concatenate(sums, axis=0)
    pick = spots[...] == lanes((tok, experts * slots))
    grad_ref[...] = mm(pick.astype(bf16), sums[:, :col].astype(bf16)).astype(bf16)
    gate = mm(pick.astype(f32), sums[:, col:], precision=lax.Precision.HIGHEST)
    gate_ref[...] = gate[:, 0:1] + gate[:, 1:2]
    diagonal = lanes((experts, experts)) == sublanes((experts, experts))
    count = stats[:, 2:3] + stats[:, 3:4]
    prob = stats[:, 4:5] + stats[:, 5:6] + stats[:, 6:7]
    stats_ref[0:1, :] = jnp.sum(jnp.where(diagonal, count, 0.0), axis=0, keepdims=True)
    stats_ref[1:2, :] = jnp.sum(jnp.where(diagonal, prob, 0.0), axis=0, keepdims=True)


def backward_kernel(
    scale, valid_total, scalars, packed, expert_grad, gate_grad, stats, residual_ref, scale_two, normed_two,
    router_ref, routes, w_router, w_output, weights_ref, qkv, wq, wk, wv, scale_one,
    late_ref, first_ref, own_ref, small_ref, parts,
):
    tok = routes.shape[0]
    heads_here = weights_ref.shape[0]
    col = wq.shape[1]
    size = col // heads_here
    width, experts = w_router.shape
    blocks = width // col
    valid = (sublanes((tok, 1)) < scalars[0]).astype(f32)
    route_hot = (lanes((tok, experts)) == routes[...]).astype(f32)
    router = router_ref[...]
    fraction = stats[0:1, :] * (1.0 / valid_total)
    prob_grad = route_hot * gate_grad[...] + aux_weight * experts / valid_total * fraction * valid
    logit_grad = router * (prob_grad - jnp.sum(router * prob_grad, axis=1, keepdims=True))
    logit_grad = logit_grad.astype(bf16)
    small_ref[0:experts, :] = mm(logit_grad, normed_two[...], tn)
    normed_grad = mm(logit_grad, w_router[...], nt) + wide(expert_grad, 0, tok)
    unit = residual_ref[...] * scale_two[...]
    gain_rows = wide(packed, 2 * tok, 16)
    gain_one, gain_two = gain_rows[0:1], gain_rows[1:2]
    small_ref[experts : experts + 1, :] = jnp.sum(normed_grad * unit, axis=0, keepdims=True)
    unit_grad = normed_grad * gain_two
    mean = jnp.sum(unit_grad * unit, axis=1, keepdims=True) * (1.0 / width)
    residual_grad = wide(packed, tok, tok) + scale_two[...] * (unit_grad - unit * mean)
    for i in range(blocks):
        parts[i] = residual_grad[:, i * col : (i + 1) * col]
    own = parts[scalars[1]]
    own_ref[...] = own
    branch = residual_grad.astype(bf16)
    attended_grad = mm(branch, w_output[...], nt).astype(bf16)
    flip = (lanes((tok, tok)) + sublanes((tok, tok)) == tok - 1).astype(bf16)
    query, key, value = (qkv[:, i * col : (i + 1) * col] for i in range(3))
    grads = [[], [], []]
    small_ref[experts + 2 :, :] = jnp.zeros((6, width), f32)
    for h in range(heads_here):
        at = slice(h * size, (h + 1) * size)
        out = attended_grad[:, at]
        weights = weights_ref[h]
        mass = mm(out, value[:, at], nt)
        score = weights * (mass - jnp.sum(weights * mass, axis=1, keepdims=True))
        score = score.astype(bf16)
        grads[0].append(mm(score, key[:, at]) * scale)
        grads[1].append(mm(score, query[:, at], tn) * scale)
        grads[2].append(mm(weights.astype(bf16), out, tn))
        flipped = jnp.concatenate([mm(flip, score), jnp.zeros((tok, tok), f32)], axis=1)
        rolled = pltpu.roll(flipped, 0, 1, stride=1, stride_axis=0)
        small_ref[experts + 2 + h : experts + 3 + h, : 2 * tok] = jnp.sum(rolled, axis=0, keepdims=True)
    first = jnp.zeros((tok, width), f32)
    row = jnp.zeros((tok, 1), f32)
    for i, w in enumerate((wq, wk, wv)):
        grad = jnp.concatenate(grads[i], axis=1)
        low = grad.astype(bf16)
        late_ref[0:tok, i * col : (i + 1) * col] = low
        first = first + mm(low, w[...], nt)
        row = row + jnp.sum(low.astype(f32) * qkv[:, i * col : (i + 1) * col].astype(f32), axis=1, keepdims=True)
    late_ref[0:tok, 3 * col :] = own.astype(bf16)
    unit_one = wide(packed, 0, tok) * scale_one[...]
    small_ref[experts + 1 : experts + 2, :] = jnp.sum(first * unit_one, axis=0, keepdims=True)
    late_ref[tok:, :] = small_ref[...].astype(bf16)
    side = side_lanes(tok, 256 - col, high_low(row))
    for i in range(blocks):
        first_ref[i] = jnp.concatenate([first[:, i * col : (i + 1) * col], side], axis=1).astype(bf16)


def finish_kernel(
    came, first, spots, gate, residual_own, residual_grad_own, inputs, gain, scale_one, block_ref, input_ref
):
    tok, col = inputs.shape
    heads = first.shape[0]
    pick = (spots[...] == lanes((tok, came.shape[0]))).astype(bf16)
    returned = mm(pick, came[...])
    block_ref[...] = (residual_own[...] + gate[...] * returned).astype(bf16)
    total = first[0].astype(f32)
    for i in range(1, heads):
        total = total + first[i].astype(f32)
    mean = (total[:, col : col + 1] + total[:, col + 1 : col + 2]) * (1.0 / (heads * col))
    unit = inputs[...].astype(f32) * scale_one[...]
    input_ref[...] = residual_grad_own[...] + scale_one[...] * (total[:, :col] * gain[...].astype(f32) - unit * mean)


def turn_kernel(all_in, all_attended, packed, tok, normed_ref, turned_ref):
    groups, heads, rows, col = all_in.shape
    gain = wide(packed, 2 * tok, 16)[0:1]
    for b in range(groups):
        x = jnp.concatenate([all_in[b, i].astype(f32) for i in range(heads)], axis=1)
        normed_ref[b * rows : (b + 1) * rows, :] = (x * row_scale(x) * gain).astype(bf16)
        turned_ref[b * rows : (b + 1) * rows, :] = jnp.concatenate(
            [all_attended[b, i].astype(f32) for i in range(heads)], axis=1
        ).astype(bf16)


def products_kernel(late, normed, turned, q_ref, k_ref, v_ref, out_ref, small_ref):
    groups, rows, width = late.shape
    tok = normed.shape[0] // groups
    heads, col = out_ref.shape[0], q_ref.shape[1]
    joined = jnp.concatenate([late[b, :tok, :] for b in range(groups)], axis=0)
    for i, ref in enumerate((q_ref, k_ref, v_ref)):
        ref[...] = mm(normed[...], joined[:, i * col : (i + 1) * col], tn)
    out = mm(turned[...], joined[:, 3 * col :], tn)
    small = late[0, tok:, :].astype(f32)
    for b in range(1, groups):
        small = small + late[b, tok:, :].astype(f32)
    small_ref[...] = small
    spare = rows - tok
    gains = small[spare - 7 : spare - 6, :]
    top = sublanes((16, col)) == 0
    for i in range(heads):
        out_ref[i, 0:col, :] = out[i * col : (i + 1) * col, :].astype(bf16)
        mine = gains[:, i * col : (i + 1) * col]
        high, low = high_low(mine)
        out_ref[i, col:, :] = jnp.where(
            top, high, jnp.where(sublanes((16, col)) == 1, low, 0.0)
        ).astype(bf16)


def few_experts():
    return lax.axis_size("expert") <= 8


def shards(
    inputs,
    out_grad,
    lengths,
    routes,
    buckets,
    gain_attn,
    w_query,
    w_key,
    w_value,
    w_output,
    bias_table,
    gain_ffn,
    w_router,
    w_in,
    w_out,
):
    tok, col = inputs.shape
    heads_here = bias_table.shape[1]
    head_size = w_query.shape[1] // heads_here
    width, experts = w_router.shape
    bucket_count = bias_table.shape[0]
    heads = width // col
    groups = lax.axis_size("expert")
    me_head, me_expert = lax.axis_index("head"), lax.axis_index("expert")
    capacity = max(2, (4 * tok + 3 * experts - 1) // (3 * experts))
    slots = -(-(capacity + 1) // 8) * 8
    valid_total = 3 * tok * groups // 4
    scale = head_size ** (-0.5)
    w_in, w_out = w_in[0], w_out[0]
    scalars = jnp.stack([lengths[0], me_head.astype(jnp.int32), me_expert.astype(jnp.int32)])
    buckets_row = jnp.pad(buckets, (0, 1), constant_values=-1)[None]

    packed = jnp.concatenate(
        [inputs, out_grad, gain_attn[None], gain_ffn[None], jnp.zeros((14, col), bf16)], axis=0
    )
    packed = lax.all_gather(packed, "head")
    w_output_full = lax.all_gather(w_output, "head")
    qkv, weights, attended, scale_one = call(
        functools.partial(attend_kernel, scale),
        [((tok, 3 * col), bf16), ((heads_here, tok, tok), f32), ((tok, col), bf16), ((tok, 1), f32)],
        scalars, packed, w_query, w_key, w_value, buckets_row, bias_table,
    )

    attended_parts = lax.all_gather(attended, "head")
    residual, residual_own, scale_two, normed_two, router, gate, spots, send = call(
        functools.partial(route_kernel, capacity),
        [
            ((tok, width), f32), ((tok, col), f32), ((tok, 1), f32), ((tok, width), bf16),
            ((tok, experts), f32), ((tok, 1), f32), ((tok, 1), jnp.int32),
            ((experts, slots, 2 * width), bf16),
        ],
        scalars, packed, attended_parts, w_output_full, routes, w_router,
        scratch=[pltpu.VMEM((heads, tok, col), f32)],
    )
    rows = lax.all_to_all(send, "expert", split_axis=0, concat_axis=0, tiled=True)
    rows = rows.reshape(experts * slots, 2 * width)

    back, part, hidden, before_grad, back_rows = call(
        functools.partial(expert_kernel, capacity),
        [
            ((experts * heads, slots, 256), bf16), ((heads, experts * slots, col), f32),
            ((experts * slots, width), bf16), ((experts * slots, width), bf16),
            ((experts * slots, width), bf16),
        ],
        scalars, rows, w_in, w_out, w_router,
    )
    produced = lax.psum_scatter(part, "head", scatter_dimension=0)
    came = lax.all_to_all(back, ("expert", "head"), split_axis=0, concat_axis=0, tiled=True)
    grad_own, gate_grad, stats = call(
        collect_kernel,
        [((tok, col), bf16), ((tok, 1), f32), ((8, experts), f32)],
        came, spots,
    )
    expert_grad = lax.all_gather(grad_own, "head")

    late, first, residual_grad_own, small = call(
        functools.partial(backward_kernel, scale, valid_total),
        [
            ((tok + experts + 8, width), bf16), ((heads, tok, 256), bf16), ((tok, col), f32),
            ((experts + 8, width), f32),
        ],
        scalars, packed, expert_grad, gate_grad, stats, residual, scale_two, normed_two, router, routes,
        w_router, w_output, weights, qkv, w_query, w_key, w_value, scale_one,
        scratch=[pltpu.VMEM((heads, tok, col), f32)],
    )
    if few_experts():
        late_all = lax.all_gather(late, "expert")
        all_in = lax.all_gather(inputs, ("expert", "head")).reshape(groups, heads, tok, col)
        all_attended = lax.all_gather(attended, ("expert", "head")).reshape(groups, heads, tok, col)

    first, produced, rows_after, hidden, _ = lax.optimization_barrier((first, produced, rows, hidden, late))
    first = lax.all_to_all(first, "head", split_axis=0, concat_axis=0, tiled=True)
    returned = lax.all_to_all(
        produced.astype(bf16).reshape(experts, slots, col), "expert", split_axis=0, concat_axis=0, tiled=True
    )
    block_out, input_grad = call(
        finish_kernel,
        [((tok, col), bf16), ((tok, col), f32)],
        returned.reshape(experts * slots, col), first, spots, gate, residual_own, residual_grad_own,
        inputs, gain_attn[None], scale_one,
    )
    in_weight_grad, out_weight_grad = call(
        weights_kernel, [((width, width), f32)] * 2, rows_after, hidden, before_grad, back_rows
    )

    if few_experts():
        normed_all, attended_all = call(
            lambda a, b, c, d, e: turn_kernel(a, b, c, tok, d, e),
            [((groups * tok, width), bf16)] * 2,
            all_in, all_attended, packed,
        )
        q_grad, k_grad, v_grad, traded, small = call(
            products_kernel,
            [((width, col), f32)] * 3 + [((heads, col + 16, col), bf16), ((experts + 8, width), f32)],
            late_all, normed_all, attended_all,
        )
        traded = lax.all_to_all(traded, "head", split_axis=0, concat_axis=0, tiled=True)
        output_grad = jnp.transpose(traded[:, :col], (1, 0, 2)).reshape(col, width).astype(f32)
        gain_one_grad = jnp.sum(traded[:, col : col + 2].astype(f32), axis=(0, 1))
    else:
        x = jnp.transpose(packed[:, :tok], (1, 0, 2)).reshape(tok, width).astype(f32)
        normed = (x * scale_one * packed[:, 2 * tok].reshape(1, width).astype(f32)).astype(bf16)
        summed = lax.psum(
            [mm(normed, late[:tok, i * col : (i + 1) * col], tn) for i in range(3)] + [small], "expert"
        )
        q_grad, k_grad, v_grad, small = summed
        branch = lax.all_gather(late[:tok, 3 * col :], "head", axis=1, tiled=True)
        output_grad = lax.psum(mm(attended, branch, tn), "expert")
        gain_one_grad = lax.psum_scatter(small[experts + 1], "head", tiled=True)
    router_grad = small[:experts].T
    gain_two_grad = lax.dynamic_slice_in_dim(small[experts], me_head * col, col)
    offset_grad = small[experts + 2 : experts + 2 + heads_here, : 2 * tok - 1]
    hot = (buckets[None, :] == jnp.arange(bucket_count)[:, None]).astype(f32)
    table_grad = mm(hot, offset_grad, nt, lax.Precision.HIGHEST)
    aux_loss = experts * jnp.sum(stats[0] * stats[1]) / (valid_total * valid_total)
    return (
        block_out,
        input_grad,
        aux_loss,
        gain_one_grad,
        q_grad,
        k_grad,
        v_grad,
        output_grad,
        table_grad,
        gain_two_grad,
        router_grad,
        in_weight_grad[None],
        out_weight_grad[None],
    )


def solution(mesh):
    return jax.shard_map(
        shards,
        mesh=mesh,
        in_specs=(
            P("expert", "head"),
            P("expert", "head"),
            P("expert"),
            P("expert", None),
            P(),
            P("head"),
            P(None, "head"),
            P(None, "head"),
            P(None, "head"),
            P("head", None),
            P(None, "head"),
            P("head"),
            P(),
            P("expert", None, "head"),
            P("expert", "head", None),
        ),
        out_specs=(
            P("expert", "head"),
            P("expert", "head"),
            P(),
            P("head"),
            P(None, "head"),
            P(None, "head"),
            P(None, "head"),
            P("head", None),
            P(None, "head"),
            P("head"),
            P(),
            P("expert", None, "head"),
            P("expert", "head", None),
        ),
        check_vma=False,
    )
```

time: 300 us -> 262 us (0.87); the launches traced: 295 us -> 261 us
  starting transfers between devices: 101 us -> 7.25 us
  blocking collectives: 0 us -> 73.6 us
  other arithmetic: 28.1 us -> 2.47 us
  matrix products: 25.3 us -> 0.72 us
  Pallas kernels: 0 us -> 17.6 us
  waiting for transfers between devices: 79.8 us -> 96.3 us
    ppermute x70 -> x0, starting transfers between devices: 101 us -> none  [swap(): return lax.ppermute(block, axis, [(i, i ^ offset) for i in range(size)])]
    all_gather x2 -> x4, waiting for transfers between devices: 0.02 us -> 91.5 us  [the longest x1 56.6 us: shards(): lax.all_gather(attended, ('expert', 'head'))]
    ppermute x70 -> x0, waiting for transfers between devices: 79.7 us -> none  [swap(): return lax.ppermute(block, axis, [(i, i ^ offset) for i in range(size)])]
    all_to_all x0 -> x3, blocking collectives: none -> 50.7 us  [the longest x1 22.7 us: shards(): lax.all_to_all(send, 'expert', split_axis=0, concat_axis=0, tiled=True)]
    unnamed x149 -> x109, local copies, waits for them, and re-layouts: 7.09 us -> 36.6 us
    dot_general x27 -> x1, matrix products: 25.3 us -> 0.72 us  [mm(): lax.dot_general(left, right, (dims, ((), ())), precision=precision, prefe...]
    all_gather x0 -> x3, blocking collectives: none -> 23 us  [the longest x1 9.78 us: shards(): packed = lax.all_gather(packed, 'head')]
    pallas_call x0 -> x9, Pallas kernels: none -> 17.6 us  [call(): pl.pallas_call(body, out_shape=[jax.ShapeDtypeStruct(shape, kind) for sha...]
  transfers between devices with their start and end apart: 72 -> 7, of which waited for: 28 -> 4; matrix products, arithmetic and copies ran while one was open for 28% -> 6% of each run, Pallas kernels for 0% -> 4%
where the time goes in v2:
time: 262 us; the launch traced here: 261 us
  waiting for transfers between devices  96.3 us (37%)
  blocking collectives  73.6 us (28%)
  local copies, waits for them, and re-layouts  44.5 us (17%)
  between operations  18.6 us (7%)
  Pallas kernels  17.6 us (7%)
  starting transfers between devices  7.25 us (3%)
    all_gather x1, waiting for transfers between devices, shards(): lax.all_gather(attended, ('expert', 'head'))  56.6 us
    unnamed x109, local copies, waits for them, and re-layouts  36.6 us
    all_gather x1, waiting for transfers between devices, shards(): late_all = lax.all_gather(late, 'expert')  27 us
    all_to_all x1, blocking collectives, shards(): lax.all_to_all(send, 'expert', split_axis=0, concat_axis=0, tiled=True)  22.7 us
    pallas_call x9, Pallas kernels, call(): pl.pallas_call(body, out_shape=[jax.ShapeDtypeStruct(shape, kind) for sha...  17.6 us
    all_to_all x1, blocking collectives, shards(): lax.all_to_all(back, ('expert', 'head'), split_axis=0, concat_axis=0, til...  16.4 us
    all_to_all x1, blocking collectives, shards(): lax.all_to_all(produced.astype(bf16).reshape(experts, slots, col), 'exper...  11.7 us
    all_gather x1, blocking collectives, shards(): packed = lax.all_gather(packed, 'head')  9.78 us
  transfers between devices with their start and end apart: 7, of which 4 were waited for; matrix products, arithmetic and copies ran while one was open for 6% of the time, Pallas kernels for 4%

profile of v2, /device:TPU:0, one launch (start us, length us, event | category | flops | bytes accessed | tf_op | source)
XLA Modules:
  0.0 261.1 jit_solution(368623320200024197)
XLA Ops:
  9.5 0.9 copy.72.inputs
  10.4 0.9 copy.73
  12.7 1.1 copy.74.wq
  13.8 1.1 copy.75.wk
  15.8 9.8 %all-gather = bf16[1088,192]{1,0:T(8,128)(2,1)S(1)} all-gather(bf16[272,192]{1,0:T(8,128)(2,1)S(1)} %concatenate.3), channel_id=2, replica_groups=mesh['expert'=8,'head'=4] {'head'}, dimensions={0}, use_global_device_ids=true | all-gather | bytes 522240 | tf_op jit(solution)/shard_map/all_gather | solution.py:390
  25.6 2.4 shard_map.246
  29.3 7.4 %all-gather.1 = bf16[512,192]{1,0:T(8,128)(2,1)S(1)} all-gather(bf16[128,192]{1,0:T(8,128)(2,1)} %get-tuple-element.51), channel_id=3, replica_groups=mesh['expert'=8,'head'=4] {'head'}, dimensions={0}, use_global_device_ids=true | all-gather | bytes 245760 | tf_op jit(solution)/shard_map/all_gather | solution.py:398
  36.7 1.3 copy-done.7
  38.0 2.2 shard_map.247
  41.5 22.7 %all_to_all.25 = bf16[8,24,1536]{2,1,0:T(8,128)(2,1)S(1)} all-to-all(bf16[8,24,1536]{2,1,0:T(8,128)(2,1)S(1)} %get-tuple-element.52), channel_id=1, replica_groups=mesh['expert'=8,'head'=4] {'expert'}, dimensions={0} | all-to-all | bytes 1179648 | tf_op jit(solution)/shard_map/all_to_all | solution.py:409
  64.2 2.7 %shard_map.248 = (bf16[32,24,256]{2,1,0:T(8,128)(2,1)S(1)}, f32[4,192,192]{2,1,0:T(8,128)S(1)}, bf16[192,768]{1,0:T(8,128)(2,1)S(1)}, bf16[192,768]{1,0:T(8,128)(2,1)S(1)}, bf16[192,768]{1,0:T(8,128)(2,1)S(1)}) custom-call(s32[3]{0:T(128)S(1)} %pad_add_fusion.scalars, bf16[192,1536]{1,0:T(8,128)(2,1)S(1)} %bitcast.29, bf16[768,768]{1,0:T(8,128)(2,1)S(1)} %bitcast.34, ...), custom_call_target="tpu_custom_call" | custom-call | tf_op jit(solution)/shard_map/pallas_call | solution.py:29
  66.9 0.9 copy-done.10
  71.9 16.4 %all_to_all.26.came = bf16[32,24,256]{2,1,0:T(8,128)(2,1)S(1)} all-to-all(bf16[32,24,256]{2,1,0:T(8,128)(2,1)} %copy-done.17), channel_id=1, replica_groups=mesh['expert'=8,'head'=4] {'expert','head'}, dimensions={0} | all-to-all | bytes 786432 | tf_op jit(solution)/shard_map/all_to_all | solution.py:422
  88.7 5.8 %all-gather.3 = bf16[512,192]{1,0:T(8,128)(2,1)S(1)} all-gather(bf16[128,192]{1,0:T(8,128)(2,1)S(1)} %get-tuple-element.55), channel_id=5, replica_groups=mesh['expert'=8,'head'=4] {'head'}, dimensions={0}, use_global_device_ids=true | all-gather | bytes 245760 | tf_op jit(solution)/shard_map/all_gather | solution.py:428
  94.5 3.3 %shard_map.250 = (bf16[144,768]{1,0:T(8,128)(2,1)S(1)}, bf16[4,128,256]{2,1,0:T(8,128)(2,1)S(1)}, f32[128,192]{1,0:T(8,128)S(1)}, f32[16,768]{1,0:T(8,128)}) custom-call(s32[3]{0:T(128)S(1)} %pad_add_fusion.scalars, bf16[4,272,192]{2,1,0:T(8,128)(2,1)S(1)} %bitcast.26, bf16[4,128,192]{2,1,0:T(8,128)(2,1)S(1)} %bitcast.36, ...), custom_call_target="tpu_custom_call" | custom-call | tf_op jit(solution)/shard_map/pallas_call | solution.py:29
  99.9 0.9 convert_element_type.16
  100.8 11.7 %all_to_all.27 = bf16[8,24,192]{2,1,0:T(8,128)(2,1)} all-to-all(bf16[8,24,192]{2,1,0:T(8,128)(2,1)S(1)} %bitcast.41), channel_id=1, replica_groups=mesh['expert'=8,'head'=4] {'expert'}, dimensions={0} | all-to-all | bytes 147456 | tf_op jit(solution)/shard_map/all_to_all | solution.py:447
  112.5 3.6 %all-to-all-start.3 = ((bf16[4,128,256]{2,1,0:T(8,128)(2,1)}), bf16[4,128,256]{2,1,0:T(8,128)(2,1)S(1)}, u32[]{:S(2)}, u32[]{:S(2)}) async-start(bf16[4,128,256]{2,1,0:T(8,128)(2,1)} %copy-done.27), calls=%async_computation.4 | async-start | bytes 524288 | tf_op jit(solution)/shard_map/all_to_all | solution.py:446
  116.1 8.0 %all-gather.16.cloned.1.call-done = bf16[4096,192]{0,1:T(8,128)(2,1)} async-done(((bf16[128,192]{0,1:T(8,128)(2,1)}), bf16[4096,192]{0,1:T(8,128)(2,1)}) %all-gather.16.cloned.1.call-update) | async-done | bytes 1572880 | tf_op jit(solution)/shard_map/all_gather | solution.py:442
  124.0 3.1 %copy.87 = bf16[4096,192]{1,0:T(8,128)(2,1)S(1)} copy(bf16[4096,192]{0,1:T(8,128)(2,1)} %all-gather.16.cloned.1.call-done) | data formatting | bytes 3145728 | tf_op jit(solution)/shard_map/all_gather | solution.py:442
  127.2 56.6 %all-gather.18.cloned.1.call-done = bf16[4096,192]{1,0:T(8,128)(2,1)} async-done(((bf16[128,192]{1,0:T(8,128)(2,1)}), bf16[4096,192]{1,0:T(8,128)(2,1)}) %all-gather.18.cloned.1.call-update) | async-done | bytes 1572880 | tf_op jit(solution)/shard_map/all_gather | solution.py:443
  183.7 1.6 copy-done
  185.3 1.5 shard_map.252
  186.8 1.2 copy-done.2
  188.0 1.2 copy-done.4
  190.6 1.0 copy-done.20
  191.5 1.0 copy-done.22
  192.5 1.0 copy-done.24
  193.5 2.8 %shard_map.254 = (f32[768,768]{1,0:T(8,128)}, f32[768,768]{1,0:T(8,128)}) custom-call(bf16[192,1536]{1,0:T(8,128)(2,1)S(1)} %bitcast.30, bf16[192,768]{1,0:T(8,128)(2,1)S(1)} %copy-done.20, bf16[192,768]{1,0:T(8,128)(2,1)S(1)} %copy-done.22, bf16[192,768]{1,0:T(8,128)(2,1)S(1)} %copy-done.24), custom_call_target="tpu_custom_call" | custom-call | tf_op jit(solution)/shard_map/pallas_call | solution.py:29
  196.3 0.8 copy-done.16
  197.1 0.9 copy-done.18
  198.0 0.8 copy-done.26
  199.7 0.9 copy-done.38
  200.6 0.9 copy-done.40
  201.5 0.8 copy-done.42
  204.0 27.0 %all-gather.14.cloned.1.call-done = bf16[1152,768]{1,0:T(8,128)(2,1)} async-done(((bf16[144,768]{1,0:T(8,128)(2,1)}), bf16[1152,768]{1,0:T(8,128)(2,1)}) %all-gather.14.cloned.1.call-update) | async-done | bytes 1769488 | tf_op jit(solution)/shard_map/all_gather | solution.py:441
  231.0 1.5 copy-done.1
  232.5 1.4 copy-done.5
  233.9 2.2 shard_map.253
  236.1 0.9 copy-done.11
  237.0 0.9 copy-done.13
  238.6 1.0 copy.88
  239.5 3.5 %all-to-all-start.4 = ((bf16[4,208,192]{1,2,0:T(8,128)(2,1)}), bf16[4,208,192]{1,2,0:T(8,128)(2,1)S(1)}, u32[]{:S(2)}, u32[]{:S(2)}) async-start(bf16[4,208,192]{1,2,0:T(8,128)(2,1)} %copy.88), calls=%async_computation.5 | async-start | bytes 786432 | tf_op jit(solution)/shard_map/all_to_all | solution.py:471
  243.7 1.1 copy.92
  244.7 1.1 copy.93
  245.8 1.1 copy.94
  247.5 2.9 %all-to-all-done.4 = bf16[4,208,192]{1,2,0:T(8,128)(2,1)S(1)} async-done(((bf16[4,208,192]{1,2,0:T(8,128)(2,1)}), bf16[4,208,192]{1,2,0:T(8,128)(2,1)S(1)}, u32[]{:S(2)}, u32[]{:S(2)}) %all-to-all-start.4) | async-done | bytes 319520 | tf_op jit(solution)/shard_map/all_to_all | solution.py:471
  250.5 1.1 copy.95
  (112 shorter events, 18.1 us)
Async XLA Ops:
  8.0 6.9 %copy-start.43 = (bf16[768,192]{0,1:T(8,128)(2,1)S(1)}, bf16[768,192]{0,1:T(8,128)(2,1)}, u32[]{:S(2)}) copy-start(bf16[768,192]{0,1:T(8,128)(2,1)} %param.23) | copy-start | bytes 884740
  8.0 7.1 %copy-start.45 = (f32[32,3]{0,1:T(4,128)S(1)}, f32[32,3]{0,1:T(4,128)}, u32[]{:S(2)}) copy-start(f32[32,3]{0,1:T(4,128)} %param.25) | copy-start | bytes 1156
  8.0 7.2 %copy-start.47 = (s32[128,1]{0,1:T(1,128)S(1)}, s32[128,1]{0,1:T(1,128)}, u32[]{:S(2)}) copy-start(s32[128,1]{0,1:T(1,128)} %param.18) | copy-start | bytes 1540
  8.0 7.3 %copy-start.44 = (bf16[768,8]{0,1:T(8,128)(2,1)S(1)}, bf16[768,8]{0,1:T(8,128)(2,1)}, u32[]{:S(2)}) copy-start(bf16[768,8]{0,1:T(8,128)(2,1)} %param.27) | copy-start | bytes 36868
  8.1 7.5 %copy-start.46 = (s32[255]{0:T(256)S(1)}, s32[255]{0:T(256)}, u32[]{:S(2)}) copy-start(s32[255]{0:T(256)} %param.19) | copy-start | bytes 3064
  8.1 28.7 %all-gather.12.cloned.1.call-start = ((), (), s32[]{:S(2)}) async-start(), calls=%async_computation.7 | async-start | bytes 1474560 | tf_op jit(solution)/shard_map/all_gather | solution.py:391
  8.8 91.1 %reduce-scatter.2.cloned.1.call-start = ((), (), s32[]{:S(2)}) async-start(), calls=%async_computation.6 | async-start | bytes 983040 | tf_op jit(solution)/shard_map/reduce_scatter | solution.py:421
  10.4 15.2 %copy-start.15 = (bf16[128,192]{1,0:T(8,128)(2,1)}, bf16[128,192]{1,0:T(8,128)(2,1)S(1)}, u32[]{:S(2)}) copy-start(bf16[128,192]{1,0:T(8,128)(2,1)S(1)} %copy.72.inputs) | copy-start | bytes 147460
  29.3 65.2 %copy-start.25 = (f32[128,1]{1,0:T(8,128)}, f32[128,1]{1,0:T(8,128)S(1)}, u32[]{:S(2)}) copy-start(f32[128,1]{1,0:T(8,128)S(1)} %get-tuple-element.64.scale_one) | copy-start | bytes 1540
  36.7 1.3 copy-start.7
  38.0 26.2 %copy-start.8 = (bf16[1,768,768]{2,1,0:T(8,128)(2,1)S(1)}, bf16[1,768,768]{2,1,0:T(8,128)(2,1)}, u32[]{:S(2)}) copy-start(bf16[1,768,768]{2,1,0:T(8,128)(2,1)} %param.28) | copy-start | bytes 3538948
  38.0 26.2 %copy-start.9 = (bf16[1,768,768]{2,1,0:T(8,128)(2,1)S(1)}, bf16[1,768,768]{2,1,0:T(8,128)(2,1)}, u32[]{:S(2)}) copy-start(bf16[1,768,768]{2,1,0:T(8,128)(2,1)} %param.29) | copy-start | bytes 3538948
  41.5 22.7 %copy-start.41 = (f32[128,1]{1,0:T(8,128)}, f32[128,1]{1,0:T(8,128)S(1)}, u32[]{:S(2)}) copy-start(f32[128,1]{1,0:T(8,128)S(1)} %get-tuple-element.71.gate) | copy-start | bytes 1540
  41.5 46.8 %copy-start.28 = (s32[128,1]{1,0:T(8,128)}, s32[128,1]{1,0:T(8,128)S(1)}, u32[]{:S(2)}) copy-start(s32[128,1]{1,0:T(8,128)S(1)} %get-tuple-element.54.spots) | copy-start | bytes 1540
  66.9 0.9 copy-start.10
  67.7 0.7 copy-start.17
  68.5 0.7 copy-start.19
  69.2 0.7 copy-start.21
  69.9 0.7 copy-start.23
  70.6 23.9 %copy-start.6 = (bf16[192,768]{1,0:T(8,128)(2,1)S(1)}, bf16[192,768]{1,0:T(8,128)(2,1)}, u32[]{:S(2)}) copy-start(bf16[192,768]{1,0:T(8,128)(2,1)} %w_output.1) | copy-start | bytes 884740
  70.7 53.4 %all-gather.16.cloned.1.call-start = ((), (), s32[]{:S(2)}) async-start(), calls=%async_computation.9 | async-start | bytes 1622016 | tf_op jit(solution)/shard_map/all_gather | solution.py:442
  71.2 112.5 %all-gather.18.cloned.1.call-start = ((), (), s32[]{:S(2)}) async-start(), calls=%async_computation.10 | async-start | bytes 2162688 | tf_op jit(solution)/shard_map/all_gather | solution.py:443
  71.8 159.2 %all-gather.14.cloned.1.call-start = ((), (), s32[]{:S(2)}) async-start(), calls=%async_computation.8 | async-start | bytes 1990656 | tf_op jit(solution)/shard_map/all_gather | solution.py:441
  71.9 22.6 %copy-start.32 = (f32[3,128,128]{2,1,0:T(8,128)S(1)}, f32[3,128,128]{2,1,0:T(8,128)}, u32[]{:S(2)}) copy-start(f32[3,128,128]{2,1,0:T(8,128)} %copy-done.31) | copy-start | bytes 589828
  71.9 22.6 %copy-start.34 = (bf16[128,768]{1,0:T(8,128)(2,1)S(1)}, bf16[128,768]{1,0:T(8,128)(2,1)}, u32[]{:S(2)}) copy-start(bf16[128,768]{1,0:T(8,128)(2,1)} %copy-done.33) | copy-start | bytes 589828
  71.9 22.6 %copy-start.36 = (bf16[128,576]{1,0:T(8,128)(2,1)S(1)}, bf16[128,576]{1,0:T(8,128)(2,1)}, u32[]{:S(2)}) copy-start(bf16[128,576]{1,0:T(8,128)(2,1)} %copy-done.35) | copy-start | bytes 442372
  112.5 83.8 %all-to-all-start.3 = ((bf16[4,128,256]{2,1,0:T(8,128)(2,1)}), bf16[4,128,256]{2,1,0:T(8,128)(2,1)S(1)}, u32[]{:S(2)}, u32[]{:S(2)}) async-start(bf16[4,128,256]{2,1,0:T(8,128)(2,1)} %copy-done.27), calls=%async_computation.4 | async-start | bytes 524288 | tf_op jit(solution)/shard_map/all_to_all | solution.py:446
  183.7 1.6 copy-start
  186.8 1.2 copy-start.2
  188.0 1.2 copy-start.4
  189.8 41.2 %copy-start.3 = (bf16[1024,768]{1,0:T(8,128)(2,1)S(1)}, bf16[1024,768]{1,0:T(8,128)(2,1)}, u32[]{:S(2)}) copy-start(bf16[1024,768]{1,0:T(8,128)(2,1)} %copy-done.2) | copy-start | bytes 4718596
  190.6 1.0 copy-start.20
  191.5 1.0 copy-start.22
  192.5 1.0 copy-start.24
  196.3 0.8 copy-start.16
  197.1 0.9 copy-start.18
  198.0 0.8 copy-start.26
  198.8 0.8 copy-start.29
  199.7 0.9 copy-start.38
  200.6 0.9 copy-start.40
  201.5 0.8 copy-start.42
  231.0 1.5 copy-start.1
  232.5 1.4 copy-start.5
  236.1 0.9 copy-start.11
  237.0 0.9 copy-start.13
  237.9 5.8 %copy-start.14 = (f32[768,192]{1,0:T(8,128)S(1)}, f32[768,192]{1,0:T(8,128)}, u32[]{:S(2)}) copy-start(f32[768,192]{1,0:T(8,128)} %copy-done.13) | copy-start | bytes 1769476
  237.9 6.9 %copy-start.12 = (f32[768,192]{1,0:T(8,128)S(1)}, f32[768,192]{1,0:T(8,128)}, u32[]{:S(2)}) copy-start(f32[768,192]{1,0:T(8,128)} %copy-done.11) | copy-start | bytes 1769476
  239.5 10.9 %all-to-all-start.4 = ((bf16[4,208,192]{1,2,0:T(8,128)(2,1)}), bf16[4,208,192]{1,2,0:T(8,128)(2,1)S(1)}, u32[]{:S(2)}, u32[]{:S(2)}) async-start(bf16[4,208,192]{1,2,0:T(8,128)(2,1)} %copy.88), calls=%async_computation.5 | async-start | bytes 786432 | tf_op jit(solution)/shard_map/all_to_all | solution.py:471
  (7 other events, 4.7 us)
Sparse Core Ops, SparseCore 0:
  10.5 21.0 all-gather.11
  70.8 22.3 reduce-scatter.1
Sparse Core Ops, SparseCore 1:
  74.4 49.6 all-gather.15
  127.7 55.9 all-gather.17
  186.0 44.9 all-gather.13

commit v3 on v2

v3 whole, which is shorter than its diff:
```python
import functools

import jax
import jax.numpy as jnp
from jax import lax
from jax.experimental import pallas as pl
from jax.experimental.pallas import tpu as pltpu
from jax.sharding import PartitionSpec as P

eps = 1e-06
aux_weight = 0.01
f32 = jnp.float32
bf16 = jnp.bfloat16
gelu_scale = 0.7978845608028654
gelu_cube = 0.044715
highest = lax.Precision.HIGHEST
nt = ((1,), (1,))
tn = ((0,), (0,))


def mm(left, right, dims=((1,), (0,)), precision=None):
    return lax.dot_general(left, right, (dims, ((), ())), precision=precision, preferred_element_type=f32)


def call(body, outs, *args, scratch=()):
    scalar_memory = pl.BlockSpec(memory_space=pltpu.SMEM)
    in_specs = [scalar_memory if a.dtype == jnp.int32 and a.ndim == 1 else pl.BlockSpec() for a in args]
    shapes = []
    for shape, kind, *far in outs:
        shapes.append(pltpu.HBM(shape, kind) if far else jax.ShapeDtypeStruct(shape, kind))
    return pl.pallas_call(
        body,
        out_shape=shapes,
        in_specs=in_specs,
        scratch_shapes=list(scratch),
        compiler_params=pltpu.CompilerParams(vmem_limit_bytes=40 * 1024 * 1024),
    )(*args)


def tall(ref, first, rows):
    return jnp.concatenate([ref[i, first : first + rows, :].astype(f32) for i in range(ref.shape[0])], axis=0)


def gain_columns(block):
    turned = jnp.transpose(block.astype(f32))
    return [jnp.concatenate([turned[:, i : i + 1], turned[:64, i + 1 : i + 2]], axis=0) for i in (0, 2)]


def all_gains(packed):
    first = 2 * packed.shape[2] * 3 // 2
    pairs = [gain_columns(packed[i, first : first + 16, :]) for i in range(packed.shape[0])]
    return [jnp.concatenate([pair[i] for pair in pairs], axis=0) for i in range(2)]


def token_scale(values):
    return lax.rsqrt(jnp.sum(values * values, axis=0, keepdims=True) * (1.0 / values.shape[0]) + eps)


def lanes(shape):
    return lax.broadcasted_iota(jnp.int32, shape, len(shape) - 1)


def sublanes(shape):
    return lax.broadcasted_iota(jnp.int32, shape, len(shape) - 2)


def side_lanes(rows, width, columns):
    spot = lanes((rows, width))
    out = jnp.zeros((rows, width), f32)
    for i, column in enumerate(columns):
        out = jnp.where(spot == i, column, out)
    return out


def side_rows(rows, width, lines):
    spot = sublanes((rows, width))
    out = jnp.zeros((rows, width), f32)
    for i, line in enumerate(lines):
        out = jnp.where(spot == i, line, out)
    return out


def high_low(values, count=2):
    pieces = []
    for _ in range(count):
        piece = values.astype(bf16).astype(f32)
        pieces.append(piece)
        values = values - piece
    return pieces


def softmax(values, axis):
    raised = jnp.exp(values - jnp.max(values, axis=axis, keepdims=True))
    return raised / jnp.sum(raised, axis=axis, keepdims=True)


def gelu_parts(u):
    t = jnp.tanh(gelu_scale * (u + gelu_cube * u * u * u))
    value = 0.5 * u * (1.0 + t)
    slope = 0.5 * (1.0 + t) + 0.5 * u * (1.0 - t * t) * gelu_scale * (1.0 + 3.0 * gelu_cube * u * u)
    return value, slope


def fold_lanes(rows):
    return jnp.concatenate([rows[:, i : i + 128] for i in range(0, rows.shape[1], 128)], axis=0)


def unfold_lanes(rows, pieces):
    size = rows.shape[0] // pieces
    return jnp.concatenate([rows[i * size : (i + 1) * size] for i in range(pieces)], axis=1)


def pick_slots(spots, count):
    return sublanes((count, spots.shape[1])) == spots


def attend_kernel(scale, scalars, packed, wq, wk, wv, buckets, table, qkv_ref, weights_ref, attended_ref):
    heads, tok, _ = weights_ref.shape
    col = wq.shape[0]
    size = col // heads
    x = tall(packed, 0, col)
    normed = (x * token_scale(x) * all_gains(packed)[0]).astype(bf16)
    projected = []
    for i, w in enumerate((wq, wk, wv)):
        rows = mm(w[...], normed).astype(bf16)
        qkv_ref[i] = rows
        projected.append(rows)
    query, key, value = projected
    hot = (sublanes((table.shape[1], 2 * tok)) == buckets[...]).astype(f32)
    offsets = mm(table[...], hot, precision=highest)
    open_keys = lanes((tok, tok)) < scalars[0]
    outs = []
    for h in range(heads):
        at = slice(h * size, (h + 1) * size)
        spread = jnp.broadcast_to(offsets[h : h + 1, :], (tok, 2 * tok))
        bias = pltpu.roll(spread, tok + 1, 1, stride=1, stride_axis=0)[:, :tok]
        scores = mm(query[at], key[at], tn) * scale + bias
        weights = softmax(jnp.where(open_keys, scores, -1000000000.0), 1)
        weights_ref[h] = weights
        outs.append(mm(value[at], weights.astype(bf16), nt))
    attended_ref[...] = jnp.concatenate(outs, axis=0).astype(bf16)


def second_norm(residual, gain, w_router):
    scale = token_scale(residual)
    unit = residual * scale
    normed = (unit * gain).astype(bf16)
    return scale, unit, normed, softmax(mm(w_router, normed), 0)


def route_kernel(capacity, scalars, packed, attended, w_output, routes, w_router, residual_ref, side_ref, send_ref):
    tok = routes.shape[1]
    experts, slots, _ = send_ref.shape
    heads, col, _ = residual_ref.shape
    width = heads * col
    branch = mm(tall(attended, 0, col).astype(bf16), w_output[...], tn)
    residual = tall(packed, 0, col) + jnp.transpose(branch)
    for i in range(heads):
        residual_ref[i] = residual[i * col : (i + 1) * col]
    _, _, normed, router = second_norm(residual, all_gains(packed)[1], w_router[...])
    route_hot = (sublanes((experts, tok)) == routes[...]).astype(f32)
    gate = jnp.sum(router * route_hot, axis=0, keepdims=True)
    before = (sublanes((tok, tok)) < lanes((tok, tok))).astype(bf16)
    slot = jnp.sum(mm(route_hot.astype(bf16), before) * route_hot, axis=0, keepdims=True)
    spots = routes[...].astype(f32) * slots + slot
    side_ref[...] = side_rows(8, tok, [gate, spots])
    valid = (lanes((1, tok)) < scalars[0]).astype(f32)
    counts = jnp.sum(route_hot * valid, axis=1, keepdims=True)
    probs = high_low(jnp.sum(router * valid, axis=1, keepdims=True), 3)
    pick = pick_slots(spots.astype(jnp.int32), experts * slots).astype(bf16)
    rows = mm(pick, normed, nt)
    grads = mm(pick, tall(packed, col, col).astype(bf16), nt)
    for e in range(experts):
        at = slice(e * slots, (e + 1) * slots)
        send_ref[e, :, :width] = rows[at].astype(bf16)
        stats = side_lanes(1, width, [counts[e : e + 1]] + [piece[e : e + 1] for piece in probs])
        filled = jnp.where(sublanes((slots, width)) == capacity, stats, grads[at])
        send_ref[e, :, width:] = filled.astype(bf16)


def expert_kernel(
    capacity, scalars, rows_ref, w_in, w_out, w_router, back_ref, part_ref, hidden_ref, before_ref, grads_ref
):
    total = rows_ref.shape[0]
    experts, width = w_router.shape
    heads = part_ref.shape[0]
    col = width // heads
    slots = total // experts
    half = total // 2
    rows = rows_ref[:, :width]
    grads = rows_ref[:, width:].astype(f32)
    hidden, slope = gelu_parts(mm(rows, w_in[...]))
    hidden = hidden.astype(bf16)
    hidden_ref[...] = hidden
    produced = mm(hidden, w_out[...])
    for i in range(heads):
        mine = produced[:, i * col : (i + 1) * col]
        rest = mine[:, 128:]
        part_ref[i] = jnp.concatenate(
            [mine[:, :128], jnp.concatenate([rest[:half], rest[half:]], axis=1)], axis=0
        ).astype(bf16)
    probs = softmax(mm(rows, w_router[...], nt), 1)
    gate = jnp.sum(jnp.where(lanes((total, experts)) == scalars[2], probs, 0.0), axis=1, keepdims=True)
    back = (gate * grads).astype(bf16)
    grads_ref[...] = back
    before = (mm(back, w_out[...], nt) * slope).astype(bf16)
    before_ref[...] = before
    rows_grad = mm(before, w_in[...], nt)
    gate_grad = jnp.sum(grads * produced, axis=1, keepdims=True)
    stats = jnp.zeros((1, 128), f32)
    for b in range(experts):
        stats = stats + grads[b * slots + capacity : b * slots + capacity + 1, :128]
    prob = stats[:, 1:2] + stats[:, 2:3] + stats[:, 3:4]
    side = side_lanes(
        total, 256 - col, high_low(gate_grad) + high_low(stats[:, 0:1]) + high_low(prob, 3)
    )
    for b in range(experts):
        at = slice(b * slots, (b + 1) * slots)
        for i in range(heads):
            back_ref[b * heads + i] = jnp.concatenate(
                [rows_grad[at, i * col : (i + 1) * col], side[at]], axis=1
            ).astype(bf16)


def weights_kernel(rows_ref, hidden, before, grads, in_ref, out_ref):
    width = in_ref.shape[0]
    in_ref[...] = mm(rows_ref[:, :width], before[...], tn)
    out_ref[...] = mm(hidden[...], grads[...], tn)


def collect_kernel(came, side, grad_ref, gate_ref, stats_ref):
    col, tok = grad_ref.shape
    experts = stats_ref.shape[0]
    sources, slots, _ = came.shape
    heads = sources // experts
    sums = []
    for e in range(experts):
        total = came[e * heads].astype(f32)
        for i in range(1, heads):
            total = total + came[e * heads + i].astype(f32)
        sums.append(total)
    stats = jnp.concatenate([total[0:1, col:] for total in sums], axis=0) * (1.0 / heads)
    sums = jnp.concatenate(sums, axis=0)
    pick = pick_slots(side[1:2, :].astype(jnp.int32), experts * slots)
    grad_ref[...] = mm(sums[:, :col].astype(bf16), pick.astype(bf16), tn).astype(bf16)
    gate = mm(sums[:, col:], pick.astype(f32), tn, highest)
    gate_ref[...] = jnp.broadcast_to(gate[0:1] + gate[1:2], gate_ref.shape)
    count = stats[:, 2:3] + stats[:, 3:4]
    prob = stats[:, 4:5] + stats[:, 5:6] + stats[:, 6:7]
    stats_ref[...] = side_lanes(experts, 128, [count, prob])


def backward_kernel(
    scale, valid_total, scalars, packed, expert_grad, gate_grad, stats, residual_ref, routes, w_router,
    w_output, weights_ref, qkv, wq, wk, wv, attended, part, late_ref, first_ref, own_ref, small_ref, product_ref,
):
    tok = routes.shape[1]
    heads_here = weights_ref.shape[0]
    blocks, col, _ = residual_ref.shape
    experts, width = w_router.shape
    size = col // heads_here
    gain_one, gain_two = all_gains(packed)
    residual = tall(residual_ref, 0, col)
    scale_two, unit, normed, router = second_norm(residual, gain_two, w_router[...])
    valid = (lanes((1, tok)) < scalars[0]).astype(f32)
    route_hot = (sublanes((experts, tok)) == routes[...]).astype(f32)
    fraction = stats[:, 0:1] * (aux_weight * experts / (valid_total * valid_total))
    prob_grad = route_hot * gate_grad[0:1, :] + fraction * valid
    logit_grad = router * (prob_grad - jnp.sum(router * prob_grad, axis=0, keepdims=True))
    logit_grad = logit_grad.astype(bf16)
    normed_grad = mm(w_router[...], logit_grad, tn) + tall(expert_grad, 0, col)
    unit_grad = normed_grad * gain_two
    mean = jnp.sum(unit_grad * unit, axis=0, keepdims=True) * (1.0 / width)
    residual_grad = tall(packed, col, col) + scale_two * (unit_grad - unit * mean)
    branch = residual_grad.astype(bf16)
    attended_grad = mm(w_output[...], branch).astype(bf16)
    flip = (lanes((tok, tok)) + sublanes((tok, tok)) == tok - 1).astype(bf16)
    query, key, value = qkv[0], qkv[1], qkv[2]
    grads = [[], [], []]
    offsets = []
    for h in range(heads_here):
        at = slice(h * size, (h + 1) * size)
        out = attended_grad[at]
        weights = weights_ref[h]
        mass = mm(out, value[at], tn)
        score = weights * (mass - jnp.sum(weights * mass, axis=1, keepdims=True))
        score = score.astype(bf16)
        grads[0].append(mm(key[at], score, nt) * scale)
        grads[1].append(mm(query[at], score) * scale)
        grads[2].append(mm(out, weights.astype(bf16)))
        flipped = jnp.concatenate([mm(flip, score), jnp.zeros((tok, tok), f32)], axis=1)
        rolled = pltpu.roll(flipped, 0, 1, stride=1, stride_axis=0)
        offsets.append(jnp.sum(rolled, axis=0, keepdims=True))
    first = jnp.zeros((width, tok), f32)
    row = jnp.zeros((1, tok), f32)
    for i, w in enumerate((wq, wk, wv)):
        low = jnp.concatenate(grads[i], axis=0).astype(bf16)
        late_ref[i * col : (i + 1) * col, :] = low
        first = first + mm(w[...], low, tn)
        row = row + jnp.sum(low.astype(f32) * qkv[i].astype(f32), axis=0, keepdims=True)
    side = side_rows(16, tok, high_low(row))
    for i in range(blocks):
        at = slice(i * col, (i + 1) * col)
        first_ref[i, : col + 16, :] = jnp.concatenate([first[at], side], axis=0).astype(bf16)
        first_ref[i, col + 16 :, :] = part[i]

    product_ref[...] = mm(attended[...], branch, nt).astype(product_ref.dtype)
    gain_two_grad = jnp.sum(normed_grad * unit, axis=1, keepdims=True)
    gains = jnp.zeros((col, 1), f32)
    own = jnp.zeros((col, tok), f32)
    for i in range(blocks):
        at = slice(i * col, (i + 1) * col)
        gains = jnp.where(scalars[1] == i, gain_two_grad[at], gains)
        own = jnp.where(scalars[1] == i, residual_grad[at], own)
    own_ref[...] = own
    gains = jnp.transpose(side_lanes(col, 128, [gains]))[0:8]
    router_grad = mm(logit_grad, normed, nt)
    offsets = jnp.concatenate(offsets, axis=0)
    offsets = jnp.concatenate([offsets, jnp.zeros((8 - heads_here, 2 * tok), f32)], axis=0)
    gains = jnp.concatenate([gains, jnp.zeros((8, 64), f32)], axis=1)
    small_ref[...] = jnp.concatenate(
        [fold_lanes(router_grad), fold_lanes(offsets), fold_lanes(gains)], axis=0
    )


def first_kernel(joined, scalars, came, packed, own, small, ret_ref, sums_ref, input_ref):
    col, tok = own.shape
    heads = came.shape[0]
    experts = ret_ref.shape[0]
    total = came[0].astype(f32)
    for i in range(1, heads):
        total = total + came[i].astype(f32)
    mean = (total[col : col + 1] + total[col + 1 : col + 2]) * (1.0 / (heads * col))
    scale = token_scale(tall(packed, 0, col))
    mine = packed[scalars[1]].astype(f32)
    unit = mine[:col] * scale
    gain = gain_columns(mine[2 * col : 2 * col + 16])[0]
    input_ref[...] = own[...] + scale * (total[:col] * gain - unit * mean)
    gain_grad = jnp.sum(total[:col] * unit, axis=1, keepdims=True)
    gain_grad = jnp.transpose(side_lanes(col, 128, [jnp.zeros_like(gain_grad), gain_grad]))[0:8]
    gain_grad = jnp.concatenate([gain_grad, jnp.zeros((8, 64), f32)], axis=1)
    kept = small.shape[0] - 16
    sums = jnp.concatenate([small[:kept, :], small[kept:, :] + fold_lanes(gain_grad)], axis=0)
    sums_ref[...] = sums
    produced = total[col + 16 :]
    count = produced.shape[0] * 2 // 3
    half = count // 2
    top = produced[:count]
    rest = jnp.concatenate([produced[count:, :64], produced[count:, 64:]], axis=0)
    rest = jnp.concatenate([rest, jnp.zeros((count, 64), f32)], axis=1)
    slots = count // experts
    for e in range(experts):
        at = slice(e * slots, (e + 1) * slots)
        pieces = [top[at], rest[at]]
        if joined:
            pieces.append(sums)
        ret_ref[e] = jnp.concatenate(pieces, axis=0).astype(bf16)


def last_kernel(slots, scalars, came, side, residual, stats, buckets, *refs):
    block_ref, aux_ref, refs = refs[0], refs[1], refs[2:]
    experts = came.shape[0]
    heads, col, tok = residual.shape
    blocks = [came[e].astype(f32) for e in range(experts)]
    top = jnp.concatenate([block[:slots] for block in blocks], axis=0).astype(bf16)
    rest = jnp.concatenate([block[slots : 2 * slots] for block in blocks], axis=0).astype(bf16)
    pick = pick_slots(side[1:2, :].astype(jnp.int32), experts * slots).astype(bf16)
    returned = jnp.concatenate([mm(top, pick, tn), mm(rest, pick, tn)[: col - 128]], axis=0)
    block_ref[...] = (residual[scalars[1]] + side[0:1, :] * returned).astype(bf16)
    product = stats[:, 0:1] * stats[:, 1:2]
    valid_total = 3 * tok * experts // 4
    aux_ref[...] = jnp.sum(product, axis=0, keepdims=True) * (experts / (valid_total * valid_total))
    if refs:
        router_ref, table_ref, gains_ref = refs
        total = blocks[0][2 * slots :]
        for block in blocks[1:]:
            total = total + block[2 * slots :]
        wide = 6 * experts
        router_ref[...] = unfold_lanes(total[:wide], 6)
        offsets = unfold_lanes(total[wide : wide + 16], 2)
        hot = (sublanes((table_ref.shape[1], 2 * tok)) == buckets[...]).astype(f32)
        table_ref[...] = mm(offsets, hot, nt, highest)[: table_ref.shape[0]]
        gains_ref[...] = unfold_lanes(total[wide + 16 :], 2)


def turn_kernel(all_in, packed, normed_ref):
    groups, heads, col, tok = all_in.shape
    gain = all_gains(packed)[0]
    for b in range(groups):
        x = jnp.concatenate([all_in[b, i].astype(f32) for i in range(heads)], axis=0)
        normed_ref[:, b * tok : (b + 1) * tok] = (x * token_scale(x) * gain).astype(bf16)


def products_kernel(late, normed, q_ref, k_ref, v_ref):
    col = q_ref.shape[0]
    joined = jnp.concatenate([late[b] for b in range(late.shape[0])], axis=1)
    for i, ref in enumerate((q_ref, k_ref, v_ref)):
        ref[...] = mm(joined[i * col : (i + 1) * col], normed[...], nt)


def few_experts():
    return lax.axis_size("expert") <= 8


def shards(
    inputs,
    out_grad,
    lengths,
    routes,
    buckets,
    gain_attn,
    w_query,
    w_key,
    w_value,
    w_output,
    bias_table,
    gain_ffn,
    w_router,
    w_in,
    w_out,
):
    tok, col = inputs.shape
    heads_here = bias_table.shape[1]
    head_size = w_query.shape[1] // heads_here
    width, experts = w_router.shape
    bucket_count = bias_table.shape[0]
    heads = width // col
    groups = lax.axis_size("expert")
    me_head, me_expert = lax.axis_index("head"), lax.axis_index("expert")
    capacity = max(2, (4 * tok + 3 * experts - 1) // (3 * experts))
    slots = -(-(capacity + 1) // 8) * 8
    total = experts * slots
    valid_total = 3 * tok * groups // 4
    scale = head_size ** (-0.5)
    joined = few_experts()
    w_in, w_out = w_in[0], w_out[0]
    wq, wk, wv = w_query.T, w_key.T, w_value.T
    routes_row = routes.T
    router_rows = w_router.T
    scalars = jnp.stack([lengths[0], me_head.astype(jnp.int32), me_expert.astype(jnp.int32)])
    buckets_row = jnp.pad(buckets, (0, 1), constant_values=-1)[None]

    gains = jnp.pad(jnp.stack([gain_attn, gain_ffn]), ((0, 6), (0, 64))).reshape(16, 128)
    packed = lax.all_gather(jnp.concatenate([inputs.T, out_grad.T, gains], axis=0), "head")
    w_output_full = lax.all_gather(w_output, "head", tiled=True)
    if joined:
        all_in = lax.all_gather(inputs.T, ("expert", "head")).reshape(groups, heads, col, tok)
    qkv, weights, attended = call(
        functools.partial(attend_kernel, scale),
        [((3, col, tok), bf16, 1), ((heads_here, tok, tok), f32, 1), ((col, tok), bf16)],
        scalars, packed, wq, wk, wv, buckets_row, bias_table.T,
    )

    attended_parts = lax.all_gather(attended, "head")
    residual, side, send = call(
        functools.partial(route_kernel, capacity),
        [((heads, col, tok), f32, 1), ((8, tok), f32, 1), ((experts, slots, 2 * width), bf16)],
        scalars, packed, attended_parts, w_output_full, routes_row, router_rows,
    )
    rows = lax.all_to_all(send, "expert", split_axis=0, concat_axis=0, tiled=True)
    rows = rows.reshape(total, 2 * width)

    back, part, hidden, before_grad, back_rows = call(
        functools.partial(expert_kernel, capacity),
        [((experts * heads, slots, 256), bf16), ((heads, total * 3 // 2, 128), bf16, 1)]
        + [((total, width), bf16, 1)] * 3,
        scalars, rows, w_in, w_out, router_rows,
    )
    came = lax.all_to_all(back, ("expert", "head"), split_axis=0, concat_axis=0, tiled=True)
    grad_own, gate_grad, stats = call(
        collect_kernel,
        [((col, tok), bf16), ((8, tok), f32, 1), ((experts, 128), f32, 1)],
        came, side,
    )
    expert_grad = lax.all_gather(grad_own, "head")

    late, first, residual_grad_own, small, product = call(
        functools.partial(backward_kernel, scale, valid_total),
        [
            ((3 * col, tok), bf16, 1), ((heads, col + 16 + total * 3 // 2, 128), bf16), ((col, tok), f32, 1),
            ((6 * experts + 32, 128), f32, 1), ((col, width), bf16 if joined else f32, 1),
        ],
        scalars, packed, expert_grad, gate_grad, stats, residual, routes_row, router_rows,
        w_output, weights, qkv, wq, wk, wv, attended, part,
    )

    output_grad = lax.psum(product, "expert").astype(f32)
    if joined:
        late_all = lax.all_gather(late, "expert")

    first = lax.all_to_all(first, "head", split_axis=0, concat_axis=0, tiled=True)
    ret, sums, input_grad = call(
        functools.partial(first_kernel, joined),
        [
            ((experts, 2 * slots + (6 * experts + 32 if joined else 0), 128), bf16),
            ((6 * experts + 32, 128), f32, 1), ((col, tok), f32),
        ],
        scalars, first, packed, residual_grad_own, small,
    )
    ret = lax.all_to_all(ret, "expert", split_axis=0, concat_axis=0, tiled=True)
    out = call(
        functools.partial(last_kernel, slots),
        [((col, tok), bf16), ((1, 1), f32)]
        + ([((experts, width), f32), ((heads_here, bucket_count), f32), ((8, 256), f32)] if joined else []),
        scalars, ret, side, residual, stats, buckets_row,
    )
    block_out, aux_loss = out[:2]
    in_weight_grad, out_weight_grad = call(
        weights_kernel, [((width, width), f32)] * 2, rows, hidden, before_grad, back_rows
    )
    if joined:
        router_grad, table_grad, gain_grads = out[2:]
        normed_all = call(turn_kernel, [((width, groups * tok), bf16)], all_in, packed)[0]
        q_grad, k_grad, v_grad = call(products_kernel, [((col, width), f32)] * 3, late_all, normed_all)
    else:
        gain = packed[:, 2 * col : 2 * col + 2].reshape(heads, 256)[:, :col].reshape(width, 1)
        x = packed[:, :col].reshape(width, tok).astype(f32)
        normed = (x * token_scale(x) * gain.astype(f32)).astype(bf16)
        products = [mm(late[i * col : (i + 1) * col], normed, nt) for i in range(3)]
        q_grad, k_grad, v_grad, sums = lax.psum(products + [sums], "expert")
        wide = 6 * experts
        router_grad = unfold_lanes(sums[:wide], 6)
        offsets = unfold_lanes(sums[wide : wide + 16], 2)[:heads_here, : 2 * tok - 1]
        hot = (buckets[None, :] == jnp.arange(bucket_count)[:, None]).astype(f32)
        table_grad = mm(offsets, hot, nt, highest)
        gain_grads = unfold_lanes(sums[wide + 16 :], 2)
    return (
        block_out.T,
        input_grad.T,
        aux_loss.reshape(()),
        gain_grads[1, :col],
        q_grad.T,
        k_grad.T,
        v_grad.T,
        output_grad,
        table_grad.T,
        gain_grads[0, :col],
        router_grad.T,
        in_weight_grad[None],
        out_weight_grad[None],
    )


def solution(mesh):
    return jax.shard_map(
        shards,
        mesh=mesh,
        in_specs=(
            P("expert", "head"),
            P("expert", "head"),
            P("expert"),
            P("expert", None),
            P(),
            P("head"),
            P(None, "head"),
            P(None, "head"),
            P(None, "head"),
            P("head", None),
            P(None, "head"),
            P("head"),
            P(),
            P("expert", None, "head"),
            P("expert", "head", None),
        ),
        out_specs=(
            P("expert", "head"),
            P("expert", "head"),
            P(),
            P("head"),
            P(None, "head"),
            P(None, "head"),
            P(None, "head"),
            P("head", None),
            P(None, "head"),
            P("head"),
            P(),
            P("expert", None, "head"),
            P("expert", "head", None),
        ),
        check_vma=False,
    )
```

time: 262 us -> 218 us (0.83)
  local copies, waits for them, and re-layouts: 44.5 us -> 16.5 us
  waiting for transfers between devices: 96.3 us -> 86.8 us
  between operations: 18.6 us -> 14.7 us
  Pallas kernels: 17.6 us -> 21.5 us
  starting transfers between devices: 7.25 us -> 3.57 us
  blocking collectives: 73.6 us -> 70.9 us
    all_gather x3 -> x2, waiting for transfers between devices: 64.5 us -> 0.01 us  [the longest x1 0.01 us: shards(): w_output_full = lax.all_gather(w_output, 'head', tiled=True)]
    psum x0 -> x1, waiting for transfers between devices: none -> 46.2 us  [shards(): output_grad = lax.psum(product, 'expert').astype(f32)]
    unnamed x109 -> x80, local copies, waits for them, and re-layouts: 36.6 us -> 13.9 us
    all_gather x1, waiting for transfers between devices: 27 us -> 38.6 us  [shards(): late_all = lax.all_gather(late, 'expert')]
    pallas_call x9 -> x10, Pallas kernels: 17.6 us -> 21.5 us  [call(): pl.pallas_call(body, out_shape=shapes, in_specs=in_specs, scratch_shapes=...]
    all_to_all x2 -> x1, starting transfers between devices: 7.05 us -> 3.41 us  [shards(): ret = lax.all_to_all(ret, 'expert', split_axis=0, concat_axis=0, tiled=True)]
    all_gather x1 -> x0, local copies, waits for them, and re-layouts: 3.15 us -> none  [shards(): lax.all_gather(inputs, ('expert', 'head')).reshape(groups, heads, tok, col)]
    all_to_all x2 -> x1, waiting for transfers between devices: 2.95 us -> 0.01 us  [shards(): ret = lax.all_to_all(ret, 'expert', split_axis=0, concat_axis=0, tiled=True)]
  transfers between devices with their start and end apart: 7 -> 5, of which waited for: 4 -> 2; matrix products, arithmetic and copies ran while one was open for 6% -> 2% of each run, Pallas kernels for 4% -> 9%
where the time goes in v3:
time: 218 us; the launch traced here: 217 us
  waiting for transfers between devices  86.8 us (40%)
  blocking collectives  70.9 us (33%)
  Pallas kernels  21.5 us (10%)
  local copies, waits for them, and re-layouts  16.5 us (8%)
  between operations  14.7 us (7%)
  starting transfers between devices  3.57 us (2%)
  other arithmetic  2.73 us (1%)
    psum x1, waiting for transfers between devices, shards(): output_grad = lax.psum(product, 'expert').astype(f32)  46.2 us
    all_gather x1, waiting for transfers between devices, shards(): late_all = lax.all_gather(late, 'expert')  38.6 us
    all_to_all x1, blocking collectives, shards(): lax.all_to_all(send, 'expert', split_axis=0, concat_axis=0, tiled=True)  23.5 us
    pallas_call x10, Pallas kernels, call(): pl.pallas_call(body, out_shape=shapes, in_specs=in_specs, scratch_shapes=...  21.5 us
    all_to_all x1, blocking collectives, shards(): lax.all_to_all(back, ('expert', 'head'), split_axis=0, concat_axis=0, til...  16.9 us
    unnamed x80, local copies, waits for them, and re-layouts  13.9 us
    all_to_all x1, blocking collectives, shards(): lax.all_to_all(first, 'head', split_axis=0, concat_axis=0, tiled=True)  11.1 us
    all_gather x1, blocking collectives, shards(): lax.all_gather(jnp.concatenate([inputs.T, out_grad.T, gains], axis=0), 'h...  8.02 us
  transfers between devices with their start and end apart: 5, of which 2 were waited for; matrix products, arithmetic and copies ran while one was open for 2% of the time, Pallas kernels for 9%

profile of v3, /device:TPU:0, one launch (start us, length us, event | category | flops | bytes accessed | tf_op | source)
XLA Modules:
  0.0 216.6 jit_solution(13184295691329214367)
XLA Ops:
  7.2 0.0 all-gather.9.cloned.1.call-start
  7.2 0.7 all-gather.9.cloned.1.call-update
  7.9 0.0 all-gather.13.cloned.1.call-start
  8.0 0.7 all-gather.13.cloned.1.call-update
  8.7 0.0 all-reduce.4.cloned.1.call-start
  9.4 0.7 stack.21
  10.0 0.7 stack.22
  10.7 0.7 pad.9
  11.4 0.1 pad_add_fusion.scalars
  11.5 0.8 pad_maximum_fusion
  12.3 8.0 %all-gather = bf16[1600,128]{1,0:T(8,128)(2,1)S(1)} all-gather(bf16[400,128]{1,0:T(8,128)(2,1)S(1)} %pad_maximum_fusion), channel_id=2, replica_groups=mesh['expert'=8,'head'=4] {'head'}, dimensions={0}, use_global_device_ids=true | all-gather | bytes 512000 | tf_op jit(solution)/shard_map/all_gather | solution.py:444
  20.4 1.0 copy-done.7
  21.3 1.0 copy-done.9
  22.3 1.0 copy-done.11
  23.2 0.7 copy-done.37
  23.9 2.6 %shard_map.246 = (bf16[3,192,128]{2,1,0:T(8,128)(2,1)}, f32[3,128,128]{2,1,0:T(8,128)}, bf16[192,128]{1,0:T(8,128)(2,1)S(1)}) custom-call(s32[3]{0:T(128)S(1)} %pad_add_fusion.scalars, bf16[4,400,128]{2,1,0:T(8,128)(2,1)S(1)} %bitcast.31, bf16[192,768]{1,0:T(8,128)(2,1)S(1)} %bitcast.42, bf16[192,768]{1,0:T(8,128)(2,1)S(1)} %bitcast.44, ...), custom_call_target="tpu_custom_call" | custom-call | tf_op jit(solution)/shard_map/pallas_call | solution.py:31
  26.5 5.7 %all-gather.1 = bf16[768,128]{1,0:T(8,128)(2,1)S(1)} all-gather(bf16[192,128]{1,0:T(8,128)(2,1)S(1)} %get-tuple-element.44.attended), channel_id=3, replica_groups=mesh['expert'=8,'head'=4] {'head'}, dimensions={0}, use_global_device_ids=true | all-gather | bytes 245760 | tf_op jit(solution)/shard_map/all_gather | solution.py:454
  32.2 0.6 copy-done.17
  32.9 1.3 copy-done.4
  34.1 2.1 shard_map.247
  36.2 23.5 %all_to_all.20 = bf16[8,24,1536]{2,1,0:T(8,128)(2,1)S(1)} all-to-all(bf16[8,24,1536]{2,1,0:T(8,128)(2,1)S(1)} %get-tuple-element.45), channel_id=1, replica_groups=mesh['expert'=8,'head'=4] {'expert'}, dimensions={0} | all-to-all | bytes 1179648 | tf_op jit(solution)/shard_map/all_to_all | solution.py:460
  59.8 1.3 copy-done.3
  61.0 0.7 copy-done.22
  61.8 0.7 copy-done.27
  62.5 3.1 %shard_map.248 = (bf16[32,24,256]{2,1,0:T(8,128)(2,1)S(1)}, bf16[4,288,128]{2,1,0:T(8,128)(2,1)}, bf16[192,768]{1,0:T(8,128)(2,1)}, bf16[192,768]{1,0:T(8,128)(2,1)}, bf16[192,768]{1,0:T(8,128)(2,1)}) custom-call(s32[3]{0:T(128)S(1)} %copy-done.27, bf16[192,1536]{1,0:T(8,128)(2,1)S(1)} %bitcast.36, bf16[768,768]{1,0:T(8,128)(2,1)S(1)} %bitcast.39, ...), custom_call_target="tpu_custom_call" | custom-call | tf_op jit(solution)/shard_map/pallas_call | solution.py:31
  65.6 16.9 %all_to_all.21.came = bf16[32,24,256]{2,1,0:T(8,128)(2,1)S(1)} all-to-all(bf16[32,24,256]{2,1,0:T(8,128)(2,1)S(1)} %get-tuple-element.46), channel_id=1, replica_groups=mesh['expert'=8,'head'=4] {'expert','head'}, dimensions={0} | all-to-all | bytes 786432 | tf_op jit(solution)/shard_map/all_to_all | solution.py:469
  82.5 1.0 shard_map.249
  83.5 5.6 %all-gather.2 = bf16[768,128]{1,0:T(8,128)(2,1)S(1)} all-gather(bf16[192,128]{1,0:T(8,128)(2,1)S(1)} %get-tuple-element.48), channel_id=4, replica_groups=mesh['expert'=8,'head'=4] {'head'}, dimensions={0}, use_global_device_ids=true | all-gather | bytes 245760 | tf_op jit(solution)/shard_map/all_gather | solution.py:475
  89.2 0.7 copy-done.32
  89.9 0.7 copy-done.36
  90.5 3.7 %shard_map.250 = (bf16[576,128]{1,0:T(8,128)(2,1)}, bf16[4,496,128]{2,1,0:T(8,128)(2,1)S(1)}, f32[192,128]{1,0:T(8,128)}, f32[80,128]{1,0:T(8,128)}, bf16[192,768]{1,0:T(8,128)(2,1)}) custom-call(s32[3]{0:T(128)S(1)} %copy-done.28, bf16[4,400,128]{2,1,0:T(8,128)(2,1)S(1)} %bitcast.33, bf16[4,192,128]{2,1,0:T(8,128)(2,1)S(1)} %bitcast.49, ...), custom_call_target="tpu_custom_call" | custom-call | tf_op jit(solution)/shard_map/pallas_call | solution.py:31
  94.3 0.0 all-gather.11.cloned.1.call-start
  94.3 0.5 all-gather.11.cloned.1.call-update
  94.8 11.1 %all_to_all.22.came = bf16[4,496,128]{2,1,0:T(8,128)(2,1)S(1)} all-to-all(bf16[4,496,128]{2,1,0:T(8,128)(2,1)S(1)} %get-tuple-element.55), channel_id=1, replica_groups=mesh['expert'=8,'head'=4] {'head'}, dimensions={0} | all-to-all | bytes 1015808 | tf_op jit(solution)/shard_map/all_to_all | solution.py:491
  105.9 0.9 copy-done.24
  106.8 0.8 copy-done.25
  107.6 1.6 shard_map.251
  109.2 3.4 %all-to-all-start.3 = ((bf16[8,128,128]{2,1,0:T(8,128)(2,1)}), bf16[8,128,128]{2,1,0:T(8,128)(2,1)S(1)}, u32[]{:S(2)}, u32[]{:S(2)}) async-start(bf16[8,128,128]{2,1,0:T(8,128)(2,1)} %get-tuple-element.58), calls=%async_computation.3 | async-start | bytes 524288 | tf_op jit(solution)/shard_map/all_to_all | solution.py:500
  112.7 2.8 %shard_map.255 = (f32[768,768]{1,0:T(8,128)}, f32[768,768]{1,0:T(8,128)}) custom-call(bf16[192,1536]{1,0:T(8,128)(2,1)S(1)} %bitcast.37, bf16[192,768]{1,0:T(8,128)(2,1)S(1)} %copy-done.13, bf16[192,768]{1,0:T(8,128)(2,1)S(1)} %copy-done.14, bf16[192,768]{1,0:T(8,128)(2,1)S(1)} %copy-done.15), custom_call_target="tpu_custom_call" | custom-call | tf_op jit(solution)/shard_map/pallas_call | solution.py:31
  115.5 1.4 copy-done
  116.9 0.8 shard_map.253.normed
  117.6 46.2 %all-reduce.4.cloned.1.call-done = bf16[192,768]{1,0:T(8,128)(2,1)} async-done(((bf16[192,768]{1,0:T(8,128)(2,1)}), bf16[192,768]{1,0:T(8,128)(2,1)}) %all-reduce.4.cloned.1.call-update) | async-done | bytes 294928 | tf_op jit(solution)/shard_map/psum | solution.py:487
  163.8 1.8 convert_element_type.5
  165.7 1.4 shard_map.252
  167.1 0.6 fusion.6
  167.6 38.6 %all-gather.11.cloned.1.call-done = bf16[4608,128]{1,0:T(8,128)(2,1)} async-done(((bf16[576,128]{1,0:T(8,128)(2,1)}), bf16[4608,128]{1,0:T(8,128)(2,1)}) %all-gather.11.cloned.1.call-update) | async-done | bytes 1179664 | tf_op jit(solution)/shard_map/all_gather | solution.py:489
  206.3 1.3 copy-done.6
  207.5 2.5 %shard_map.254 = (f32[192,768]{1,0:T(8,128)}, f32[192,768]{1,0:T(8,128)}, f32[192,768]{1,0:T(8,128)}) custom-call(bf16[8,576,128]{2,1,0:T(8,128)(2,1)S(1)} %bitcast.41, bf16[768,1024]{1,0:T(8,128)(2,1)S(1)} %shard_map.253.normed), custom_call_target="tpu_custom_call" | custom-call | tf_op jit(solution)/shard_map/pallas_call | solution.py:31
  (71 shorter events, 0.2 us)
Async XLA Ops:
  7.2 25.7 %copy-start.21 = (bf16[768,8]{0,1:T(8,128)(2,1)S(1)}, bf16[768,8]{0,1:T(8,128)(2,1)}, u32[]{:S(2)}) copy-start(bf16[768,8]{0,1:T(8,128)(2,1)} %param.27) | copy-start | bytes 36868
  7.2 25.7 %copy-start.38 = (s32[128,1]{0,1:T(1,128)S(1)}, s32[128,1]{0,1:T(1,128)}, u32[]{:S(2)}) copy-start(s32[128,1]{0,1:T(1,128)} %param.18) | copy-start | bytes 1540
  7.2 25.7 %all-gather.9.cloned.1.call-start = ((), (), s32[]{:S(2)}) async-start(), calls=%async_computation.4 | async-start | bytes 1474560 | tf_op jit(solution)/shard_map/all_gather | solution.py:445
  7.9 107.5 %all-gather.13.cloned.1.call-start = ((), (), s32[]{:S(2)}) async-start(), calls=%async_computation.7 | async-start | bytes 1622016 | tf_op jit(solution)/shard_map/all_gather | solution.py:447
  8.7 155.1 %all-reduce.4.cloned.1.call-start = ((), (), s32[]{:S(2)}) async-start(), calls=%async_computation.5 | async-start | bytes 589824 | tf_op jit(solution)/shard_map/psum | solution.py:487
  11.4 15.1 %copy-start.34 = (s32[256]{0:T(256)}, s32[256]{0:T(256)S(1)}, u32[]{:S(2)}) copy-start(s32[256]{0:T(256)S(1)} %pad.9) | copy-start | bytes 3076
  11.5 24.7 %copy-start.26 = (s32[3]{0:T(128)}, s32[3]{0:T(128)S(1)}, u32[]{:S(2)}) copy-start(s32[3]{0:T(128)S(1)} %pad_add_fusion.scalars) | copy-start | bytes 40
  20.4 1.0 copy-start.7
  21.3 1.0 copy-start.9
  22.3 1.0 copy-start.11
  23.2 0.7 copy-start.37
  26.5 33.3 %copy-start.2 = (bf16[1,768,768]{2,1,0:T(8,128)(2,1)S(1)}, bf16[1,768,768]{2,1,0:T(8,128)(2,1)}, u32[]{:S(2)}) copy-start(bf16[1,768,768]{2,1,0:T(8,128)(2,1)} %param.28) | copy-start | bytes 3538948
  32.2 0.6 copy-start.17
  32.9 1.3 copy-start.4
  59.8 1.3 copy-start.3
  61.0 0.7 copy-start.22
  61.8 0.7 copy-start.27
  62.4 20.1 %copy-start.30 = (f32[8,128]{1,0:T(8,128)S(1)}, f32[8,128]{1,0:T(8,128)}, u32[]{:S(2)}) copy-start(f32[8,128]{1,0:T(8,128)} %get-tuple-element.47.side) | copy-start | bytes 12292
  62.4 26.7 %copy-start.1 = (f32[4,192,128]{2,1,0:T(8,128)S(1)}, f32[4,192,128]{2,1,0:T(8,128)}, u32[]{:S(2)}) copy-start(f32[4,192,128]{2,1,0:T(8,128)} %get-tuple-element.51.residual_ref.residual) | copy-start | bytes 1179652
  62.4 26.7 %copy-start.5 = (bf16[192,768]{1,0:T(8,128)(2,1)S(1)}, bf16[192,768]{1,0:T(8,128)(2,1)}, u32[]{:S(2)}) copy-start(bf16[192,768]{1,0:T(8,128)(2,1)} %w_output.1) | copy-start | bytes 884740
  62.4 26.7 %copy-start.8 = (bf16[768,192]{0,1:T(8,128)(2,1)S(1)}, bf16[768,192]{0,1:T(8,128)(2,1)}, u32[]{:S(2)}) copy-start(bf16[768,192]{0,1:T(8,128)(2,1)} %param.21) | copy-start | bytes 884740
  62.4 26.7 %copy-start.10 = (bf16[768,192]{0,1:T(8,128)(2,1)S(1)}, bf16[768,192]{0,1:T(8,128)(2,1)}, u32[]{:S(2)}) copy-start(bf16[768,192]{0,1:T(8,128)(2,1)} %param.22) | copy-start | bytes 884740
  62.4 26.7 %copy-start.12 = (bf16[768,192]{0,1:T(8,128)(2,1)S(1)}, bf16[768,192]{0,1:T(8,128)(2,1)}, u32[]{:S(2)}) copy-start(bf16[768,192]{0,1:T(8,128)(2,1)} %param.23) | copy-start | bytes 884740
  62.4 26.7 %copy-start.18 = (bf16[192,128]{1,0:T(8,128)(2,1)S(1)}, bf16[192,128]{1,0:T(8,128)(2,1)}, u32[]{:S(2)}) copy-start(bf16[192,128]{1,0:T(8,128)(2,1)} %copy-done.17) | copy-start | bytes 147460
  62.5 26.7 %copy-start.19 = (f32[3,128,128]{2,1,0:T(8,128)S(1)}, f32[3,128,128]{2,1,0:T(8,128)}, u32[]{:S(2)}) copy-start(f32[3,128,128]{2,1,0:T(8,128)} %get-tuple-element.52.weights_ref) | copy-start | bytes 589828
  62.5 26.7 %copy-start.20 = (bf16[3,192,128]{2,1,0:T(8,128)(2,1)S(1)}, bf16[3,192,128]{2,1,0:T(8,128)(2,1)}, u32[]{:S(2)}) copy-start(bf16[3,192,128]{2,1,0:T(8,128)(2,1)} %get-tuple-element.53.qkv) | copy-start | bytes 442372
  62.5 26.7 %copy-start.23 = (bf16[768,8]{0,1:T(8,128)(2,1)S(1)}, bf16[768,8]{0,1:T(8,128)(2,1)}, u32[]{:S(2)}) copy-start(bf16[768,8]{0,1:T(8,128)(2,1)} %param.27) | copy-start | bytes 36868
  62.5 26.7 %copy-start.28 = (s32[3]{0:T(128)S(1)}, s32[3]{0:T(128)}, u32[]{:S(2)}) copy-start(s32[3]{0:T(128)} %copy-done.26) | copy-start | bytes 40
  62.5 26.7 %copy-start.39 = (s32[128,1]{0,1:T(1,128)S(1)}, s32[128,1]{0,1:T(1,128)}, u32[]{:S(2)}) copy-start(s32[128,1]{0,1:T(1,128)} %param.18) | copy-start | bytes 1540
  65.6 23.6 %copy-start.16 = (bf16[4,288,128]{2,1,0:T(8,128)(2,1)S(1)}, bf16[4,288,128]{2,1,0:T(8,128)(2,1)}, u32[]{:S(2)}) copy-start(bf16[4,288,128]{2,1,0:T(8,128)(2,1)} %get-tuple-element.54.part) | copy-start | bytes 884740
  89.2 0.7 copy-start.32
  89.9 0.7 copy-start.36
  90.5 15.4 %copy-start.29 = (s32[3]{0:T(128)S(1)}, s32[3]{0:T(128)}, u32[]{:S(2)}) copy-start(s32[3]{0:T(128)} %copy-done.26) | copy-start | bytes 40
  94.2 18.4 %copy-start.13 = (bf16[192,768]{1,0:T(8,128)(2,1)S(1)}, bf16[192,768]{1,0:T(8,128)(2,1)}, u32[]{:S(2)}) copy-start(bf16[192,768]{1,0:T(8,128)(2,1)} %get-tuple-element.70.hidden) | copy-start | bytes 884740
  94.2 18.4 %copy-start.14 = (bf16[192,768]{1,0:T(8,128)(2,1)S(1)}, bf16[192,768]{1,0:T(8,128)(2,1)}, u32[]{:S(2)}) copy-start(bf16[192,768]{1,0:T(8,128)(2,1)} %get-tuple-element.71.before) | copy-start | bytes 884740
  94.2 18.4 %copy-start.15 = (bf16[192,768]{1,0:T(8,128)(2,1)S(1)}, bf16[192,768]{1,0:T(8,128)(2,1)}, u32[]{:S(2)}) copy-start(bf16[192,768]{1,0:T(8,128)(2,1)} %get-tuple-element.72.grads) | copy-start | bytes 884740
  94.3 112.0 %all-gather.11.cloned.1.call-start = ((), (), s32[]{:S(2)}) async-start(), calls=%async_computation.6 | async-start | bytes 1327104 | tf_op jit(solution)/shard_map/all_gather | solution.py:489
  105.9 0.9 copy-start.24
  106.8 0.8 copy-start.25
  109.2 56.4 %all-to-all-start.3 = ((bf16[8,128,128]{2,1,0:T(8,128)(2,1)}), bf16[8,128,128]{2,1,0:T(8,128)(2,1)S(1)}, u32[]{:S(2)}, u32[]{:S(2)}) async-start(bf16[8,128,128]{2,1,0:T(8,128)(2,1)} %get-tuple-element.58), calls=%async_computation.3 | async-start | bytes 524288 | tf_op jit(solution)/shard_map/all_to_all | solution.py:500
  115.5 1.4 copy-start
  116.9 48.8 %copy-start.31 = (f32[8,128]{1,0:T(8,128)S(1)}, f32[8,128]{1,0:T(8,128)}, u32[]{:S(2)}) copy-start(f32[8,128]{1,0:T(8,128)} %get-tuple-element.47.side) | copy-start | bytes 12292
  116.9 48.8 %copy-start.33 = (f32[8,128]{1,0:T(8,128)S(1)}, f32[8,128]{1,0:T(8,128)}, u32[]{:S(2)}) copy-start(f32[8,128]{1,0:T(8,128)} %get-tuple-element.50.stats) | copy-start | bytes 12292
  116.9 48.8 %copy-start.35 = (s32[256]{0:T(256)S(1)}, s32[256]{0:T(256)}, u32[]{:S(2)}) copy-start(s32[256]{0:T(256)} %copy-done.34) | copy-start | bytes 3076
  206.3 1.3 copy-start.6
Sparse Core Ops, SparseCore 0:
  9.6 20.1 all-gather.8
  32.7 56.8 all-gather.12
  94.4 69.4 all-reduce.3
  166.1 40.1 all-gather.10

commit v4 on v3

--- a/solution.py
+++ b/solution.py
@@ -35,6 +35,10 @@
         scratch_shapes=list(scratch),
         compiler_params=pltpu.CompilerParams(vmem_limit_bytes=40 * 1024 * 1024),
     )(*args)
+
+
+def far(array):
+    return pltpu.with_memory_space_constraint(array, pltpu.HBM)
 
 
 def tall(ref, first, rows):
@@ -304,7 +308,11 @@
         first_ref[i, : col + 16, :] = jnp.concatenate([first[at], side], axis=0).astype(bf16)
         first_ref[i, col + 16 :, :] = part[i]
 
-    product_ref[...] = mm(attended[...], branch, nt).astype(product_ref.dtype)
+    product = mm(attended[...], branch, nt)
+    pieces = product_ref.shape[0]
+    for b in range(pieces):
+        at = slice(b * (col // pieces), (b + 1) * (col // pieces))
+        product_ref[b] = (product if pieces == 1 else fold_lanes(product[at])).astype(product_ref.dtype)
     gain_two_grad = jnp.sum(normed_grad * unit, axis=1, keepdims=True)
     gains = jnp.zeros((col, 1), f32)
     own = jnp.zeros((col, tok), f32)
@@ -323,7 +331,8 @@
     )
 
 
-def first_kernel(joined, scalars, came, packed, own, small, ret_ref, sums_ref, input_ref):
+def first_kernel(scalars, came, packed, own, small, *refs):
+    product, (ret_ref, sums_ref, input_ref) = refs[:-3], refs[-3:]
     col, tok = own.shape
     heads = came.shape[0]
     experts = ret_ref.shape[0]
@@ -352,8 +361,8 @@
     for e in range(experts):
         at = slice(e * slots, (e + 1) * slots)
         pieces = [top[at], rest[at]]
-        if joined:
-            pieces.append(sums)
+        if product:
+            pieces += [sums, product[0][e].astype(f32)]
         ret_ref[e] = jnp.concatenate(pieces, axis=0).astype(bf16)
 
 
@@ -371,16 +380,18 @@
     valid_total = 3 * tok * experts // 4
     aux_ref[...] = jnp.sum(product, axis=0, keepdims=True) * (experts / (valid_total * valid_total))
     if refs:
-        router_ref, table_ref, gains_ref = refs
+        router_ref, table_ref, gains_ref, share_ref = refs
         total = blocks[0][2 * slots :]
         for block in blocks[1:]:
             total = total + block[2 * slots :]
         wide = 6 * experts
+        for e in range(experts):
+            share_ref[e] = total[wide + 32 :].astype(bf16)
         router_ref[...] = unfold_lanes(total[:wide], 6)
         offsets = unfold_lanes(total[wide : wide + 16], 2)
         hot = (sublanes((table_ref.shape[1], 2 * tok)) == buckets[...]).astype(f32)
         table_ref[...] = mm(offsets, hot, nt, highest)[: table_ref.shape[0]]
-        gains_ref[...] = unfold_lanes(total[wide + 16 :], 2)
+        gains_ref[...] = unfold_lanes(total[wide + 16 : wide + 32], 2)
 
 
 def turn_kernel(all_in, packed, normed_ref):
@@ -391,7 +402,11 @@
         normed_ref[:, b * tok : (b + 1) * tok] = (x * token_scale(x) * gain).astype(bf16)
 
 
-def products_kernel(late, normed, q_ref, k_ref, v_ref):
+def products_kernel(late, normed, shares, q_ref, k_ref, v_ref, out_ref):
+    groups = shares.shape[0]
+    size = out_ref.shape[0] // groups
+    for b in range(groups):
+        out_ref[b * size : (b + 1) * size, :] = unfold_lanes(shares[b].astype(f32), 6)
     col = q_ref.shape[0]
     joined = jnp.concatenate([late[b] for b in range(late.shape[0])], axis=1)
     for i, ref in enumerate((q_ref, k_ref, v_ref)):
@@ -440,7 +455,8 @@
     scalars = jnp.stack([lengths[0], me_head.astype(jnp.int32), me_expert.astype(jnp.int32)])
     buckets_row = jnp.pad(buckets, (0, 1), constant_values=-1)[None]
 
-    gains = jnp.pad(jnp.stack([gain_attn, gain_ffn]), ((0, 6), (0, 64))).reshape(16, 128)
+    space = jnp.zeros((64,), bf16)
+    gains = jnp.concatenate([gain_attn, space, gain_ffn, space, jnp.zeros((1536,), bf16)]).reshape(16, 128)
     packed = lax.all_gather(jnp.concatenate([inputs.T, out_grad.T, gains], axis=0), "head")
     w_output_full = lax.all_gather(w_output, "head", tiled=True)
     if joined:
@@ -448,14 +464,14 @@
     qkv, weights, attended = call(
         functools.partial(attend_kernel, scale),
         [((3, col, tok), bf16, 1), ((heads_here, tok, tok), f32, 1), ((col, tok), bf16)],
-        scalars, packed, wq, wk, wv, buckets_row, bias_table.T,
+        scalars, packed, far(wq), far(wk), far(wv), far(buckets_row), far(bias_table.T),
     )
 
     attended_parts = lax.all_gather(attended, "head")
     residual, side, send = call(
         functools.partial(route_kernel, capacity),
         [((heads, col, tok), f32, 1), ((8, tok), f32, 1), ((experts, slots, 2 * width), bf16)],
-        scalars, packed, attended_parts, w_output_full, routes_row, router_rows,
+        scalars, packed, attended_parts, far(w_output_full), far(routes_row), far(router_rows),
     )
     rows = lax.all_to_all(send, "expert", split_axis=0, concat_axis=0, tiled=True)
     rows = rows.reshape(total, 2 * width)
@@ -464,13 +480,13 @@
         functools.partial(expert_kernel, capacity),
         [((experts * heads, slots, 256), bf16), ((heads, total * 3 // 2, 128), bf16, 1)]
         + [((total, width), bf16, 1)] * 3,
-        scalars, rows, w_in, w_out, router_rows,
+        scalars, rows, far(w_in), far(w_out), far(router_rows),
     )
     came = lax.all_to_all(back, ("expert", "head"), split_axis=0, concat_axis=0, tiled=True)
     grad_own, gate_grad, stats = call(
         collect_kernel,
         [((col, tok), bf16), ((8, tok), f32, 1), ((experts, 128), f32, 1)],
-        came, side,
+        came, far(side),
     )
     expert_grad = lax.all_gather(grad_own, "head")
 
@@ -478,46 +494,49 @@
         functools.partial(backward_kernel, scale, valid_total),
         [
             ((3 * col, tok), bf16, 1), ((heads, col + 16 + total * 3 // 2, 128), bf16), ((col, tok), f32, 1),
-            ((6 * experts + 32, 128), f32, 1), ((col, width), bf16 if joined else f32, 1),
+            ((6 * experts + 32, 128), f32, 1),
+            ((groups, col // groups * 6, 128), bf16, 1) if joined else ((1, col, width), f32, 1),
         ],
-        scalars, packed, expert_grad, gate_grad, stats, residual, routes_row, router_rows,
-        w_output, weights, qkv, wq, wk, wv, attended, part,
-    )
-
-    output_grad = lax.psum(product, "expert").astype(f32)
+        scalars, packed, expert_grad, far(gate_grad), far(stats), far(residual), far(routes_row),
+        far(router_rows), far(w_output), far(weights), far(qkv), far(wq), far(wk), far(wv), far(attended), far(part),
+    )
+
     if joined:
         late_all = lax.all_gather(late, "expert")
 
     first = lax.all_to_all(first, "head", split_axis=0, concat_axis=0, tiled=True)
     ret, sums, input_grad = call(
-        functools.partial(first_kernel, joined),
+        first_kernel,
         [
-            ((experts, 2 * slots + (6 * experts + 32 if joined else 0), 128), bf16),
+            ((experts, 2 * slots + (6 * experts + 32 + product.shape[1] if joined else 0), 128), bf16),
             ((6 * experts + 32, 128), f32, 1), ((col, tok), f32),
         ],
-        scalars, first, packed, residual_grad_own, small,
+        scalars, first, far(packed), far(residual_grad_own), far(small), *([far(product)] if joined else []),
     )
     ret = lax.all_to_all(ret, "expert", split_axis=0, concat_axis=0, tiled=True)
     out = call(
         functools.partial(last_kernel, slots),
         [((col, tok), bf16), ((1, 1), f32)]
-        + ([((experts, width), f32), ((heads_here, bucket_count), f32), ((8, 256), f32)] if joined else []),
-        scalars, ret, side, residual, stats, buckets_row,
+        + ([((experts, width), f32), ((heads_here, bucket_count), f32), ((8, 256), f32), (product.shape, bf16)] if joined else []),
+        scalars, ret, far(side), far(residual), far(stats), far(buckets_row),
     )
     block_out, aux_loss = out[:2]
     in_weight_grad, out_weight_grad = call(
-        weights_kernel, [((width, width), f32)] * 2, rows, hidden, before_grad, back_rows
+        weights_kernel, [((width, width), f32)] * 2, far(rows), far(hidden), far(before_grad), far(back_rows)
     )
     if joined:
-        router_grad, table_grad, gain_grads = out[2:]
-        normed_all = call(turn_kernel, [((width, groups * tok), bf16)], all_in, packed)[0]
-        q_grad, k_grad, v_grad = call(products_kernel, [((col, width), f32)] * 3, late_all, normed_all)
+        router_grad, table_grad, gain_grads, share = out[2:]
+        shares = lax.all_to_all(share, "expert", split_axis=0, concat_axis=0, tiled=True)
+        normed_all = call(turn_kernel, [((width, groups * tok), bf16, 1)], far(all_in), far(packed))[0]
+        q_grad, k_grad, v_grad, output_grad = call(
+            products_kernel, [((col, width), f32, 1)] * 4, far(late_all), far(normed_all), shares
+        )
     else:
         gain = packed[:, 2 * col : 2 * col + 2].reshape(heads, 256)[:, :col].reshape(width, 1)
         x = packed[:, :col].reshape(width, tok).astype(f32)
         normed = (x * token_scale(x) * gain.astype(f32)).astype(bf16)
         products = [mm(late[i * col : (i + 1) * col], normed, nt) for i in range(3)]
-        q_grad, k_grad, v_grad, sums = lax.psum(products + [sums], "expert")
+        q_grad, k_grad, v_grad, sums, output_grad = lax.psum(products + [sums, product[0]], "expert")
         wide = 6 * experts
         router_grad = unfold_lanes(sums[:wide], 6)
         offsets = unfold_lanes(sums[wide : wide + 16], 2)[:heads_here, : 2 * tok - 1]

time: 218 us -> 152 us (0.70)
  waiting for transfers between devices: 86.8 us -> 5.67 us
  blocking collectives: 70.9 us -> 90.5 us
  local copies, waits for them, and re-layouts: 16.5 us -> 3.24 us
  Pallas kernels: 21.5 us -> 32.9 us
    psum x1 -> x0, waiting for transfers between devices: 46.2 us -> none  [shards(): output_grad = lax.psum(product, 'expert').astype(f32)]
    all_gather x1, waiting for transfers between devices: 38.6 us -> 0.01 us  [shards(): late_all = lax.all_gather(late, 'expert')]
    all_to_all x0 -> x1, blocking collectives: none -> 20.4 us  [shards(): ret = lax.all_to_all(ret, 'expert', split_axis=0, concat_axis=0, tiled=True)]
    unnamed x80 -> x6, local copies, waits for them, and re-layouts: 13.9 us -> 0.01 us
    pallas_call x10, Pallas kernels: 21.5 us -> 32.9 us  [call(): pl.pallas_call(body, out_shape=shapes, in_specs=in_specs, scratch_shapes=...]
    all_to_all x1, waiting for transfers between devices: 0.01 us -> 4.27 us  [shards(): lax.all_to_all(share, 'expert', split_axis=0, concat_axis=0, tiled=True)]
  transfers between devices with their start and end apart: 5 -> 4, of which waited for: 2 -> 1; matrix products, arithmetic and copies ran while one was open for 2% -> 3% of each run, Pallas kernels for 9% -> 19%
where the time goes in v4:
time: 152 us; the launch traced here: 151 us
  blocking collectives  90.5 us (60%)
  Pallas kernels  32.9 us (22%)
  between operations  14.4 us (9%)
  waiting for transfers between devices  5.67 us (4%)
  starting transfers between devices  3.54 us (2%)
  local copies, waits for them, and re-layouts  3.24 us (2%)
    pallas_call x10, Pallas kernels, call(): pl.pallas_call(body, out_shape=shapes, in_specs=in_specs, scratch_shapes=...  32.9 us
    all_to_all x1, blocking collectives, shards(): lax.all_to_all(send, 'expert', split_axis=0, concat_axis=0, tiled=True)  23.4 us
    all_to_all x1, blocking collectives, shards(): ret = lax.all_to_all(ret, 'expert', split_axis=0, concat_axis=0, tiled=True)  20.4 us
    all_to_all x1, blocking collectives, shards(): lax.all_to_all(back, ('expert', 'head'), split_axis=0, concat_axis=0, til...  16.1 us
    all_to_all x1, blocking collectives, shards(): lax.all_to_all(first, 'head', split_axis=0, concat_axis=0, tiled=True)  11.1 us
    all_gather x1, blocking collectives, shards(): lax.all_gather(jnp.concatenate([inputs.T, out_grad.T, gains], axis=0), 'h...  8.01 us
    all_gather x1, blocking collectives, shards(): attended_parts = lax.all_gather(attended, 'head')  5.88 us
    all_gather x1, blocking collectives, shards(): expert_grad = lax.all_gather(grad_own, 'head')  5.59 us
  transfers between devices with their start and end apart: 4, of which 1 were waited for; matrix products, arithmetic and copies ran while one was open for 3% of the time, Pallas kernels for 19%

profile of v4, /device:TPU:0, one launch (start us, length us, event | category | flops | bytes accessed | tf_op | source)
XLA Modules:
  0.0 151.2 jit_solution(3678141033164577162)
XLA Ops:
  7.2 0.0 all-gather.9.cloned.1.call-start
  7.2 0.7 all-gather.9.cloned.1.call-update
  7.9 0.0 all-gather.13.cloned.1.call-start
  8.0 0.7 all-gather.13.cloned.1.call-update
  8.7 0.0 all-gather.11.cloned.1.call-start
  9.4 1.2 pad.4
  10.6 1.4 concatenate.6
  12.0 0.1 pad_add_fusion.scalars
  12.1 0.8 pad_maximum_fusion
  12.9 8.0 %all-gather = bf16[1600,128]{1,0:T(8,128)(2,1)S(1)} all-gather(bf16[400,128]{1,0:T(8,128)(2,1)S(1)} %pad_maximum_fusion), channel_id=2, replica_groups=mesh['expert'=8,'head'=4] {'head'}, dimensions={0}, use_global_device_ids=true | all-gather | bytes 512000 | tf_op jit(solution)/shard_map/all_gather | solution.py:460
  20.9 0.0 copy-start
  20.9 3.3 %shard_map.246 = (bf16[3,192,128]{2,1,0:T(8,128)(2,1)}, f32[3,128,128]{2,1,0:T(8,128)}, bf16[192,128]{1,0:T(8,128)(2,1)S(1)}) custom-call(s32[3]{0:T(128)S(1)} %pad_add_fusion.scalars, bf16[4,400,128]{2,1,0:T(8,128)(2,1)S(1)} %bitcast.32, bf16[192,768]{1,0:T(8,128)(2,1)} %bitcast.45, bf16[192,768]{1,0:T(8,128)(2,1)} %bitcast.47, bf16[192,768]{1,0:T(8,128)(2,1)} %bitcast.49, ...), custom_call_target="tpu_custom_call" | custom-call | tf_op jit(solution)/shard_map/pallas_call | solution.py:31
  24.3 0.0 copy-start.2
  24.3 5.9 %all-gather.1 = bf16[768,128]{1,0:T(8,128)(2,1)S(1)} all-gather(bf16[192,128]{1,0:T(8,128)(2,1)S(1)} %get-tuple-element.46.attended), channel_id=3, replica_groups=mesh['expert'=8,'head'=4] {'head'}, dimensions={0}, use_global_device_ids=true | all-gather | bytes 245760 | tf_op jit(solution)/shard_map/all_gather | solution.py:470
  30.2 0.0 all-gather.9.cloned.1.call-done.w_output
  30.2 2.8 %shard_map.247 = (f32[4,192,128]{2,1,0:T(8,128)}, f32[8,128]{1,0:T(8,128)}, bf16[8,24,1536]{2,1,0:T(8,128)(2,1)S(1)}) custom-call(s32[3]{0:T(128)S(1)} %pad_add_fusion.scalars, bf16[4,400,128]{2,1,0:T(8,128)(2,1)S(1)} %bitcast.33, bf16[4,192,128]{2,1,0:T(8,128)(2,1)S(1)} %bitcast.39, bf16[768,768]{1,0:T(8,128)(2,1)} %all-gather.9.cloned.1.call-done.w_output, ...), custom_call_target="tpu_custom_call" | custom-call | tf_op jit(solution)/shard_map/pallas_call | solution.py:31
  33.0 23.4 %all_to_all.25 = bf16[8,24,1536]{2,1,0:T(8,128)(2,1)S(1)} all-to-all(bf16[8,24,1536]{2,1,0:T(8,128)(2,1)S(1)} %get-tuple-element.47), channel_id=1, replica_groups=mesh['expert'=8,'head'=4] {'expert'}, dimensions={0} | all-to-all | bytes 1179648 | tf_op jit(solution)/shard_map/all_to_all | solution.py:476
  56.4 0.0 copy-done.2
  56.4 0.0 copy-start.1
  56.4 4.4 %shard_map.248 = (bf16[32,24,256]{2,1,0:T(8,128)(2,1)S(1)}, bf16[4,288,128]{2,1,0:T(8,128)(2,1)}, bf16[192,768]{1,0:T(8,128)(2,1)}, bf16[192,768]{1,0:T(8,128)(2,1)}, bf16[192,768]{1,0:T(8,128)(2,1)}) custom-call(s32[3]{0:T(128)S(1)} %pad_add_fusion.scalars, bf16[192,1536]{1,0:T(8,128)(2,1)S(1)} %bitcast.37, bf16[768,768]{1,0:T(8,128)(2,1)} %bitcast.42, ...), custom_call_target="tpu_custom_call" | custom-call | tf_op jit(solution)/shard_map/pallas_call | solution.py:31
  60.8 16.1 %all_to_all.26.came = bf16[32,24,256]{2,1,0:T(8,128)(2,1)S(1)} all-to-all(bf16[32,24,256]{2,1,0:T(8,128)(2,1)S(1)} %get-tuple-element.48), channel_id=1, replica_groups=mesh['expert'=8,'head'=4] {'expert','head'}, dimensions={0} | all-to-all | bytes 786432 | tf_op jit(solution)/shard_map/all_to_all | solution.py:485
  76.9 0.0 copy-done.1
  76.9 1.6 %shard_map.249 = (bf16[192,128]{1,0:T(8,128)(2,1)S(1)}, f32[8,128]{1,0:T(8,128)}, f32[8,128]{1,0:T(8,128)}) custom-call(bf16[32,24,256]{2,1,0:T(8,128)(2,1)S(1)} %all_to_all.26.came, f32[8,128]{1,0:T(8,128)} %get-tuple-element.49.side), custom_call_target="tpu_custom_call" | custom-call | tf_op jit(solution)/shard_map/pallas_call | solution.py:31
  78.5 5.6 %all-gather.2 = bf16[768,128]{1,0:T(8,128)(2,1)S(1)} all-gather(bf16[192,128]{1,0:T(8,128)(2,1)S(1)} %get-tuple-element.50), channel_id=4, replica_groups=mesh['expert'=8,'head'=4] {'head'}, dimensions={0}, use_global_device_ids=true | all-gather | bytes 245760 | tf_op jit(solution)/shard_map/all_gather | solution.py:491
  84.1 0.0 copy-done
  84.1 4.8 %shard_map.250 = (bf16[576,128]{1,0:T(8,128)(2,1)}, bf16[4,496,128]{2,1,0:T(8,128)(2,1)S(1)}, f32[192,128]{1,0:T(8,128)}, f32[80,128]{1,0:T(8,128)}, bf16[8,144,128]{2,1,0:T(8,128)(2,1)}) custom-call(s32[3]{0:T(128)S(1)} %pad_add_fusion.scalars, bf16[4,400,128]{2,1,0:T(8,128)(2,1)S(1)} %bitcast.34, bf16[4,192,128]{2,1,0:T(8,128)(2,1)S(1)} %bitcast.40, ...), custom_call_target="tpu_custom_call" | custom-call | tf_op jit(solution)/shard_map/pallas_call | solution.py:31
  88.9 0.0 all-gather.11.cloned.1.call-update
  88.9 11.1 %all_to_all.27.came = bf16[4,496,128]{2,1,0:T(8,128)(2,1)S(1)} all-to-all(bf16[4,496,128]{2,1,0:T(8,128)(2,1)S(1)} %get-tuple-element.57), channel_id=1, replica_groups=mesh['expert'=8,'head'=4] {'head'}, dimensions={0} | all-to-all | bytes 1015808 | tf_op jit(solution)/shard_map/all_to_all | solution.py:507
  100.0 2.1 %shard_map.251 = (bf16[8,272,128]{2,1,0:T(8,128)(2,1)S(1)}, f32[80,128]{1,0:T(8,128)}, f32[192,128]{1,0:T(8,128)}) custom-call(s32[3]{0:T(128)S(1)} %pad_add_fusion.scalars, bf16[4,496,128]{2,1,0:T(8,128)(2,1)S(1)} %all_to_all.27.came, bf16[4,400,128]{2,1,0:T(8,128)(2,1)} %bitcast.35, f32[192,128]{1,0:T(8,128)} %get-tuple-element.58.own, ...), custom_call_target="tpu_custom_call" | custom-call | tf_op jit(solution)/shard_map/pallas_call | solution.py:31
  102.1 20.4 %all_to_all.28.came = bf16[8,272,128]{2,1,0:T(8,128)(2,1)S(1)} all-to-all(bf16[8,272,128]{2,1,0:T(8,128)(2,1)S(1)} %get-tuple-element.61), channel_id=1, replica_groups=mesh['expert'=8,'head'=4] {'expert'}, dimensions={0} | all-to-all | bytes 1114112 | tf_op jit(solution)/shard_map/all_to_all | solution.py:516
  122.5 2.0 %shard_map.252 = (bf16[192,128]{1,0:T(8,128)(2,1)}, f32[1,1]{1,0:T(1,128)}, f32[8,768]{1,0:T(8,128)}, f32[3,32]{1,0:T(4,128)}, f32[8,256]{1,0:T(8,128)S(1)}, /*index=5*/bf16[8,144,128]{2,1,0:T(8,128)(2,1)}) custom-call(s32[3]{0:T(128)S(1)} %pad_add_fusion.scalars, bf16[8,272,128]{2,1,0:T(8,128)(2,1)S(1)} %all_to_all.28.came, ...), custom_call_target="tpu_custom_call" | custom-call | tf_op jit(solution)/shard_map/pallas_call | solution.py:31
  124.5 3.4 %all-to-all-start.4 = ((bf16[8,144,128]{2,1,0:T(8,128)(2,1)}), bf16[8,144,128]{2,1,0:T(8,128)(2,1)S(1)}, u32[]{:S(2)}, u32[]{:S(2)}) async-start(bf16[8,144,128]{2,1,0:T(8,128)(2,1)} %get-tuple-element.67), calls=%async_computation.4 | async-start | bytes 589824 | tf_op jit(solution)/shard_map/all_to_all | solution.py:529
  128.0 4.1 %shard_map.255 = (f32[768,768]{1,0:T(8,128)}, f32[768,768]{1,0:T(8,128)}) custom-call(bf16[192,1536]{1,0:T(8,128)(2,1)} %bitcast.38, bf16[192,768]{1,0:T(8,128)(2,1)} %get-tuple-element.74.hidden, bf16[192,768]{1,0:T(8,128)(2,1)} %get-tuple-element.75.before, bf16[192,768]{1,0:T(8,128)(2,1)} %get-tuple-element.76.grads), custom_call_target="tpu_custom_call" | custom-call | tf_op jit(solution)/shard_map/pallas_call | solution.py:31
  132.1 0.0 all-gather.13.cloned.1.call-done
  132.1 3.4 %shard_map.253.normed = bf16[768,1024]{1,0:T(8,128)(2,1)} custom-call(bf16[8,4,192,128]{3,2,1,0:T(8,128)(2,1)} %bitcast.41, bf16[4,400,128]{2,1,0:T(8,128)(2,1)} %bitcast.36), custom_call_target="tpu_custom_call" | custom-call | tf_op jit(solution)/shard_map/pallas_call | solution.py:31
  135.4 0.6 fusion
  136.0 4.3 %all-to-all-done.4.shares = bf16[8,144,128]{2,1,0:T(8,128)(2,1)S(1)} async-done(((bf16[8,144,128]{2,1,0:T(8,128)(2,1)}), bf16[8,144,128]{2,1,0:T(8,128)(2,1)S(1)}, u32[]{:S(2)}, u32[]{:S(2)}) %all-to-all-start.4) | async-done | bytes 294944 | tf_op jit(solution)/shard_map/all_to_all | solution.py:529
  140.3 0.0 all-gather.11.cloned.1.call-done
  140.3 4.4 %shard_map.254 = (f32[192,768]{1,0:T(8,128)}, f32[192,768]{1,0:T(8,128)}, f32[192,768]{1,0:T(8,128)}, f32[192,768]{1,0:T(8,128)}) custom-call(bf16[8,576,128]{2,1,0:T(8,128)(2,1)} %bitcast.44, bf16[768,1024]{1,0:T(8,128)(2,1)} %shard_map.253.normed, bf16[8,144,128]{2,1,0:T(8,128)(2,1)S(1)} %all-to-all-done.4.shares), custom_call_target="tpu_custom_call" | custom-call | tf_op jit(solution)/shard_map/pallas_call | solution.py:31
  (2 shorter events, 0.0 us)
Async XLA Ops:
  7.2 23.0 %all-gather.9.cloned.1.call-start = ((), (), s32[]{:S(2)}) async-start(), calls=%async_computation.5 | async-start | bytes 1474560 | tf_op jit(solution)/shard_map/all_gather | solution.py:461
  7.9 124.2 %all-gather.13.cloned.1.call-start = ((), (), s32[]{:S(2)}) async-start(), calls=%async_computation.7 | async-start | bytes 1622016 | tf_op jit(solution)/shard_map/all_gather | solution.py:463
  8.7 131.6 %all-gather.11.cloned.1.call-start = ((), (), s32[]{:S(2)}) async-start(), calls=%async_computation.6 | async-start | bytes 1327104 | tf_op jit(solution)/shard_map/all_gather | solution.py:505
  20.9 63.2 %copy-start = (bf16[1600,128]{1,0:T(8,128)(2,1)}, bf16[1600,128]{1,0:T(8,128)(2,1)S(1)}, u32[]{:S(2)}) copy-start(bf16[1600,128]{1,0:T(8,128)(2,1)S(1)} %all-gather) | copy-start | bytes 1228804
  24.3 32.1 %copy-start.2 = (bf16[192,128]{1,0:T(8,128)(2,1)}, bf16[192,128]{1,0:T(8,128)(2,1)S(1)}, u32[]{:S(2)}) copy-start(bf16[192,128]{1,0:T(8,128)(2,1)S(1)} %get-tuple-element.46.attended) | copy-start | bytes 147460
  56.4 20.5 %copy-start.1 = (bf16[8,24,1536]{2,1,0:T(8,128)(2,1)}, bf16[8,24,1536]{2,1,0:T(8,128)(2,1)S(1)}, u32[]{:S(2)}) copy-start(bf16[8,24,1536]{2,1,0:T(8,128)(2,1)S(1)} %all_to_all.25) | copy-start | bytes 1769476
  124.5 15.8 %all-to-all-start.4 = ((bf16[8,144,128]{2,1,0:T(8,128)(2,1)}), bf16[8,144,128]{2,1,0:T(8,128)(2,1)S(1)}, u32[]{:S(2)}, u32[]{:S(2)}) async-start(bf16[8,144,128]{2,1,0:T(8,128)(2,1)} %get-tuple-element.67), calls=%async_computation.4 | async-start | bytes 589824 | tf_op jit(solution)/shard_map/all_to_all | solution.py:529
Sparse Core Ops, SparseCore 0:
  9.6 20.4 all-gather.8
  33.0 56.5 all-gather.12
  91.8 45.4 all-gather.10

commit v5 on v4

--- a/solution.py
+++ b/solution.py
@@ -22,19 +22,95 @@
     return lax.dot_general(left, right, (dims, ((), ())), precision=precision, preferred_element_type=f32)
 
 
-def call(body, outs, *args, scratch=()):
-    scalar_memory = pl.BlockSpec(memory_space=pltpu.SMEM)
-    in_specs = [scalar_memory if a.dtype == jnp.int32 and a.ndim == 1 else pl.BlockSpec() for a in args]
-    shapes = []
-    for shape, kind, *far in outs:
-        shapes.append(pltpu.HBM(shape, kind) if far else jax.ShapeDtypeStruct(shape, kind))
+class Later:
+    def __init__(self, source, space, semaphore):
+        self.space, self.shape, self.waited = space, space.shape, False
+        self.copy = pltpu.make_async_copy(source, space, semaphore)
+        self.copy.start()
+
+    def wait(self):
+        if not self.waited:
+            self.copy.wait()
+            self.waited = True
+
+    def __getitem__(self, index):
+        self.wait()
+        return self.space[index]
+
+
+class Sent:
+    def __init__(self, space, target, semaphore):
+        self.space, self.shape, self.dtype, self.copy = space, space.shape, space.dtype, None
+        self.target, self.semaphore = target, semaphore
+
+    def __setitem__(self, index, value):
+        self.space[index] = value
+
+    def __getitem__(self, index):
+        return self.space[index]
+
+    def send(self):
+        if self.copy is None:
+            self.copy = pltpu.make_async_copy(self.space, self.target, self.semaphore)
+            self.copy.start()
+
+
+class Lazy:
+    def __init__(self, array):
+        self.array = array
+
+
+def lazy(array):
+    return Lazy(array)
+
+
+def call(body, outs, *args):
+    hbm = pl.BlockSpec(memory_space=pltpu.HBM)
+    in_specs, operands, out_specs, shapes, scratch = [], [], [], [], []
+    late_in, late_out = [], []
+    for i, a in enumerate(args):
+        if isinstance(a, Lazy):
+            late_in.append(i)
+            in_specs.append(hbm)
+            operands.append(far(a.array))
+            scratch.append(pltpu.VMEM(a.array.shape, a.array.dtype))
+        else:
+            whole = a.dtype == jnp.int32 and a.ndim == 1
+            in_specs.append(pl.BlockSpec(memory_space=pltpu.SMEM) if whole else pl.BlockSpec())
+            operands.append(a)
+    for i, (shape, kind, *mode) in enumerate(outs):
+        shapes.append(pltpu.HBM(shape, kind) if mode else jax.ShapeDtypeStruct(shape, kind))
+        out_specs.append(hbm if mode == [2] else pl.BlockSpec())
+        if mode == [2]:
+            late_out.append(i)
+            scratch.append(pltpu.VMEM(shape, kind))
+    count = len(scratch)
+    if count:
+        scratch.append(pltpu.SemaphoreType.DMA((count,)))
+
+    def run(*refs):
+        ins, results, spare = refs[: len(args)], refs[len(args) : len(args) + len(outs)], refs[len(args) + len(outs) :]
+        ins, results = list(ins), list(results)
+        for k, i in enumerate(late_in):
+            ins[i] = Later(ins[i], spare[k], spare[-1].at[k])
+        for k, i in enumerate(late_out, len(late_in)):
+            results[i] = Sent(spare[k], results[i], spare[-1].at[k])
+        body(*ins, *results)
+        for i in late_in:
+            ins[i].wait()
+        for i in late_out:
+            results[i].send()
+        for i in late_out:
+            results[i].copy.wait()
+
     return pl.pallas_call(
-        body,
+        run,
         out_shape=shapes,
         in_specs=in_specs,
-        scratch_shapes=list(scratch),
+        out_specs=out_specs,
+        scratch_shapes=scratch,
         compiler_params=pltpu.CompilerParams(vmem_limit_bytes=40 * 1024 * 1024),
-    )(*args)
+    )(*operands)
 
 
 def far(array):
@@ -130,6 +206,7 @@
         qkv_ref[i] = rows
         projected.append(rows)
     query, key, value = projected
+    qkv_ref.send()
     hot = (sublanes((table.shape[1], 2 * tok)) == buckets[...]).astype(f32)
     offsets = mm(table[...], hot, precision=highest)
     open_keys = lanes((tok, tok)) < scalars[0]
@@ -161,6 +238,7 @@
     residual = tall(packed, 0, col) + jnp.transpose(branch)
     for i in range(heads):
         residual_ref[i] = residual[i * col : (i + 1) * col]
+    residual_ref.send()
     _, _, normed, router = second_norm(residual, all_gains(packed)[1], w_router[...])
     route_hot = (sublanes((experts, tok)) == routes[...]).astype(f32)
     gate = jnp.sum(router * route_hot, axis=0, keepdims=True)
@@ -196,6 +274,7 @@
     hidden, slope = gelu_parts(mm(rows, w_in[...]))
     hidden = hidden.astype(bf16)
     hidden_ref[...] = hidden
+    hidden_ref.send()
     produced = mm(hidden, w_out[...])
     for i in range(heads):
         mine = produced[:, i * col : (i + 1) * col]
@@ -203,12 +282,15 @@
         part_ref[i] = jnp.concatenate(
             [mine[:, :128], jnp.concatenate([rest[:half], rest[half:]], axis=1)], axis=0
         ).astype(bf16)
+    part_ref.send()
     probs = softmax(mm(rows, w_router[...], nt), 1)
     gate = jnp.sum(jnp.where(lanes((total, experts)) == scalars[2], probs, 0.0), axis=1, keepdims=True)
     back = (gate * grads).astype(bf16)
     grads_ref[...] = back
+    grads_ref.send()
     before = (mm(back, w_out[...], nt) * slope).astype(bf16)
     before_ref[...] = before
+    before_ref.send()
     rows_grad = mm(before, w_in[...], nt)
     gate_grad = jnp.sum(grads * produced, axis=1, keepdims=True)
     stats = jnp.zeros((1, 128), f32)
@@ -229,6 +311,7 @@
 def weights_kernel(rows_ref, hidden, before, grads, in_ref, out_ref):
     width = in_ref.shape[0]
     in_ref[...] = mm(rows_ref[:, :width], before[...], tn)
+    in_ref.send()
     out_ref[...] = mm(hidden[...], grads[...], tn)
 
 
@@ -302,6 +385,7 @@
         late_ref[i * col : (i + 1) * col, :] = low
         first = first + mm(w[...], low, tn)
         row = row + jnp.sum(low.astype(f32) * qkv[i].astype(f32), axis=0, keepdims=True)
+    late_ref.send()
     side = side_rows(16, tok, high_low(row))
     for i in range(blocks):
         at = slice(i * col, (i + 1) * col)
@@ -326,9 +410,11 @@
     offsets = jnp.concatenate(offsets, axis=0)
     offsets = jnp.concatenate([offsets, jnp.zeros((8 - heads_here, 2 * tok), f32)], axis=0)
     gains = jnp.concatenate([gains, jnp.zeros((8, 64), f32)], axis=1)
-    small_ref[...] = jnp.concatenate(
-        [fold_lanes(router_grad), fold_lanes(offsets), fold_lanes(gains)], axis=0
-    )
+    pieces = [fold_lanes(gains), fold_lanes(offsets), fold_lanes(router_grad)]
+    spare = small_ref.shape[0] - 6 * experts - 32
+    if spare:
+        pieces.append(jnp.zeros((spare, 128), f32))
+    small_ref[...] = jnp.concatenate(pieces, axis=0)
 
 
 def first_kernel(scalars, came, packed, own, small, *refs):
@@ -348,8 +434,7 @@
     gain_grad = jnp.sum(total[:col] * unit, axis=1, keepdims=True)
     gain_grad = jnp.transpose(side_lanes(col, 128, [jnp.zeros_like(gain_grad), gain_grad]))[0:8]
     gain_grad = jnp.concatenate([gain_grad, jnp.zeros((8, 64), f32)], axis=1)
-    kept = small.shape[0] - 16
-    sums = jnp.concatenate([small[:kept, :], small[kept:, :] + fold_lanes(gain_grad)], axis=0)
+    sums = jnp.concatenate([small[:16, :] + fold_lanes(gain_grad), small[16:, :]], axis=0)
     sums_ref[...] = sums
     produced = total[col + 16 :]
     count = produced.shape[0] * 2 // 3
@@ -362,11 +447,12 @@
         at = slice(e * slots, (e + 1) * slots)
         pieces = [top[at], rest[at]]
         if product:
-            pieces += [sums, product[0][e].astype(f32)]
+            chunk = sums.shape[0] // experts
+            pieces += [sums[e * chunk : (e + 1) * chunk], product[0][e].astype(f32)]
         ret_ref[e] = jnp.concatenate(pieces, axis=0).astype(bf16)
 
 
-def last_kernel(slots, scalars, came, side, residual, stats, buckets, *refs):
+def last_kernel(slots, scalars, came, side, residual, stats, *refs):
     block_ref, aux_ref, refs = refs[0], refs[1], refs[2:]
     experts = came.shape[0]
     heads, col, tok = residual.shape
@@ -380,37 +466,42 @@
     valid_total = 3 * tok * experts // 4
     aux_ref[...] = jnp.sum(product, axis=0, keepdims=True) * (experts / (valid_total * valid_total))
     if refs:
-        router_ref, table_ref, gains_ref, share_ref = refs
         total = blocks[0][2 * slots :]
         for block in blocks[1:]:
             total = total + block[2 * slots :]
-        wide = 6 * experts
         for e in range(experts):
-            share_ref[e] = total[wide + 32 :].astype(bf16)
-        router_ref[...] = unfold_lanes(total[:wide], 6)
-        offsets = unfold_lanes(total[wide : wide + 16], 2)
-        hot = (sublanes((table_ref.shape[1], 2 * tok)) == buckets[...]).astype(f32)
-        table_ref[...] = mm(offsets, hot, nt, highest)[: table_ref.shape[0]]
-        gains_ref[...] = unfold_lanes(total[wide + 16 : wide + 32], 2)
+            refs[0][e] = total.astype(bf16)
 
 
 def turn_kernel(all_in, packed, normed_ref):
-    groups, heads, col, tok = all_in.shape
+    heads, groups, col, tok = all_in.shape
     gain = all_gains(packed)[0]
     for b in range(groups):
-        x = jnp.concatenate([all_in[b, i].astype(f32) for i in range(heads)], axis=0)
+        x = jnp.concatenate([all_in[i, b].astype(f32) for i in range(heads)], axis=0)
         normed_ref[:, b * tok : (b + 1) * tok] = (x * token_scale(x) * gain).astype(bf16)
 
 
-def products_kernel(late, normed, shares, q_ref, k_ref, v_ref, out_ref):
+def products_kernel(
+    late, normed, shares, buckets, q_ref, k_ref, v_ref, out_ref, router_ref, table_ref, gains_ref
+):
     groups = shares.shape[0]
-    size = out_ref.shape[0] // groups
+    col = q_ref.shape[0]
+    experts = router_ref.shape[0]
+    size = col // groups
+    blocks = [shares[b].astype(f32) for b in range(groups)]
+    chunk = blocks[0].shape[0] - 6 * size
     for b in range(groups):
-        out_ref[b * size : (b + 1) * size, :] = unfold_lanes(shares[b].astype(f32), 6)
-    col = q_ref.shape[0]
-    joined = jnp.concatenate([late[b] for b in range(late.shape[0])], axis=1)
+        out_ref[b * size : (b + 1) * size, :] = unfold_lanes(blocks[b][chunk:], 6)
+    out_ref.send()
+    joined = jnp.concatenate([late[b] for b in range(groups)], axis=1)
     for i, ref in enumerate((q_ref, k_ref, v_ref)):
         ref[...] = mm(joined[i * col : (i + 1) * col], normed[...], nt)
+        ref.send()
+    small = jnp.concatenate([block[:chunk] for block in blocks], axis=0)
+    gains_ref[...] = unfold_lanes(small[:16], 2)
+    hot = (sublanes((table_ref.shape[1], buckets.shape[1])) == buckets[...]).astype(f32)
+    table_ref[...] = mm(unfold_lanes(small[16:32], 2), hot, nt, highest)[: table_ref.shape[0]]
+    router_ref[...] = unfold_lanes(small[32 : 32 + 6 * experts], 6)
 
 
 def few_experts():
@@ -445,6 +536,7 @@
     capacity = max(2, (4 * tok + 3 * experts - 1) // (3 * experts))
     slots = -(-(capacity + 1) // 8) * 8
     total = experts * slots
+    small_rows = 6 * experts + 32 + (48 if few_experts() else 0)
     valid_total = 3 * tok * groups // 4
     scale = head_size ** (-0.5)
     joined = few_experts()
@@ -460,27 +552,30 @@
     packed = lax.all_gather(jnp.concatenate([inputs.T, out_grad.T, gains], axis=0), "head")
     w_output_full = lax.all_gather(w_output, "head", tiled=True)
     if joined:
-        all_in = lax.all_gather(inputs.T, ("expert", "head")).reshape(groups, heads, col, tok)
+        all_in = lax.all_gather(inputs.T, "expert")
     qkv, weights, attended = call(
         functools.partial(attend_kernel, scale),
-        [((3, col, tok), bf16, 1), ((heads_here, tok, tok), f32, 1), ((col, tok), bf16)],
-        scalars, packed, far(wq), far(wk), far(wv), far(buckets_row), far(bias_table.T),
+        [((3, col, tok), bf16, 2), ((heads_here, tok, tok), f32, 2), ((col, tok), bf16)],
+        scalars, packed, lazy(wq), lazy(wk), lazy(wv), far(buckets_row), far(bias_table.T),
     )
 
     attended_parts = lax.all_gather(attended, "head")
     residual, side, send = call(
         functools.partial(route_kernel, capacity),
-        [((heads, col, tok), f32, 1), ((8, tok), f32, 1), ((experts, slots, 2 * width), bf16)],
-        scalars, packed, attended_parts, far(w_output_full), far(routes_row), far(router_rows),
+        [((heads, col, tok), f32, 2), ((8, tok), f32, 1), ((experts, slots, 2 * width), bf16)],
+        scalars, packed, attended_parts, lazy(w_output_full), far(routes_row), far(router_rows),
     )
     rows = lax.all_to_all(send, "expert", split_axis=0, concat_axis=0, tiled=True)
     rows = rows.reshape(total, 2 * width)
+    if joined:
+        rows, all_in = lax.optimization_barrier((rows, all_in))
+        all_in = lax.all_gather(all_in, "head")
 
     back, part, hidden, before_grad, back_rows = call(
         functools.partial(expert_kernel, capacity),
-        [((experts * heads, slots, 256), bf16), ((heads, total * 3 // 2, 128), bf16, 1)]
-        + [((total, width), bf16, 1)] * 3,
-        scalars, rows, far(w_in), far(w_out), far(router_rows),
+        [((experts * heads, slots, 256), bf16), ((heads, total * 3 // 2, 128), bf16, 2)]
+        + [((total, width), bf16, 2)] * 3,
+        scalars, rows, lazy(w_in), lazy(w_out), far(router_rows),
     )
     came = lax.all_to_all(back, ("expert", "head"), split_axis=0, concat_axis=0, tiled=True)
     grad_own, gate_grad, stats = call(
@@ -493,12 +588,13 @@
     late, first, residual_grad_own, small, product = call(
         functools.partial(backward_kernel, scale, valid_total),
         [
-            ((3 * col, tok), bf16, 1), ((heads, col + 16 + total * 3 // 2, 128), bf16), ((col, tok), f32, 1),
-            ((6 * experts + 32, 128), f32, 1),
-            ((groups, col // groups * 6, 128), bf16, 1) if joined else ((1, col, width), f32, 1),
+            ((3 * col, tok), bf16, 2), ((heads, col + 16 + total * 3 // 2, 128), bf16), ((col, tok), f32, 2),
+            ((small_rows, 128), f32, 1),
+            ((groups, col // groups * 6, 128), bf16, 2) if joined else ((1, col, width), f32, 2),
         ],
-        scalars, packed, expert_grad, far(gate_grad), far(stats), far(residual), far(routes_row),
-        far(router_rows), far(w_output), far(weights), far(qkv), far(wq), far(wk), far(wv), far(attended), far(part),
+        scalars, lazy(packed), expert_grad, far(gate_grad), far(stats), lazy(residual), far(routes_row),
+        far(router_rows), lazy(w_output), lazy(weights), lazy(qkv), lazy(wq), lazy(wk), lazy(wv), lazy(attended),
+        lazy(part),
     )
 
     if joined:
@@ -508,28 +604,30 @@
     ret, sums, input_grad = call(
         first_kernel,
         [
-            ((experts, 2 * slots + (6 * experts + 32 + product.shape[1] if joined else 0), 128), bf16),
-            ((6 * experts + 32, 128), f32, 1), ((col, tok), f32),
+            ((experts, 2 * slots + (small_rows // experts + product.shape[1] if joined else 0), 128), bf16),
+            ((small_rows, 128), f32, 1), ((col, tok), f32, 2),
         ],
-        scalars, first, far(packed), far(residual_grad_own), far(small), *([far(product)] if joined else []),
+        scalars, first, lazy(packed), lazy(residual_grad_own), far(small), *([lazy(product)] if joined else []),
     )
     ret = lax.all_to_all(ret, "expert", split_axis=0, concat_axis=0, tiled=True)
     out = call(
         functools.partial(last_kernel, slots),
         [((col, tok), bf16), ((1, 1), f32)]
-        + ([((experts, width), f32), ((heads_here, bucket_count), f32), ((8, 256), f32), (product.shape, bf16)] if joined else []),
-        scalars, ret, far(side), far(residual), far(stats), far(buckets_row),
+        + ([((groups, small_rows // groups + product.shape[1], 128), bf16)] if joined else []),
+        scalars, ret, far(side), lazy(residual), far(stats),
     )
     block_out, aux_loss = out[:2]
     in_weight_grad, out_weight_grad = call(
-        weights_kernel, [((width, width), f32)] * 2, far(rows), far(hidden), far(before_grad), far(back_rows)
+        weights_kernel, [((width, width), f32, 2)] * 2, lazy(rows), lazy(hidden), lazy(before_grad), lazy(back_rows)
     )
     if joined:
-        router_grad, table_grad, gain_grads, share = out[2:]
-        shares = lax.all_to_all(share, "expert", split_axis=0, concat_axis=0, tiled=True)
-        normed_all = call(turn_kernel, [((width, groups * tok), bf16, 1)], far(all_in), far(packed))[0]
-        q_grad, k_grad, v_grad, output_grad = call(
-            products_kernel, [((col, width), f32, 1)] * 4, far(late_all), far(normed_all), shares
+        shares = lax.all_to_all(out[2], "expert", split_axis=0, concat_axis=0, tiled=True)
+        normed_all = call(turn_kernel, [((width, groups * tok), bf16, 1)], lazy(all_in), far(packed))[0]
+        q_grad, k_grad, v_grad, output_grad, router_grad, table_grad, gain_grads = call(
+            products_kernel,
+            [((col, width), f32, 2)] * 4
+            + [((experts, width), f32), ((heads_here, bucket_count), f32), ((8, 256), f32)],
+            lazy(late_all), lazy(normed_all), shares, far(buckets_row),
         )
     else:
         gain = packed[:, 2 * col : 2 * col + 2].reshape(heads, 256)[:, :col].reshape(width, 1)
@@ -537,12 +635,11 @@
         normed = (x * token_scale(x) * gain.astype(f32)).astype(bf16)
         products = [mm(late[i * col : (i + 1) * col], normed, nt) for i in range(3)]
         q_grad, k_grad, v_grad, sums, output_grad = lax.psum(products + [sums, product[0]], "expert")
-        wide = 6 * experts
-        router_grad = unfold_lanes(sums[:wide], 6)
-        offsets = unfold_lanes(sums[wide : wide + 16], 2)[:heads_here, : 2 * tok - 1]
+        router_grad = unfold_lanes(sums[32 : 32 + 6 * experts], 6)
+        offsets = unfold_lanes(sums[16:32], 2)[:heads_here, : 2 * tok - 1]
         hot = (buckets[None, :] == jnp.arange(bucket_count)[:, None]).astype(f32)
         table_grad = mm(offsets, hot, nt, highest)
-        gain_grads = unfold_lanes(sums[wide + 16 :], 2)
+        gain_grads = unfold_lanes(sums[:16], 2)
     return (
         block_out.T,
         input_grad.T,

time: 152 us -> 180 us (1.18)
  blocking collectives: 90.5 us -> 108 us
  Pallas kernels: 32.9 us -> 41.9 us
  starting transfers between devices: 3.54 us -> 9.08 us
  waiting for transfers between devices: 5.67 us -> 1.41 us
    all_gather x0 -> x1, blocking collectives: none -> 41.5 us  [shards(): all_in = lax.all_gather(inputs.T, 'expert')]
    all_to_all x1 -> x0, blocking collectives: 23.4 us -> none  [shards(): lax.all_to_all(send, 'expert', split_axis=0, concat_axis=0, tiled=True)]
    pallas_call x10, Pallas kernels: 32.9 us -> 41.9 us  [call(): pl.pallas_call(run, out_shape=shapes, in_specs=in_specs, out_specs=out_sp...]
    all_to_all x1 -> x2, starting transfers between devices: 3.42 us -> 8.96 us  [the longest x1 5.52 us: shards(): lax.all_to_all(send, 'expert', split_axis=0, concat_axis=0, tiled=True)]
    all_to_all x1 -> x2, waiting for transfers between devices: 4.27 us -> 0.67 us  [the longest x1 0.67 us: shards(): lax.all_to_all(out[2], 'expert', split_axis=0, concat_axis=0, tiled=True)]
  transfers between devices with their start and end apart: 4 -> 5, of which waited for: 1 -> 1; matrix products, arithmetic and copies ran while one was open for 3% -> 2% of each run, Pallas kernels for 19% -> 18%
where the time goes in v5:
time: 180 us; the launch traced here: 179 us
  blocking collectives  108 us (60%)
  Pallas kernels  41.9 us (23%)
  between operations  14.6 us (8%)
  starting transfers between devices  9.08 us (5%)
  local copies, waits for them, and re-layouts  3.25 us (2%)
    pallas_call x10, Pallas kernels, call(): pl.pallas_call(run, out_shape=shapes, in_specs=in_specs, out_specs=out_sp...  41.9 us
    all_gather x1, blocking collectives, shards(): all_in = lax.all_gather(inputs.T, 'expert')  41.5 us
    all_to_all x1, blocking collectives, shards(): ret = lax.all_to_all(ret, 'expert', split_axis=0, concat_axis=0, tiled=True)  21.1 us
    all_to_all x1, blocking collectives, shards(): lax.all_to_all(back, ('expert', 'head'), split_axis=0, concat_axis=0, til...  14.9 us
    all_to_all x1, blocking collectives, shards(): lax.all_to_all(first, 'head', split_axis=0, concat_axis=0, tiled=True)  11.1 us
    all_gather x1, blocking collectives, shards(): lax.all_gather(jnp.concatenate([inputs.T, out_grad.T, gains], axis=0), 'h...  8.01 us
    all_gather x1, blocking collectives, shards(): attended_parts = lax.all_gather(attended, 'head')  6.06 us
    all_gather x1, blocking collectives, shards(): expert_grad = lax.all_gather(grad_own, 'head')  5.59 us
  transfers between devices with their start and end apart: 5, of which 1 were waited for; matrix products, arithmetic and copies ran while one was open for 2% of the time, Pallas kernels for 18%

profile of v5, /device:TPU:0, one launch (start us, length us, event | category | flops | bytes accessed | tf_op | source)
XLA Modules:
  0.0 179.3 jit_solution(1232595533712316481)
XLA Ops:
  7.2 0.0 all-gather.10.cloned.1.call-start
  7.2 0.7 all-gather.10.cloned.1.call-update
  8.6 1.2 pad.4
  9.8 1.4 concatenate.6
  11.2 0.1 pad_add_fusion.refs_0_
  11.3 0.8 pad_maximum_fusion
  12.1 8.0 %all-gather = bf16[1600,128]{1,0:T(8,128)(2,1)S(1)} all-gather(bf16[400,128]{1,0:T(8,128)(2,1)S(1)} %pad_maximum_fusion), channel_id=2, replica_groups=mesh['expert'=8,'head'=4] {'head'}, dimensions={0}, use_global_device_ids=true | all-gather | bytes 512000 | tf_op jit(solution)/shard_map/all_gather | solution.py:552
  20.1 0.0 copy-start
  20.2 3.9 %shard_map.246 = (bf16[3,192,128]{2,1,0:T(8,128)(2,1)}, f32[3,128,128]{2,1,0:T(8,128)}, bf16[192,128]{1,0:T(8,128)(2,1)S(1)}) custom-call(s32[3]{0:T(128)S(1)} %pad_add_fusion.refs_0_, bf16[4,400,128]{2,1,0:T(8,128)(2,1)S(1)} %bitcast.33, bf16[192,768]{1,0:T(8,128)(2,1)} %bitcast.47, bf16[192,768]{1,0:T(8,128)(2,1)} %bitcast.49, bf16[192,768]{1,0:T(8,128)(2,1)} %bitcast.51, ...), custom_call_target="tpu_custom_call" | custom-call | tf_op jit(solution)/shard_map/pallas_call | solution.py:106
  24.1 0.0 copy-start.2
  24.1 0.0 copy-start.3
  24.1 6.1 %all-gather.1 = bf16[768,128]{1,0:T(8,128)(2,1)S(1)} all-gather(bf16[192,128]{1,0:T(8,128)(2,1)S(1)} %get-tuple-element.48.refs_14_), channel_id=3, replica_groups=mesh['expert'=8,'head'=4] {'head'}, dimensions={0}, use_global_device_ids=true | all-gather | bytes 245760 | tf_op jit(solution)/shard_map/all_gather | solution.py:562
  30.2 0.0 all-gather.10.cloned.1.call-done.refs_3_
  30.2 4.5 %shard_map.247 = (f32[4,192,128]{2,1,0:T(8,128)}, f32[8,128]{1,0:T(8,128)}, bf16[8,24,1536]{2,1,0:T(8,128)(2,1)}) custom-call(s32[3]{0:T(128)S(1)} %pad_add_fusion.refs_0_, bf16[4,400,128]{2,1,0:T(8,128)(2,1)S(1)} %bitcast.34, bf16[4,192,128]{2,1,0:T(8,128)(2,1)S(1)} %bitcast.40, bf16[768,768]{1,0:T(8,128)(2,1)} %all-gather.10.cloned.1.call-done.refs_3_, ...), custom_call_target="tpu_custom_call" | custom-call | tf_op jit(solution)/shard_map/pallas_call | solution.py:106
  34.7 0.0 copy-done
  34.7 0.0 copy-done.2
  34.7 5.5 %all-to-all-start = ((bf16[8,24,1536]{2,1,0:T(8,128)(2,1)}), bf16[8,24,1536]{2,1,0:T(8,128)(2,1)S(1)}, u32[]{:S(2)}, u32[]{:S(2)}) async-start(bf16[8,24,1536]{2,1,0:T(8,128)(2,1)} %get-tuple-element.49), calls=%async_computation | async-start | bytes 1179648 | tf_op jit(solution)/shard_map/all_to_all | solution.py:568
  40.2 0.0 all-gather.14.cloned.1.call-start
  40.3 0.0 copy-done.3
  40.3 41.5 %all-gather.2 = bf16[1536,128]{1,0:T(8,128)(2,1)} all-gather(bf16[192,128]{1,0:T(8,128)(2,1)S(1)} %bitcast.54), channel_id=4, replica_groups=mesh['expert'=8,'head'=4] {'expert'}, dimensions={0}, use_global_device_ids=true | all-gather | bytes 442368 | tf_op jit(solution)/shard_map/all_gather | solution.py:555
  81.8 0.0 all-to-all-done
  81.8 0.0 copy-start.1
  81.8 0.0 all-gather.14.cloned.1.call-update
  81.8 0.0 all-gather.12.cloned.1.call-start
  81.9 4.8 %shard_map.248 = (bf16[32,24,256]{2,1,0:T(8,128)(2,1)S(1)}, bf16[4,288,128]{2,1,0:T(8,128)(2,1)}, bf16[192,768]{1,0:T(8,128)(2,1)}, bf16[192,768]{1,0:T(8,128)(2,1)}, bf16[192,768]{1,0:T(8,128)(2,1)}) custom-call(s32[3]{0:T(128)S(1)} %pad_add_fusion.refs_0_, bf16[192,1536]{1,0:T(8,128)(2,1)S(1)} %bitcast.38, bf16[768,768]{1,0:T(8,128)(2,1)} %bitcast.44, ...), custom_call_target="tpu_custom_call" | custom-call | tf_op jit(solution)/shard_map/pallas_call | solution.py:106
  86.7 0.0 copy-done.1
  86.7 14.9 %all_to_all.25.refs_0_ = bf16[32,24,256]{2,1,0:T(8,128)(2,1)S(1)} all-to-all(bf16[32,24,256]{2,1,0:T(8,128)(2,1)S(1)} %get-tuple-element.51), channel_id=1, replica_groups=mesh['expert'=8,'head'=4] {'expert','head'}, dimensions={0} | all-to-all | bytes 786432 | tf_op jit(solution)/shard_map/all_to_all | solution.py:580
  101.6 1.6 shard_map.249
  103.2 5.6 %all-gather.3 = bf16[768,128]{1,0:T(8,128)(2,1)S(1)} all-gather(bf16[192,128]{1,0:T(8,128)(2,1)S(1)} %get-tuple-element.53), channel_id=5, replica_groups=mesh['expert'=8,'head'=4] {'head'}, dimensions={0}, use_global_device_ids=true | all-gather | bytes 245760 | tf_op jit(solution)/shard_map/all_gather | solution.py:586
  108.8 6.7 %shard_map.250 = (bf16[576,128]{1,0:T(8,128)(2,1)}, bf16[4,496,128]{2,1,0:T(8,128)(2,1)S(1)}, f32[192,128]{1,0:T(8,128)}, f32[128,128]{1,0:T(8,128)}, bf16[8,144,128]{2,1,0:T(8,128)(2,1)}) custom-call(s32[3]{0:T(128)S(1)} %pad_add_fusion.refs_0_, bf16[4,400,128]{2,1,0:T(8,128)(2,1)} %bitcast.35, bf16[4,192,128]{2,1,0:T(8,128)(2,1)S(1)} %bitcast.41, ...), custom_call_target="tpu_custom_call" | custom-call | tf_op jit(solution)/shard_map/pallas_call | solution.py:106
  115.6 0.0 all-gather.12.cloned.1.call-update
  115.6 11.1 %all_to_all.26.refs_1_ = bf16[4,496,128]{2,1,0:T(8,128)(2,1)S(1)} all-to-all(bf16[4,496,128]{2,1,0:T(8,128)(2,1)S(1)} %get-tuple-element.60), channel_id=1, replica_groups=mesh['expert'=8,'head'=4] {'head'}, dimensions={0} | all-to-all | bytes 1015808 | tf_op jit(solution)/shard_map/all_to_all | solution.py:603
  126.7 3.5 %shard_map.251 = (bf16[8,208,128]{2,1,0:T(8,128)(2,1)S(1)}, f32[128,128]{1,0:T(8,128)}, f32[192,128]{1,0:T(8,128)}) custom-call(s32[3]{0:T(128)S(1)} %pad_add_fusion.refs_0_, bf16[4,496,128]{2,1,0:T(8,128)(2,1)S(1)} %all_to_all.26.refs_1_, bf16[4,400,128]{2,1,0:T(8,128)(2,1)} %bitcast.36, f32[192,128]{1,0:T(8,128)} %get-tuple-element.61.refs_3_, ...), custom_call_target="tpu_custom_call" | custom-call | tf_op jit(solution)/shard_map/pallas_call | solution.py:106
  130.2 21.1 %all_to_all.27.refs_1_ = bf16[8,208,128]{2,1,0:T(8,128)(2,1)S(1)} all-to-all(bf16[8,208,128]{2,1,0:T(8,128)(2,1)S(1)} %get-tuple-element.64), channel_id=1, replica_groups=mesh['expert'=8,'head'=4] {'expert'}, dimensions={0} | all-to-all | bytes 851968 | tf_op jit(solution)/shard_map/all_to_all | solution.py:612
  151.3 2.5 %shard_map.252 = (bf16[192,128]{1,0:T(8,128)(2,1)}, f32[1,1]{1,0:T(1,128)}, bf16[8,160,128]{2,1,0:T(8,128)(2,1)}) custom-call(s32[3]{0:T(128)S(1)} %pad_add_fusion.refs_0_, bf16[8,208,128]{2,1,0:T(8,128)(2,1)S(1)} %all_to_all.27.refs_1_, f32[8,128]{1,0:T(8,128)} %get-tuple-element.52.refs_1_.refs_2_, f32[4,192,128]{2,1,0:T(8,128)} %get-tuple-element.56.refs_5_.refs_3_, ...), custom_call_target="tpu_custom_call" | custom-call | tf_op jit(solution)/shard_map/pallas_call | solution.py:106
  153.8 3.4 %all-to-all-start.4 = ((bf16[8,160,128]{2,1,0:T(8,128)(2,1)}), bf16[8,160,128]{2,1,0:T(8,128)(2,1)S(1)}, u32[]{:S(2)}, u32[]{:S(2)}) async-start(bf16[8,160,128]{2,1,0:T(8,128)(2,1)} %get-tuple-element.70), calls=%async_computation.4 | async-start | bytes 655360 | tf_op jit(solution)/shard_map/all_to_all | solution.py:624
  157.3 4.1 %shard_map.255 = (f32[768,768]{1,0:T(8,128)}, f32[768,768]{1,0:T(8,128)}) custom-call(bf16[192,1536]{1,0:T(8,128)(2,1)} %bitcast.39, bf16[192,768]{1,0:T(8,128)(2,1)} %get-tuple-element.78.refs_1_, bf16[192,768]{1,0:T(8,128)(2,1)} %get-tuple-element.79.refs_2_, bf16[192,768]{1,0:T(8,128)(2,1)} %get-tuple-element.80.refs_3_), custom_call_target="tpu_custom_call" | custom-call | tf_op jit(solution)/shard_map/pallas_call | solution.py:106
  161.3 0.0 all-gather.14.cloned.1.call-done
  161.4 4.3 %shard_map.253.refs_1_ = bf16[768,1024]{1,0:T(8,128)(2,1)} custom-call(bf16[4,8,192,128]{3,2,1,0:T(8,128)(2,1)} %bitcast.42, bf16[4,400,128]{2,1,0:T(8,128)(2,1)} %bitcast.37), custom_call_target="tpu_custom_call" | custom-call | tf_op jit(solution)/shard_map/pallas_call | solution.py:106
  165.6 0.7 all-to-all-done.4.refs_2_
  166.3 0.0 all-gather.12.cloned.1.call-done
  166.3 5.8 %shard_map.254 = (f32[192,768]{1,0:T(8,128)}, f32[192,768]{1,0:T(8,128)}, f32[192,768]{1,0:T(8,128)}, f32[192,768]{1,0:T(8,128)}, f32[8,768]{1,0:T(8,128)}, /*index=5*/f32[3,32]{1,0:T(4,128)}, f32[8,256]{1,0:T(8,128)S(1)}) custom-call(bf16[8,576,128]{2,1,0:T(8,128)(2,1)} %bitcast.46, bf16[768,1024]{1,0:T(8,128)(2,1)} %shard_map.253.refs_1_, ...), custom_call_target="tpu_custom_call" | custom-call | tf_op jit(solution)/shard_map/pallas_call | solution.py:106
  172.2 0.6 fusion
  (2 shorter events, 0.0 us)
Async XLA Ops:
  7.2 23.0 %all-gather.10.cloned.1.call-start = ((), (), s32[]{:S(2)}) async-start(), calls=%async_computation.5 | async-start | bytes 1474560 | tf_op jit(solution)/shard_map/all_gather | solution.py:553
  20.1 14.5 %copy-start = (bf16[1600,128]{1,0:T(8,128)(2,1)}, bf16[1600,128]{1,0:T(8,128)(2,1)S(1)}, u32[]{:S(2)}) copy-start(bf16[1600,128]{1,0:T(8,128)(2,1)S(1)} %all-gather) | copy-start | bytes 1228804
  24.1 10.6 %copy-start.2 = (bf16[192,128]{1,0:T(8,128)(2,1)}, bf16[192,128]{1,0:T(8,128)(2,1)S(1)}, u32[]{:S(2)}) copy-start(bf16[192,128]{1,0:T(8,128)(2,1)S(1)} %get-tuple-element.48.refs_14_) | copy-start | bytes 147460
  24.1 16.2 %copy-start.3 = (bf16[128,192]{0,1:T(8,128)(2,1)S(1)}, bf16[128,192]{0,1:T(8,128)(2,1)}, u32[]{:S(2)}) copy-start(bf16[128,192]{0,1:T(8,128)(2,1)} %param.15) | copy-start | bytes 147460
  34.7 47.1 %all-to-all-start = ((bf16[8,24,1536]{2,1,0:T(8,128)(2,1)}), bf16[8,24,1536]{2,1,0:T(8,128)(2,1)S(1)}, u32[]{:S(2)}, u32[]{:S(2)}) async-start(bf16[8,24,1536]{2,1,0:T(8,128)(2,1)} %get-tuple-element.49), calls=%async_computation | async-start | bytes 1179648 | tf_op jit(solution)/shard_map/all_to_all | solution.py:568
  40.2 121.1 %all-gather.14.cloned.1.call-start = ((), (), s32[]{:S(2)}) async-start(), calls=%async_computation.7 | async-start | bytes 1966080 | tf_op jit(solution)/shard_map/all_gather | solution.py:572
  81.8 4.9 %copy-start.1 = (bf16[8,24,1536]{2,1,0:T(8,128)(2,1)}, bf16[8,24,1536]{2,1,0:T(8,128)(2,1)S(1)}, u32[]{:S(2)}) copy-start(bf16[8,24,1536]{2,1,0:T(8,128)(2,1)S(1)} %all-to-all-done) | copy-start | bytes 1769476
  81.8 84.5 %all-gather.12.cloned.1.call-start = ((), (), s32[]{:S(2)}) async-start(), calls=%async_computation.6 | async-start | bytes 1327104 | tf_op jit(solution)/shard_map/all_gather | solution.py:601
  153.8 12.5 %all-to-all-start.4 = ((bf16[8,160,128]{2,1,0:T(8,128)(2,1)}), bf16[8,160,128]{2,1,0:T(8,128)(2,1)S(1)}, u32[]{:S(2)}, u32[]{:S(2)}) async-start(bf16[8,160,128]{2,1,0:T(8,128)(2,1)} %get-tuple-element.70), calls=%async_computation.4 | async-start | bytes 655360 | tf_op jit(solution)/shard_map/all_to_all | solution.py:624
Sparse Core Ops, SparseCore 0:
  9.6 20.5 all-gather.9
  82.0 20.4 all-gather.13
  115.7 39.7 all-gather.11

commit v6 on v4

--- a/solution.py
+++ b/solution.py
@@ -22,17 +22,16 @@
     return lax.dot_general(left, right, (dims, ((), ())), precision=precision, preferred_element_type=f32)
 
 
-def call(body, outs, *args, scratch=()):
+def call(body, outs, *args):
     scalar_memory = pl.BlockSpec(memory_space=pltpu.SMEM)
     in_specs = [scalar_memory if a.dtype == jnp.int32 and a.ndim == 1 else pl.BlockSpec() for a in args]
     shapes = []
-    for shape, kind, *far in outs:
-        shapes.append(pltpu.HBM(shape, kind) if far else jax.ShapeDtypeStruct(shape, kind))
+    for shape, kind, *remote in outs:
+        shapes.append(pltpu.HBM(shape, kind) if remote else jax.ShapeDtypeStruct(shape, kind))
     return pl.pallas_call(
         body,
         out_shape=shapes,
         in_specs=in_specs,
-        scratch_shapes=list(scratch),
         compiler_params=pltpu.CompilerParams(vmem_limit_bytes=40 * 1024 * 1024),
     )(*args)
 
@@ -118,7 +117,9 @@
     return sublanes((count, spots.shape[1])) == spots
 
 
-def attend_kernel(scale, scalars, packed, wq, wk, wv, buckets, table, qkv_ref, weights_ref, attended_ref):
+def attend_kernel(
+    scale, scalars, packed, wq, wk, wv, w_output, buckets, table, qkv_ref, weights_ref, attended_ref, branch_ref
+):
     heads, tok, _ = weights_ref.shape
     col = wq.shape[0]
     size = col // heads
@@ -142,7 +143,11 @@
         weights = softmax(jnp.where(open_keys, scores, -1000000000.0), 1)
         weights_ref[h] = weights
         outs.append(mm(value[at], weights.astype(bf16), nt))
-    attended_ref[...] = jnp.concatenate(outs, axis=0).astype(bf16)
+    attended = jnp.concatenate(outs, axis=0).astype(bf16)
+    attended_ref[...] = attended
+    branch = mm(w_output[...], attended, tn)
+    for i in range(branch_ref.shape[0]):
+        branch_ref[i] = branch[i * col : (i + 1) * col].astype(bf16)
 
 
 def second_norm(residual, gain, w_router):
@@ -152,38 +157,41 @@
     return scale, unit, normed, softmax(mm(w_router, normed), 0)
 
 
-def route_kernel(capacity, scalars, packed, attended, w_output, routes, w_router, residual_ref, side_ref, send_ref):
-    tok = routes.shape[1]
+def route_kernel(capacity, scalars, came, inputs, out_grad, routes, residual_ref, low_ref, side_ref, send_ref):
+    col, tok = inputs.shape
     experts, slots, _ = send_ref.shape
-    heads, col, _ = residual_ref.shape
-    width = heads * col
-    branch = mm(tall(attended, 0, col).astype(bf16), w_output[...], tn)
-    residual = tall(packed, 0, col) + jnp.transpose(branch)
-    for i in range(heads):
-        residual_ref[i] = residual[i * col : (i + 1) * col]
-    _, _, normed, router = second_norm(residual, all_gains(packed)[1], w_router[...])
+    residual = inputs[...].astype(f32)
+    for i in range(came.shape[0]):
+        residual = residual + came[i].astype(f32)
+    residual_ref[...] = residual
+    low = residual.astype(bf16)
+    low_ref[...] = low
     route_hot = (sublanes((experts, tok)) == routes[...]).astype(f32)
-    gate = jnp.sum(router * route_hot, axis=0, keepdims=True)
     before = (sublanes((tok, tok)) < lanes((tok, tok))).astype(bf16)
     slot = jnp.sum(mm(route_hot.astype(bf16), before) * route_hot, axis=0, keepdims=True)
     spots = routes[...].astype(f32) * slots + slot
-    side_ref[...] = side_rows(8, tok, [gate, spots])
+    side_ref[...] = side_rows(8, tok, [spots])
     valid = (lanes((1, tok)) < scalars[0]).astype(f32)
     counts = jnp.sum(route_hot * valid, axis=1, keepdims=True)
-    probs = high_low(jnp.sum(router * valid, axis=1, keepdims=True), 3)
     pick = pick_slots(spots.astype(jnp.int32), experts * slots).astype(bf16)
-    rows = mm(pick, normed, nt)
-    grads = mm(pick, tall(packed, col, col).astype(bf16), nt)
+    rows = mm(pick, jnp.concatenate([low, out_grad[...]], axis=0), nt)
+    spare = (sublanes((slots, 2 * col)) == capacity) & (lanes((slots, 2 * col)) == col)
     for e in range(experts):
-        at = slice(e * slots, (e + 1) * slots)
-        send_ref[e, :, :width] = rows[at].astype(bf16)
-        stats = side_lanes(1, width, [counts[e : e + 1]] + [piece[e : e + 1] for piece in probs])
-        filled = jnp.where(sublanes((slots, width)) == capacity, stats, grads[at])
-        send_ref[e, :, width:] = filled.astype(bf16)
+        block = rows[e * slots : (e + 1) * slots]
+        send_ref[e] = jnp.where(spare, counts[e : e + 1], block).astype(bf16)
+
+
+def gain_row(packed, first, line):
+    pieces = []
+    for i in range(packed.shape[0]):
+        block = packed[i, first : first + 16, :].astype(f32)
+        pieces += [block[line : line + 1, :], block[line + 1 : line + 2, :64]]
+    return jnp.concatenate(pieces, axis=1)
 
 
 def expert_kernel(
-    capacity, scalars, rows_ref, w_in, w_out, w_router, back_ref, part_ref, hidden_ref, before_ref, grads_ref
+    capacity, scalars, quarters, packed, w_in, w_out, w_router,
+    back_ref, part_ref, hidden_ref, before_ref, grads_ref, rows_ref,
 ):
     total = rows_ref.shape[0]
     experts, width = w_router.shape
@@ -191,8 +199,12 @@
     col = width // heads
     slots = total // experts
     half = total // 2
-    rows = rows_ref[:, :width]
-    grads = rows_ref[:, width:].astype(f32)
+    parts = [quarters[i].astype(f32) for i in range(heads)]
+    residual = jnp.concatenate([block[:, :col] for block in parts], axis=1)
+    grads = jnp.concatenate([block[:, col:] for block in parts], axis=1)
+    inverse = lax.rsqrt(jnp.sum(residual * residual, axis=1, keepdims=True) * (1.0 / width) + eps)
+    rows = (residual * inverse * gain_row(packed, 2 * col, 2)).astype(bf16)
+    rows_ref[...] = rows
     hidden, slope = gelu_parts(mm(rows, w_in[...]))
     hidden = hidden.astype(bf16)
     hidden_ref[...] = hidden
@@ -214,10 +226,7 @@
     stats = jnp.zeros((1, 128), f32)
     for b in range(experts):
         stats = stats + grads[b * slots + capacity : b * slots + capacity + 1, :128]
-    prob = stats[:, 1:2] + stats[:, 2:3] + stats[:, 3:4]
-    side = side_lanes(
-        total, 256 - col, high_low(gate_grad) + high_low(stats[:, 0:1]) + high_low(prob, 3)
-    )
+    side = side_lanes(total, 256 - col, high_low(gate_grad) + high_low(stats[:, 0:1]))
     for b in range(experts):
         at = slice(b * slots, (b + 1) * slots)
         for i in range(heads):
@@ -227,13 +236,12 @@
 
 
 def weights_kernel(rows_ref, hidden, before, grads, in_ref, out_ref):
-    width = in_ref.shape[0]
-    in_ref[...] = mm(rows_ref[:, :width], before[...], tn)
+    in_ref[...] = mm(rows_ref[...], before[...], tn)
     out_ref[...] = mm(hidden[...], grads[...], tn)
 
 
-def collect_kernel(came, side, grad_ref, gate_ref, stats_ref):
-    col, tok = grad_ref.shape
+def collect_kernel(came, side, low, grad_ref, gate_ref, stats_ref):
+    col, tok = low.shape
     experts = stats_ref.shape[0]
     sources, slots, _ = came.shape
     heads = sources // experts
@@ -245,30 +253,32 @@
         sums.append(total)
     stats = jnp.concatenate([total[0:1, col:] for total in sums], axis=0) * (1.0 / heads)
     sums = jnp.concatenate(sums, axis=0)
-    pick = pick_slots(side[1:2, :].astype(jnp.int32), experts * slots)
-    grad_ref[...] = mm(sums[:, :col].astype(bf16), pick.astype(bf16), tn).astype(bf16)
+    pick = pick_slots(side[0:1, :].astype(jnp.int32), experts * slots)
+    grad_ref[:col, :] = mm(sums[:, :col].astype(bf16), pick.astype(bf16), tn).astype(bf16)
+    grad_ref[col:, :] = low[...]
     gate = mm(sums[:, col:], pick.astype(f32), tn, highest)
     gate_ref[...] = jnp.broadcast_to(gate[0:1] + gate[1:2], gate_ref.shape)
     count = stats[:, 2:3] + stats[:, 3:4]
-    prob = stats[:, 4:5] + stats[:, 5:6] + stats[:, 6:7]
-    stats_ref[...] = side_lanes(experts, 128, [count, prob])
+    stats_ref[...] = side_lanes(experts, 128, [count])
 
 
 def backward_kernel(
-    scale, valid_total, scalars, packed, expert_grad, gate_grad, stats, residual_ref, routes, w_router,
-    w_output, weights_ref, qkv, wq, wk, wv, attended, part, late_ref, first_ref, own_ref, small_ref, product_ref,
+    scale, valid_total, scalars, packed, expert_grad, gate_grad, stats, routes, w_router, w_output, weights_ref,
+    qkv, wq, wk, wv, attended, part, late_ref, first_ref, own_ref, small_ref, product_ref, gate_ref,
 ):
     tok = routes.shape[1]
     heads_here = weights_ref.shape[0]
-    blocks, col, _ = residual_ref.shape
+    blocks, col = packed.shape[0], wq.shape[0]
     experts, width = w_router.shape
     size = col // heads_here
     gain_one, gain_two = all_gains(packed)
-    residual = tall(residual_ref, 0, col)
+    residual = tall(expert_grad, col, col)
     scale_two, unit, normed, router = second_norm(residual, gain_two, w_router[...])
     valid = (lanes((1, tok)) < scalars[0]).astype(f32)
     route_hot = (sublanes((experts, tok)) == routes[...]).astype(f32)
     fraction = stats[:, 0:1] * (aux_weight * experts / (valid_total * valid_total))
+    gate = jnp.sum(router * route_hot, axis=0, keepdims=True)
+    gate_ref[...] = jnp.broadcast_to(gate, gate_ref.shape)
     prob_grad = route_hot * gate_grad[0:1, :] + fraction * valid
     logit_grad = router * (prob_grad - jnp.sum(router * prob_grad, axis=0, keepdims=True))
     logit_grad = logit_grad.astype(bf16)
@@ -321,14 +331,19 @@
         gains = jnp.where(scalars[1] == i, gain_two_grad[at], gains)
         own = jnp.where(scalars[1] == i, residual_grad[at], own)
     own_ref[...] = own
-    gains = jnp.transpose(side_lanes(col, 128, [gains]))[0:8]
+    probs = jnp.sum(router * valid, axis=1, keepdims=True)
+    if experts < col:
+        probs = jnp.concatenate([probs, jnp.zeros((col - experts, 1), f32)], axis=0)
+    gains = jnp.transpose(side_lanes(col, 128, [gains, jnp.zeros_like(gains)] + high_low(probs)))[0:8]
     router_grad = mm(logit_grad, normed, nt)
     offsets = jnp.concatenate(offsets, axis=0)
     offsets = jnp.concatenate([offsets, jnp.zeros((8 - heads_here, 2 * tok), f32)], axis=0)
     gains = jnp.concatenate([gains, jnp.zeros((8, 64), f32)], axis=1)
-    small_ref[...] = jnp.concatenate(
-        [fold_lanes(router_grad), fold_lanes(offsets), fold_lanes(gains)], axis=0
-    )
+    pieces = [fold_lanes(gains), fold_lanes(offsets), fold_lanes(router_grad)]
+    spare = small_ref.shape[0] - 6 * experts - 32
+    if spare:
+        pieces.append(jnp.zeros((spare, 128), f32))
+    small_ref[...] = jnp.concatenate(pieces, axis=0)
 
 
 def first_kernel(scalars, came, packed, own, small, *refs):
@@ -348,8 +363,7 @@
     gain_grad = jnp.sum(total[:col] * unit, axis=1, keepdims=True)
     gain_grad = jnp.transpose(side_lanes(col, 128, [jnp.zeros_like(gain_grad), gain_grad]))[0:8]
     gain_grad = jnp.concatenate([gain_grad, jnp.zeros((8, 64), f32)], axis=1)
-    kept = small.shape[0] - 16
-    sums = jnp.concatenate([small[:kept, :], small[kept:, :] + fold_lanes(gain_grad)], axis=0)
+    sums = jnp.concatenate([small[:16, :] + fold_lanes(gain_grad), small[16:, :]], axis=0)
     sums_ref[...] = sums
     produced = total[col + 16 :]
     count = produced.shape[0] * 2 // 3
@@ -362,36 +376,27 @@
         at = slice(e * slots, (e + 1) * slots)
         pieces = [top[at], rest[at]]
         if product:
-            pieces += [sums, product[0][e].astype(f32)]
+            chunk = sums.shape[0] // experts
+            pieces += [sums[e * chunk : (e + 1) * chunk], product[0][e].astype(f32)]
         ret_ref[e] = jnp.concatenate(pieces, axis=0).astype(bf16)
 
 
-def last_kernel(slots, scalars, came, side, residual, stats, buckets, *refs):
-    block_ref, aux_ref, refs = refs[0], refs[1], refs[2:]
+def last_kernel(slots, came, side, gate, residual, *refs):
+    block_ref, refs = refs[0], refs[1:]
     experts = came.shape[0]
-    heads, col, tok = residual.shape
+    col, tok = residual.shape
     blocks = [came[e].astype(f32) for e in range(experts)]
     top = jnp.concatenate([block[:slots] for block in blocks], axis=0).astype(bf16)
     rest = jnp.concatenate([block[slots : 2 * slots] for block in blocks], axis=0).astype(bf16)
-    pick = pick_slots(side[1:2, :].astype(jnp.int32), experts * slots).astype(bf16)
+    pick = pick_slots(side[0:1, :].astype(jnp.int32), experts * slots).astype(bf16)
     returned = jnp.concatenate([mm(top, pick, tn), mm(rest, pick, tn)[: col - 128]], axis=0)
-    block_ref[...] = (residual[scalars[1]] + side[0:1, :] * returned).astype(bf16)
-    product = stats[:, 0:1] * stats[:, 1:2]
-    valid_total = 3 * tok * experts // 4
-    aux_ref[...] = jnp.sum(product, axis=0, keepdims=True) * (experts / (valid_total * valid_total))
+    block_ref[...] = (residual[...] + gate[0:1, :] * returned).astype(bf16)
     if refs:
-        router_ref, table_ref, gains_ref, share_ref = refs
         total = blocks[0][2 * slots :]
         for block in blocks[1:]:
             total = total + block[2 * slots :]
-        wide = 6 * experts
         for e in range(experts):
-            share_ref[e] = total[wide + 32 :].astype(bf16)
-        router_ref[...] = unfold_lanes(total[:wide], 6)
-        offsets = unfold_lanes(total[wide : wide + 16], 2)
-        hot = (sublanes((table_ref.shape[1], 2 * tok)) == buckets[...]).astype(f32)
-        table_ref[...] = mm(offsets, hot, nt, highest)[: table_ref.shape[0]]
-        gains_ref[...] = unfold_lanes(total[wide + 16 : wide + 32], 2)
+            refs[0][e] = total.astype(bf16)
 
 
 def turn_kernel(all_in, packed, normed_ref):
@@ -402,15 +407,31 @@
         normed_ref[:, b * tok : (b + 1) * tok] = (x * token_scale(x) * gain).astype(bf16)
 
 
-def products_kernel(late, normed, shares, q_ref, k_ref, v_ref, out_ref):
+def products_kernel(
+    late, normed, shares, buckets, stats, q_ref, k_ref, v_ref, out_ref, router_ref, table_ref, gains_ref, aux_ref
+):
     groups = shares.shape[0]
-    size = out_ref.shape[0] // groups
+    col = q_ref.shape[0]
+    experts = router_ref.shape[0]
+    size = col // groups
+    blocks = [shares[b].astype(f32) for b in range(groups)]
+    chunk = blocks[0].shape[0] - 6 * size
     for b in range(groups):
-        out_ref[b * size : (b + 1) * size, :] = unfold_lanes(shares[b].astype(f32), 6)
-    col = q_ref.shape[0]
-    joined = jnp.concatenate([late[b] for b in range(late.shape[0])], axis=1)
+        out_ref[b * size : (b + 1) * size, :] = unfold_lanes(blocks[b][chunk:], 6)
+    joined = jnp.concatenate([late[b] for b in range(groups)], axis=1)
     for i, ref in enumerate((q_ref, k_ref, v_ref)):
         ref[...] = mm(joined[i * col : (i + 1) * col], normed[...], nt)
+    small = jnp.concatenate([block[:chunk] for block in blocks], axis=0)
+    gains = unfold_lanes(small[:16], 2)
+    gains_ref[...] = gains
+    probs = gains[2:3, :experts] + gains[3:4, :experts]
+    same = lanes((experts, experts)) == sublanes((experts, experts))
+    share = jnp.sum(jnp.where(same, stats[:, 0:1] * probs, 0.0), axis=0, keepdims=True)
+    valid_total = 3 * normed.shape[1] // 4
+    aux_ref[...] = jnp.sum(share, axis=1, keepdims=True) * (experts / (valid_total * valid_total))
+    hot = (sublanes((table_ref.shape[1], buckets.shape[1])) == buckets[...]).astype(f32)
+    table_ref[...] = mm(unfold_lanes(small[16:32], 2), hot, nt, highest)[: table_ref.shape[0]]
+    router_ref[...] = unfold_lanes(small[32 : 32 + 6 * experts], 6)
 
 
 def few_experts():
@@ -445,6 +466,7 @@
     capacity = max(2, (4 * tok + 3 * experts - 1) // (3 * experts))
     slots = -(-(capacity + 1) // 8) * 8
     total = experts * slots
+    small_rows = 6 * experts + 32 + (48 if few_experts() else 0)
     valid_total = 3 * tok * groups // 4
     scale = head_size ** (-0.5)
     joined = few_experts()
@@ -458,47 +480,51 @@
     space = jnp.zeros((64,), bf16)
     gains = jnp.concatenate([gain_attn, space, gain_ffn, space, jnp.zeros((1536,), bf16)]).reshape(16, 128)
     packed = lax.all_gather(jnp.concatenate([inputs.T, out_grad.T, gains], axis=0), "head")
-    w_output_full = lax.all_gather(w_output, "head", tiled=True)
     if joined:
         all_in = lax.all_gather(inputs.T, ("expert", "head")).reshape(groups, heads, col, tok)
-    qkv, weights, attended = call(
+    qkv, weights, attended, branch = call(
         functools.partial(attend_kernel, scale),
-        [((3, col, tok), bf16, 1), ((heads_here, tok, tok), f32, 1), ((col, tok), bf16)],
-        scalars, packed, far(wq), far(wk), far(wv), far(buckets_row), far(bias_table.T),
-    )
-
-    attended_parts = lax.all_gather(attended, "head")
-    residual, side, send = call(
+        [
+            ((3, col, tok), bf16, 1), ((heads_here, tok, tok), f32, 1), ((col, tok), bf16, 1),
+            ((heads, col, tok), bf16),
+        ],
+        scalars, packed, far(wq), far(wk), far(wv), far(w_output), far(buckets_row), far(bias_table.T),
+    )
+
+    branch = lax.all_to_all(branch, "head", split_axis=0, concat_axis=0, tiled=True)
+    residual, low, side, send = call(
         functools.partial(route_kernel, capacity),
-        [((heads, col, tok), f32, 1), ((8, tok), f32, 1), ((experts, slots, 2 * width), bf16)],
-        scalars, packed, attended_parts, far(w_output_full), far(routes_row), far(router_rows),
-    )
-    rows = lax.all_to_all(send, "expert", split_axis=0, concat_axis=0, tiled=True)
-    rows = rows.reshape(total, 2 * width)
-
-    back, part, hidden, before_grad, back_rows = call(
+        [((col, tok), f32, 1), ((col, tok), bf16, 1), ((8, tok), f32, 1), ((experts, slots, 2 * col), bf16)],
+        scalars, branch, far(inputs.T), far(out_grad.T), far(routes_row),
+    )
+    quarter = lax.all_to_all(send, "expert", split_axis=0, concat_axis=0, tiled=True)
+    quarters = lax.all_gather(quarter.reshape(total, 2 * col), "head")
+
+    back, part, hidden, before_grad, back_rows, rows = call(
         functools.partial(expert_kernel, capacity),
         [((experts * heads, slots, 256), bf16), ((heads, total * 3 // 2, 128), bf16, 1)]
-        + [((total, width), bf16, 1)] * 3,
-        scalars, rows, far(w_in), far(w_out), far(router_rows),
+        + [((total, width), bf16, 1)] * 4,
+        scalars, quarters, far(packed), far(w_in), far(w_out), far(router_rows),
     )
     came = lax.all_to_all(back, ("expert", "head"), split_axis=0, concat_axis=0, tiled=True)
     grad_own, gate_grad, stats = call(
         collect_kernel,
-        [((col, tok), bf16), ((8, tok), f32, 1), ((experts, 128), f32, 1)],
-        came, far(side),
+        [((2 * col, tok), bf16), ((8, tok), f32, 1), ((experts, 128), f32, 1)],
+        came, far(side), far(low),
     )
     expert_grad = lax.all_gather(grad_own, "head")
 
-    late, first, residual_grad_own, small, product = call(
+    late, first, residual_grad_own, small, product, gate = call(
         functools.partial(backward_kernel, scale, valid_total),
         [
             ((3 * col, tok), bf16, 1), ((heads, col + 16 + total * 3 // 2, 128), bf16), ((col, tok), f32, 1),
-            ((6 * experts + 32, 128), f32, 1),
+            ((small_rows, 128), f32, 1),
             ((groups, col // groups * 6, 128), bf16, 1) if joined else ((1, col, width), f32, 1),
+            ((8, tok), f32, 1),
         ],
-        scalars, packed, expert_grad, far(gate_grad), far(stats), far(residual), far(routes_row),
-        far(router_rows), far(w_output), far(weights), far(qkv), far(wq), far(wk), far(wv), far(attended), far(part),
+        scalars, far(packed), expert_grad, far(gate_grad), far(stats), far(routes_row),
+        far(router_rows), far(w_output), far(weights), far(qkv), far(wq), far(wk), far(wv), far(attended),
+        far(part),
     )
 
     if joined:
@@ -508,28 +534,30 @@
     ret, sums, input_grad = call(
         first_kernel,
         [
-            ((experts, 2 * slots + (6 * experts + 32 + product.shape[1] if joined else 0), 128), bf16),
-            ((6 * experts + 32, 128), f32, 1), ((col, tok), f32),
+            ((experts, 2 * slots + (small_rows // experts + product.shape[1] if joined else 0), 128), bf16),
+            ((small_rows, 128), f32, 1), ((col, tok), f32, 1),
         ],
         scalars, first, far(packed), far(residual_grad_own), far(small), *([far(product)] if joined else []),
     )
     ret = lax.all_to_all(ret, "expert", split_axis=0, concat_axis=0, tiled=True)
     out = call(
         functools.partial(last_kernel, slots),
-        [((col, tok), bf16), ((1, 1), f32)]
-        + ([((experts, width), f32), ((heads_here, bucket_count), f32), ((8, 256), f32), (product.shape, bf16)] if joined else []),
-        scalars, ret, far(side), far(residual), far(stats), far(buckets_row),
-    )
-    block_out, aux_loss = out[:2]
+        [((col, tok), bf16)]
+        + ([((groups, small_rows // groups + product.shape[1], 128), bf16)] if joined else []),
+        ret, far(side), far(gate), far(residual),
+    )
+    block_out = out[0]
     in_weight_grad, out_weight_grad = call(
-        weights_kernel, [((width, width), f32)] * 2, far(rows), far(hidden), far(before_grad), far(back_rows)
+        weights_kernel, [((width, width), f32, 1)] * 2, far(rows), far(hidden), far(before_grad), far(back_rows)
     )
     if joined:
-        router_grad, table_grad, gain_grads, share = out[2:]
-        shares = lax.all_to_all(share, "expert", split_axis=0, concat_axis=0, tiled=True)
+        shares = lax.all_to_all(out[1], "expert", split_axis=0, concat_axis=0, tiled=True)
         normed_all = call(turn_kernel, [((width, groups * tok), bf16, 1)], far(all_in), far(packed))[0]
-        q_grad, k_grad, v_grad, output_grad = call(
-            products_kernel, [((col, width), f32, 1)] * 4, far(late_all), far(normed_all), shares
+        q_grad, k_grad, v_grad, output_grad, router_grad, table_grad, gain_grads, aux_loss = call(
+            products_kernel,
+            [((col, width), f32, 1)] * 4
+            + [((experts, width), f32), ((heads_here, bucket_count), f32), ((8, 256), f32), ((1, 1), f32)],
+            far(late_all), far(normed_all), shares, far(buckets_row), far(stats),
         )
     else:
         gain = packed[:, 2 * col : 2 * col + 2].reshape(heads, 256)[:, :col].reshape(width, 1)
@@ -537,12 +565,13 @@
         normed = (x * token_scale(x) * gain.astype(f32)).astype(bf16)
         products = [mm(late[i * col : (i + 1) * col], normed, nt) for i in range(3)]
         q_grad, k_grad, v_grad, sums, output_grad = lax.psum(products + [sums, product[0]], "expert")
-        wide = 6 * experts
-        router_grad = unfold_lanes(sums[:wide], 6)
-        offsets = unfold_lanes(sums[wide : wide + 16], 2)[:heads_here, : 2 * tok - 1]
+        router_grad = unfold_lanes(sums[32 : 32 + 6 * experts], 6)
+        offsets = unfold_lanes(sums[16:32], 2)[:heads_here, : 2 * tok - 1]
         hot = (buckets[None, :] == jnp.arange(bucket_count)[:, None]).astype(f32)
         table_grad = mm(offsets, hot, nt, highest)
-        gain_grads = unfold_lanes(sums[wide + 16 :], 2)
+        gain_grads = unfold_lanes(sums[:16], 2)
+        probs = gain_grads[2, :experts] + gain_grads[3, :experts]
+        aux_loss = experts * jnp.sum(stats[:, 0] * probs) / (valid_total * valid_total)
     return (
         block_out.T,
         input_grad.T,

time: 152 us -> 147 us (0.967)
  waiting for transfers between devices: 5.67 us -> 2.72 us
    all_to_all x1, blocking collectives: 23.4 us -> 13.3 us  [shards(): lax.all_to_all(send, 'expert', split_axis=0, concat_axis=0, tiled=True)]
    all_to_all x0 -> x1, blocking collectives: none -> 7.69 us  [shards(): lax.all_to_all(branch, 'head', split_axis=0, concat_axis=0, tiled=True)]
    all_to_all x1, waiting for transfers between devices: 4.27 us -> 2.02 us  [shards(): lax.all_to_all(out[1], 'expert', split_axis=0, concat_axis=0, tiled=True)]
  transfers between devices with their start and end apart: 4 -> 3, of which waited for: 1 -> 1; matrix products, arithmetic and copies ran while one was open for 3% -> 2% of each run, Pallas kernels for 19% -> 19%
where the time goes in v6:
time: 147 us; the launch traced here: 146 us
  blocking collectives  89 us (61%)
  Pallas kernels  32 us (22%)
  between operations  14.7 us (10%)
  starting transfers between devices  3.56 us (2%)
  local copies, waits for them, and re-layouts  3.23 us (2%)
  waiting for transfers between devices  2.72 us (2%)
    pallas_call x10, Pallas kernels, call(): pl.pallas_call(body, out_shape=shapes, in_specs=in_specs, compiler_params...  32 us
    all_to_all x1, blocking collectives, shards(): ret = lax.all_to_all(ret, 'expert', split_axis=0, concat_axis=0, tiled=True)  19 us
    all_to_all x1, blocking collectives, shards(): lax.all_to_all(back, ('expert', 'head'), split_axis=0, concat_axis=0, til...  17 us
    all_to_all x1, blocking collectives, shards(): lax.all_to_all(send, 'expert', split_axis=0, concat_axis=0, tiled=True)  13.3 us
    all_to_all x1, blocking collectives, shards(): lax.all_to_all(first, 'head', split_axis=0, concat_axis=0, tiled=True)  11.1 us
    all_gather x1, blocking collectives, shards(): lax.all_gather(jnp.concatenate([inputs.T, out_grad.T, gains], axis=0), 'h...  8.01 us
    all_to_all x1, blocking collectives, shards(): lax.all_to_all(branch, 'head', split_axis=0, concat_axis=0, tiled=True)  7.69 us
    all_gather x1, blocking collectives, shards(): quarters = lax.all_gather(quarter.reshape(total, 2 * col), 'head')  6.68 us
  transfers between devices with their start and end apart: 3, of which 1 were waited for; matrix products, arithmetic and copies ran while one was open for 2% of the time, Pallas kernels for 19%

profile of v6, /device:TPU:0, one launch (start us, length us, event | category | flops | bytes accessed | tf_op | source)
XLA Modules:
  0.0 146.2 jit_solution(5537251305467187701)
XLA Ops:
  7.2 0.0 all-gather.9.cloned.1.call-start
  7.2 0.7 all-gather.9.cloned.1.call-update
  7.9 0.0 all-gather.7.cloned.1.call-start
  8.6 1.2 pad.4
  9.9 1.4 concatenate.6
  11.3 0.1 pad_add_fusion.scalars
  11.3 0.8 pad_maximum_fusion
  12.2 8.0 %all-gather = bf16[1600,128]{1,0:T(8,128)(2,1)S(1)} all-gather(bf16[400,128]{1,0:T(8,128)(2,1)S(1)} %pad_maximum_fusion), channel_id=2, replica_groups=mesh['expert'=8,'head'=4] {'head'}, dimensions={0}, use_global_device_ids=true | all-gather | bytes 512000 | tf_op jit(solution)/shard_map/all_gather | solution.py:482
  20.2 0.0 copy-start
  20.2 3.5 %shard_map.246 = (bf16[3,192,128]{2,1,0:T(8,128)(2,1)}, f32[3,128,128]{2,1,0:T(8,128)}, bf16[192,128]{1,0:T(8,128)(2,1)}, bf16[4,192,128]{2,1,0:T(8,128)(2,1)S(1)}) custom-call(s32[3]{0:T(128)S(1)} %pad_add_fusion.scalars, bf16[4,400,128]{2,1,0:T(8,128)(2,1)S(1)} %bitcast.31, bf16[192,768]{1,0:T(8,128)(2,1)} %bitcast.38, bf16[192,768]{1,0:T(8,128)(2,1)} %bitcast.40, ...), custom_call_target="tpu_custom_call" | custom-call | tf_op jit(solution)/shard_map/pallas_call | solution.py:31
  23.7 7.7 %all_to_all.30.came = bf16[4,192,128]{2,1,0:T(8,128)(2,1)S(1)} all-to-all(bf16[4,192,128]{2,1,0:T(8,128)(2,1)S(1)} %get-tuple-element.50), channel_id=1, replica_groups=mesh['expert'=8,'head'=4] {'head'}, dimensions={0} | all-to-all | bytes 393216 | tf_op jit(solution)/shard_map/all_to_all | solution.py:494
  31.4 1.6 %shard_map.247 = (f32[192,128]{1,0:T(8,128)}, bf16[192,128]{1,0:T(8,128)(2,1)}, f32[8,128]{1,0:T(8,128)}, bf16[8,24,384]{2,1,0:T(8,128)(2,1)S(1)}) custom-call(s32[3]{0:T(128)S(1)} %pad_add_fusion.scalars, bf16[4,192,128]{2,1,0:T(8,128)(2,1)S(1)} %all_to_all.30.came, bf16[192,128]{1,0:T(8,128)(2,1)} %bitcast.50, bf16[192,128]{1,0:T(8,128)(2,1)} %bitcast.52, ...), custom_call_target="tpu_custom_call" | custom-call | tf_op jit(solution)/shard_map/pallas_call | solution.py:31
  33.0 13.3 %all_to_all.31 = bf16[8,24,384]{2,1,0:T(8,128)(2,1)S(1)} all-to-all(bf16[8,24,384]{2,1,0:T(8,128)(2,1)S(1)} %get-tuple-element.51), channel_id=1, replica_groups=mesh['expert'=8,'head'=4] {'expert'}, dimensions={0} | all-to-all | bytes 294912 | tf_op jit(solution)/shard_map/all_to_all | solution.py:500
  46.3 6.7 %all_gather.29.quarters = bf16[4,192,384]{2,1,0:T(8,128)(2,1)S(1)} all-gather(bf16[1,192,384]{2,1,0:T(8,128)(2,1)S(1)} %bitcast.47), channel_id=1, replica_groups=mesh['expert'=8,'head'=4] {'head'}, dimensions={0}, use_global_device_ids=true | all-gather | bytes 737280 | tf_op jit(solution)/shard_map/all_gather | solution.py:501
  53.0 0.0 copy-done
  53.0 4.4 %shard_map.248 = (bf16[32,24,256]{2,1,0:T(8,128)(2,1)S(1)}, bf16[4,288,128]{2,1,0:T(8,128)(2,1)}, bf16[192,768]{1,0:T(8,128)(2,1)}, bf16[192,768]{1,0:T(8,128)(2...) custom-call(s32[3]{0:T(128)S(1)} %pad_add_fusion.scalars, bf16[4,192,384]{2,1,0:T(8,128)(2,1)S(1)} %all_gather.29.quarters, ...), custom_call_target="tpu_custom_call" | custom-call | tf_op jit(solution)/shard_map/pallas_call | solution.py:31
  57.4 17.0 %all_to_all.32.came = bf16[32,24,256]{2,1,0:T(8,128)(2,1)S(1)} all-to-all(bf16[32,24,256]{2,1,0:T(8,128)(2,1)S(1)} %get-tuple-element.52), channel_id=1, replica_groups=mesh['expert'=8,'head'=4] {'expert','head'}, dimensions={0} | all-to-all | bytes 786432 | tf_op jit(solution)/shard_map/all_to_all | solution.py:509
  74.5 1.8 %shard_map.249 = (bf16[384,128]{1,0:T(8,128)(2,1)S(1)}, f32[8,128]{1,0:T(8,128)}, f32[8,128]{1,0:T(8,128)}) custom-call(bf16[32,24,256]{2,1,0:T(8,128)(2,1)S(1)} %all_to_all.32.came, f32[8,128]{1,0:T(8,128)} %get-tuple-element.53.side, bf16[192,128]{1,0:T(8,128)(2,1)} %get-tuple-element.54.low), custom_call_target="tpu_custom_call" | custom-call | tf_op jit(solution)/shard_map/pallas_call | solution.py:31
  76.2 6.2 %all-gather.1 = bf16[1536,128]{1,0:T(8,128)(2,1)S(1)} all-gather(bf16[384,128]{1,0:T(8,128)(2,1)S(1)} %get-tuple-element.55), channel_id=3, replica_groups=mesh['expert'=8,'head'=4] {'head'}, dimensions={0}, use_global_device_ids=true | all-gather | bytes 491520 | tf_op jit(solution)/shard_map/all_gather | solution.py:515
  82.5 4.8 %shard_map.250 = (bf16[576,128]{1,0:T(8,128)(2,1)}, bf16[4,496,128]{2,1,0:T(8,128)(2,1)S(1)}, f32[192,128]{1,0:T(8,128)}, f32[128,128]{1,0:T(8,128)}, bf16[8,144,128]{2,1,0:T(8,128)(2,1)}, /*index=5*/f32[8,128]{1,0:T(8,128)}) custom-call(s32[3]{0:T(128)S(1)} %pad_add_fusion.scalars, bf16[4,400,128]{2,1,0:T(8,128)(2,1)} %bitcast.33, ...), custom_call_target="tpu_custom_call" | custom-call | tf_op jit(solution)/shard_map/pallas_call | solution.py:31
  87.3 0.0 all-gather.7.cloned.1.call-update
  87.3 11.1 %all_to_all.33.came = bf16[4,496,128]{2,1,0:T(8,128)(2,1)S(1)} all-to-all(bf16[4,496,128]{2,1,0:T(8,128)(2,1)S(1)} %get-tuple-element.62), channel_id=1, replica_groups=mesh['expert'=8,'head'=4] {'head'}, dimensions={0} | all-to-all | bytes 1015808 | tf_op jit(solution)/shard_map/all_to_all | solution.py:533
  98.4 2.2 %shard_map.251 = (bf16[8,208,128]{2,1,0:T(8,128)(2,1)S(1)}, f32[128,128]{1,0:T(8,128)}, f32[192,128]{1,0:T(8,128)}) custom-call(s32[3]{0:T(128)S(1)} %pad_add_fusion.scalars, bf16[4,496,128]{2,1,0:T(8,128)(2,1)S(1)} %all_to_all.33.came, bf16[4,400,128]{2,1,0:T(8,128)(2,1)} %bitcast.34, f32[192,128]{1,0:T(8,128)} %get-tuple-element.63.own, ...), custom_call_target="tpu_custom_call" | custom-call | tf_op jit(solution)/shard_map/pallas_call | solution.py:31
  100.6 19.0 %all_to_all.34.came = bf16[8,208,128]{2,1,0:T(8,128)(2,1)S(1)} all-to-all(bf16[8,208,128]{2,1,0:T(8,128)(2,1)S(1)} %get-tuple-element.66), channel_id=1, replica_groups=mesh['expert'=8,'head'=4] {'expert'}, dimensions={0} | all-to-all | bytes 851968 | tf_op jit(solution)/shard_map/all_to_all | solution.py:542
  119.5 1.9 %shard_map.252 = (bf16[192,128]{1,0:T(8,128)(2,1)}, bf16[8,160,128]{2,1,0:T(8,128)(2,1)}) custom-call(bf16[8,208,128]{2,1,0:T(8,128)(2,1)S(1)} %all_to_all.34.came, f32[8,128]{1,0:T(8,128)} %get-tuple-element.53.side, f32[8,128]{1,0:T(8,128)} %get-tuple-element.67.gate, f32[192,128]{1,0:T(8,128)} %get-tuple-element.68.residual), custom_call_target="tpu_custom_call" | custom-call | tf_op jit(solution)/shard_map/pallas_call | solution.py:31
  121.4 3.5 %all-to-all-start.5 = ((bf16[8,160,128]{2,1,0:T(8,128)(2,1)}), bf16[8,160,128]{2,1,0:T(8,128)(2,1)S(1)}, u32[]{:S(2)}, u32[]{:S(2)}) async-start(bf16[8,160,128]{2,1,0:T(8,128)(2,1)} %get-tuple-element.72), calls=%async_computation.5 | async-start | bytes 655360 | tf_op jit(solution)/shard_map/all_to_all | solution.py:554
  124.9 4.0 %shard_map.255 = (f32[768,768]{1,0:T(8,128)}, f32[768,768]{1,0:T(8,128)}) custom-call(bf16[192,768]{1,0:T(8,128)(2,1)} %get-tuple-element.81.rows_ref, bf16[192,768]{1,0:T(8,128)(2,1)} %get-tuple-element.82.hidden, bf16[192,768]{1,0:T(8,128)(2,1)} %get-tuple-element.83.before, bf16[192,768]{1,0:T(8,128)(2,1)} %get-tuple-element.84.grads), custom_call_target="tpu_custom_call" | custom-call | tf_op jit(solution)/shard_map/pallas_call | solution.py:31
  128.9 0.0 all-gather.9.cloned.1.call-done
  128.9 3.4 %shard_map.253.normed = bf16[768,1024]{1,0:T(8,128)(2,1)} custom-call(bf16[8,4,192,128]{3,2,1,0:T(8,128)(2,1)} %bitcast.37, bf16[4,400,128]{2,1,0:T(8,128)(2,1)} %bitcast.35), custom_call_target="tpu_custom_call" | custom-call | tf_op jit(solution)/shard_map/pallas_call | solution.py:31
  132.3 2.0 %all-to-all-done.5.shares = bf16[8,160,128]{2,1,0:T(8,128)(2,1)S(1)} async-done(((bf16[8,160,128]{2,1,0:T(8,128)(2,1)}), bf16[8,160,128]{2,1,0:T(8,128)(2,1)S(1)}, u32[]{:S(2)}, u32[]{:S(2)}) %all-to-all-start.5) | async-done | bytes 327712 | tf_op jit(solution)/shard_map/all_to_all | solution.py:554
  134.3 0.0 all-gather.7.cloned.1.call-done
  134.3 4.5 %shard_map.254 = (f32[192,768]{1,0:T(8,128)}, f32[192,768]{1,0:T(8,128)}, f32[192,768]{1,0:T(8,128)}, f32[192,768]{1,0:T(8,128)}, f32[8,768]{1,0:T(8,128)}, /*in...) custom-call(bf16[8,576,128]{2,1,0:T(8,128)(2,1)} %bitcast.46, bf16[768,1024]{1,0:T(8,128)(2,1)} %shard_map.253.normed, ...), custom_call_target="tpu_custom_call" | custom-call | tf_op jit(solution)/shard_map/pallas_call | solution.py:31
  138.7 0.6 fusion
  (2 shorter events, 0.0 us)
Async XLA Ops:
  7.2 121.7 %all-gather.9.cloned.1.call-start = ((), (), s32[]{:S(2)}) async-start(), calls=%async_computation.7 | async-start | bytes 1622016 | tf_op jit(solution)/shard_map/all_gather | solution.py:484
  7.9 126.4 %all-gather.7.cloned.1.call-start = ((), (), s32[]{:S(2)}) async-start(), calls=%async_computation.6 | async-start | bytes 1327104 | tf_op jit(solution)/shard_map/all_gather | solution.py:531
  20.2 32.8 %copy-start = (bf16[1600,128]{1,0:T(8,128)(2,1)}, bf16[1600,128]{1,0:T(8,128)(2,1)S(1)}, u32[]{:S(2)}) copy-start(bf16[1600,128]{1,0:T(8,128)(2,1)S(1)} %all-gather) | copy-start | bytes 1228804
  121.4 12.9 %all-to-all-start.5 = ((bf16[8,160,128]{2,1,0:T(8,128)(2,1)}), bf16[8,160,128]{2,1,0:T(8,128)(2,1)S(1)}, u32[]{:S(2)}, u32[]{:S(2)}) async-start(bf16[8,160,128]{2,1,0:T(8,128)(2,1)} %get-tuple-element.72), calls=%async_computation.5 | async-start | bytes 655360 | tf_op jit(solution)/shard_map/all_to_all | solution.py:554
Sparse Core Ops, SparseCore 0:
  10.9 60.0 all-gather.8
  87.4 40.6 all-gather.6

commit v7 on v6

--- a/solution.py
+++ b/solution.py
@@ -111,6 +111,33 @@
 def unfold_lanes(rows, pieces):
     size = rows.shape[0] // pieces
     return jnp.concatenate([rows[i * size : (i + 1) * size] for i in range(pieces)], axis=1)
+
+
+def fold_rest(rest, side):
+    groups = [rest[i : i + 8] for i in range(0, rest.shape[0], 8)]
+    count = side.shape[1]
+    spot = lanes((8, 64))
+    last = jnp.zeros((8, 64), f32)
+    for g in range(len(groups)):
+        for j in range(count):
+            last = jnp.where(spot == g * count + j, side[8 * g : 8 * g + 8, j : j + 1], last)
+    groups.append(last)
+    if len(groups) % 2:
+        groups.append(jnp.zeros((8, 64), f32))
+    return [jnp.concatenate(groups[i : i + 2], axis=1) for i in range(0, len(groups), 2)]
+
+
+def unfold_rest(blocks, slots, count):
+    halves = []
+    for i in range(0, blocks.shape[0], 8):
+        halves += [blocks[i : i + 8, :64], blocks[i : i + 8, 64:]]
+    number = slots // 8
+    side = [halves[number][:, g * count : (g + 1) * count] for g in range(number)]
+    return jnp.concatenate(halves[:number], axis=0), jnp.concatenate(side, axis=0)
+
+
+def folded_rows(slots):
+    return slots + 8 * ((slots // 8 + 2) // 2)
 
 
 def pick_slots(spots, count):
@@ -131,8 +158,9 @@
         qkv_ref[i] = rows
         projected.append(rows)
     query, key, value = projected
-    hot = (sublanes((table.shape[1], 2 * tok)) == buckets[...]).astype(f32)
+    hot = (sublanes((table.shape[1], 2 * tok - 1)) == buckets[...]).astype(f32)
     offsets = mm(table[...], hot, precision=highest)
+    offsets = jnp.concatenate([offsets, jnp.zeros((heads, 1), f32)], axis=1)
     open_keys = lanes((tok, tok)) < scalars[0]
     outs = []
     for h in range(heads):
@@ -226,12 +254,13 @@
     stats = jnp.zeros((1, 128), f32)
     for b in range(experts):
         stats = stats + grads[b * slots + capacity : b * slots + capacity + 1, :128]
-    side = side_lanes(total, 256 - col, high_low(gate_grad) + high_low(stats[:, 0:1]))
+    side = side_lanes(total, 4, high_low(gate_grad) + high_low(stats[:, 0:1]))
     for b in range(experts):
         at = slice(b * slots, (b + 1) * slots)
         for i in range(heads):
+            mine = rows_grad[at, i * col : (i + 1) * col]
             back_ref[b * heads + i] = jnp.concatenate(
-                [rows_grad[at, i * col : (i + 1) * col], side[at]], axis=1
+                [mine[:, :128]] + fold_rest(mine[:, 128:], side[at]), axis=0
             ).astype(bf16)
 
 
@@ -240,31 +269,33 @@
     out_ref[...] = mm(hidden[...], grads[...], tn)
 
 
-def collect_kernel(came, side, low, grad_ref, gate_ref, stats_ref):
+def collect_kernel(slots, came, side, low, grad_ref, gate_ref, stats_ref):
     col, tok = low.shape
     experts = stats_ref.shape[0]
-    sources, slots, _ = came.shape
-    heads = sources // experts
-    sums = []
+    heads = came.shape[0] // experts
+    tops, rests, scalars = [], [], []
     for e in range(experts):
         total = came[e * heads].astype(f32)
         for i in range(1, heads):
             total = total + came[e * heads + i].astype(f32)
-        sums.append(total)
-    stats = jnp.concatenate([total[0:1, col:] for total in sums], axis=0) * (1.0 / heads)
-    sums = jnp.concatenate(sums, axis=0)
+        rest, columns = unfold_rest(total[slots:], slots, 4)
+        tops.append(total[:slots])
+        rests.append(rest)
+        scalars.append(columns)
+    counts = jnp.concatenate([columns[0:1] for columns in scalars], axis=0) * (1.0 / heads)
     pick = pick_slots(side[0:1, :].astype(jnp.int32), experts * slots)
-    grad_ref[:col, :] = mm(sums[:, :col].astype(bf16), pick.astype(bf16), tn).astype(bf16)
+    for first, pieces in ((0, tops), (128, rests)):
+        block = jnp.concatenate(pieces, axis=0).astype(bf16)
+        grad_ref[first : min(first + 128, col), :] = mm(block, pick.astype(bf16), tn).astype(bf16)
     grad_ref[col:, :] = low[...]
-    gate = mm(sums[:, col:], pick.astype(f32), tn, highest)
+    gate = mm(jnp.concatenate(scalars, axis=0), pick.astype(f32), tn, highest)
     gate_ref[...] = jnp.broadcast_to(gate[0:1] + gate[1:2], gate_ref.shape)
-    count = stats[:, 2:3] + stats[:, 3:4]
-    stats_ref[...] = side_lanes(experts, 128, [count])
+    stats_ref[...] = side_lanes(experts, 128, [counts[:, 2:3] + counts[:, 3:4]])
 
 
 def backward_kernel(
     scale, valid_total, scalars, packed, expert_grad, gate_grad, stats, routes, w_router, w_output, weights_ref,
-    qkv, wq, wk, wv, attended, part, late_ref, first_ref, own_ref, small_ref, product_ref, gate_ref,
+    qkv, wq, wk, wv, attended, part, late_ref, first_ref, own_ref, gate_ref, *share_refs,
 ):
     tok = routes.shape[1]
     heads_here = weights_ref.shape[0]
@@ -319,10 +350,6 @@
         first_ref[i, col + 16 :, :] = part[i]
 
     product = mm(attended[...], branch, nt)
-    pieces = product_ref.shape[0]
-    for b in range(pieces):
-        at = slice(b * (col // pieces), (b + 1) * (col // pieces))
-        product_ref[b] = (product if pieces == 1 else fold_lanes(product[at])).astype(product_ref.dtype)
     gain_two_grad = jnp.sum(normed_grad * unit, axis=1, keepdims=True)
     gains = jnp.zeros((col, 1), f32)
     own = jnp.zeros((col, tok), f32)
@@ -334,20 +361,29 @@
     probs = jnp.sum(router * valid, axis=1, keepdims=True)
     if experts < col:
         probs = jnp.concatenate([probs, jnp.zeros((col - experts, 1), f32)], axis=0)
-    gains = jnp.transpose(side_lanes(col, 128, [gains, jnp.zeros_like(gains)] + high_low(probs)))[0:8]
+    gains = jnp.transpose(side_lanes(col, 128, [gains] + high_low(probs)))[0:8]
     router_grad = mm(logit_grad, normed, nt)
     offsets = jnp.concatenate(offsets, axis=0)
     offsets = jnp.concatenate([offsets, jnp.zeros((8 - heads_here, 2 * tok), f32)], axis=0)
     gains = jnp.concatenate([gains, jnp.zeros((8, 64), f32)], axis=1)
     pieces = [fold_lanes(gains), fold_lanes(offsets), fold_lanes(router_grad)]
-    spare = small_ref.shape[0] - 6 * experts - 32
-    if spare:
-        pieces.append(jnp.zeros((spare, 128), f32))
-    small_ref[...] = jnp.concatenate(pieces, axis=0)
-
-
-def first_kernel(scalars, came, packed, own, small, *refs):
-    product, (ret_ref, sums_ref, input_ref) = refs[:-3], refs[-3:]
+    if len(share_refs) == 2:
+        share_refs[0][...] = jnp.concatenate(pieces, axis=0)
+        share_refs[1][...] = product
+    else:
+        share_ref = share_refs[0]
+        groups = share_ref.shape[0]
+        size = col // groups
+        chunk = share_ref.shape[1] - 6 * size
+        small = jnp.concatenate(pieces + [jnp.zeros((groups * chunk - 6 * experts - 32, 128), f32)], axis=0)
+        for b in range(groups):
+            share_ref[b] = jnp.concatenate(
+                [small[b * chunk : (b + 1) * chunk], fold_lanes(product[b * size : (b + 1) * size])], axis=0
+            ).astype(bf16)
+
+
+def first_kernel(scalars, came, packed, own, *refs):
+    shares, (ret_ref, gain_ref, input_ref) = refs[:-3], refs[-3:]
     col, tok = own.shape
     heads = came.shape[0]
     experts = ret_ref.shape[0]
@@ -361,42 +397,38 @@
     gain = gain_columns(mine[2 * col : 2 * col + 16])[0]
     input_ref[...] = own[...] + scale * (total[:col] * gain - unit * mean)
     gain_grad = jnp.sum(total[:col] * unit, axis=1, keepdims=True)
-    gain_grad = jnp.transpose(side_lanes(col, 128, [jnp.zeros_like(gain_grad), gain_grad]))[0:8]
-    gain_grad = jnp.concatenate([gain_grad, jnp.zeros((8, 64), f32)], axis=1)
-    sums = jnp.concatenate([small[:16, :] + fold_lanes(gain_grad), small[16:, :]], axis=0)
-    sums_ref[...] = sums
+    gain_grad = jnp.transpose(side_lanes(col, 128, [gain_grad]))[0:8]
+    gain_grad = fold_lanes(jnp.concatenate([gain_grad, jnp.zeros((8, 64), f32)], axis=1))
+    gain_ref[...] = gain_grad
     produced = total[col + 16 :]
     count = produced.shape[0] * 2 // 3
-    half = count // 2
     top = produced[:count]
     rest = jnp.concatenate([produced[count:, :64], produced[count:, 64:]], axis=0)
     rest = jnp.concatenate([rest, jnp.zeros((count, 64), f32)], axis=1)
     slots = count // experts
+    joined = []
+    if shares:
+        share = shares[0][0].astype(f32)
+        for e in range(1, experts):
+            share = share + shares[0][e].astype(f32)
+        joined = [gain_grad, share]
     for e in range(experts):
         at = slice(e * slots, (e + 1) * slots)
-        pieces = [top[at], rest[at]]
-        if product:
-            chunk = sums.shape[0] // experts
-            pieces += [sums[e * chunk : (e + 1) * chunk], product[0][e].astype(f32)]
-        ret_ref[e] = jnp.concatenate(pieces, axis=0).astype(bf16)
-
-
-def last_kernel(slots, came, side, gate, residual, *refs):
-    block_ref, refs = refs[0], refs[1:]
-    experts = came.shape[0]
-    col, tok = residual.shape
-    blocks = [came[e].astype(f32) for e in range(experts)]
+        ret_ref[e] = jnp.concatenate([top[at], rest[at]] + joined, axis=0).astype(bf16)
+
+
+def add_returned(slots, blocks, side, gate, residual):
+    col = residual.shape[0]
     top = jnp.concatenate([block[:slots] for block in blocks], axis=0).astype(bf16)
     rest = jnp.concatenate([block[slots : 2 * slots] for block in blocks], axis=0).astype(bf16)
-    pick = pick_slots(side[0:1, :].astype(jnp.int32), experts * slots).astype(bf16)
+    pick = pick_slots(side[0:1, :].astype(jnp.int32), len(blocks) * slots).astype(bf16)
     returned = jnp.concatenate([mm(top, pick, tn), mm(rest, pick, tn)[: col - 128]], axis=0)
-    block_ref[...] = (residual[...] + gate[0:1, :] * returned).astype(bf16)
-    if refs:
-        total = blocks[0][2 * slots :]
-        for block in blocks[1:]:
-            total = total + block[2 * slots :]
-        for e in range(experts):
-            refs[0][e] = total.astype(bf16)
+    return (residual[...] + gate[0:1, :] * returned).astype(bf16)
+
+
+def last_kernel(slots, came, side, gate, residual, block_ref):
+    blocks = [came[e].astype(f32) for e in range(came.shape[0])]
+    block_ref[...] = add_returned(slots, blocks, side, gate, residual)
 
 
 def turn_kernel(all_in, packed, normed_ref):
@@ -404,33 +436,43 @@
     gain = all_gains(packed)[0]
     for b in range(groups):
         x = jnp.concatenate([all_in[b, i].astype(f32) for i in range(heads)], axis=0)
-        normed_ref[:, b * tok : (b + 1) * tok] = (x * token_scale(x) * gain).astype(bf16)
+        normed_ref[b * tok : (b + 1) * tok, :] = jnp.transpose(x * token_scale(x) * gain).astype(bf16)
 
 
 def products_kernel(
-    late, normed, shares, buckets, stats, q_ref, k_ref, v_ref, out_ref, router_ref, table_ref, gains_ref, aux_ref
+    slots, late, normed, came, buckets, stats, side, gate, residual,
+    q_ref, k_ref, v_ref, out_ref, block_ref, router_ref, table_ref, gains_ref, aux_ref,
 ):
-    groups = shares.shape[0]
+    groups = came.shape[0]
     col = q_ref.shape[0]
     experts = router_ref.shape[0]
     size = col // groups
-    blocks = [shares[b].astype(f32) for b in range(groups)]
-    chunk = blocks[0].shape[0] - 6 * size
+    blocks = [came[b].astype(f32) for b in range(groups)]
+    block_ref[...] = add_returned(slots, blocks, side, gate, residual)
+    gain_one = blocks[0][2 * slots : 2 * slots + 16]
+    for block in blocks[1:]:
+        gain_one = gain_one + block[2 * slots : 2 * slots + 16]
+    shares = [block[2 * slots + 16 :] for block in blocks]
+    chunk = shares[0].shape[0] - 6 * size
     for b in range(groups):
-        out_ref[b * size : (b + 1) * size, :] = unfold_lanes(blocks[b][chunk:], 6)
+        out_ref[b * size : (b + 1) * size, :] = unfold_lanes(shares[b][chunk:], 6)
     joined = jnp.concatenate([late[b] for b in range(groups)], axis=1)
+    product = mm(joined, normed[...])
     for i, ref in enumerate((q_ref, k_ref, v_ref)):
-        ref[...] = mm(joined[i * col : (i + 1) * col], normed[...], nt)
-    small = jnp.concatenate([block[:chunk] for block in blocks], axis=0)
+        ref[...] = product[i * col : (i + 1) * col]
+    small = jnp.concatenate([share[:chunk] for share in shares], axis=0)
     gains = unfold_lanes(small[:16], 2)
-    gains_ref[...] = gains
-    probs = gains[2:3, :experts] + gains[3:4, :experts]
+    gains_ref[0:8, :] = gains
+    gains_ref[8:16, :] = unfold_lanes(gain_one, 2)
+    probs = gains[1:2, :experts] + gains[2:3, :experts]
     same = lanes((experts, experts)) == sublanes((experts, experts))
     share = jnp.sum(jnp.where(same, stats[:, 0:1] * probs, 0.0), axis=0, keepdims=True)
-    valid_total = 3 * normed.shape[1] // 4
+    valid_total = 3 * normed.shape[0] // 4
     aux_ref[...] = jnp.sum(share, axis=1, keepdims=True) * (experts / (valid_total * valid_total))
-    hot = (sublanes((table_ref.shape[1], buckets.shape[1])) == buckets[...]).astype(f32)
-    table_ref[...] = mm(unfold_lanes(small[16:32], 2), hot, nt, highest)[: table_ref.shape[0]]
+    span = buckets.shape[1]
+    hot = (sublanes((table_ref.shape[1], span)) == buckets[...]).astype(f32)
+    offsets = unfold_lanes(small[16:32], 2)[:, :span]
+    table_ref[...] = mm(offsets, hot, nt, highest)[: table_ref.shape[0]]
     router_ref[...] = unfold_lanes(small[32 : 32 + 6 * experts], 6)
 
 
@@ -466,16 +508,17 @@
     capacity = max(2, (4 * tok + 3 * experts - 1) // (3 * experts))
     slots = -(-(capacity + 1) // 8) * 8
     total = experts * slots
-    small_rows = 6 * experts + 32 + (48 if few_experts() else 0)
     valid_total = 3 * tok * groups // 4
     scale = head_size ** (-0.5)
     joined = few_experts()
+    small_rows = 6 * experts + 32
+    chunk = -(-small_rows // (16 * groups)) * 16
     w_in, w_out = w_in[0], w_out[0]
     wq, wk, wv = w_query.T, w_key.T, w_value.T
     routes_row = routes.T
     router_rows = w_router.T
     scalars = jnp.stack([lengths[0], me_head.astype(jnp.int32), me_expert.astype(jnp.int32)])
-    buckets_row = jnp.pad(buckets, (0, 1), constant_values=-1)[None]
+    buckets_row = buckets[None]
 
     space = jnp.zeros((64,), bf16)
     gains = jnp.concatenate([gain_attn, space, gain_ffn, space, jnp.zeros((1536,), bf16)]).reshape(16, 128)
@@ -502,26 +545,29 @@
 
     back, part, hidden, before_grad, back_rows, rows = call(
         functools.partial(expert_kernel, capacity),
-        [((experts * heads, slots, 256), bf16), ((heads, total * 3 // 2, 128), bf16, 1)]
+        [((experts * heads, folded_rows(slots), 128), bf16), ((heads, total * 3 // 2, 128), bf16, 1)]
         + [((total, width), bf16, 1)] * 4,
         scalars, quarters, far(packed), far(w_in), far(w_out), far(router_rows),
     )
     came = lax.all_to_all(back, ("expert", "head"), split_axis=0, concat_axis=0, tiled=True)
     grad_own, gate_grad, stats = call(
-        collect_kernel,
+        functools.partial(collect_kernel, slots),
         [((2 * col, tok), bf16), ((8, tok), f32, 1), ((experts, 128), f32, 1)],
         came, far(side), far(low),
     )
     expert_grad = lax.all_gather(grad_own, "head")
 
-    late, first, residual_grad_own, small, product, gate = call(
+    late, first, residual_grad_own, gate, *shares = call(
         functools.partial(backward_kernel, scale, valid_total),
         [
             ((3 * col, tok), bf16, 1), ((heads, col + 16 + total * 3 // 2, 128), bf16), ((col, tok), f32, 1),
-            ((small_rows, 128), f32, 1),
-            ((groups, col // groups * 6, 128), bf16, 1) if joined else ((1, col, width), f32, 1),
             ((8, tok), f32, 1),
-        ],
+        ]
+        + (
+            [((groups, chunk + 6 * col // groups, 128), bf16)]
+            if joined
+            else [((small_rows, 128), f32, 1), ((col, width), f32, 1)]
+        ),
         scalars, far(packed), expert_grad, far(gate_grad), far(stats), far(routes_row),
         far(router_rows), far(w_output), far(weights), far(qkv), far(wq), far(wk), far(wv), far(attended),
         far(part),
@@ -530,53 +576,53 @@
     if joined:
         late_all = lax.all_gather(late, "expert")
 
+    if joined:
+        shares = [lax.all_to_all(shares[0], "expert", split_axis=0, concat_axis=0, tiled=True)]
     first = lax.all_to_all(first, "head", split_axis=0, concat_axis=0, tiled=True)
-    ret, sums, input_grad = call(
+    ret, gain_one_part, input_grad = call(
         first_kernel,
         [
-            ((experts, 2 * slots + (small_rows // experts + product.shape[1] if joined else 0), 128), bf16),
-            ((small_rows, 128), f32, 1), ((col, tok), f32, 1),
+            ((experts, 2 * slots + (16 + shares[0].shape[1] if joined else 0), 128), bf16),
+            ((16, 128), f32, 1), ((col, tok), f32, 1),
         ],
-        scalars, first, far(packed), far(residual_grad_own), far(small), *([far(product)] if joined else []),
+        scalars, first, far(packed), far(residual_grad_own), *(shares if joined else []),
     )
     ret = lax.all_to_all(ret, "expert", split_axis=0, concat_axis=0, tiled=True)
-    out = call(
-        functools.partial(last_kernel, slots),
-        [((col, tok), bf16)]
-        + ([((groups, small_rows // groups + product.shape[1], 128), bf16)] if joined else []),
-        ret, far(side), far(gate), far(residual),
-    )
-    block_out = out[0]
     in_weight_grad, out_weight_grad = call(
         weights_kernel, [((width, width), f32, 1)] * 2, far(rows), far(hidden), far(before_grad), far(back_rows)
     )
     if joined:
-        shares = lax.all_to_all(out[1], "expert", split_axis=0, concat_axis=0, tiled=True)
-        normed_all = call(turn_kernel, [((width, groups * tok), bf16, 1)], far(all_in), far(packed))[0]
-        q_grad, k_grad, v_grad, output_grad, router_grad, table_grad, gain_grads, aux_loss = call(
-            products_kernel,
+        normed_all = call(turn_kernel, [((groups * tok, width), bf16, 1)], far(all_in), far(packed))[0]
+        q_grad, k_grad, v_grad, output_grad, block_out, router_grad, table_grad, gain_grads, aux_loss = call(
+            functools.partial(products_kernel, slots),
             [((col, width), f32, 1)] * 4
-            + [((experts, width), f32), ((heads_here, bucket_count), f32), ((8, 256), f32), ((1, 1), f32)],
-            far(late_all), far(normed_all), shares, far(buckets_row), far(stats),
+            + [((col, tok), bf16), ((experts, width), f32), ((heads_here, bucket_count), f32)]
+            + [((16, 256), f32), ((1, 1), f32)],
+            far(late_all), far(normed_all), ret, far(buckets_row), far(stats), far(side), far(gate), far(residual),
         )
     else:
+        block_out = call(
+            functools.partial(last_kernel, slots), [((col, tok), bf16)], ret, far(side), far(gate), far(residual)
+        )[0]
         gain = packed[:, 2 * col : 2 * col + 2].reshape(heads, 256)[:, :col].reshape(width, 1)
         x = packed[:, :col].reshape(width, tok).astype(f32)
         normed = (x * token_scale(x) * gain.astype(f32)).astype(bf16)
         products = [mm(late[i * col : (i + 1) * col], normed, nt) for i in range(3)]
-        q_grad, k_grad, v_grad, sums, output_grad = lax.psum(products + [sums, product[0]], "expert")
+        q_grad, k_grad, v_grad, sums, gain_one, output_grad = lax.psum(
+            products + [shares[0], gain_one_part, shares[1]], "expert"
+        )
         router_grad = unfold_lanes(sums[32 : 32 + 6 * experts], 6)
         offsets = unfold_lanes(sums[16:32], 2)[:heads_here, : 2 * tok - 1]
         hot = (buckets[None, :] == jnp.arange(bucket_count)[:, None]).astype(f32)
         table_grad = mm(offsets, hot, nt, highest)
-        gain_grads = unfold_lanes(sums[:16], 2)
-        probs = gain_grads[2, :experts] + gain_grads[3, :experts]
+        gain_grads = jnp.concatenate([unfold_lanes(sums[:16], 2), unfold_lanes(gain_one, 2)], axis=0)
+        probs = gain_grads[1, :experts] + gain_grads[2, :experts]
         aux_loss = experts * jnp.sum(stats[:, 0] * probs) / (valid_total * valid_total)
     return (
         block_out.T,
         input_grad.T,
         aux_loss.reshape(()),
-        gain_grads[1, :col],
+        gain_grads[8, :col],
         q_grad.T,
         k_grad.T,
         v_grad.T,

time: 147 us -> 147 us (level)
  waiting for transfers between devices: 2.72 us -> 10.8 us
  blocking collectives: 89 us -> 83.3 us
  Pallas kernels: 32 us -> 30.5 us
    all_to_all x1, waiting for transfers between devices: 2.02 us -> 10.1 us  [shards(): ret = lax.all_to_all(ret, 'expert', split_axis=0, concat_axis=0, tiled=True)]
    all_to_all x1, blocking collectives: 19 us -> 14.4 us  [shards(): lax.all_to_all(shares[0], 'expert', split_axis=0, concat_axis=0, tiled=True)]
    pallas_call x10 -> x9, Pallas kernels: 32 us -> 30.5 us  [call(): pl.pallas_call(body, out_shape=shapes, in_specs=in_specs, compiler_params...]
  transfers between devices with their start and end apart: 3 -> 3, of which waited for: 1 -> 1; matrix products, arithmetic and copies ran while one was open for 2% -> 2% of each run, Pallas kernels for 19% -> 18%
where the time goes in v7:
time: 147 us; the launch traced here: 146 us
  blocking collectives  83.3 us (57%)
  Pallas kernels  30.5 us (21%)
  between operations  14.7 us (10%)
  waiting for transfers between devices  10.8 us (7%)
  starting transfers between devices  3.55 us (2%)
  local copies, waits for them, and re-layouts  2 us (1%)
    pallas_call x9, Pallas kernels, call(): pl.pallas_call(body, out_shape=shapes, in_specs=in_specs, compiler_params...  30.5 us
    all_to_all x1, blocking collectives, shards(): lax.all_to_all(back, ('expert', 'head'), split_axis=0, concat_axis=0, til...  15.7 us
    all_to_all x1, blocking collectives, shards(): lax.all_to_all(shares[0], 'expert', split_axis=0, concat_axis=0, tiled=True)  14.4 us
    all_to_all x1, blocking collectives, shards(): lax.all_to_all(send, 'expert', split_axis=0, concat_axis=0, tiled=True)  13.5 us
    all_to_all x1, blocking collectives, shards(): lax.all_to_all(first, 'head', split_axis=0, concat_axis=0, tiled=True)  11.1 us
    all_to_all x1, waiting for transfers between devices, shards(): ret = lax.all_to_all(ret, 'expert', split_axis=0, concat_axis=0, tiled=True)  10.1 us
    all_gather x1, blocking collectives, shards(): lax.all_gather(jnp.concatenate([inputs.T, out_grad.T, gains], axis=0), 'h...  8.01 us
    all_to_all x1, blocking collectives, shards(): lax.all_to_all(branch, 'head', split_axis=0, concat_axis=0, tiled=True)  7.69 us
  transfers between devices with their start and end apart: 3, of which 1 were waited for; matrix products, arithmetic and copies ran while one was open for 2% of the time, Pallas kernels for 18%

profile of v7, /device:TPU:0, one launch (start us, length us, event | category | flops | bytes accessed | tf_op | source)
XLA Modules:
  0.0 145.8 jit_solution(18304863156727114569)
XLA Ops:
  7.2 0.0 all-gather.9.cloned.1.call-start
  7.2 0.7 all-gather.9.cloned.1.call-update
  7.9 0.0 all-gather.7.cloned.1.call-start
  8.6 1.4 concatenate.6
  10.0 0.1 pad_add_fusion.scalars
  10.1 0.8 pad_maximum_fusion
  11.0 8.0 %all-gather = bf16[1600,128]{1,0:T(8,128)(2,1)S(1)} all-gather(bf16[400,128]{1,0:T(8,128)(2,1)S(1)} %pad_maximum_fusion), channel_id=2, replica_groups=mesh['expert'=8,'head'=4] {'head'}, dimensions={0}, use_global_device_ids=true | all-gather | bytes 512000 | tf_op jit(solution)/shard_map/all_gather | solution.py:525
  19.0 0.0 copy-start
  19.0 3.5 %shard_map.246 = (bf16[3,192,128]{2,1,0:T(8,128)(2,1)}, f32[3,128,128]{2,1,0:T(8,128)}, bf16[192,128]{1,0:T(8,128)(2,1)}, bf16[4,192,128]{2,1,0:T(8,128)(2,1)S(1)}) custom-call(s32[3]{0:T(128)S(1)} %pad_add_fusion.scalars, bf16[4,400,128]{2,1,0:T(8,128)(2,1)S(1)} %bitcast.31, bf16[192,768]{1,0:T(8,128)(2,1)} %bitcast.38, bf16[192,768]{1,0:T(8,128)(2,1)} %bitcast.40, ...), custom_call_target="tpu_custom_call" | custom-call | tf_op jit(solution)/shard_map/pallas_call | solution.py:31
  22.5 7.7 %all_to_all.30.came = bf16[4,192,128]{2,1,0:T(8,128)(2,1)S(1)} all-to-all(bf16[4,192,128]{2,1,0:T(8,128)(2,1)S(1)} %get-tuple-element.48), channel_id=1, replica_groups=mesh['expert'=8,'head'=4] {'head'}, dimensions={0} | all-to-all | bytes 393216 | tf_op jit(solution)/shard_map/all_to_all | solution.py:537
  30.2 1.6 %shard_map.247 = (f32[192,128]{1,0:T(8,128)}, bf16[192,128]{1,0:T(8,128)(2,1)}, f32[8,128]{1,0:T(8,128)}, bf16[8,24,384]{2,1,0:T(8,128)(2,1)S(1)}) custom-call(s32[3]{0:T(128)S(1)} %pad_add_fusion.scalars, bf16[4,192,128]{2,1,0:T(8,128)(2,1)S(1)} %all_to_all.30.came, bf16[192,128]{1,0:T(8,128)(2,1)} %bitcast.50, bf16[192,128]{1,0:T(8,128)(2,1)} %bitcast.52, ...), custom_call_target="tpu_custom_call" | custom-call | tf_op jit(solution)/shard_map/pallas_call | solution.py:31
  31.7 13.5 %all_to_all.31 = bf16[8,24,384]{2,1,0:T(8,128)(2,1)S(1)} all-to-all(bf16[8,24,384]{2,1,0:T(8,128)(2,1)S(1)} %get-tuple-element.49), channel_id=1, replica_groups=mesh['expert'=8,'head'=4] {'expert'}, dimensions={0} | all-to-all | bytes 294912 | tf_op jit(solution)/shard_map/all_to_all | solution.py:543
  45.3 6.7 %all_gather.29.quarters = bf16[4,192,384]{2,1,0:T(8,128)(2,1)S(1)} all-gather(bf16[1,192,384]{2,1,0:T(8,128)(2,1)S(1)} %bitcast.47), channel_id=1, replica_groups=mesh['expert'=8,'head'=4] {'head'}, dimensions={0}, use_global_device_ids=true | all-gather | bytes 737280 | tf_op jit(solution)/shard_map/all_gather | solution.py:544
  51.9 0.0 copy-done
  51.9 4.8 %shard_map.248 = (bf16[32,40,128]{2,1,0:T(8,128)(2,1)S(1)}, bf16[4,288,128]{2,1,0:T(8,128)(2,1)}, bf16[192,768]{1,0:T(8,128)(2,1)}, bf16[192,768]{1,0:T(8,128)(2...) custom-call(s32[3]{0:T(128)S(1)} %pad_add_fusion.scalars, bf16[4,192,384]{2,1,0:T(8,128)(2,1)S(1)} %all_gather.29.quarters, ...), custom_call_target="tpu_custom_call" | custom-call | tf_op jit(solution)/shard_map/pallas_call | solution.py:31
  56.7 15.7 %all_to_all.32.came = bf16[32,40,128]{2,1,0:T(8,128)(2,1)S(1)} all-to-all(bf16[32,40,128]{2,1,0:T(8,128)(2,1)S(1)} %get-tuple-element.50), channel_id=1, replica_groups=mesh['expert'=8,'head'=4] {'expert','head'}, dimensions={0} | all-to-all | bytes 655360 | tf_op jit(solution)/shard_map/all_to_all | solution.py:552
  72.4 1.8 %shard_map.249 = (bf16[384,128]{1,0:T(8,128)(2,1)S(1)}, f32[8,128]{1,0:T(8,128)}, f32[8,128]{1,0:T(8,128)}) custom-call(bf16[32,40,128]{2,1,0:T(8,128)(2,1)S(1)} %all_to_all.32.came, f32[8,128]{1,0:T(8,128)} %get-tuple-element.51.side, bf16[192,128]{1,0:T(8,128)(2,1)} %get-tuple-element.52.low), custom_call_target="tpu_custom_call" | custom-call | tf_op jit(solution)/shard_map/pallas_call | solution.py:31
  74.3 6.2 %all-gather.1 = bf16[1536,128]{1,0:T(8,128)(2,1)S(1)} all-gather(bf16[384,128]{1,0:T(8,128)(2,1)S(1)} %get-tuple-element.53), channel_id=3, replica_groups=mesh['expert'=8,'head'=4] {'head'}, dimensions={0}, use_global_device_ids=true | all-gather | bytes 491520 | tf_op jit(solution)/shard_map/all_gather | solution.py:558
  80.5 4.7 %shard_map.250 = (bf16[576,128]{1,0:T(8,128)(2,1)}, bf16[4,496,128]{2,1,0:T(8,128)(2,1)S(1)}, f32[192,128]{1,0:T(8,128)}, f32[8,128]{1,0:T(8,128)}, bf16[8,160,128]{2,1,0:T(8,128)(2,1)S(1)}) custom-call(s32[3]{0:T(128)S(1)} %pad_add_fusion.scalars, bf16[4,400,128]{2,1,0:T(8,128)(2,1)} %bitcast.33, bf16[4,384,128]{2,1,0:T(8,128)(2,1)S(1)} %bitcast.36, ...), custom_call_target="tpu_custom_call" | custom-call | tf_op jit(solution)/shard_map/pallas_call | solution.py:31
  85.2 0.0 all-gather.7.cloned.1.call-update
  85.2 11.1 %all_to_all.33.came = bf16[4,496,128]{2,1,0:T(8,128)(2,1)S(1)} all-to-all(bf16[4,496,128]{2,1,0:T(8,128)(2,1)S(1)} %get-tuple-element.61), channel_id=1, replica_groups=mesh['expert'=8,'head'=4] {'head'}, dimensions={0} | all-to-all | bytes 1015808 | tf_op jit(solution)/shard_map/all_to_all | solution.py:581
  96.2 14.4 %all_to_all.34.refs_0_ = bf16[8,160,128]{2,1,0:T(8,128)(2,1)S(1)} all-to-all(bf16[8,160,128]{2,1,0:T(8,128)(2,1)S(1)} %get-tuple-element.63), channel_id=1, replica_groups=mesh['expert'=8,'head'=4] {'expert'}, dimensions={0} | all-to-all | bytes 655360 | tf_op jit(solution)/shard_map/all_to_all | solution.py:580
  110.6 2.2 %shard_map.252 = (bf16[8,224,128]{2,1,0:T(8,128)(2,1)}, f32[16,128]{1,0:T(8,128)}, f32[192,128]{1,0:T(8,128)}) custom-call(s32[3]{0:T(128)S(1)} %pad_add_fusion.scalars, bf16[4,496,128]{2,1,0:T(8,128)(2,1)S(1)} %all_to_all.33.came, bf16[4,400,128]{2,1,0:T(8,128)(2,1)} %bitcast.34, f32[192,128]{1,0:T(8,128)} %get-tuple-element.62.own, ...), custom_call_target="tpu_custom_call" | custom-call | tf_op jit(solution)/shard_map/pallas_call | solution.py:31
  112.8 3.5 %all-to-all-start.5 = ((bf16[8,224,128]{2,1,0:T(8,128)(2,1)}), bf16[8,224,128]{2,1,0:T(8,128)(2,1)S(1)}, u32[]{:S(2)}, u32[]{:S(2)}) async-start(bf16[8,224,128]{2,1,0:T(8,128)(2,1)} %get-tuple-element.64), calls=%async_computation.5 | async-start | bytes 917504 | tf_op jit(solution)/shard_map/all_to_all | solution.py:590
  116.3 4.0 %shard_map.254 = (f32[768,768]{1,0:T(8,128)}, f32[768,768]{1,0:T(8,128)}) custom-call(bf16[192,768]{1,0:T(8,128)(2,1)} %get-tuple-element.77.rows_ref, bf16[192,768]{1,0:T(8,128)(2,1)} %get-tuple-element.78.hidden, bf16[192,768]{1,0:T(8,128)(2,1)} %get-tuple-element.79.before, bf16[192,768]{1,0:T(8,128)(2,1)} %get-tuple-element.80.grads), custom_call_target="tpu_custom_call" | custom-call | tf_op jit(solution)/shard_map/pallas_call | solution.py:31
  120.3 0.0 all-gather.9.cloned.1.call-done
  120.3 3.7 %shard_map.251.normed = bf16[1024,768]{1,0:T(8,128)(2,1)} custom-call(bf16[8,4,192,128]{3,2,1,0:T(8,128)(2,1)} %bitcast.37, bf16[4,400,128]{2,1,0:T(8,128)(2,1)} %bitcast.35), custom_call_target="tpu_custom_call" | custom-call | tf_op jit(solution)/shard_map/pallas_call | solution.py:31
  124.0 10.1 %all-to-all-done.5.came = bf16[8,224,128]{2,1,0:T(8,128)(2,1)S(1)} async-done(((bf16[8,224,128]{2,1,0:T(8,128)(2,1)}), bf16[8,224,128]{2,1,0:T(8,128)(2,1)S(1)}, u32[]{:S(2)}, u32[]{:S(2)}) %all-to-all-start.5) | async-done | bytes 458784 | tf_op jit(solution)/shard_map/all_to_all | solution.py:590
  134.1 0.0 all-gather.7.cloned.1.call-done
  134.1 4.3 %shard_map.253 = (f32[192,768]{1,0:T(8,128)}, f32[192,768]{1,0:T(8,128)}, f32[192,768]{1,0:T(8,128)}, f32[192,768]{1,0:T(8,128)}, bf16[192,128]{1,0:T(8,128)(2,1...) custom-call(bf16[8,576,128]{2,1,0:T(8,128)(2,1)} %bitcast.44, ...), custom_call_target="tpu_custom_call" | custom-call | tf_op jit(solution)/shard_map/pallas_call | solution.py:31
  138.4 0.6 fusion
  (2 shorter events, 0.0 us)
Async XLA Ops:
  7.2 113.2 %all-gather.9.cloned.1.call-start = ((), (), s32[]{:S(2)}) async-start(), calls=%async_computation.7 | async-start | bytes 1622016 | tf_op jit(solution)/shard_map/all_gather | solution.py:527
  7.9 126.2 %all-gather.7.cloned.1.call-start = ((), (), s32[]{:S(2)}) async-start(), calls=%async_computation.6 | async-start | bytes 1327104 | tf_op jit(solution)/shard_map/all_gather | solution.py:577
  19.0 33.0 %copy-start = (bf16[1600,128]{1,0:T(8,128)(2,1)}, bf16[1600,128]{1,0:T(8,128)(2,1)S(1)}, u32[]{:S(2)}) copy-start(bf16[1600,128]{1,0:T(8,128)(2,1)S(1)} %all-gather) | copy-start | bytes 1228804
  112.8 21.3 %all-to-all-start.5 = ((bf16[8,224,128]{2,1,0:T(8,128)(2,1)}), bf16[8,224,128]{2,1,0:T(8,128)(2,1)S(1)}, u32[]{:S(2)}, u32[]{:S(2)}) async-start(bf16[8,224,128]{2,1,0:T(8,128)(2,1)} %get-tuple-element.64), calls=%async_computation.5 | async-start | bytes 917504 | tf_op jit(solution)/shard_map/all_to_all | solution.py:590
Sparse Core Ops, SparseCore 0:
  10.9 58.8 all-gather.8
  85.3 47.5 all-gather.6

commit v8 on v7

--- a/solution.py
+++ b/solution.py
@@ -431,12 +431,13 @@
     block_ref[...] = add_returned(slots, blocks, side, gate, residual)
 
 
-def turn_kernel(all_in, packed, normed_ref):
+def turn_kernel(scalars, all_in, packed, normed_ref):
     groups, heads, col, tok = all_in.shape
     gain = all_gains(packed)[0]
     for b in range(groups):
         x = jnp.concatenate([all_in[b, i].astype(f32) for i in range(heads)], axis=0)
-        normed_ref[b * tok : (b + 1) * tok, :] = jnp.transpose(x * token_scale(x) * gain).astype(bf16)
+        spot = pl.multiple_of((b ^ (scalars[2] & 1)) * tok, tok)
+        normed_ref[pl.ds(spot, tok), :] = jnp.transpose(x * token_scale(x) * gain).astype(bf16)
 
 
 def products_kernel(
@@ -574,10 +575,20 @@
     )
 
     if joined:
-        late_all = lax.all_gather(late, "expert")
+        pair = lax.ppermute(late, "expert", [(i, i ^ 1) for i in range(groups)])
+        late = jnp.stack([late, pair])
+        lines = [[i for i in range(groups) if i % 2 == x] for x in range(2)]
+        late_all = lax.all_gather(late, "expert", axis_index_groups=lines).reshape(groups, 3 * col, tok)
+
+    in_weight_grad, out_weight_grad = call(
+        weights_kernel, [((width, width), f32, 1)] * 2, far(rows), far(hidden), far(before_grad), far(back_rows)
+    )
 
     if joined:
         shares = [lax.all_to_all(shares[0], "expert", split_axis=0, concat_axis=0, tiled=True)]
+    first, late, in_weight_grad, out_weight_grad = lax.optimization_barrier(
+        (first, late, in_weight_grad, out_weight_grad)
+    )
     first = lax.all_to_all(first, "head", split_axis=0, concat_axis=0, tiled=True)
     ret, gain_one_part, input_grad = call(
         first_kernel,
@@ -588,11 +599,8 @@
         scalars, first, far(packed), far(residual_grad_own), *(shares if joined else []),
     )
     ret = lax.all_to_all(ret, "expert", split_axis=0, concat_axis=0, tiled=True)
-    in_weight_grad, out_weight_grad = call(
-        weights_kernel, [((width, width), f32, 1)] * 2, far(rows), far(hidden), far(before_grad), far(back_rows)
-    )
     if joined:
-        normed_all = call(turn_kernel, [((groups * tok, width), bf16, 1)], far(all_in), far(packed))[0]
+        normed_all = call(turn_kernel, [((groups * tok, width), bf16, 1)], scalars, far(all_in), far(packed))[0]
         q_grad, k_grad, v_grad, output_grad, block_out, router_grad, table_grad, gain_grads, aux_loss = call(
             functools.partial(products_kernel, slots),
             [((col, width), f32, 1)] * 4

time: 147 us -> 160 us (1.088)
  blocking collectives: 83.3 us -> 89.9 us
  waiting for transfers between devices: 10.8 us -> 15.1 us
  other arithmetic: 0.91 us -> 2.56 us
    all_to_all x1, blocking collectives: 14.4 us -> 21 us  [shards(): lax.all_to_all(shares[0], 'expert', split_axis=0, concat_axis=0, tiled=True)]
    ppermute x0 -> x1, waiting for transfers between devices: none -> 4.99 us  [shards(): pair = lax.ppermute(late, 'expert', [(i, i ^ 1) for i in range(groups)])]
    another operation x0 -> x1, other arithmetic: none -> 1.65 us  [shards(): late = jnp.stack([late, pair])]
  transfers between devices with their start and end apart: 3 -> 4, of which waited for: 1 -> 2; matrix products, arithmetic and copies ran while one was open for 2% -> 2% of each run, Pallas kernels for 18% -> 16%
where the time goes in v8:
time: 160 us
  blocking collectives  89.9 us (56%)
  Pallas kernels  30.5 us (19%)
  waiting for transfers between devices  15.1 us (9%)
  between operations  14.8 us (9%)
  starting transfers between devices  4.87 us (3%)
  other arithmetic  2.56 us (2%)
  local copies, waits for them, and re-layouts  2 us (1%)
    pallas_call x9, Pallas kernels, call(): pl.pallas_call(body, out_shape=shapes, in_specs=in_specs, compiler_params...  30.5 us
    all_to_all x1, blocking collectives, shards(): lax.all_to_all(shares[0], 'expert', split_axis=0, concat_axis=0, tiled=True)  21 us
    all_to_all x1, blocking collectives, shards(): lax.all_to_all(back, ('expert', 'head'), split_axis=0, concat_axis=0, til...  15.7 us
    all_to_all x1, blocking collectives, shards(): lax.all_to_all(send, 'expert', split_axis=0, concat_axis=0, tiled=True)  13.5 us
    all_to_all x1, blocking collectives, shards(): lax.all_to_all(first, 'head', split_axis=0, concat_axis=0, tiled=True)  11.1 us
    all_to_all x1, waiting for transfers between devices, shards(): ret = lax.all_to_all(ret, 'expert', split_axis=0, concat_axis=0, tiled=True)  9.35 us
    all_gather x1, blocking collectives, shards(): lax.all_gather(jnp.concatenate([inputs.T, out_grad.T, gains], axis=0), 'h...  8.01 us
    all_to_all x1, blocking collectives, shards(): lax.all_to_all(branch, 'head', split_axis=0, concat_axis=0, tiled=True)  7.69 us
  transfers between devices with their start and end apart: 4, of which 2 were waited for; matrix products, arithmetic and copies ran while one was open for 2% of the time, Pallas kernels for 16%

profile of v8, /device:TPU:0, one launch (start us, length us, event | category | flops | bytes accessed | tf_op | source)
XLA Modules:
  0.0 159.7 jit_solution(14674246063868589565)
XLA Ops:
  7.2 0.0 all-gather.9.cloned.1.call-start
  7.2 0.7 all-gather.9.cloned.1.call-update
  7.9 0.0 all-gather.7.cloned.1.call-start
  8.6 1.4 concatenate.6
  10.0 0.1 pad_add_fusion.scalars
  10.1 0.8 pad_maximum_fusion.1
  11.0 8.0 %all-gather = bf16[1600,128]{1,0:T(8,128)(2,1)S(1)} all-gather(bf16[400,128]{1,0:T(8,128)(2,1)S(1)} %pad_maximum_fusion.1), channel_id=2, replica_groups=mesh['expert'=8,'head'=4] {'head'}, dimensions={0}, use_global_device_ids=true | all-gather | bytes 512000 | tf_op jit(solution)/shard_map/all_gather | solution.py:526
  19.0 0.0 copy-start
  19.0 3.5 %shard_map.246 = (bf16[3,192,128]{2,1,0:T(8,128)(2,1)}, f32[3,128,128]{2,1,0:T(8,128)}, bf16[192,128]{1,0:T(8,128)(2,1)}, bf16[4,192,128]{2,1,0:T(8,128)(2,1)S(1)}) custom-call(s32[3]{0:T(128)S(1)} %pad_add_fusion.scalars, bf16[4,400,128]{2,1,0:T(8,128)(2,1)S(1)} %bitcast.32, bf16[192,768]{1,0:T(8,128)(2,1)} %bitcast.39, bf16[192,768]{1,0:T(8,128)(2,1)} %bitcast.41, ...), custom_call_target="tpu_custom_call" | custom-call | tf_op jit(solution)/shard_map/pallas_call | solution.py:31
  22.5 7.7 %all_to_all.30.came = bf16[4,192,128]{2,1,0:T(8,128)(2,1)S(1)} all-to-all(bf16[4,192,128]{2,1,0:T(8,128)(2,1)S(1)} %get-tuple-element.51), channel_id=1, replica_groups=mesh['expert'=8,'head'=4] {'head'}, dimensions={0} | all-to-all | bytes 393216 | tf_op jit(solution)/shard_map/all_to_all | solution.py:538
  30.2 1.6 shard_map.247
  31.7 13.5 %all_to_all.31 = bf16[8,24,384]{2,1,0:T(8,128)(2,1)S(1)} all-to-all(bf16[8,24,384]{2,1,0:T(8,128)(2,1)S(1)} %get-tuple-element.52), channel_id=1, replica_groups=mesh['expert'=8,'head'=4] {'expert'}, dimensions={0} | all-to-all | bytes 294912 | tf_op jit(solution)/shard_map/all_to_all | solution.py:544
  45.3 6.7 %all_gather.29.quarters = bf16[4,192,384]{2,1,0:T(8,128)(2,1)S(1)} all-gather(bf16[1,192,384]{2,1,0:T(8,128)(2,1)S(1)} %bitcast.47), channel_id=1, replica_groups=mesh['expert'=8,'head'=4] {'head'}, dimensions={0}, use_global_device_ids=true | all-gather | bytes 737280 | tf_op jit(solution)/shard_map/all_gather | solution.py:545
  51.9 0.0 copy-done
  51.9 4.8 %shard_map.248 = (bf16[32,40,128]{2,1,0:T(8,128)(2,1)S(1)}, bf16[4,288,128]{2,1,0:T(8,128)(2,1)}, bf16[192,768]{1,0:T(8,128)(2,1)}, bf16[192,768]{1,0:T(8,128)(2...) custom-call(s32[3]{0:T(128)S(1)} %pad_add_fusion.scalars, bf16[4,192,384]{2,1,0:T(8,128)(2,1)S(1)} %all_gather.29.quarters, ...), custom_call_target="tpu_custom_call" | custom-call | tf_op jit(solution)/shard_map/pallas_call | solution.py:31
  56.7 15.7 %all_to_all.32.came = bf16[32,40,128]{2,1,0:T(8,128)(2,1)S(1)} all-to-all(bf16[32,40,128]{2,1,0:T(8,128)(2,1)S(1)} %get-tuple-element.53), channel_id=1, replica_groups=mesh['expert'=8,'head'=4] {'expert','head'}, dimensions={0} | all-to-all | bytes 655360 | tf_op jit(solution)/shard_map/all_to_all | solution.py:553
  72.4 1.8 %shard_map.249 = (bf16[384,128]{1,0:T(8,128)(2,1)S(1)}, f32[8,128]{1,0:T(8,128)}, f32[8,128]{1,0:T(8,128)}) custom-call(bf16[32,40,128]{2,1,0:T(8,128)(2,1)S(1)} %all_to_all.32.came, f32[8,128]{1,0:T(8,128)} %get-tuple-element.54.side, bf16[192,128]{1,0:T(8,128)(2,1)} %get-tuple-element.55.low), custom_call_target="tpu_custom_call" | custom-call | tf_op jit(solution)/shard_map/pallas_call | solution.py:31
  74.3 6.2 %all-gather.1 = bf16[1536,128]{1,0:T(8,128)(2,1)S(1)} all-gather(bf16[384,128]{1,0:T(8,128)(2,1)S(1)} %get-tuple-element.56), channel_id=3, replica_groups=mesh['expert'=8,'head'=4] {'head'}, dimensions={0}, use_global_device_ids=true | all-gather | bytes 491520 | tf_op jit(solution)/shard_map/all_gather | solution.py:559
  80.5 4.7 %shard_map.250 = (bf16[576,128]{1,0:T(8,128)(2,1)}, bf16[4,496,128]{2,1,0:T(8,128)(2,1)S(1)}, f32[192,128]{1,0:T(8,128)}, f32[8,128]{1,0:T(8,128)}, bf16[8,160,128]{2,1,0:T(8,128)(2,1)S(1)}) custom-call(s32[3]{0:T(128)S(1)} %pad_add_fusion.scalars, bf16[4,400,128]{2,1,0:T(8,128)(2,1)} %bitcast.34, bf16[4,384,128]{2,1,0:T(8,128)(2,1)S(1)} %bitcast.37, ...), custom_call_target="tpu_custom_call" | custom-call | tf_op jit(solution)/shard_map/pallas_call | solution.py:31
  85.2 1.3 collective-permute-start
  86.5 5.0 %collective-permute-done = bf16[576,128]{1,0:T(8,128)(2,1)S(1)} collective-permute-done((bf16[576,128]{1,0:T(8,128)(2,1)}, bf16[576,128]{1,0:T(8,128)(2,1)S(1)}, u32[]{:S(2)}, u32[]{:S(2)}) %collective-permute-start) | collective-permute-done | bytes 147488 | tf_op jit(solution)/shard_map/ppermute | solution.py:578
  91.5 1.7 %pad_maximum_fusion = bf16[2,576,128]{2,1,0:T(8,128)(2,1)} fusion(bf16[1,576,128]{2,1,0:T(8,128)(2,1)S(1)} %bitcast.54, bf16[1,576,128]{2,1,0:T(8,128)(2,1)} %bitcast.53), kind=kLoop, calls=%fused_computation | loop fusion | flops 147456 | bytes 589824 | tf_op jit(solution)/shard_map/stack | solution.py:579
  93.1 0.0 all-gather.7.cloned.1.call-update
  93.1 4.0 %shard_map.252 = (f32[768,768]{1,0:T(8,128)}, f32[768,768]{1,0:T(8,128)}) custom-call(bf16[192,768]{1,0:T(8,128)(2,1)} %get-tuple-element.65.rows_ref, bf16[192,768]{1,0:T(8,128)(2,1)} %get-tuple-element.66.hidden, bf16[192,768]{1,0:T(8,128)(2,1)} %get-tuple-element.67.before, bf16[192,768]{1,0:T(8,128)(2,1)} %get-tuple-element.68.grads), custom_call_target="tpu_custom_call" | custom-call | tf_op jit(solution)/shard_map/pallas_call | solution.py:31
  97.2 11.1 %all_to_all.33.came = bf16[4,496,128]{2,1,0:T(8,128)(2,1)S(1)} all-to-all(bf16[4,496,128]{2,1,0:T(8,128)(2,1)S(1)} %get-tuple-element.71), channel_id=1, replica_groups=mesh['expert'=8,'head'=4] {'head'}, dimensions={0} | all-to-all | bytes 1015808 | tf_op jit(solution)/shard_map/all_to_all | solution.py:592
  108.2 21.0 %all_to_all.34.refs_0_ = bf16[8,160,128]{2,1,0:T(8,128)(2,1)S(1)} all-to-all(bf16[8,160,128]{2,1,0:T(8,128)(2,1)S(1)} %get-tuple-element.73), channel_id=1, replica_groups=mesh['expert'=8,'head'=4] {'expert'}, dimensions={0} | all-to-all | bytes 655360 | tf_op jit(solution)/shard_map/all_to_all | solution.py:588
  129.2 2.2 %shard_map.253 = (bf16[8,224,128]{2,1,0:T(8,128)(2,1)}, f32[16,128]{1,0:T(8,128)}, f32[192,128]{1,0:T(8,128)}) custom-call(s32[3]{0:T(128)S(1)} %pad_add_fusion.scalars, bf16[4,496,128]{2,1,0:T(8,128)(2,1)S(1)} %all_to_all.33.came, bf16[4,400,128]{2,1,0:T(8,128)(2,1)} %bitcast.35, f32[192,128]{1,0:T(8,128)} %get-tuple-element.72.own, ...), custom_call_target="tpu_custom_call" | custom-call | tf_op jit(solution)/shard_map/pallas_call | solution.py:31
  131.4 3.5 %all-to-all-start.5 = ((bf16[8,224,128]{2,1,0:T(8,128)(2,1)}), bf16[8,224,128]{2,1,0:T(8,128)(2,1)S(1)}, u32[]{:S(2)}, u32[]{:S(2)}) async-start(bf16[8,224,128]{2,1,0:T(8,128)(2,1)} %get-tuple-element.74), calls=%async_computation.5 | async-start | bytes 917504 | tf_op jit(solution)/shard_map/all_to_all | solution.py:601
  134.9 0.0 all-gather.9.cloned.1.call-done
  134.9 3.7 %shard_map.251.normed = bf16[1024,768]{1,0:T(8,128)(2,1)} custom-call(s32[3]{0:T(128)S(1)} %pad_add_fusion.scalars, bf16[8,4,192,128]{3,2,1,0:T(8,128)(2,1)} %bitcast.38, bf16[4,400,128]{2,1,0:T(8,128)(2,1)} %bitcast.36), custom_call_target="tpu_custom_call" | custom-call | tf_op jit(solution)/shard_map/pallas_call | solution.py:31
  138.6 9.4 %all-to-all-done.5.came = bf16[8,224,128]{2,1,0:T(8,128)(2,1)S(1)} async-done(((bf16[8,224,128]{2,1,0:T(8,128)(2,1)}), bf16[8,224,128]{2,1,0:T(8,128)(2,1)S(1)}, u32[]{:S(2)}, u32[]{:S(2)}) %all-to-all-start.5) | async-done | bytes 458784 | tf_op jit(solution)/shard_map/all_to_all | solution.py:601
  147.9 0.0 all-gather.7.cloned.1.call-done.late
  147.9 4.3 %shard_map.254 = (f32[192,768]{1,0:T(8,128)}, f32[192,768]{1,0:T(8,128)}, f32[192,768]{1,0:T(8,128)}, f32[192,768]{1,0:T(8,128)}, bf16[192,128]{1,0:T(8,128)(2,1...) custom-call(bf16[8,576,128]{2,1,0:T(8,128)(2,1)} %all-gather.7.cloned.1.call-done.late, ...), custom_call_target="tpu_custom_call" | custom-call | tf_op jit(solution)/shard_map/pallas_call | solution.py:31
  152.3 0.6 fusion
  (2 shorter events, 0.0 us)
Async XLA Ops:
  7.2 127.7 %all-gather.9.cloned.1.call-start = ((), (), s32[]{:S(2)}) async-start(), calls=%async_computation.7 | async-start | bytes 1622016 | tf_op jit(solution)/shard_map/all_gather | solution.py:528
  7.9 140.0 %all-gather.7.cloned.1.call-start = ((), (), s32[]{:S(2)}) async-start(), calls=%async_computation.6 | async-start | bytes 1474560 | tf_op jit(solution)/shard_map/all_gather | solution.py:581
  19.0 33.0 %copy-start = (bf16[1600,128]{1,0:T(8,128)(2,1)}, bf16[1600,128]{1,0:T(8,128)(2,1)S(1)}, u32[]{:S(2)}) copy-start(bf16[1600,128]{1,0:T(8,128)(2,1)S(1)} %all-gather) | copy-start | bytes 1228804
  85.2 6.3 %collective-permute-start = (bf16[576,128]{1,0:T(8,128)(2,1)}, bf16[576,128]{1,0:T(8,128)(2,1)S(1)}, u32[]{:S(2)}, u32[]{:S(2)}) collective-permute-start(bf16[576,128]{1,0:T(8,128)(2,1)} %get-tuple-element.63), channel_id=1, source_target_pairs={{0,4},{4,0},{8,12},{12,8},{16,20},{20,16},{24,28},{28,24},{1,5},{5... | collective-permute-start | bytes 442376 | tf_op jit(solution)/shard_map/ppermute | solution.py:578
  131.4 16.5 %all-to-all-start.5 = ((bf16[8,224,128]{2,1,0:T(8,128)(2,1)}), bf16[8,224,128]{2,1,0:T(8,128)(2,1)S(1)}, u32[]{:S(2)}, u32[]{:S(2)}) async-start(bf16[8,224,128]{2,1,0:T(8,128)(2,1)} %get-tuple-element.74), calls=%async_computation.5 | async-start | bytes 917504 | tf_op jit(solution)/shard_map/all_to_all | solution.py:601
Sparse Core Ops, SparseCore 0:
  10.9 58.8 all-gather.8
  93.3 35.9 all-gather.6

commit v9 on v7

--- a/solution.py
+++ b/solution.py
@@ -22,18 +22,71 @@
     return lax.dot_general(left, right, (dims, ((), ())), precision=precision, preferred_element_type=f32)
 
 
+class Pieces:
+    def __init__(self, refs):
+        self.refs, self.size = refs, refs[0].shape[0]
+        self.shape = (self.size * len(refs),) + tuple(refs[0].shape[1:])
+
+    def __getitem__(self, index):
+        if index is Ellipsis:
+            return jnp.concatenate([ref[...] for ref in self.refs], axis=0)
+        at, rest = (index[0], index[1:]) if isinstance(index, tuple) else (index, ())
+        return self.refs[at // self.size][(at % self.size,) + rest]
+
+
+class Split:
+    def __init__(self, array, count):
+        self.array, self.count = array, count
+
+
+def block_of(array, count, i):
+    shape = (array.shape[0] // count,) + array.shape[1:]
+    return pl.BlockSpec(shape, lambda step: (i,) + (0,) * (array.ndim - 1))
+
+
+def whole_map(rank):
+    return lambda step: (0,) * rank
+
+
 def call(body, outs, *args):
-    scalar_memory = pl.BlockSpec(memory_space=pltpu.SMEM)
-    in_specs = [scalar_memory if a.dtype == jnp.int32 and a.ndim == 1 else pl.BlockSpec() for a in args]
+    in_specs, operands, counts = [], [], []
+    for a in args:
+        if isinstance(a, Split):
+            held = far(a.array)
+            in_specs += [block_of(held, a.count, i) for i in range(a.count)]
+            operands += [held] * a.count
+            counts.append(a.count)
+            continue
+        whole = a.dtype == jnp.int32 and a.ndim == 1
+        in_specs.append(pl.BlockSpec(memory_space=pltpu.SMEM) if whole else pl.BlockSpec())
+        operands.append(a)
+        counts.append(0)
     shapes = []
     for shape, kind, *remote in outs:
         shapes.append(pltpu.HBM(shape, kind) if remote else jax.ShapeDtypeStruct(shape, kind))
+
+    def run(*refs):
+        ins, at = [], 0
+        for count in counts:
+            ins.append(Pieces(refs[at : at + count]) if count else refs[at])
+            at += max(count, 1)
+        body(*ins, *refs[at:])
+
+    extra = {}
+    if any(counts):
+        extra["grid"] = (1,)
+        extra["out_specs"] = [pl.BlockSpec(shape.shape, whole_map(len(shape.shape))) for shape in shapes]
+        in_specs = [
+            pl.BlockSpec(a.shape, whole_map(a.ndim)) if spec.block_shape is None and spec.memory_space is None else spec
+            for spec, a in zip(in_specs, operands)
+        ]
     return pl.pallas_call(
-        body,
+        run,
         out_shape=shapes,
         in_specs=in_specs,
+        **extra,
         compiler_params=pltpu.CompilerParams(vmem_limit_bytes=40 * 1024 * 1024),
-    )(*args)
+    )(*operands)
 
 
 def far(array):
@@ -392,12 +445,15 @@
         total = total + came[i].astype(f32)
     mean = (total[col : col + 1] + total[col + 1 : col + 2]) * (1.0 / (heads * col))
     scale = token_scale(tall(packed, 0, col))
-    mine = packed[scalars[1]].astype(f32)
+    mine = packed[0].astype(f32)
+    for i in range(1, heads):
+        mine = jnp.where(scalars[1] == i, packed[i].astype(f32), mine)
     unit = mine[:col] * scale
     gain = gain_columns(mine[2 * col : 2 * col + 16])[0]
     input_ref[...] = own[...] + scale * (total[:col] * gain - unit * mean)
     gain_grad = jnp.sum(total[:col] * unit, axis=1, keepdims=True)
-    gain_grad = jnp.transpose(side_lanes(col, 128, [gain_grad]))[0:8]
+    unused = jnp.zeros_like(gain_grad)
+    gain_grad = jnp.transpose(side_lanes(col, 128, [unused, unused, unused, gain_grad]))[0:8]
     gain_grad = fold_lanes(jnp.concatenate([gain_grad, jnp.zeros((8, 64), f32)], axis=1))
     gain_ref[...] = gain_grad
     produced = total[col + 16 :]
@@ -406,15 +462,23 @@
     rest = jnp.concatenate([produced[count:, :64], produced[count:, 64:]], axis=0)
     rest = jnp.concatenate([rest, jnp.zeros((count, 64), f32)], axis=1)
     slots = count // experts
-    joined = []
-    if shares:
-        share = shares[0][0].astype(f32)
-        for e in range(1, experts):
-            share = share + shares[0][e].astype(f32)
-        joined = [gain_grad, share]
     for e in range(experts):
         at = slice(e * slots, (e + 1) * slots)
-        ret_ref[e] = jnp.concatenate([top[at], rest[at]] + joined, axis=0).astype(bf16)
+        pieces = [top[at], rest[at]]
+        if shares:
+            share = shares[0][e].astype(f32)
+            if e == 0:
+                share = jnp.concatenate([share[:16] + gain_grad, share[16:]], axis=0)
+            pieces.append(share)
+        ret_ref[e] = jnp.concatenate(pieces, axis=0).astype(bf16)
+
+
+def share_kernel(slots, came, share_ref):
+    total = came[0].astype(f32)
+    for e in range(1, came.shape[0]):
+        total = total + came[e].astype(f32)
+    for e in range(came.shape[0]):
+        share_ref[e] = total[2 * slots :].astype(bf16)
 
 
 def add_returned(slots, blocks, side, gate, residual):
@@ -440,19 +504,13 @@
 
 
 def products_kernel(
-    slots, late, normed, came, buckets, stats, side, gate, residual,
-    q_ref, k_ref, v_ref, out_ref, block_ref, router_ref, table_ref, gains_ref, aux_ref,
+    late, normed, came, buckets, stats, q_ref, k_ref, v_ref, out_ref, router_ref, table_ref, gains_ref, aux_ref,
 ):
     groups = came.shape[0]
     col = q_ref.shape[0]
     experts = router_ref.shape[0]
     size = col // groups
-    blocks = [came[b].astype(f32) for b in range(groups)]
-    block_ref[...] = add_returned(slots, blocks, side, gate, residual)
-    gain_one = blocks[0][2 * slots : 2 * slots + 16]
-    for block in blocks[1:]:
-        gain_one = gain_one + block[2 * slots : 2 * slots + 16]
-    shares = [block[2 * slots + 16 :] for block in blocks]
+    shares = [came[b].astype(f32) for b in range(groups)]
     chunk = shares[0].shape[0] - 6 * size
     for b in range(groups):
         out_ref[b * size : (b + 1) * size, :] = unfold_lanes(shares[b][chunk:], 6)
@@ -462,8 +520,7 @@
         ref[...] = product[i * col : (i + 1) * col]
     small = jnp.concatenate([share[:chunk] for share in shares], axis=0)
     gains = unfold_lanes(small[:16], 2)
-    gains_ref[0:8, :] = gains
-    gains_ref[8:16, :] = unfold_lanes(gain_one, 2)
+    gains_ref[...] = gains
     probs = gains[1:2, :experts] + gains[2:3, :experts]
     same = lanes((experts, experts)) == sublanes((experts, experts))
     share = jnp.sum(jnp.where(same, stats[:, 0:1] * probs, 0.0), axis=0, keepdims=True)
@@ -547,7 +604,7 @@
         functools.partial(expert_kernel, capacity),
         [((experts * heads, folded_rows(slots), 128), bf16), ((heads, total * 3 // 2, 128), bf16, 1)]
         + [((total, width), bf16, 1)] * 4,
-        scalars, quarters, far(packed), far(w_in), far(w_out), far(router_rows),
+        scalars, Split(quarters, heads), far(packed), Split(w_in, 4), Split(w_out, 4), far(router_rows),
     )
     came = lax.all_to_all(back, ("expert", "head"), split_axis=0, concat_axis=0, tiled=True)
     grad_own, gate_grad, stats = call(
@@ -564,46 +621,48 @@
             ((8, tok), f32, 1),
         ]
         + (
-            [((groups, chunk + 6 * col // groups, 128), bf16)]
+            [((groups, chunk + 6 * col // groups, 128), bf16, 1)]
             if joined
             else [((small_rows, 128), f32, 1), ((col, width), f32, 1)]
         ),
         scalars, far(packed), expert_grad, far(gate_grad), far(stats), far(routes_row),
         far(router_rows), far(w_output), far(weights), far(qkv), far(wq), far(wk), far(wv), far(attended),
-        far(part),
+        Split(part, heads),
     )
 
     if joined:
         late_all = lax.all_gather(late, "expert")
 
-    if joined:
-        shares = [lax.all_to_all(shares[0], "expert", split_axis=0, concat_axis=0, tiled=True)]
     first = lax.all_to_all(first, "head", split_axis=0, concat_axis=0, tiled=True)
     ret, gain_one_part, input_grad = call(
         first_kernel,
         [
-            ((experts, 2 * slots + (16 + shares[0].shape[1] if joined else 0), 128), bf16),
+            ((experts, 2 * slots + (shares[0].shape[1] if joined else 0), 128), bf16),
             ((16, 128), f32, 1), ((col, tok), f32, 1),
         ],
-        scalars, first, far(packed), far(residual_grad_own), *(shares if joined else []),
+        scalars, first, Split(packed, heads), far(residual_grad_own), *([Split(shares[0], groups)] if joined else []),
     )
     ret = lax.all_to_all(ret, "expert", split_axis=0, concat_axis=0, tiled=True)
+    if joined:
+        share = call(
+            functools.partial(share_kernel, slots), [(shares[0].shape, bf16)], ret
+        )[0]
+        share = lax.all_to_all(share, "expert", split_axis=0, concat_axis=0, tiled=True)
+    block_out = call(
+        functools.partial(last_kernel, slots), [((col, tok), bf16, 1)], far(ret), far(side), far(gate), far(residual)
+    )[0]
     in_weight_grad, out_weight_grad = call(
         weights_kernel, [((width, width), f32, 1)] * 2, far(rows), far(hidden), far(before_grad), far(back_rows)
     )
     if joined:
-        normed_all = call(turn_kernel, [((groups * tok, width), bf16, 1)], far(all_in), far(packed))[0]
-        q_grad, k_grad, v_grad, output_grad, block_out, router_grad, table_grad, gain_grads, aux_loss = call(
-            functools.partial(products_kernel, slots),
+        normed_all = call(turn_kernel, [((groups * tok, width), bf16, 1)], Split(all_in, groups), Split(packed, heads))[0]
+        q_grad, k_grad, v_grad, output_grad, router_grad, table_grad, gain_grads, aux_loss = call(
+            products_kernel,
             [((col, width), f32, 1)] * 4
-            + [((col, tok), bf16), ((experts, width), f32), ((heads_here, bucket_count), f32)]
-            + [((16, 256), f32), ((1, 1), f32)],
-            far(late_all), far(normed_all), ret, far(buckets_row), far(stats), far(side), far(gate), far(residual),
+            + [((experts, width), f32), ((heads_here, bucket_count), f32), ((8, 256), f32), ((1, 1), f32)],
+            Split(late_all, groups), Split(normed_all, groups), share, far(buckets_row), far(stats),
         )
     else:
-        block_out = call(
-            functools.partial(last_kernel, slots), [((col, tok), bf16)], ret, far(side), far(gate), far(residual)
-        )[0]
         gain = packed[:, 2 * col : 2 * col + 2].reshape(heads, 256)[:, :col].reshape(width, 1)
         x = packed[:, :col].reshape(width, tok).astype(f32)
         normed = (x * token_scale(x) * gain.astype(f32)).astype(bf16)
@@ -615,14 +674,14 @@
         offsets = unfold_lanes(sums[16:32], 2)[:heads_here, : 2 * tok - 1]
         hot = (buckets[None, :] == jnp.arange(bucket_count)[:, None]).astype(f32)
         table_grad = mm(offsets, hot, nt, highest)
-        gain_grads = jnp.concatenate([unfold_lanes(sums[:16], 2), unfold_lanes(gain_one, 2)], axis=0)
+        gain_grads = unfold_lanes(sums[:16] + gain_one, 2)
         probs = gain_grads[1, :experts] + gain_grads[2, :experts]
         aux_loss = experts * jnp.sum(stats[:, 0] * probs) / (valid_total * valid_total)
     return (
         block_out.T,
         input_grad.T,
         aux_loss.reshape(()),
-        gain_grads[8, :col],
+        gain_grads[3, :col],
         q_grad.T,
         k_grad.T,
         v_grad.T,

time: 147 us -> 145 us (0.986)
  waiting for transfers between devices: 10.8 us -> 0.71 us
  blocking collectives: 83.3 us -> 89 us
  Pallas kernels: 30.5 us -> 33.7 us
    all_to_all x1, waiting for transfers between devices: 10.1 us -> 0.01 us  [shards(): lax.all_to_all(share, 'expert', split_axis=0, concat_axis=0, tiled=True)]
    all_to_all x1, blocking collectives: 14.4 us -> 20 us  [shards(): ret = lax.all_to_all(ret, 'expert', split_axis=0, concat_axis=0, tiled=True)]
    pallas_call x9 -> x11, Pallas kernels: 30.5 us -> 33.7 us  [call(): pl.pallas_call(run, out_shape=shapes, in_specs=in_specs, **extra, compile...]
  transfers between devices with their start and end apart: 3 -> 3, of which waited for: 1 -> 0; matrix products, arithmetic and copies ran while one was open for 2% -> 2% of each run, Pallas kernels for 18% -> 20%
where the time goes in v9:
time: 145 us
  blocking collectives  89 us (61%)
  Pallas kernels  33.7 us (23%)
  between operations  14.8 us (10%)
  starting transfers between devices  3.51 us (2%)
  local copies, waits for them, and re-layouts  2 us (1%)
    pallas_call x11, Pallas kernels, call(): pl.pallas_call(run, out_shape=shapes, in_specs=in_specs, **extra, compile...  33.7 us
    all_to_all x1, blocking collectives, shards(): ret = lax.all_to_all(ret, 'expert', split_axis=0, concat_axis=0, tiled=True)  20 us
    all_to_all x1, blocking collectives, shards(): lax.all_to_all(back, ('expert', 'head'), split_axis=0, concat_axis=0, til...  15.3 us
    all_to_all x1, blocking collectives, shards(): lax.all_to_all(send, 'expert', split_axis=0, concat_axis=0, tiled=True)  13.5 us
    all_to_all x1, blocking collectives, shards(): lax.all_to_all(first, 'head', split_axis=0, concat_axis=0, tiled=True)  11.1 us
    all_gather x1, blocking collectives, shards(): lax.all_gather(jnp.concatenate([inputs.T, out_grad.T, gains], axis=0), 'h...  8.01 us
    all_to_all x1, blocking collectives, shards(): lax.all_to_all(branch, 'head', split_axis=0, concat_axis=0, tiled=True)  7.69 us
    all_gather x1, blocking collectives, shards(): quarters = lax.all_gather(quarter.reshape(total, 2 * col), 'head')  7.12 us
  transfers between devices with their start and end apart: 3, of which 0 were waited for; matrix products, arithmetic and copies ran while one was open for 2% of the time, Pallas kernels for 20%

profile of v9, /device:TPU:0, one launch (start us, length us, event | category | flops | bytes accessed | tf_op | source)
XLA Modules:
  0.0 144.6 jit_solution(1690858402970675173)
XLA Ops:
  7.2 0.0 all-gather.9.cloned.1.call-start
  7.2 0.7 all-gather.9.cloned.1.call-update
  7.9 0.0 all-gather.7.cloned.1.call-start
  8.6 1.4 concatenate.6
  10.0 0.1 pad_add_fusion.refs_0_
  10.1 0.8 pad_maximum_fusion
  11.0 8.0 %all-gather = bf16[1600,128]{1,0:T(8,128)(2,1)S(1)} all-gather(bf16[400,128]{1,0:T(8,128)(2,1)S(1)} %pad_maximum_fusion), channel_id=2, replica_groups=mesh['expert'=8,'head'=4] {'head'}, dimensions={0}, use_global_device_ids=true | all-gather | bytes 512000 | tf_op jit(solution)/shard_map/all_gather | solution.py:582
  19.0 0.0 copy-start
  19.0 3.5 %shard_map.246 = (bf16[3,192,128]{2,1,0:T(8,128)(2,1)}, f32[3,128,128]{2,1,0:T(8,128)}, bf16[192,128]{1,0:T(8,128)(2,1)}, bf16[4,192,128]{2,1,0:T(8,128)(2,1)S(1)}) custom-call(s32[3]{0:T(128)S(1)} %pad_add_fusion.refs_0_, bf16[4,400,128]{2,1,0:T(8,128)(2,1)S(1)} %bitcast.31, bf16[192,768]{1,0:T(8,128)(2,1)} %bitcast.67, bf16[192,768]{1,0:T(8,128)(2,1)} %bitcast.69, ...), custom_call_target="tpu_custom_call" | custom-call | tf_op jit(solution)/shard_map/pallas_call | solution.py:83
  22.5 7.7 %all_to_all.30.refs_1_ = bf16[4,192,128]{2,1,0:T(8,128)(2,1)S(1)} all-to-all(bf16[4,192,128]{2,1,0:T(8,128)(2,1)S(1)} %get-tuple-element.47), channel_id=1, replica_groups=mesh['expert'=8,'head'=4] {'head'}, dimensions={0} | all-to-all | bytes 393216 | tf_op jit(solution)/shard_map/all_to_all | solution.py:594
  30.2 1.6 %shard_map.247 = (f32[192,128]{1,0:T(8,128)}, bf16[192,128]{1,0:T(8,128)(2,1)}, f32[8,128]{1,0:T(8,128)}, bf16[8,24,384]{2,1,0:T(8,128)(2,1)S(1)}) custom-call(s32[3]{0:T(128)S(1)} %pad_add_fusion.refs_0_, bf16[4,192,128]{2,1,0:T(8,128)(2,1)S(1)} %all_to_all.30.refs_1_, bf16[192,128]{1,0:T(8,128)(2,1)} %bitcast.76, bf16[192,128]{1,0:T(8,128)(2,1)} %bitcast.78, ...), custom_call_target="tpu_custom_call" | custom-call | tf_op jit(solution)/shard_map/pallas_call | solution.py:83
  31.7 13.5 %all_to_all.31 = bf16[8,24,384]{2,1,0:T(8,128)(2,1)S(1)} all-to-all(bf16[8,24,384]{2,1,0:T(8,128)(2,1)S(1)} %get-tuple-element.48), channel_id=1, replica_groups=mesh['expert'=8,'head'=4] {'expert'}, dimensions={0} | all-to-all | bytes 294912 | tf_op jit(solution)/shard_map/all_to_all | solution.py:600
  45.3 7.1 %all_gather.29.refs_1_.refs_2_.refs_3_.refs_4_ = bf16[4,192,384]{2,1,0:T(8,128)(2,1)} all-gather(bf16[1,192,384]{2,1,0:T(8,128)(2,1)S(1)} %bitcast.73), channel_id=1, replica_groups=mesh['expert'=8,'head'=4] {'head'}, dimensions={0}, use_global_device_ids=true | all-gather | bytes 737280 | tf_op jit(solution)/shard_map/all_gather | solution.py:601
  52.4 0.0 copy-done
  52.4 5.0 %shard_map.248 = (bf16[32,40,128]{2,1,0:T(8,128)(2,1)S(1)}, bf16[4,288,128]{2,1,0:T(8,128)(2,1)}, bf16[192,768]{1,0:T(8,128)(2,1)}, bf16[192,768]{1,0:T(8,128)(2...) custom-call(s32[3]{0:T(128)S(1)} %pad_add_fusion.refs_0_, ...), custom_call_target="tpu_custom_call" | custom-call | tf_op jit(solution)/shard_map/pallas_call | solution.py:83
  57.4 15.3 %all_to_all.32.refs_0_ = bf16[32,40,128]{2,1,0:T(8,128)(2,1)S(1)} all-to-all(bf16[32,40,128]{2,1,0:T(8,128)(2,1)S(1)} %get-tuple-element.49), channel_id=1, replica_groups=mesh['expert'=8,'head'=4] {'expert','head'}, dimensions={0} | all-to-all | bytes 655360 | tf_op jit(solution)/shard_map/all_to_all | solution.py:609
  72.7 1.8 %shard_map.249 = (bf16[384,128]{1,0:T(8,128)(2,1)S(1)}, f32[8,128]{1,0:T(8,128)}, f32[8,128]{1,0:T(8,128)}) custom-call(bf16[32,40,128]{2,1,0:T(8,128)(2,1)S(1)} %all_to_all.32.refs_0_, f32[8,128]{1,0:T(8,128)} %get-tuple-element.50.refs_1_, bf16[192,128]{1,0:T(8,128)(2,1)} %get-tuple-element.51.refs_2_), custom_call_target="tpu_custom_call" | custom-call | tf_op jit(solution)/shard_map/pallas_call | solution.py:83
  74.5 6.3 %all-gather.1 = bf16[1536,128]{1,0:T(8,128)(2,1)S(1)} all-gather(bf16[384,128]{1,0:T(8,128)(2,1)S(1)} %get-tuple-element.52), channel_id=3, replica_groups=mesh['expert'=8,'head'=4] {'head'}, dimensions={0}, use_global_device_ids=true | all-gather | bytes 491520 | tf_op jit(solution)/shard_map/all_gather | solution.py:615
  80.8 4.9 %shard_map.250 = (bf16[576,128]{1,0:T(8,128)(2,1)}, bf16[4,496,128]{2,1,0:T(8,128)(2,1)S(1)}, f32[192,128]{1,0:T(8,128)}, f32[8,128]{1,0:T(8,128)}, bf16[8,160,128]{2,1,0:T(8,128)(2,1)}) custom-call(s32[3]{0:T(128)S(1)} %pad_add_fusion.refs_0_, bf16[4,400,128]{2,1,0:T(8,128)(2,1)} %bitcast.33, bf16[4,384,128]{2,1,0:T(8,128)(2,1)S(1)} %bitcast.42, ...), custom_call_target="tpu_custom_call" | custom-call | tf_op jit(solution)/shard_map/pallas_call | solution.py:83
  85.7 0.0 all-gather.7.cloned.1.call-update
  85.7 11.1 %all_to_all.33.refs_1_ = bf16[4,496,128]{2,1,0:T(8,128)(2,1)S(1)} all-to-all(bf16[4,496,128]{2,1,0:T(8,128)(2,1)S(1)} %get-tuple-element.59), channel_id=1, replica_groups=mesh['expert'=8,'head'=4] {'head'}, dimensions={0} | all-to-all | bytes 1015808 | tf_op jit(solution)/shard_map/all_to_all | solution.py:636
  96.8 2.2 %shard_map.251 = (bf16[8,208,128]{2,1,0:T(8,128)(2,1)S(1)}, f32[16,128]{1,0:T(8,128)}, f32[192,128]{1,0:T(8,128)}) custom-call(s32[3]{0:T(128)S(1)} %pad_add_fusion.refs_0_, bf16[4,496,128]{2,1,0:T(8,128)(2,1)S(1)} %all_to_all.33.refs_1_, bf16[4,400,128]{2,1,0:T(8,128)(2,1)} %bitcast.34, bf16[4,400,128]{2,1,0:T(8,128)(2,1)} %bitcast.35, ...), custom_call_target="tpu_custom_call" | custom-call | tf_op jit(solution)/shard_map/pallas_call | solution.py:83
  98.9 20.0 %all_to_all.34.refs_0_ = bf16[8,208,128]{2,1,0:T(8,128)(2,1)S(1)} all-to-all(bf16[8,208,128]{2,1,0:T(8,128)(2,1)S(1)} %get-tuple-element.62), channel_id=1, replica_groups=mesh['expert'=8,'head'=4] {'expert'}, dimensions={0} | all-to-all | bytes 851968 | tf_op jit(solution)/shard_map/all_to_all | solution.py:645
  118.9 0.0 copy-start.1
  118.9 0.9 shard_map.254
  119.8 3.4 %all-to-all-start.5 = ((bf16[8,160,128]{2,1,0:T(8,128)(2,1)}), bf16[8,160,128]{2,1,0:T(8,128)(2,1)S(1)}, u32[]{:S(2)}, u32[]{:S(2)}) async-start(bf16[8,160,128]{2,1,0:T(8,128)(2,1)} %shard_map.254), calls=%async_computation.5 | async-start | bytes 655360 | tf_op jit(solution)/shard_map/all_to_all | solution.py:650
  123.2 4.0 %shard_map.256 = (f32[768,768]{1,0:T(8,128)}, f32[768,768]{1,0:T(8,128)}) custom-call(bf16[192,768]{1,0:T(8,128)(2,1)} %get-tuple-element.75.refs_0_, bf16[192,768]{1,0:T(8,128)(2,1)} %get-tuple-element.76.refs_1_, bf16[192,768]{1,0:T(8,128)(2,1)} %get-tuple-element.77.refs_2_, bf16[192,768]{1,0:T(8,128)(2,1)} %get-tuple-element.78.refs_3_), custom_call_target="tpu_custom_call" | custom-call | tf_op jit(solution)/shard_map/pallas_call | solution.py:83
  127.2 0.0 copy-done.1
  127.2 1.9 %shard_map.252 = bf16[192,128]{1,0:T(8,128)(2,1)} custom-call(bf16[8,208,128]{2,1,0:T(8,128)(2,1)} %copy-done.1, f32[8,128]{1,0:T(8,128)} %get-tuple-element.50.refs_1_, f32[8,128]{1,0:T(8,128)} %get-tuple-element.63.refs_2_, f32[192,128]{1,0:T(8,128)} %get-tuple-element.64.refs_3_), custom_call_target="tpu_custom_call" | custom-call | tf_op jit(solution)/shard_map/pallas_call | solution.py:83
  129.1 0.0 all-gather.9.cloned.1.call-done
  129.1 3.7 %shard_map.253.refs_8_.refs_9_.refs_10_.refs_11_.refs_12_.refs_13_.refs_14_.refs_15_ = bf16[1024,768]{1,0:T(8,128)(2,1)} custom-call(bf16[8,4,192,128]{3,2,1,0:T(8,128)(2,1)} %bitcast.43, bf16[8,4,192,128]{3,2,1,0:T(8,128)(2,1)} %bitcast.44, bf16[8,4,192,128]{3,2,1,0:T(8,128)(2,1)} %bitcast.45, bf16[8,4,192,128]{3,2,1,0:T(8,128)(2,1)} %bitcast.46, ...), custom_call_target="tpu_custom_call" | custom-call | tf_op jit(solution)/shard_map/pallas_call | solution.py:83
  132.8 0.0 all-to-all-done.5.refs_16_
  132.9 0.0 all-gather.7.cloned.1.call-done
  132.9 4.3 %shard_map.255 = (f32[192,768]{1,0:T(8,128)}, f32[192,768]{1,0:T(8,128)}, f32[192,768]{1,0:T(8,128)}, f32[192,768]{1,0:T(8,128)}, f32[8,768]{1,0:T(8,128)}, /*in...) custom-call(bf16[8,576,128]{2,1,0:T(8,128)(2,1)} %bitcast.51, bf16[8,576,128]{2,1,0:T(8,128)(2,1)} %bitcast.52, ...), custom_call_target="tpu_custom_call" | custom-call | tf_op jit(solution)/shard_map/pallas_call | solution.py:83
  137.2 0.6 fusion
  (2 shorter events, 0.0 us)
Async XLA Ops:
  7.2 121.9 %all-gather.9.cloned.1.call-start = ((), (), s32[]{:S(2)}) async-start(), calls=%async_computation.7 | async-start | bytes 1622016 | tf_op jit(solution)/shard_map/all_gather | solution.py:584
  7.9 125.0 %all-gather.7.cloned.1.call-start = ((), (), s32[]{:S(2)}) async-start(), calls=%async_computation.6 | async-start | bytes 1327104 | tf_op jit(solution)/shard_map/all_gather | solution.py:634
  19.0 33.4 %copy-start = (bf16[1600,128]{1,0:T(8,128)(2,1)}, bf16[1600,128]{1,0:T(8,128)(2,1)S(1)}, u32[]{:S(2)}) copy-start(bf16[1600,128]{1,0:T(8,128)(2,1)S(1)} %all-gather) | copy-start | bytes 1228804
  118.9 8.3 %copy-start.1 = (bf16[8,208,128]{2,1,0:T(8,128)(2,1)}, bf16[8,208,128]{2,1,0:T(8,128)(2,1)S(1)}, u32[]{:S(2)}) copy-start(bf16[8,208,128]{2,1,0:T(8,128)(2,1)S(1)} %all_to_all.34.refs_0_) | copy-start | bytes 1277956
  119.8 13.1 %all-to-all-start.5 = ((bf16[8,160,128]{2,1,0:T(8,128)(2,1)}), bf16[8,160,128]{2,1,0:T(8,128)(2,1)S(1)}, u32[]{:S(2)}, u32[]{:S(2)}) async-start(bf16[8,160,128]{2,1,0:T(8,128)(2,1)} %shard_map.254), calls=%async_computation.5 | async-start | bytes 655360 | tf_op jit(solution)/shard_map/all_to_all | solution.py:650
Sparse Core Ops, SparseCore 0:
  10.9 58.9 all-gather.8
  85.8 40.6 all-gather.6

commit v10 on v9

--- a/solution.py
+++ b/solution.py
@@ -22,71 +22,32 @@
     return lax.dot_general(left, right, (dims, ((), ())), precision=precision, preferred_element_type=f32)
 
 
-class Pieces:
-    def __init__(self, refs):
-        self.refs, self.size = refs, refs[0].shape[0]
-        self.shape = (self.size * len(refs),) + tuple(refs[0].shape[1:])
-
-    def __getitem__(self, index):
-        if index is Ellipsis:
-            return jnp.concatenate([ref[...] for ref in self.refs], axis=0)
-        at, rest = (index[0], index[1:]) if isinstance(index, tuple) else (index, ())
-        return self.refs[at // self.size][(at % self.size,) + rest]
-
-
-class Split:
-    def __init__(self, array, count):
-        self.array, self.count = array, count
-
-
-def block_of(array, count, i):
-    shape = (array.shape[0] // count,) + array.shape[1:]
-    return pl.BlockSpec(shape, lambda step: (i,) + (0,) * (array.ndim - 1))
-
-
-def whole_map(rank):
-    return lambda step: (0,) * rank
-
-
 def call(body, outs, *args):
-    in_specs, operands, counts = [], [], []
-    for a in args:
-        if isinstance(a, Split):
-            held = far(a.array)
-            in_specs += [block_of(held, a.count, i) for i in range(a.count)]
-            operands += [held] * a.count
-            counts.append(a.count)
-            continue
-        whole = a.dtype == jnp.int32 and a.ndim == 1
-        in_specs.append(pl.BlockSpec(memory_space=pltpu.SMEM) if whole else pl.BlockSpec())
-        operands.append(a)
-        counts.append(0)
+    scalar_memory = pl.BlockSpec(memory_space=pltpu.SMEM)
+    in_specs = [scalar_memory if a.dtype == jnp.int32 and a.ndim == 1 else pl.BlockSpec() for a in args]
     shapes = []
     for shape, kind, *remote in outs:
         shapes.append(pltpu.HBM(shape, kind) if remote else jax.ShapeDtypeStruct(shape, kind))
-
-    def run(*refs):
-        ins, at = [], 0
-        for count in counts:
-            ins.append(Pieces(refs[at : at + count]) if count else refs[at])
-            at += max(count, 1)
-        body(*ins, *refs[at:])
-
-    extra = {}
-    if any(counts):
-        extra["grid"] = (1,)
-        extra["out_specs"] = [pl.BlockSpec(shape.shape, whole_map(len(shape.shape))) for shape in shapes]
-        in_specs = [
-            pl.BlockSpec(a.shape, whole_map(a.ndim)) if spec.block_shape is None and spec.memory_space is None else spec
-            for spec, a in zip(in_specs, operands)
-        ]
     return pl.pallas_call(
-        run,
+        body,
         out_shape=shapes,
         in_specs=in_specs,
-        **extra,
         compiler_params=pltpu.CompilerParams(vmem_limit_bytes=40 * 1024 * 1024),
-    )(*operands)
+    )(*args)
+
+
+def grid_call(body, steps, outs, *args):
+    def spec(block, along):
+        return pl.BlockSpec(block, lambda step: tuple(step if i == along else 0 for i in range(len(block))))
+
+    return pl.pallas_call(
+        body,
+        grid=(steps,),
+        out_shape=[pltpu.HBM(*kind) for kind, _, _ in outs],
+        in_specs=[spec(block, along) for _, block, along in args],
+        out_specs=[spec(block, along) for _, block, along in outs],
+        compiler_params=pltpu.CompilerParams(vmem_limit_bytes=40 * 1024 * 1024),
+    )(*(far(array) for array, _, _ in args))
 
 
 def far(array):
@@ -99,7 +60,10 @@
 
 def gain_columns(block):
     turned = jnp.transpose(block.astype(f32))
-    return [jnp.concatenate([turned[:, i : i + 1], turned[:64, i + 1 : i + 2]], axis=0) for i in (0, 2)]
+    return [
+        jnp.concatenate([turned[:, 0:1], turned[:64, 1:2]], axis=0),
+        jnp.concatenate([turned[64:, 1:2], turned[:, 2:3]], axis=0),
+    ]
 
 
 def all_gains(packed):
@@ -262,11 +226,11 @@
         send_ref[e] = jnp.where(spare, counts[e : e + 1], block).astype(bf16)
 
 
-def gain_row(packed, first, line):
+def second_gain_row(packed, first):
     pieces = []
     for i in range(packed.shape[0]):
         block = packed[i, first : first + 16, :].astype(f32)
-        pieces += [block[line : line + 1, :], block[line + 1 : line + 2, :64]]
+        pieces += [block[1:2, 64:], block[2:3, :]]
     return jnp.concatenate(pieces, axis=1)
 
 
@@ -284,7 +248,7 @@
     residual = jnp.concatenate([block[:, :col] for block in parts], axis=1)
     grads = jnp.concatenate([block[:, col:] for block in parts], axis=1)
     inverse = lax.rsqrt(jnp.sum(residual * residual, axis=1, keepdims=True) * (1.0 / width) + eps)
-    rows = (residual * inverse * gain_row(packed, 2 * col, 2)).astype(bf16)
+    rows = (residual * inverse * second_gain_row(packed, 2 * col)).astype(bf16)
     rows_ref[...] = rows
     hidden, slope = gelu_parts(mm(rows, w_in[...]))
     hidden = hidden.astype(bf16)
@@ -496,11 +460,9 @@
 
 
 def turn_kernel(all_in, packed, normed_ref):
-    groups, heads, col, tok = all_in.shape
+    x = jnp.concatenate([all_in[0, i].astype(f32) for i in range(all_in.shape[1])], axis=0)
     gain = all_gains(packed)[0]
-    for b in range(groups):
-        x = jnp.concatenate([all_in[b, i].astype(f32) for i in range(heads)], axis=0)
-        normed_ref[b * tok : (b + 1) * tok, :] = jnp.transpose(x * token_scale(x) * gain).astype(bf16)
+    normed_ref[...] = jnp.transpose(x * token_scale(x) * gain).astype(bf16)
 
 
 def products_kernel(
@@ -508,29 +470,32 @@
 ):
     groups = came.shape[0]
     col = q_ref.shape[0]
-    experts = router_ref.shape[0]
-    size = col // groups
-    shares = [came[b].astype(f32) for b in range(groups)]
-    chunk = shares[0].shape[0] - 6 * size
-    for b in range(groups):
-        out_ref[b * size : (b + 1) * size, :] = unfold_lanes(shares[b][chunk:], 6)
     joined = jnp.concatenate([late[b] for b in range(groups)], axis=1)
     product = mm(joined, normed[...])
     for i, ref in enumerate((q_ref, k_ref, v_ref)):
         ref[...] = product[i * col : (i + 1) * col]
-    small = jnp.concatenate([share[:chunk] for share in shares], axis=0)
-    gains = unfold_lanes(small[:16], 2)
-    gains_ref[...] = gains
-    probs = gains[1:2, :experts] + gains[2:3, :experts]
-    same = lanes((experts, experts)) == sublanes((experts, experts))
-    share = jnp.sum(jnp.where(same, stats[:, 0:1] * probs, 0.0), axis=0, keepdims=True)
-    valid_total = 3 * normed.shape[0] // 4
-    aux_ref[...] = jnp.sum(share, axis=1, keepdims=True) * (experts / (valid_total * valid_total))
-    span = buckets.shape[1]
-    hot = (sublanes((table_ref.shape[1], span)) == buckets[...]).astype(f32)
-    offsets = unfold_lanes(small[16:32], 2)[:, :span]
-    table_ref[...] = mm(offsets, hot, nt, highest)[: table_ref.shape[0]]
-    router_ref[...] = unfold_lanes(small[32 : 32 + 6 * experts], 6)
+
+    @pl.when(pl.program_id(0) == 0)
+    def _():
+        experts = router_ref.shape[0]
+        size = col // groups
+        shares = [came[b].astype(f32) for b in range(groups)]
+        chunk = shares[0].shape[0] - 6 * size
+        for b in range(groups):
+            out_ref[b * size : (b + 1) * size, :] = unfold_lanes(shares[b][chunk:], 6)
+        small = jnp.concatenate([share[:chunk] for share in shares], axis=0)
+        gains = unfold_lanes(small[:16], 2)
+        gains_ref[...] = gains
+        probs = gains[1:2, :experts] + gains[2:3, :experts]
+        same = lanes((experts, experts)) == sublanes((experts, experts))
+        share = jnp.sum(jnp.where(same, stats[:, 0:1] * probs, 0.0), axis=0, keepdims=True)
+        valid_total = 3 * normed.shape[0] // 4
+        aux_ref[...] = jnp.sum(share, axis=1, keepdims=True) * (experts / (valid_total * valid_total))
+        span = buckets.shape[1]
+        hot = (sublanes((table_ref.shape[1], span)) == buckets[...]).astype(f32)
+        offsets = unfold_lanes(small[16:32], 2)[:, :span]
+        table_ref[...] = mm(offsets, hot, nt, highest)[: table_ref.shape[0]]
+        router_ref[...] = unfold_lanes(small[32 : 32 + 6 * experts], 6)
 
 
 def few_experts():
@@ -577,9 +542,9 @@
     scalars = jnp.stack([lengths[0], me_head.astype(jnp.int32), me_expert.astype(jnp.int32)])
     buckets_row = buckets[None]
 
-    space = jnp.zeros((64,), bf16)
-    gains = jnp.concatenate([gain_attn, space, gain_ffn, space, jnp.zeros((1536,), bf16)]).reshape(16, 128)
-    packed = lax.all_gather(jnp.concatenate([inputs.T, out_grad.T, gains], axis=0), "head")
+    gains = jnp.concatenate([gain_attn, gain_ffn]).reshape(3, 128)
+    gains = jnp.concatenate([inputs.T, out_grad.T, gains, jnp.zeros((13, 128), bf16)], axis=0)
+    packed = lax.all_gather(gains, "head")
     if joined:
         all_in = lax.all_gather(inputs.T, ("expert", "head")).reshape(groups, heads, col, tok)
     qkv, weights, attended, branch = call(
@@ -604,7 +569,7 @@
         functools.partial(expert_kernel, capacity),
         [((experts * heads, folded_rows(slots), 128), bf16), ((heads, total * 3 // 2, 128), bf16, 1)]
         + [((total, width), bf16, 1)] * 4,
-        scalars, Split(quarters, heads), far(packed), Split(w_in, 4), Split(w_out, 4), far(router_rows),
+        scalars, quarters, far(packed), far(w_in), far(w_out), far(router_rows),
     )
     came = lax.all_to_all(back, ("expert", "head"), split_axis=0, concat_axis=0, tiled=True)
     grad_own, gate_grad, stats = call(
@@ -627,7 +592,7 @@
         ),
         scalars, far(packed), expert_grad, far(gate_grad), far(stats), far(routes_row),
         far(router_rows), far(w_output), far(weights), far(qkv), far(wq), far(wk), far(wv), far(attended),
-        Split(part, heads),
+        far(part),
     )
 
     if joined:
@@ -640,7 +605,7 @@
             ((experts, 2 * slots + (shares[0].shape[1] if joined else 0), 128), bf16),
             ((16, 128), f32, 1), ((col, tok), f32, 1),
         ],
-        scalars, first, Split(packed, heads), far(residual_grad_own), *([Split(shares[0], groups)] if joined else []),
+        scalars, first, far(packed), far(residual_grad_own), *([far(shares[0])] if joined else []),
     )
     ret = lax.all_to_all(ret, "expert", split_axis=0, concat_axis=0, tiled=True)
     if joined:
@@ -651,19 +616,37 @@
     block_out = call(
         functools.partial(last_kernel, slots), [((col, tok), bf16, 1)], far(ret), far(side), far(gate), far(residual)
     )[0]
-    in_weight_grad, out_weight_grad = call(
-        weights_kernel, [((width, width), f32, 1)] * 2, far(rows), far(hidden), far(before_grad), far(back_rows)
+    third = width // 3
+    in_weight_grad, out_weight_grad = grid_call(
+        weights_kernel,
+        3,
+        [(((width, width), f32), (third, width), 0)] * 2,
+        (rows, (total, third), 1), (hidden, (total, third), 1),
+        (before_grad, (total, width), None), (back_rows, (total, width), None),
     )
     if joined:
-        normed_all = call(turn_kernel, [((groups * tok, width), bf16, 1)], Split(all_in, groups), Split(packed, heads))[0]
-        q_grad, k_grad, v_grad, output_grad, router_grad, table_grad, gain_grads, aux_loss = call(
+        (normed_all,) = grid_call(
+            turn_kernel,
+            groups,
+            [(((groups * tok, width), bf16), (tok, width), 0)],
+            (all_in, (1, heads, col, tok), 0), (packed, packed.shape, None),
+        )
+        q_grad, k_grad, v_grad, output_grad, router_grad, table_grad, gain_grads, aux_loss = grid_call(
             products_kernel,
-            [((col, width), f32, 1)] * 4
-            + [((experts, width), f32), ((heads_here, bucket_count), f32), ((8, 256), f32), ((1, 1), f32)],
-            Split(late_all, groups), Split(normed_all, groups), share, far(buckets_row), far(stats),
+            3,
+            [(((col, width), f32), (col, third), 1)] * 3
+            + [
+                (((col, width), f32), (col, width), None),
+                (((experts, width), f32), (experts, width), None),
+                (((heads_here, bucket_count), f32), (heads_here, bucket_count), None),
+                (((8, 256), f32), (8, 256), None),
+                (((1, 1), f32), (1, 1), None),
+            ],
+            (late_all, late_all.shape, None), (normed_all, (groups * tok, third), 1),
+            (share, share.shape, None), (buckets_row, buckets_row.shape, None), (stats, stats.shape, None),
         )
     else:
-        gain = packed[:, 2 * col : 2 * col + 2].reshape(heads, 256)[:, :col].reshape(width, 1)
+        gain = packed[:, 2 * col : 2 * col + 3].reshape(heads, 2 * col)[:, :col].reshape(width, 1)
         x = packed[:, :col].reshape(width, tok).astype(f32)
         normed = (x * token_scale(x) * gain.astype(f32)).astype(bf16)
         products = [mm(late[i * col : (i + 1) * col], normed, nt) for i in range(3)]

time: 145 us -> 150 us (1.034)
  Pallas kernels: 33.7 us -> 37.5 us
    pallas_call x11, Pallas kernels: 33.7 us -> 37.5 us  [the longest x8 21.4 us: call(): pl.pallas_call(body, out_shape=shapes, in_specs=in_specs, compiler_params...]
  transfers between devices with their start and end apart: 3 -> 3, of which waited for: 0 -> 0; matrix products, arithmetic and copies ran while one was open for 2% -> 1% of each run, Pallas kernels for 20% -> 22%
where the time goes in v10:
time: 150 us; the launch traced here: 149 us
  blocking collectives  88.9 us (59%)
  Pallas kernels  37.5 us (25%)
  between operations  14.8 us (10%)
  starting transfers between devices  3.51 us (2%)
  local copies, waits for them, and re-layouts  2.13 us (1%)
  other arithmetic  1.76 us (1%)
    pallas_call x8, Pallas kernels, call(): pl.pallas_call(body, out_shape=shapes, in_specs=in_specs, compiler_params...  21.4 us
    all_to_all x1, blocking collectives, shards(): ret = lax.all_to_all(ret, 'expert', split_axis=0, concat_axis=0, tiled=True)  19.8 us
    pallas_call x3, Pallas kernels, grid_call(): pl.pallas_call(body, grid=(steps,), out_shape=[pltpu.HBM(*kind) for kind,...  16.1 us
    all_to_all x1, blocking collectives, shards(): lax.all_to_all(back, ('expert', 'head'), split_axis=0, concat_axis=0, til...  15.7 us
    all_to_all x1, blocking collectives, shards(): lax.all_to_all(send, 'expert', split_axis=0, concat_axis=0, tiled=True)  13.7 us
    all_to_all x1, blocking collectives, shards(): lax.all_to_all(first, 'head', split_axis=0, concat_axis=0, tiled=True)  11.1 us
    all_gather x1, blocking collectives, shards(): packed = lax.all_gather(gains, 'head')  8.02 us
    all_to_all x1, blocking collectives, shards(): lax.all_to_all(branch, 'head', split_axis=0, concat_axis=0, tiled=True)  7.69 us
  transfers between devices with their start and end apart: 3, of which 0 were waited for; matrix products, arithmetic and copies ran while one was open for 1% of the time, Pallas kernels for 22%

profile of v10, /device:TPU:0, one launch (start us, length us, event | category | flops | bytes accessed | tf_op | source)
XLA Modules:
  0.0 149.2 jit_solution(11428633843665877662)
XLA Ops:
  7.2 0.0 all-gather.9.cloned.1.call-start
  7.2 0.7 all-gather.9.cloned.1.call-update
  7.9 0.0 all-gather.7.cloned.1.call-start
  8.6 0.1 pad.3.clone
  8.7 0.1 pad_add_fusion.scalars
  8.8 0.7 maximum_bitcast_fusion
  9.5 0.9 maximum_maximum_fusion
  10.5 8.0 %all-gather = bf16[1600,128]{1,0:T(8,128)(2,1)S(1)} all-gather(bf16[400,128]{1,0:T(8,128)(2,1)S(1)} %maximum_maximum_fusion), channel_id=2, replica_groups=mesh['expert'=8,'head'=4] {'head'}, dimensions={0}, use_global_device_ids=true | all-gather | bytes 512000 | tf_op jit(solution)/shard_map/all_gather | solution.py:547
  18.5 0.0 copy-start
  18.5 3.5 %shard_map.246 = (bf16[3,192,128]{2,1,0:T(8,128)(2,1)}, f32[3,128,128]{2,1,0:T(8,128)}, bf16[192,128]{1,0:T(8,128)(2,1)}, bf16[4,192,128]{2,1,0:T(8,128)(2,1)S(1)}) custom-call(s32[3]{0:T(128)S(1)} %pad_add_fusion.scalars, bf16[4,400,128]{2,1,0:T(8,128)(2,1)S(1)} %bitcast.32, bf16[192,768]{1,0:T(8,128)(2,1)} %bitcast.39, bf16[192,768]{1,0:T(8,128)(2,1)} %bitcast.41, ...), custom_call_target="tpu_custom_call" | custom-call | tf_op jit(solution)/shard_map/pallas_call | solution.py:31
  22.0 7.7 %all_to_all.30.came = bf16[4,192,128]{2,1,0:T(8,128)(2,1)S(1)} all-to-all(bf16[4,192,128]{2,1,0:T(8,128)(2,1)S(1)} %get-tuple-element.47), channel_id=1, replica_groups=mesh['expert'=8,'head'=4] {'head'}, dimensions={0} | all-to-all | bytes 393216 | tf_op jit(solution)/shard_map/all_to_all | solution.py:559
  29.7 1.6 %shard_map.247 = (f32[192,128]{1,0:T(8,128)}, bf16[192,128]{1,0:T(8,128)(2,1)}, f32[8,128]{1,0:T(8,128)}, bf16[8,24,384]{2,1,0:T(8,128)(2,1)S(1)}) custom-call(s32[3]{0:T(128)S(1)} %pad_add_fusion.scalars, bf16[4,192,128]{2,1,0:T(8,128)(2,1)S(1)} %all_to_all.30.came, bf16[192,128]{1,0:T(8,128)(2,1)} %bitcast.51, bf16[192,128]{1,0:T(8,128)(2,1)} %bitcast.53, ...), custom_call_target="tpu_custom_call" | custom-call | tf_op jit(solution)/shard_map/pallas_call | solution.py:31
  31.3 13.7 %all_to_all.31 = bf16[8,24,384]{2,1,0:T(8,128)(2,1)S(1)} all-to-all(bf16[8,24,384]{2,1,0:T(8,128)(2,1)S(1)} %get-tuple-element.48), channel_id=1, replica_groups=mesh['expert'=8,'head'=4] {'expert'}, dimensions={0} | all-to-all | bytes 294912 | tf_op jit(solution)/shard_map/all_to_all | solution.py:565
  45.0 6.7 %all_gather.29.quarters = bf16[4,192,384]{2,1,0:T(8,128)(2,1)S(1)} all-gather(bf16[1,192,384]{2,1,0:T(8,128)(2,1)S(1)} %bitcast.48), channel_id=1, replica_groups=mesh['expert'=8,'head'=4] {'head'}, dimensions={0}, use_global_device_ids=true | all-gather | bytes 737280 | tf_op jit(solution)/shard_map/all_gather | solution.py:566
  51.7 0.0 copy-done
  51.7 4.8 %shard_map.248 = (bf16[32,40,128]{2,1,0:T(8,128)(2,1)S(1)}, bf16[4,288,128]{2,1,0:T(8,128)(2,1)}, bf16[192,768]{1,0:T(8,128)(2,1)}, bf16[192,768]{1,0:T(8,128)(2...) custom-call(s32[3]{0:T(128)S(1)} %pad_add_fusion.scalars, bf16[4,192,384]{2,1,0:T(8,128)(2,1)S(1)} %all_gather.29.quarters, ...), custom_call_target="tpu_custom_call" | custom-call | tf_op jit(solution)/shard_map/pallas_call | solution.py:31
  56.5 15.7 %all_to_all.32.came = bf16[32,40,128]{2,1,0:T(8,128)(2,1)S(1)} all-to-all(bf16[32,40,128]{2,1,0:T(8,128)(2,1)S(1)} %get-tuple-element.49), channel_id=1, replica_groups=mesh['expert'=8,'head'=4] {'expert','head'}, dimensions={0} | all-to-all | bytes 655360 | tf_op jit(solution)/shard_map/all_to_all | solution.py:574
  72.2 1.8 %shard_map.249 = (bf16[384,128]{1,0:T(8,128)(2,1)S(1)}, f32[8,128]{1,0:T(8,128)}, f32[8,128]{1,0:T(8,128)}) custom-call(bf16[32,40,128]{2,1,0:T(8,128)(2,1)S(1)} %all_to_all.32.came, f32[8,128]{1,0:T(8,128)} %get-tuple-element.50.side, bf16[192,128]{1,0:T(8,128)(2,1)} %get-tuple-element.51.low), custom_call_target="tpu_custom_call" | custom-call | tf_op jit(solution)/shard_map/pallas_call | solution.py:31
  74.0 6.1 %all-gather.1 = bf16[1536,128]{1,0:T(8,128)(2,1)S(1)} all-gather(bf16[384,128]{1,0:T(8,128)(2,1)S(1)} %get-tuple-element.52), channel_id=3, replica_groups=mesh['expert'=8,'head'=4] {'head'}, dimensions={0}, use_global_device_ids=true | all-gather | bytes 491520 | tf_op jit(solution)/shard_map/all_gather | solution.py:580
  80.1 4.8 %shard_map.250 = (bf16[576,128]{1,0:T(8,128)(2,1)}, bf16[4,496,128]{2,1,0:T(8,128)(2,1)S(1)}, f32[192,128]{1,0:T(8,128)}, f32[8,128]{1,0:T(8,128)}, bf16[8,160,128]{2,1,0:T(8,128)(2,1)}) custom-call(s32[3]{0:T(128)S(1)} %pad_add_fusion.scalars, bf16[4,400,128]{2,1,0:T(8,128)(2,1)} %bitcast.34, bf16[4,384,128]{2,1,0:T(8,128)(2,1)S(1)} %bitcast.37, ...), custom_call_target="tpu_custom_call" | custom-call | tf_op jit(solution)/shard_map/pallas_call | solution.py:31
  85.0 0.0 all-gather.7.cloned.1.call-update
  85.0 11.1 %all_to_all.33.came = bf16[4,496,128]{2,1,0:T(8,128)(2,1)S(1)} all-to-all(bf16[4,496,128]{2,1,0:T(8,128)(2,1)S(1)} %get-tuple-element.59), channel_id=1, replica_groups=mesh['expert'=8,'head'=4] {'head'}, dimensions={0} | all-to-all | bytes 1015808 | tf_op jit(solution)/shard_map/all_to_all | solution.py:601
  96.1 2.1 %shard_map.251 = (bf16[8,208,128]{2,1,0:T(8,128)(2,1)S(1)}, f32[16,128]{1,0:T(8,128)}, f32[192,128]{1,0:T(8,128)}) custom-call(s32[3]{0:T(128)S(1)} %pad_add_fusion.scalars, bf16[4,496,128]{2,1,0:T(8,128)(2,1)S(1)} %all_to_all.33.came, bf16[4,400,128]{2,1,0:T(8,128)(2,1)} %bitcast.35, f32[192,128]{1,0:T(8,128)} %get-tuple-element.60.own, ...), custom_call_target="tpu_custom_call" | custom-call | tf_op jit(solution)/shard_map/pallas_call | solution.py:31
  98.2 19.8 %all_to_all.34.came = bf16[8,208,128]{2,1,0:T(8,128)(2,1)S(1)} all-to-all(bf16[8,208,128]{2,1,0:T(8,128)(2,1)S(1)} %get-tuple-element.62), channel_id=1, replica_groups=mesh['expert'=8,'head'=4] {'expert'}, dimensions={0} | all-to-all | bytes 851968 | tf_op jit(solution)/shard_map/all_to_all | solution.py:610
  118.0 0.0 copy-start.1
  118.0 0.9 shard_map.254
  118.9 3.4 %all-to-all-start.5 = ((bf16[8,160,128]{2,1,0:T(8,128)(2,1)}), bf16[8,160,128]{2,1,0:T(8,128)(2,1)S(1)}, u32[]{:S(2)}, u32[]{:S(2)}) async-start(bf16[8,160,128]{2,1,0:T(8,128)(2,1)} %shard_map.254), calls=%async_computation.5 | async-start | bytes 655360 | tf_op jit(solution)/shard_map/all_to_all | solution.py:615
  122.3 4.2 %shard_map.256 = (f32[768,768]{1,0:T(8,128)}, f32[768,768]{1,0:T(8,128)}) custom-call(bf16[192,768]{1,0:T(8,128)(2,1)} %get-tuple-element.75.rows_ref, bf16[192,768]{1,0:T(8,128)(2,1)} %get-tuple-element.76.hidden, bf16[192,768]{1,0:T(8,128)(2,1)} %get-tuple-element.77.before, bf16[192,768]{1,0:T(8,128)(2,1)} %get-tuple-element.78.grads), custom_call_target="tpu_custom_call" | custom-call | tf_op jit(solution)/shard_map/pallas_call | solution.py:43
  126.6 0.0 copy-done.1
  126.6 1.9 %shard_map.252 = bf16[192,128]{1,0:T(8,128)(2,1)} custom-call(bf16[8,208,128]{2,1,0:T(8,128)(2,1)} %copy-done.1, f32[8,128]{1,0:T(8,128)} %get-tuple-element.50.side, f32[8,128]{1,0:T(8,128)} %get-tuple-element.63.gate, f32[192,128]{1,0:T(8,128)} %get-tuple-element.64.residual), custom_call_target="tpu_custom_call" | custom-call | tf_op jit(solution)/shard_map/pallas_call | solution.py:31
  128.4 0.0 all-gather.9.cloned.1.call-done
  128.4 7.0 %shard_map.253.normed = bf16[1024,768]{1,0:T(8,128)(2,1)} custom-call(bf16[8,4,192,128]{3,2,1,0:T(8,128)(2,1)} %bitcast.38, bf16[4,400,128]{2,1,0:T(8,128)(2,1)} %bitcast.36), custom_call_target="tpu_custom_call" | custom-call | tf_op jit(solution)/shard_map/pallas_call | solution.py:43
  135.4 0.0 all-to-all-done.5.came
  135.4 0.0 copy-start.2
  135.4 0.0 all-gather.7.cloned.1.call-done
  135.4 0.7 copy-done.2
  136.1 5.0 %shard_map.255 = (f32[192,768]{1,0:T(8,128)}, f32[192,768]{1,0:T(8,128)}, f32[192,768]{1,0:T(8,128)}, f32[192,768]{1,0:T(8,128)}, f32[8,768]{1,0:T(8,128)}, /*in...) custom-call(bf16[8,576,128]{2,1,0:T(8,128)(2,1)} %bitcast.47, bf16[1024,768]{1,0:T(8,128)(2,1)} %shard_map.253.normed, ...), custom_call_target="tpu_custom_call" | custom-call | tf_op jit(solution)/shard_map/pallas_call | solution.py:43
  141.1 1.3 fusion
  (1 shorter events, 0.0 us)
Async XLA Ops:
  7.2 121.2 %all-gather.9.cloned.1.call-start = ((), (), s32[]{:S(2)}) async-start(), calls=%async_computation.7 | async-start | bytes 1622016 | tf_op jit(solution)/shard_map/all_gather | solution.py:549
  7.9 127.5 %all-gather.7.cloned.1.call-start = ((), (), s32[]{:S(2)}) async-start(), calls=%async_computation.6 | async-start | bytes 1327104 | tf_op jit(solution)/shard_map/all_gather | solution.py:599
  18.5 33.2 %copy-start = (bf16[1600,128]{1,0:T(8,128)(2,1)}, bf16[1600,128]{1,0:T(8,128)(2,1)S(1)}, u32[]{:S(2)}) copy-start(bf16[1600,128]{1,0:T(8,128)(2,1)S(1)} %all-gather) | copy-start | bytes 1228804
  118.0 8.5 %copy-start.1 = (bf16[8,208,128]{2,1,0:T(8,128)(2,1)}, bf16[8,208,128]{2,1,0:T(8,128)(2,1)S(1)}, u32[]{:S(2)}) copy-start(bf16[8,208,128]{2,1,0:T(8,128)(2,1)S(1)} %all_to_all.34.came) | copy-start | bytes 1277956
  118.9 16.5 %all-to-all-start.5 = ((bf16[8,160,128]{2,1,0:T(8,128)(2,1)}), bf16[8,160,128]{2,1,0:T(8,128)(2,1)S(1)}, u32[]{:S(2)}, u32[]{:S(2)}) async-start(bf16[8,160,128]{2,1,0:T(8,128)(2,1)} %shard_map.254), calls=%async_computation.5 | async-start | bytes 655360 | tf_op jit(solution)/shard_map/all_to_all | solution.py:615
  135.4 0.7 copy-start.2
Sparse Core Ops, SparseCore 0:
  10.9 58.9 all-gather.8
  85.1 41.2 all-gather.6

commit v11 on v9

--- a/solution.py
+++ b/solution.py
@@ -22,71 +22,18 @@
     return lax.dot_general(left, right, (dims, ((), ())), precision=precision, preferred_element_type=f32)
 
 
-class Pieces:
-    def __init__(self, refs):
-        self.refs, self.size = refs, refs[0].shape[0]
-        self.shape = (self.size * len(refs),) + tuple(refs[0].shape[1:])
-
-    def __getitem__(self, index):
-        if index is Ellipsis:
-            return jnp.concatenate([ref[...] for ref in self.refs], axis=0)
-        at, rest = (index[0], index[1:]) if isinstance(index, tuple) else (index, ())
-        return self.refs[at // self.size][(at % self.size,) + rest]
-
-
-class Split:
-    def __init__(self, array, count):
-        self.array, self.count = array, count
-
-
-def block_of(array, count, i):
-    shape = (array.shape[0] // count,) + array.shape[1:]
-    return pl.BlockSpec(shape, lambda step: (i,) + (0,) * (array.ndim - 1))
-
-
-def whole_map(rank):
-    return lambda step: (0,) * rank
-
-
 def call(body, outs, *args):
-    in_specs, operands, counts = [], [], []
-    for a in args:
-        if isinstance(a, Split):
-            held = far(a.array)
-            in_specs += [block_of(held, a.count, i) for i in range(a.count)]
-            operands += [held] * a.count
-            counts.append(a.count)
-            continue
-        whole = a.dtype == jnp.int32 and a.ndim == 1
-        in_specs.append(pl.BlockSpec(memory_space=pltpu.SMEM) if whole else pl.BlockSpec())
-        operands.append(a)
-        counts.append(0)
+    scalar_memory = pl.BlockSpec(memory_space=pltpu.SMEM)
+    in_specs = [scalar_memory if a.dtype == jnp.int32 and a.ndim == 1 else pl.BlockSpec() for a in args]
     shapes = []
     for shape, kind, *remote in outs:
         shapes.append(pltpu.HBM(shape, kind) if remote else jax.ShapeDtypeStruct(shape, kind))
-
-    def run(*refs):
-        ins, at = [], 0
-        for count in counts:
-            ins.append(Pieces(refs[at : at + count]) if count else refs[at])
-            at += max(count, 1)
-        body(*ins, *refs[at:])
-
-    extra = {}
-    if any(counts):
-        extra["grid"] = (1,)
-        extra["out_specs"] = [pl.BlockSpec(shape.shape, whole_map(len(shape.shape))) for shape in shapes]
-        in_specs = [
-            pl.BlockSpec(a.shape, whole_map(a.ndim)) if spec.block_shape is None and spec.memory_space is None else spec
-            for spec, a in zip(in_specs, operands)
-        ]
     return pl.pallas_call(
-        run,
+        body,
         out_shape=shapes,
         in_specs=in_specs,
-        **extra,
         compiler_params=pltpu.CompilerParams(vmem_limit_bytes=40 * 1024 * 1024),
-    )(*operands)
+    )(*args)
 
 
 def far(array):
@@ -99,7 +46,10 @@
 
 def gain_columns(block):
     turned = jnp.transpose(block.astype(f32))
-    return [jnp.concatenate([turned[:, i : i + 1], turned[:64, i + 1 : i + 2]], axis=0) for i in (0, 2)]
+    return [
+        jnp.concatenate([turned[:, 0:1], turned[:64, 1:2]], axis=0),
+        jnp.concatenate([turned[64:, 1:2], turned[:, 2:3]], axis=0),
+    ]
 
 
 def all_gains(packed):
@@ -262,11 +212,11 @@
         send_ref[e] = jnp.where(spare, counts[e : e + 1], block).astype(bf16)
 
 
-def gain_row(packed, first, line):
+def second_gain_row(packed, first):
     pieces = []
     for i in range(packed.shape[0]):
         block = packed[i, first : first + 16, :].astype(f32)
-        pieces += [block[line : line + 1, :], block[line + 1 : line + 2, :64]]
+        pieces += [block[1:2, 64:], block[2:3, :]]
     return jnp.concatenate(pieces, axis=1)
 
 
@@ -284,7 +234,7 @@
     residual = jnp.concatenate([block[:, :col] for block in parts], axis=1)
     grads = jnp.concatenate([block[:, col:] for block in parts], axis=1)
     inverse = lax.rsqrt(jnp.sum(residual * residual, axis=1, keepdims=True) * (1.0 / width) + eps)
-    rows = (residual * inverse * gain_row(packed, 2 * col, 2)).astype(bf16)
+    rows = (residual * inverse * second_gain_row(packed, 2 * col)).astype(bf16)
     rows_ref[...] = rows
     hidden, slope = gelu_parts(mm(rows, w_in[...]))
     hidden = hidden.astype(bf16)
@@ -577,9 +527,9 @@
     scalars = jnp.stack([lengths[0], me_head.astype(jnp.int32), me_expert.astype(jnp.int32)])
     buckets_row = buckets[None]
 
-    space = jnp.zeros((64,), bf16)
-    gains = jnp.concatenate([gain_attn, space, gain_ffn, space, jnp.zeros((1536,), bf16)]).reshape(16, 128)
-    packed = lax.all_gather(jnp.concatenate([inputs.T, out_grad.T, gains], axis=0), "head")
+    gains = jnp.concatenate([gain_attn, gain_ffn]).reshape(3, 128)
+    gains = jnp.concatenate([inputs.T, out_grad.T, gains, jnp.zeros((13, 128), bf16)], axis=0)
+    packed = lax.all_gather(gains, "head")
     if joined:
         all_in = lax.all_gather(inputs.T, ("expert", "head")).reshape(groups, heads, col, tok)
     qkv, weights, attended, branch = call(
@@ -604,7 +554,7 @@
         functools.partial(expert_kernel, capacity),
         [((experts * heads, folded_rows(slots), 128), bf16), ((heads, total * 3 // 2, 128), bf16, 1)]
         + [((total, width), bf16, 1)] * 4,
-        scalars, Split(quarters, heads), far(packed), Split(w_in, 4), Split(w_out, 4), far(router_rows),
+        scalars, quarters, far(packed), far(w_in), far(w_out), far(router_rows),
     )
     came = lax.all_to_all(back, ("expert", "head"), split_axis=0, concat_axis=0, tiled=True)
     grad_own, gate_grad, stats = call(
@@ -627,23 +577,29 @@
         ),
         scalars, far(packed), expert_grad, far(gate_grad), far(stats), far(routes_row),
         far(router_rows), far(w_output), far(weights), far(qkv), far(wq), far(wk), far(wv), far(attended),
-        Split(part, heads),
+        far(part),
     )
 
     if joined:
         late_all = lax.all_gather(late, "expert")
 
     first = lax.all_to_all(first, "head", split_axis=0, concat_axis=0, tiled=True)
+    in_weight_grad, out_weight_grad = call(
+        weights_kernel, [((width, width), f32, 1)] * 2, far(rows), far(hidden), far(before_grad), far(back_rows)
+    )
+    first, in_weight_grad, out_weight_grad = lax.optimization_barrier((first, in_weight_grad, out_weight_grad))
     ret, gain_one_part, input_grad = call(
         first_kernel,
         [
             ((experts, 2 * slots + (shares[0].shape[1] if joined else 0), 128), bf16),
             ((16, 128), f32, 1), ((col, tok), f32, 1),
         ],
-        scalars, first, Split(packed, heads), far(residual_grad_own), *([Split(shares[0], groups)] if joined else []),
+        scalars, first, far(packed), far(residual_grad_own), *([far(shares[0])] if joined else []),
     )
     ret = lax.all_to_all(ret, "expert", split_axis=0, concat_axis=0, tiled=True)
     if joined:
+        normed_all = call(turn_kernel, [((groups * tok, width), bf16, 1)], far(all_in), far(packed))[0]
+        ret, normed_all = lax.optimization_barrier((ret, normed_all))
         share = call(
             functools.partial(share_kernel, slots), [(shares[0].shape, bf16)], ret
         )[0]
@@ -651,19 +607,15 @@
     block_out = call(
         functools.partial(last_kernel, slots), [((col, tok), bf16, 1)], far(ret), far(side), far(gate), far(residual)
     )[0]
-    in_weight_grad, out_weight_grad = call(
-        weights_kernel, [((width, width), f32, 1)] * 2, far(rows), far(hidden), far(before_grad), far(back_rows)
-    )
     if joined:
-        normed_all = call(turn_kernel, [((groups * tok, width), bf16, 1)], Split(all_in, groups), Split(packed, heads))[0]
         q_grad, k_grad, v_grad, output_grad, router_grad, table_grad, gain_grads, aux_loss = call(
             products_kernel,
             [((col, width), f32, 1)] * 4
             + [((experts, width), f32), ((heads_here, bucket_count), f32), ((8, 256), f32), ((1, 1), f32)],
-            Split(late_all, groups), Split(normed_all, groups), share, far(buckets_row), far(stats),
+            far(late_all), far(normed_all), share, far(buckets_row), far(stats),
         )
     else:
-        gain = packed[:, 2 * col : 2 * col + 2].reshape(heads, 256)[:, :col].reshape(width, 1)
+        gain = packed[:, 2 * col : 2 * col + 3].reshape(heads, 2 * col)[:, :col].reshape(width, 1)
         x = packed[:, :col].reshape(width, tok).astype(f32)
         normed = (x * token_scale(x) * gain.astype(f32)).astype(bf16)
         products = [mm(late[i * col : (i + 1) * col], normed, nt) for i in range(3)]

time: 145 us -> 148 us (1.021)
  blocking collectives: 89 us -> 58 us
  waiting for transfers between devices: 0.71 us -> 27.6 us
  starting transfers between devices: 3.51 us -> 10.5 us
    all_to_all x2 -> x0, blocking collectives: 31 us -> none  [the longest x1 20 us: shards(): ret = lax.all_to_all(ret, 'expert', split_axis=0, concat_axis=0, tiled=True)]
    all_to_all x0 -> x2, waiting for transfers between devices: none -> 18.9 us  [the longest x1 14.3 us: shards(): ret = lax.all_to_all(ret, 'expert', split_axis=0, concat_axis=0, tiled=True)]
    all_to_all x1, waiting for transfers between devices: 0.01 us -> 7.93 us  [shards(): lax.all_to_all(share, 'expert', split_axis=0, concat_axis=0, tiled=True)]
    all_to_all x0 -> x2, starting transfers between devices: none -> 6.95 us  [the longest x1 3.48 us: shards(): lax.all_to_all(first, 'head', split_axis=0, concat_axis=0, tiled=True)]
  transfers between devices with their start and end apart: 3 -> 5, of which waited for: 0 -> 3; matrix products, arithmetic and copies ran while one was open for 2% -> 1% of each run, Pallas kernels for 20% -> 20%
where the time goes in v11:
time: 148 us; the launch traced here: 147 us
  blocking collectives  58 us (39%)
  Pallas kernels  33.5 us (23%)
  waiting for transfers between devices  27.6 us (19%)
  between operations  14.8 us (10%)
  starting transfers between devices  10.5 us (7%)
  other arithmetic  1.76 us (1%)
    pallas_call x11, Pallas kernels, call(): pl.pallas_call(body, out_shape=shapes, in_specs=in_specs, compiler_params...  33.5 us
    all_to_all x1, blocking collectives, shards(): lax.all_to_all(back, ('expert', 'head'), split_axis=0, concat_axis=0, til...  15.7 us
    all_to_all x1, waiting for transfers between devices, shards(): ret = lax.all_to_all(ret, 'expert', split_axis=0, concat_axis=0, tiled=True)  14.3 us
    all_to_all x1, blocking collectives, shards(): lax.all_to_all(send, 'expert', split_axis=0, concat_axis=0, tiled=True)  13.7 us
    all_gather x1, blocking collectives, shards(): packed = lax.all_gather(gains, 'head')  8.02 us
    all_to_all x1, waiting for transfers between devices, shards(): lax.all_to_all(share, 'expert', split_axis=0, concat_axis=0, tiled=True)  7.93 us
    all_to_all x1, blocking collectives, shards(): lax.all_to_all(branch, 'head', split_axis=0, concat_axis=0, tiled=True)  7.69 us
    all_gather x1, blocking collectives, shards(): quarters = lax.all_gather(quarter.reshape(total, 2 * col), 'head')  6.68 us
  transfers between devices with their start and end apart: 5, of which 3 were waited for; matrix products, arithmetic and copies ran while one was open for 1% of the time, Pallas kernels for 20%

profile of v11, /device:TPU:0, one launch (start us, length us, event | category | flops | bytes accessed | tf_op | source)
XLA Modules:
  0.0 146.7 jit_solution(6369828676629452978)
XLA Ops:
  7.2 0.0 all-gather.7.cloned.1.call-start
  7.2 0.7 all-gather.7.cloned.1.call-update
  7.9 0.0 all-gather.9.cloned.1.call-start
  8.6 0.1 pad.3.clone
  8.7 0.1 pad_add_fusion.scalars
  8.8 0.7 maximum_bitcast_fusion
  9.5 0.9 maximum_maximum_fusion
  10.5 8.0 %all-gather = bf16[1600,128]{1,0:T(8,128)(2,1)S(1)} all-gather(bf16[400,128]{1,0:T(8,128)(2,1)S(1)} %maximum_maximum_fusion), channel_id=2, replica_groups=mesh['expert'=8,'head'=4] {'head'}, dimensions={0}, use_global_device_ids=true | all-gather | bytes 512000 | tf_op jit(solution)/shard_map/all_gather | solution.py:532
  18.5 0.0 copy-start
  18.5 3.5 %shard_map.246 = (bf16[3,192,128]{2,1,0:T(8,128)(2,1)}, f32[3,128,128]{2,1,0:T(8,128)}, bf16[192,128]{1,0:T(8,128)(2,1)}, bf16[4,192,128]{2,1,0:T(8,128)(2,1)S(1)}) custom-call(s32[3]{0:T(128)S(1)} %pad_add_fusion.scalars, bf16[4,400,128]{2,1,0:T(8,128)(2,1)S(1)} %bitcast.32, bf16[192,768]{1,0:T(8,128)(2,1)} %bitcast.39, bf16[192,768]{1,0:T(8,128)(2,1)} %bitcast.41, ...), custom_call_target="tpu_custom_call" | custom-call | tf_op jit(solution)/shard_map/pallas_call | solution.py:31
  22.0 7.7 %all_to_all.30.came = bf16[4,192,128]{2,1,0:T(8,128)(2,1)S(1)} all-to-all(bf16[4,192,128]{2,1,0:T(8,128)(2,1)S(1)} %get-tuple-element.52), channel_id=1, replica_groups=mesh['expert'=8,'head'=4] {'head'}, dimensions={0} | all-to-all | bytes 393216 | tf_op jit(solution)/shard_map/all_to_all | solution.py:544
  29.7 1.6 %shard_map.247 = (f32[192,128]{1,0:T(8,128)}, bf16[192,128]{1,0:T(8,128)(2,1)}, f32[8,128]{1,0:T(8,128)}, bf16[8,24,384]{2,1,0:T(8,128)(2,1)S(1)}) custom-call(s32[3]{0:T(128)S(1)} %pad_add_fusion.scalars, bf16[4,192,128]{2,1,0:T(8,128)(2,1)S(1)} %all_to_all.30.came, bf16[192,128]{1,0:T(8,128)(2,1)} %bitcast.51, bf16[192,128]{1,0:T(8,128)(2,1)} %bitcast.53, ...), custom_call_target="tpu_custom_call" | custom-call | tf_op jit(solution)/shard_map/pallas_call | solution.py:31
  31.3 13.7 %all_to_all.31 = bf16[8,24,384]{2,1,0:T(8,128)(2,1)S(1)} all-to-all(bf16[8,24,384]{2,1,0:T(8,128)(2,1)S(1)} %get-tuple-element.53), channel_id=1, replica_groups=mesh['expert'=8,'head'=4] {'expert'}, dimensions={0} | all-to-all | bytes 294912 | tf_op jit(solution)/shard_map/all_to_all | solution.py:550
  45.0 6.7 %all_gather.29.quarters = bf16[4,192,384]{2,1,0:T(8,128)(2,1)S(1)} all-gather(bf16[1,192,384]{2,1,0:T(8,128)(2,1)S(1)} %bitcast.48), channel_id=1, replica_groups=mesh['expert'=8,'head'=4] {'head'}, dimensions={0}, use_global_device_ids=true | all-gather | bytes 737280 | tf_op jit(solution)/shard_map/all_gather | solution.py:551
  51.7 0.0 copy-done
  51.7 4.8 %shard_map.248 = (bf16[32,40,128]{2,1,0:T(8,128)(2,1)S(1)}, bf16[4,288,128]{2,1,0:T(8,128)(2,1)}, bf16[192,768]{1,0:T(8,128)(2,1)}, bf16[192,768]{1,0:T(8,128)(2...) custom-call(s32[3]{0:T(128)S(1)} %pad_add_fusion.scalars, bf16[4,192,384]{2,1,0:T(8,128)(2,1)S(1)} %all_gather.29.quarters, ...), custom_call_target="tpu_custom_call" | custom-call | tf_op jit(solution)/shard_map/pallas_call | solution.py:31
  56.5 15.7 %all_to_all.32.came = bf16[32,40,128]{2,1,0:T(8,128)(2,1)S(1)} all-to-all(bf16[32,40,128]{2,1,0:T(8,128)(2,1)S(1)} %get-tuple-element.54), channel_id=1, replica_groups=mesh['expert'=8,'head'=4] {'expert','head'}, dimensions={0} | all-to-all | bytes 655360 | tf_op jit(solution)/shard_map/all_to_all | solution.py:559
  72.2 1.8 %shard_map.249 = (bf16[384,128]{1,0:T(8,128)(2,1)S(1)}, f32[8,128]{1,0:T(8,128)}, f32[8,128]{1,0:T(8,128)}) custom-call(bf16[32,40,128]{2,1,0:T(8,128)(2,1)S(1)} %all_to_all.32.came, f32[8,128]{1,0:T(8,128)} %get-tuple-element.55.side, bf16[192,128]{1,0:T(8,128)(2,1)} %get-tuple-element.56.low), custom_call_target="tpu_custom_call" | custom-call | tf_op jit(solution)/shard_map/pallas_call | solution.py:31
  74.0 6.1 %all-gather.1 = bf16[1536,128]{1,0:T(8,128)(2,1)S(1)} all-gather(bf16[384,128]{1,0:T(8,128)(2,1)S(1)} %get-tuple-element.57), channel_id=3, replica_groups=mesh['expert'=8,'head'=4] {'head'}, dimensions={0}, use_global_device_ids=true | all-gather | bytes 491520 | tf_op jit(solution)/shard_map/all_gather | solution.py:565
  80.1 5.0 %shard_map.250 = (bf16[576,128]{1,0:T(8,128)(2,1)}, bf16[4,496,128]{2,1,0:T(8,128)(2,1)}, f32[192,128]{1,0:T(8,128)}, f32[8,128]{1,0:T(8,128)}, bf16[8,160,128]{2,1,0:T(8,128)(2,1)}) custom-call(s32[3]{0:T(128)S(1)} %pad_add_fusion.scalars, bf16[4,400,128]{2,1,0:T(8,128)(2,1)} %bitcast.34, bf16[4,384,128]{2,1,0:T(8,128)(2,1)S(1)} %bitcast.37, ...), custom_call_target="tpu_custom_call" | custom-call | tf_op jit(solution)/shard_map/pallas_call | solution.py:31
  85.1 0.0 all-gather.9.cloned.1.call-update
  85.1 3.5 %all-to-all-start.3 = ((bf16[4,496,128]{2,1,0:T(8,128)(2,1)}), bf16[4,496,128]{2,1,0:T(8,128)(2,1)S(1)}, u32[]{:S(2)}, u32[]{:S(2)}) async-start(bf16[4,496,128]{2,1,0:T(8,128)(2,1)} %get-tuple-element.64), calls=%async_computation.3 | async-start | bytes 1015808 | tf_op jit(solution)/shard_map/all_to_all | solution.py:586
  88.6 4.0 %shard_map.251 = (f32[768,768]{1,0:T(8,128)}, f32[768,768]{1,0:T(8,128)}) custom-call(bf16[192,768]{1,0:T(8,128)(2,1)} %get-tuple-element.65.rows_ref, bf16[192,768]{1,0:T(8,128)(2,1)} %get-tuple-element.66.hidden, bf16[192,768]{1,0:T(8,128)(2,1)} %get-tuple-element.67.before, bf16[192,768]{1,0:T(8,128)(2,1)} %get-tuple-element.68.grads), custom_call_target="tpu_custom_call" | custom-call | tf_op jit(solution)/shard_map/pallas_call | solution.py:31
  92.7 4.6 %all-to-all-done.3.came = bf16[4,496,128]{2,1,0:T(8,128)(2,1)S(1)} async-done(((bf16[4,496,128]{2,1,0:T(8,128)(2,1)}), bf16[4,496,128]{2,1,0:T(8,128)(2,1)S(1)}, u32[]{:S(2)}, u32[]{:S(2)}) %all-to-all-start.3) | async-done | bytes 507936 | tf_op jit(solution)/shard_map/all_to_all | solution.py:586
  97.3 2.3 %shard_map.252 = (bf16[8,208,128]{2,1,0:T(8,128)(2,1)}, f32[16,128]{1,0:T(8,128)}, f32[192,128]{1,0:T(8,128)}) custom-call(s32[3]{0:T(128)S(1)} %pad_add_fusion.scalars, bf16[4,496,128]{2,1,0:T(8,128)(2,1)S(1)} %all-to-all-done.3.came, bf16[4,400,128]{2,1,0:T(8,128)(2,1)} %bitcast.35, f32[192,128]{1,0:T(8,128)} %get-tuple-element.72.own, ...), custom_call_target="tpu_custom_call" | custom-call | tf_op jit(solution)/shard_map/pallas_call | solution.py:31
  99.6 3.5 %all-to-all-start.4 = ((bf16[8,208,128]{2,1,0:T(8,128)(2,1)}), bf16[8,208,128]{2,1,0:T(8,128)(2,1)S(1)}, u32[]{:S(2)}, u32[]{:S(2)}) async-start(bf16[8,208,128]{2,1,0:T(8,128)(2,1)} %get-tuple-element.74), calls=%async_computation.4 | async-start | bytes 851968 | tf_op jit(solution)/shard_map/all_to_all | solution.py:599
  103.0 0.0 all-gather.7.cloned.1.call-done
  103.1 3.6 %shard_map.253.normed = bf16[1024,768]{1,0:T(8,128)(2,1)} custom-call(bf16[8,4,192,128]{3,2,1,0:T(8,128)(2,1)} %bitcast.38, bf16[4,400,128]{2,1,0:T(8,128)(2,1)} %bitcast.36), custom_call_target="tpu_custom_call" | custom-call | tf_op jit(solution)/shard_map/pallas_call | solution.py:31
  106.7 14.3 %all-to-all-done.4.came = bf16[8,208,128]{2,1,0:T(8,128)(2,1)S(1)} async-done(((bf16[8,208,128]{2,1,0:T(8,128)(2,1)}), bf16[8,208,128]{2,1,0:T(8,128)(2,1)S(1)}, u32[]{:S(2)}, u32[]{:S(2)}) %all-to-all-start.4) | async-done | bytes 426016 | tf_op jit(solution)/shard_map/all_to_all | solution.py:599
  121.0 0.0 copy-start.1
  121.0 0.8 shard_map.255
  121.8 3.5 %all-to-all-start.5 = ((bf16[8,160,128]{2,1,0:T(8,128)(2,1)}), bf16[8,160,128]{2,1,0:T(8,128)(2,1)S(1)}, u32[]{:S(2)}, u32[]{:S(2)}) async-start(bf16[8,160,128]{2,1,0:T(8,128)(2,1)} %shard_map.255), calls=%async_computation.5 | async-start | bytes 655360 | tf_op jit(solution)/shard_map/all_to_all | solution.py:606
  125.3 0.0 copy-done.1
  125.3 1.9 %shard_map.254 = bf16[192,128]{1,0:T(8,128)(2,1)} custom-call(bf16[8,208,128]{2,1,0:T(8,128)(2,1)} %copy-done.1, f32[8,128]{1,0:T(8,128)} %get-tuple-element.55.side, f32[8,128]{1,0:T(8,128)} %get-tuple-element.76.gate, f32[192,128]{1,0:T(8,128)} %get-tuple-element.77.residual), custom_call_target="tpu_custom_call" | custom-call | tf_op jit(solution)/shard_map/pallas_call | solution.py:31
  127.2 0.0 all-gather.9.cloned.1.call-done
  127.2 7.9 %all-to-all-done.5.came = bf16[8,160,128]{2,1,0:T(8,128)(2,1)S(1)} async-done(((bf16[8,160,128]{2,1,0:T(8,128)(2,1)}), bf16[8,160,128]{2,1,0:T(8,128)(2,1)S(1)}, u32[]{:S(2)}, u32[]{:S(2)}) %all-to-all-start.5) | async-done | bytes 327712 | tf_op jit(solution)/shard_map/all_to_all | solution.py:606
  135.1 4.2 %shard_map.256 = (f32[192,768]{1,0:T(8,128)}, f32[192,768]{1,0:T(8,128)}, f32[192,768]{1,0:T(8,128)}, f32[192,768]{1,0:T(8,128)}, f32[8,768]{1,0:T(8,128)}, /*in...) custom-call(bf16[8,576,128]{2,1,0:T(8,128)(2,1)} %bitcast.47, bf16[1024,768]{1,0:T(8,128)(2,1)} %shard_map.253.normed, ...), custom_call_target="tpu_custom_call" | custom-call | tf_op jit(solution)/shard_map/pallas_call | solution.py:31
  139.3 0.6 fusion
  (1 shorter events, 0.0 us)
Async XLA Ops:
  7.2 95.9 %all-gather.7.cloned.1.call-start = ((), (), s32[]{:S(2)}) async-start(), calls=%async_computation.6 | async-start | bytes 1622016 | tf_op jit(solution)/shard_map/all_gather | solution.py:534
  7.9 119.3 %all-gather.9.cloned.1.call-start = ((), (), s32[]{:S(2)}) async-start(), calls=%async_computation.7 | async-start | bytes 1327104 | tf_op jit(solution)/shard_map/all_gather | solution.py:584
  18.5 33.2 %copy-start = (bf16[1600,128]{1,0:T(8,128)(2,1)}, bf16[1600,128]{1,0:T(8,128)(2,1)S(1)}, u32[]{:S(2)}) copy-start(bf16[1600,128]{1,0:T(8,128)(2,1)S(1)} %all-gather) | copy-start | bytes 1228804
  85.1 12.1 %all-to-all-start.3 = ((bf16[4,496,128]{2,1,0:T(8,128)(2,1)}), bf16[4,496,128]{2,1,0:T(8,128)(2,1)S(1)}, u32[]{:S(2)}, u32[]{:S(2)}) async-start(bf16[4,496,128]{2,1,0:T(8,128)(2,1)} %get-tuple-element.64), calls=%async_computation.3 | async-start | bytes 1015808 | tf_op jit(solution)/shard_map/all_to_all | solution.py:586
  99.6 21.4 %all-to-all-start.4 = ((bf16[8,208,128]{2,1,0:T(8,128)(2,1)}), bf16[8,208,128]{2,1,0:T(8,128)(2,1)S(1)}, u32[]{:S(2)}, u32[]{:S(2)}) async-start(bf16[8,208,128]{2,1,0:T(8,128)(2,1)} %get-tuple-element.74), calls=%async_computation.4 | async-start | bytes 851968 | tf_op jit(solution)/shard_map/all_to_all | solution.py:599
  121.0 4.3 %copy-start.1 = (bf16[8,208,128]{2,1,0:T(8,128)(2,1)}, bf16[8,208,128]{2,1,0:T(8,128)(2,1)S(1)}, u32[]{:S(2)}) copy-start(bf16[8,208,128]{2,1,0:T(8,128)(2,1)S(1)} %all-to-all-done.4.came) | copy-start | bytes 1277956
  121.8 13.3 %all-to-all-start.5 = ((bf16[8,160,128]{2,1,0:T(8,128)(2,1)}), bf16[8,160,128]{2,1,0:T(8,128)(2,1)S(1)}, u32[]{:S(2)}, u32[]{:S(2)}) async-start(bf16[8,160,128]{2,1,0:T(8,128)(2,1)} %shard_map.255), calls=%async_computation.5 | async-start | bytes 655360 | tf_op jit(solution)/shard_map/all_to_all | solution.py:606
Sparse Core Ops, SparseCore 0:
  10.9 58.9 all-gather.6
  85.3 40.4 all-gather.8

commit v12 on v11

--- a/solution.py
+++ b/solution.py
@@ -445,36 +445,34 @@
     block_ref[...] = add_returned(slots, blocks, side, gate, residual)
 
 
-def turn_kernel(all_in, packed, normed_ref):
+def products_kernel(late, all_in, packed, q_ref, k_ref, v_ref):
     groups, heads, col, tok = all_in.shape
     gain = all_gains(packed)[0]
+    normed = []
     for b in range(groups):
         x = jnp.concatenate([all_in[b, i].astype(f32) for i in range(heads)], axis=0)
-        normed_ref[b * tok : (b + 1) * tok, :] = jnp.transpose(x * token_scale(x) * gain).astype(bf16)
-
-
-def products_kernel(
-    late, normed, came, buckets, stats, q_ref, k_ref, v_ref, out_ref, router_ref, table_ref, gains_ref, aux_ref,
-):
-    groups = came.shape[0]
-    col = q_ref.shape[0]
+        normed.append((x * token_scale(x) * gain).astype(bf16))
+    joined = jnp.concatenate([late[b] for b in range(groups)], axis=1)
+    product = mm(joined, jnp.concatenate(normed, axis=1), nt)
+    for i, ref in enumerate((q_ref, k_ref, v_ref)):
+        ref[...] = product[i * col : (i + 1) * col]
+
+
+def sums_kernel(came, buckets, stats, out_ref, router_ref, table_ref, gains_ref, aux_ref):
+    groups, tok = came.shape[0], (buckets.shape[1] + 1) // 2
     experts = router_ref.shape[0]
-    size = col // groups
+    size = out_ref.shape[0] // groups
     shares = [came[b].astype(f32) for b in range(groups)]
     chunk = shares[0].shape[0] - 6 * size
     for b in range(groups):
         out_ref[b * size : (b + 1) * size, :] = unfold_lanes(shares[b][chunk:], 6)
-    joined = jnp.concatenate([late[b] for b in range(groups)], axis=1)
-    product = mm(joined, normed[...])
-    for i, ref in enumerate((q_ref, k_ref, v_ref)):
-        ref[...] = product[i * col : (i + 1) * col]
     small = jnp.concatenate([share[:chunk] for share in shares], axis=0)
     gains = unfold_lanes(small[:16], 2)
     gains_ref[...] = gains
     probs = gains[1:2, :experts] + gains[2:3, :experts]
     same = lanes((experts, experts)) == sublanes((experts, experts))
     share = jnp.sum(jnp.where(same, stats[:, 0:1] * probs, 0.0), axis=0, keepdims=True)
-    valid_total = 3 * normed.shape[0] // 4
+    valid_total = 3 * tok * groups // 4
     aux_ref[...] = jnp.sum(share, axis=1, keepdims=True) * (experts / (valid_total * valid_total))
     span = buckets.shape[1]
     hot = (sublanes((table_ref.shape[1], span)) == buckets[...]).astype(f32)
@@ -598,8 +596,6 @@
     )
     ret = lax.all_to_all(ret, "expert", split_axis=0, concat_axis=0, tiled=True)
     if joined:
-        normed_all = call(turn_kernel, [((groups * tok, width), bf16, 1)], far(all_in), far(packed))[0]
-        ret, normed_all = lax.optimization_barrier((ret, normed_all))
         share = call(
             functools.partial(share_kernel, slots), [(shares[0].shape, bf16)], ret
         )[0]
@@ -608,11 +604,17 @@
         functools.partial(last_kernel, slots), [((col, tok), bf16, 1)], far(ret), far(side), far(gate), far(residual)
     )[0]
     if joined:
-        q_grad, k_grad, v_grad, output_grad, router_grad, table_grad, gain_grads, aux_loss = call(
-            products_kernel,
-            [((col, width), f32, 1)] * 4
-            + [((experts, width), f32), ((heads_here, bucket_count), f32), ((8, 256), f32), ((1, 1), f32)],
-            far(late_all), far(normed_all), share, far(buckets_row), far(stats),
+        q_grad, k_grad, v_grad = call(
+            products_kernel, [((col, width), f32, 1)] * 3, far(late_all), far(all_in), far(packed)
+        )
+        share, q_grad, k_grad, v_grad, block_out = lax.optimization_barrier(
+            (share, q_grad, k_grad, v_grad, block_out)
+        )
+        output_grad, router_grad, table_grad, gain_grads, aux_loss = call(
+            sums_kernel,
+            [((col, width), f32, 1), ((experts, width), f32), ((heads_here, bucket_count), f32)]
+            + [((8, 256), f32), ((1, 1), f32)],
+            share, far(buckets_row), far(stats),
         )
     else:
         gain = packed[:, 2 * col : 2 * col + 3].reshape(heads, 2 * col)[:, :col].reshape(width, 1)

time: 148 us -> 143 us (0.966)
  blocking collectives: 58 us -> 79 us
  waiting for transfers between devices: 27.6 us -> 7.71 us
  starting transfers between devices: 10.5 us -> 7.22 us
  Pallas kernels: 33.5 us -> 31.5 us
    all_to_all x0 -> x1, blocking collectives: none -> 21 us  [shards(): ret = lax.all_to_all(ret, 'expert', split_axis=0, concat_axis=0, tiled=True)]
    all_to_all x1 -> x0, waiting for transfers between devices: 14.3 us -> none  [shards(): ret = lax.all_to_all(ret, 'expert', split_axis=0, concat_axis=0, tiled=True)]
    all_to_all x1, waiting for transfers between devices: 7.93 us -> 2.4 us  [shards(): lax.all_to_all(share, 'expert', split_axis=0, concat_axis=0, tiled=True)]
    all_to_all x1 -> x0, starting transfers between devices: 3.46 us -> none  [shards(): ret = lax.all_to_all(ret, 'expert', split_axis=0, concat_axis=0, tiled=True)]
    pallas_call x11, Pallas kernels: 33.5 us -> 31.5 us  [call(): pl.pallas_call(body, out_shape=shapes, in_specs=in_specs, compiler_params...]
  transfers between devices with their start and end apart: 5 -> 4, of which waited for: 3 -> 2; matrix products, arithmetic and copies ran while one was open for 1% -> 1% of each run, Pallas kernels for 20% -> 21%
where the time goes in v12:
time: 143 us
  blocking collectives  79 us (55%)
  Pallas kernels  31.5 us (22%)
  between operations  14.7 us (10%)
  waiting for transfers between devices  7.71 us (5%)
  starting transfers between devices  7.22 us (5%)
  other arithmetic  1.76 us (1%)
    pallas_call x11, Pallas kernels, call(): pl.pallas_call(body, out_shape=shapes, in_specs=in_specs, compiler_params...  31.5 us
    all_to_all x1, blocking collectives, shards(): ret = lax.all_to_all(ret, 'expert', split_axis=0, concat_axis=0, tiled=True)  21 us
    all_to_all x1, blocking collectives, shards(): lax.all_to_all(back, ('expert', 'head'), split_axis=0, concat_axis=0, til...  15.7 us
    all_to_all x1, blocking collectives, shards(): lax.all_to_all(send, 'expert', split_axis=0, concat_axis=0, tiled=True)  13.7 us
    all_gather x1, blocking collectives, shards(): packed = lax.all_gather(gains, 'head')  8.02 us
    all_to_all x1, blocking collectives, shards(): lax.all_to_all(branch, 'head', split_axis=0, concat_axis=0, tiled=True)  7.69 us
    all_gather x1, blocking collectives, shards(): quarters = lax.all_gather(quarter.reshape(total, 2 * col), 'head')  6.68 us
    all_gather x1, blocking collectives, shards(): expert_grad = lax.all_gather(grad_own, 'head')  6.16 us
  transfers between devices with their start and end apart: 4, of which 2 were waited for; matrix products, arithmetic and copies ran while one was open for 1% of the time, Pallas kernels for 21%

profile of v12, /device:TPU:0, one launch (start us, length us, event | category | flops | bytes accessed | tf_op | source)
XLA Modules:
  0.0 142.6 jit_solution(11182344324791883586)
XLA Ops:
  7.2 0.0 all-gather.9.cloned.1.call-start
  7.2 0.7 all-gather.9.cloned.1.call-update
  7.9 0.0 all-gather.7.cloned.1.call-start
  8.6 0.1 pad.3.clone
  8.7 0.1 pad_add_fusion.scalars
  8.8 0.7 maximum_bitcast_fusion
  9.5 0.9 maximum_maximum_fusion
  10.5 8.0 %all-gather = bf16[1600,128]{1,0:T(8,128)(2,1)S(1)} all-gather(bf16[400,128]{1,0:T(8,128)(2,1)S(1)} %maximum_maximum_fusion), channel_id=2, replica_groups=mesh['expert'=8,'head'=4] {'head'}, dimensions={0}, use_global_device_ids=true | all-gather | bytes 512000 | tf_op jit(solution)/shard_map/all_gather | solution.py:530
  18.5 0.0 copy-start
  18.5 3.5 %shard_map.246 = (bf16[3,192,128]{2,1,0:T(8,128)(2,1)}, f32[3,128,128]{2,1,0:T(8,128)}, bf16[192,128]{1,0:T(8,128)(2,1)}, bf16[4,192,128]{2,1,0:T(8,128)(2,1)S(1)}) custom-call(s32[3]{0:T(128)S(1)} %pad_add_fusion.scalars, bf16[4,400,128]{2,1,0:T(8,128)(2,1)S(1)} %bitcast.32, bf16[192,768]{1,0:T(8,128)(2,1)} %bitcast.39, bf16[192,768]{1,0:T(8,128)(2,1)} %bitcast.41, ...), custom_call_target="tpu_custom_call" | custom-call | tf_op jit(solution)/shard_map/pallas_call | solution.py:31
  22.0 7.7 %all_to_all.30.came = bf16[4,192,128]{2,1,0:T(8,128)(2,1)S(1)} all-to-all(bf16[4,192,128]{2,1,0:T(8,128)(2,1)S(1)} %get-tuple-element.55), channel_id=1, replica_groups=mesh['expert'=8,'head'=4] {'head'}, dimensions={0} | all-to-all | bytes 393216 | tf_op jit(solution)/shard_map/all_to_all | solution.py:542
  29.7 1.6 %shard_map.247 = (f32[192,128]{1,0:T(8,128)}, bf16[192,128]{1,0:T(8,128)(2,1)}, f32[8,128]{1,0:T(8,128)}, bf16[8,24,384]{2,1,0:T(8,128)(2,1)S(1)}) custom-call(s32[3]{0:T(128)S(1)} %pad_add_fusion.scalars, bf16[4,192,128]{2,1,0:T(8,128)(2,1)S(1)} %all_to_all.30.came, bf16[192,128]{1,0:T(8,128)(2,1)} %bitcast.51, bf16[192,128]{1,0:T(8,128)(2,1)} %bitcast.53, ...), custom_call_target="tpu_custom_call" | custom-call | tf_op jit(solution)/shard_map/pallas_call | solution.py:31
  31.3 13.7 %all_to_all.31 = bf16[8,24,384]{2,1,0:T(8,128)(2,1)S(1)} all-to-all(bf16[8,24,384]{2,1,0:T(8,128)(2,1)S(1)} %get-tuple-element.56), channel_id=1, replica_groups=mesh['expert'=8,'head'=4] {'expert'}, dimensions={0} | all-to-all | bytes 294912 | tf_op jit(solution)/shard_map/all_to_all | solution.py:548
  45.0 6.7 %all_gather.29.quarters = bf16[4,192,384]{2,1,0:T(8,128)(2,1)S(1)} all-gather(bf16[1,192,384]{2,1,0:T(8,128)(2,1)S(1)} %bitcast.48), channel_id=1, replica_groups=mesh['expert'=8,'head'=4] {'head'}, dimensions={0}, use_global_device_ids=true | all-gather | bytes 737280 | tf_op jit(solution)/shard_map/all_gather | solution.py:549
  51.7 0.0 copy-done
  51.7 4.8 %shard_map.248 = (bf16[32,40,128]{2,1,0:T(8,128)(2,1)S(1)}, bf16[4,288,128]{2,1,0:T(8,128)(2,1)}, bf16[192,768]{1,0:T(8,128)(2,1)}, bf16[192,768]{1,0:T(8,128)(2...) custom-call(s32[3]{0:T(128)S(1)} %pad_add_fusion.scalars, bf16[4,192,384]{2,1,0:T(8,128)(2,1)S(1)} %all_gather.29.quarters, ...), custom_call_target="tpu_custom_call" | custom-call | tf_op jit(solution)/shard_map/pallas_call | solution.py:31
  56.5 15.7 %all_to_all.32.came = bf16[32,40,128]{2,1,0:T(8,128)(2,1)S(1)} all-to-all(bf16[32,40,128]{2,1,0:T(8,128)(2,1)S(1)} %get-tuple-element.57), channel_id=1, replica_groups=mesh['expert'=8,'head'=4] {'expert','head'}, dimensions={0} | all-to-all | bytes 655360 | tf_op jit(solution)/shard_map/all_to_all | solution.py:557
  72.2 1.8 %shard_map.249 = (bf16[384,128]{1,0:T(8,128)(2,1)S(1)}, f32[8,128]{1,0:T(8,128)}, f32[8,128]{1,0:T(8,128)}) custom-call(bf16[32,40,128]{2,1,0:T(8,128)(2,1)S(1)} %all_to_all.32.came, f32[8,128]{1,0:T(8,128)} %get-tuple-element.58.side, bf16[192,128]{1,0:T(8,128)(2,1)} %get-tuple-element.59.low), custom_call_target="tpu_custom_call" | custom-call | tf_op jit(solution)/shard_map/pallas_call | solution.py:31
  74.0 6.2 %all-gather.1 = bf16[1536,128]{1,0:T(8,128)(2,1)S(1)} all-gather(bf16[384,128]{1,0:T(8,128)(2,1)S(1)} %get-tuple-element.60), channel_id=3, replica_groups=mesh['expert'=8,'head'=4] {'head'}, dimensions={0}, use_global_device_ids=true | all-gather | bytes 491520 | tf_op jit(solution)/shard_map/all_gather | solution.py:563
  80.2 5.0 %shard_map.250 = (bf16[576,128]{1,0:T(8,128)(2,1)}, bf16[4,496,128]{2,1,0:T(8,128)(2,1)}, f32[192,128]{1,0:T(8,128)}, f32[8,128]{1,0:T(8,128)}, bf16[8,160,128]{2,1,0:T(8,128)(2,1)}) custom-call(s32[3]{0:T(128)S(1)} %pad_add_fusion.scalars, bf16[4,400,128]{2,1,0:T(8,128)(2,1)} %bitcast.34, bf16[4,384,128]{2,1,0:T(8,128)(2,1)S(1)} %bitcast.37, ...), custom_call_target="tpu_custom_call" | custom-call | tf_op jit(solution)/shard_map/pallas_call | solution.py:31
  85.2 0.0 all-gather.7.cloned.1.call-update
  85.2 3.5 %all-to-all-start.3 = ((bf16[4,496,128]{2,1,0:T(8,128)(2,1)}), bf16[4,496,128]{2,1,0:T(8,128)(2,1)S(1)}, u32[]{:S(2)}, u32[]{:S(2)}) async-start(bf16[4,496,128]{2,1,0:T(8,128)(2,1)} %get-tuple-element.67), calls=%async_computation.3 | async-start | bytes 1015808 | tf_op jit(solution)/shard_map/all_to_all | solution.py:584
  88.7 4.0 %shard_map.251 = (f32[768,768]{1,0:T(8,128)}, f32[768,768]{1,0:T(8,128)}) custom-call(bf16[192,768]{1,0:T(8,128)(2,1)} %get-tuple-element.68.rows_ref, bf16[192,768]{1,0:T(8,128)(2,1)} %get-tuple-element.69.hidden, bf16[192,768]{1,0:T(8,128)(2,1)} %get-tuple-element.70.before, bf16[192,768]{1,0:T(8,128)(2,1)} %get-tuple-element.71.grads), custom_call_target="tpu_custom_call" | custom-call | tf_op jit(solution)/shard_map/pallas_call | solution.py:31
  92.7 4.6 %all-to-all-done.3.came = bf16[4,496,128]{2,1,0:T(8,128)(2,1)S(1)} async-done(((bf16[4,496,128]{2,1,0:T(8,128)(2,1)}), bf16[4,496,128]{2,1,0:T(8,128)(2,1)S(1)}, u32[]{:S(2)}, u32[]{:S(2)}) %all-to-all-start.3) | async-done | bytes 507936 | tf_op jit(solution)/shard_map/all_to_all | solution.py:584
  97.3 2.1 %shard_map.252 = (bf16[8,208,128]{2,1,0:T(8,128)(2,1)S(1)}, f32[16,128]{1,0:T(8,128)}, f32[192,128]{1,0:T(8,128)}) custom-call(s32[3]{0:T(128)S(1)} %pad_add_fusion.scalars, bf16[4,496,128]{2,1,0:T(8,128)(2,1)S(1)} %all-to-all-done.3.came, bf16[4,400,128]{2,1,0:T(8,128)(2,1)} %bitcast.35, f32[192,128]{1,0:T(8,128)} %get-tuple-element.75.own, ...), custom_call_target="tpu_custom_call" | custom-call | tf_op jit(solution)/shard_map/pallas_call | solution.py:31
  99.4 21.0 %all_to_all.33.came = bf16[8,208,128]{2,1,0:T(8,128)(2,1)S(1)} all-to-all(bf16[8,208,128]{2,1,0:T(8,128)(2,1)S(1)} %get-tuple-element.77), channel_id=1, replica_groups=mesh['expert'=8,'head'=4] {'expert'}, dimensions={0} | all-to-all | bytes 851968 | tf_op jit(solution)/shard_map/all_to_all | solution.py:597
  120.4 0.0 copy-start.1
  120.4 0.8 shard_map.253
  121.3 3.7 %all-to-all-start.5 = ((bf16[8,160,128]{2,1,0:T(8,128)(2,1)}), bf16[8,160,128]{2,1,0:T(8,128)(2,1)S(1)}, u32[]{:S(2)}, u32[]{:S(2)}) async-start(bf16[8,160,128]{2,1,0:T(8,128)(2,1)} %shard_map.253), calls=%async_computation.5 | async-start | bytes 655360 | tf_op jit(solution)/shard_map/all_to_all | solution.py:602
  124.9 0.0 copy-done.1
  125.0 1.9 %shard_map.255 = bf16[192,128]{1,0:T(8,128)(2,1)} custom-call(bf16[8,208,128]{2,1,0:T(8,128)(2,1)} %copy-done.1, f32[8,128]{1,0:T(8,128)} %get-tuple-element.58.side, f32[8,128]{1,0:T(8,128)} %get-tuple-element.82.gate, f32[192,128]{1,0:T(8,128)} %get-tuple-element.83.residual), custom_call_target="tpu_custom_call" | custom-call | tf_op jit(solution)/shard_map/pallas_call | solution.py:31
  126.8 0.0 all-gather.9.cloned.1.call-done
  126.8 0.0 all-gather.7.cloned.1.call-done
  126.8 4.4 %shard_map.254 = (f32[192,768]{1,0:T(8,128)}, f32[192,768]{1,0:T(8,128)}, f32[192,768]{1,0:T(8,128)}) custom-call(bf16[8,576,128]{2,1,0:T(8,128)(2,1)} %bitcast.45, bf16[8,4,192,128]{3,2,1,0:T(8,128)(2,1)} %bitcast.38, bf16[4,400,128]{2,1,0:T(8,128)(2,1)} %bitcast.36), custom_call_target="tpu_custom_call" | custom-call | tf_op jit(solution)/shard_map/pallas_call | solution.py:31
  131.2 2.4 %all-to-all-done.5.came = bf16[8,160,128]{2,1,0:T(8,128)(2,1)S(1)} async-done(((bf16[8,160,128]{2,1,0:T(8,128)(2,1)}), bf16[8,160,128]{2,1,0:T(8,128)(2,1)S(1)}, u32[]{:S(2)}, u32[]{:S(2)}) %all-to-all-start.5) | async-done | bytes 327712 | tf_op jit(solution)/shard_map/all_to_all | solution.py:602
  133.6 1.6 %shard_map.256 = (f32[192,768]{1,0:T(8,128)}, f32[8,768]{1,0:T(8,128)}, f32[3,32]{1,0:T(4,128)}, f32[8,256]{1,0:T(8,128)S(1)}, f32[1,1]{1,0:T(1,128)}) custom-call(bf16[8,160,128]{2,1,0:T(8,128)(2,1)S(1)} %all-to-all-done.5.came, s32[1,255]{1,0:T(1,128)} %bitcast.58, f32[8,128]{1,0:T(8,128)} %get-tuple-element.62.stats), custom_call_target="tpu_custom_call" | custom-call | tf_op jit(solution)/shard_map/pallas_call | solution.py:31
  135.2 0.6 fusion
  (1 shorter events, 0.0 us)
Async XLA Ops:
  7.2 119.6 %all-gather.9.cloned.1.call-start = ((), (), s32[]{:S(2)}) async-start(), calls=%async_computation.7 | async-start | bytes 1622016 | tf_op jit(solution)/shard_map/all_gather | solution.py:532
  7.9 118.9 %all-gather.7.cloned.1.call-start = ((), (), s32[]{:S(2)}) async-start(), calls=%async_computation.6 | async-start | bytes 1327104 | tf_op jit(solution)/shard_map/all_gather | solution.py:582
  18.5 33.2 %copy-start = (bf16[1600,128]{1,0:T(8,128)(2,1)}, bf16[1600,128]{1,0:T(8,128)(2,1)S(1)}, u32[]{:S(2)}) copy-start(bf16[1600,128]{1,0:T(8,128)(2,1)S(1)} %all-gather) | copy-start | bytes 1228804
  85.2 12.1 %all-to-all-start.3 = ((bf16[4,496,128]{2,1,0:T(8,128)(2,1)}), bf16[4,496,128]{2,1,0:T(8,128)(2,1)S(1)}, u32[]{:S(2)}, u32[]{:S(2)}) async-start(bf16[4,496,128]{2,1,0:T(8,128)(2,1)} %get-tuple-element.67), calls=%async_computation.3 | async-start | bytes 1015808 | tf_op jit(solution)/shard_map/all_to_all | solution.py:584
  120.4 4.5 %copy-start.1 = (bf16[8,208,128]{2,1,0:T(8,128)(2,1)}, bf16[8,208,128]{2,1,0:T(8,128)(2,1)S(1)}, u32[]{:S(2)}) copy-start(bf16[8,208,128]{2,1,0:T(8,128)(2,1)S(1)} %all_to_all.33.came) | copy-start | bytes 1277956
  121.3 12.3 %all-to-all-start.5 = ((bf16[8,160,128]{2,1,0:T(8,128)(2,1)}), bf16[8,160,128]{2,1,0:T(8,128)(2,1)S(1)}, u32[]{:S(2)}, u32[]{:S(2)}) async-start(bf16[8,160,128]{2,1,0:T(8,128)(2,1)} %shard_map.253), calls=%async_computation.5 | async-start | bytes 655360 | tf_op jit(solution)/shard_map/all_to_all | solution.py:602
Sparse Core Ops, SparseCore 0:
  10.9 59.0 all-gather.8
  85.3 40.2 all-gather.6

commit v13 on v12

--- a/solution.py
+++ b/solution.py
@@ -116,15 +116,18 @@
     return jnp.concatenate([rows[i * size : (i + 1) * size] for i in range(pieces)], axis=1)
 
 
-def fold_rest(rest, side):
-    groups = [rest[i : i + 8] for i in range(0, rest.shape[0], 8)]
+def side_block(side):
     count = side.shape[1]
     spot = lanes((8, 64))
-    last = jnp.zeros((8, 64), f32)
-    for g in range(len(groups)):
+    out = jnp.zeros((8, 64), f32)
+    for g in range(side.shape[0] // 8):
         for j in range(count):
-            last = jnp.where(spot == g * count + j, side[8 * g : 8 * g + 8, j : j + 1], last)
-    groups.append(last)
+            out = jnp.where(spot == g * count + j, side[8 * g : 8 * g + 8, j : j + 1], out)
+    return out
+
+
+def fold_rest(rest, last):
+    groups = [rest[i : i + 8] for i in range(0, rest.shape[0], 8)] + [last]
     if len(groups) % 2:
         groups.append(jnp.zeros((8, 64), f32))
     return [jnp.concatenate(groups[i : i + 2], axis=1) for i in range(0, len(groups), 2)]
@@ -148,13 +151,16 @@
 
 
 def attend_kernel(
-    scale, scalars, packed, wq, wk, wv, w_output, buckets, table, qkv_ref, weights_ref, attended_ref, branch_ref
+    scale, scalars, packed, wq, wk, wv, w_output, buckets, table, qkv_ref, weights_ref, attended_ref, branch_ref,
+    scale_ref,
 ):
     heads, tok, _ = weights_ref.shape
     col = wq.shape[0]
     size = col // heads
     x = tall(packed, 0, col)
-    normed = (x * token_scale(x) * all_gains(packed)[0]).astype(bf16)
+    scale_one = token_scale(x)
+    scale_ref[...] = jnp.broadcast_to(scale_one, scale_ref.shape)
+    normed = (x * scale_one * all_gains(packed)[0]).astype(bf16)
     projected = []
     for i, w in enumerate((wq, wk, wv)):
         rows = mm(w[...], normed).astype(bf16)
@@ -260,10 +266,11 @@
     side = side_lanes(total, 4, high_low(gate_grad) + high_low(stats[:, 0:1]))
     for b in range(experts):
         at = slice(b * slots, (b + 1) * slots)
+        last = side_block(side[at])
         for i in range(heads):
             mine = rows_grad[at, i * col : (i + 1) * col]
             back_ref[b * heads + i] = jnp.concatenate(
-                [mine[:, :128]] + fold_rest(mine[:, 128:], side[at]), axis=0
+                [mine[:, :128]] + fold_rest(mine[:, 128:], last), axis=0
             ).astype(bf16)
 
 
@@ -385,7 +392,7 @@
             ).astype(bf16)
 
 
-def first_kernel(scalars, came, packed, own, *refs):
+def first_kernel(came, block, scale_one, own, *refs):
     shares, (ret_ref, gain_ref, input_ref) = refs[:-3], refs[-3:]
     col, tok = own.shape
     heads = came.shape[0]
@@ -394,10 +401,8 @@
     for i in range(1, heads):
         total = total + came[i].astype(f32)
     mean = (total[col : col + 1] + total[col + 1 : col + 2]) * (1.0 / (heads * col))
-    scale = token_scale(tall(packed, 0, col))
-    mine = packed[0].astype(f32)
-    for i in range(1, heads):
-        mine = jnp.where(scalars[1] == i, packed[i].astype(f32), mine)
+    scale = scale_one[0:1, :]
+    mine = block[...].astype(f32)
     unit = mine[:col] * scale
     gain = gain_columns(mine[2 * col : 2 * col + 16])[0]
     input_ref[...] = own[...] + scale * (total[:col] * gain - unit * mean)
@@ -410,11 +415,11 @@
     count = produced.shape[0] * 2 // 3
     top = produced[:count]
     rest = jnp.concatenate([produced[count:, :64], produced[count:, 64:]], axis=0)
-    rest = jnp.concatenate([rest, jnp.zeros((count, 64), f32)], axis=1)
     slots = count // experts
+    none = jnp.zeros((8, 64), f32)
     for e in range(experts):
         at = slice(e * slots, (e + 1) * slots)
-        pieces = [top[at], rest[at]]
+        pieces = [top[at]] + fold_rest(rest[at], none)
         if shares:
             share = shares[0][e].astype(f32)
             if e == 0:
@@ -428,15 +433,16 @@
     for e in range(1, came.shape[0]):
         total = total + came[e].astype(f32)
     for e in range(came.shape[0]):
-        share_ref[e] = total[2 * slots :].astype(bf16)
+        share_ref[e] = total[folded_rows(slots) :].astype(bf16)
 
 
 def add_returned(slots, blocks, side, gate, residual):
     col = residual.shape[0]
     top = jnp.concatenate([block[:slots] for block in blocks], axis=0).astype(bf16)
-    rest = jnp.concatenate([block[slots : 2 * slots] for block in blocks], axis=0).astype(bf16)
+    rests = [unfold_rest(block[slots : folded_rows(slots)], slots, 1)[0] for block in blocks]
+    rest = jnp.concatenate(rests, axis=0).astype(bf16)
     pick = pick_slots(side[0:1, :].astype(jnp.int32), len(blocks) * slots).astype(bf16)
-    returned = jnp.concatenate([mm(top, pick, tn), mm(rest, pick, tn)[: col - 128]], axis=0)
+    returned = jnp.concatenate([mm(top, pick, tn), mm(rest, pick, tn)], axis=0)
     return (residual[...] + gate[0:1, :] * returned).astype(bf16)
 
 
@@ -526,15 +532,15 @@
     buckets_row = buckets[None]
 
     gains = jnp.concatenate([gain_attn, gain_ffn]).reshape(3, 128)
-    gains = jnp.concatenate([inputs.T, out_grad.T, gains, jnp.zeros((13, 128), bf16)], axis=0)
-    packed = lax.all_gather(gains, "head")
+    own_block = jnp.concatenate([inputs.T, out_grad.T, gains, jnp.zeros((13, 128), bf16)], axis=0)
+    packed = lax.all_gather(own_block, "head")
     if joined:
         all_in = lax.all_gather(inputs.T, ("expert", "head")).reshape(groups, heads, col, tok)
-    qkv, weights, attended, branch = call(
+    qkv, weights, attended, branch, scale_one = call(
         functools.partial(attend_kernel, scale),
         [
             ((3, col, tok), bf16, 1), ((heads_here, tok, tok), f32, 1), ((col, tok), bf16, 1),
-            ((heads, col, tok), bf16),
+            ((heads, col, tok), bf16), ((8, tok), f32, 1),
         ],
         scalars, packed, far(wq), far(wk), far(wv), far(w_output), far(buckets_row), far(bias_table.T),
     )
@@ -589,10 +595,10 @@
     ret, gain_one_part, input_grad = call(
         first_kernel,
         [
-            ((experts, 2 * slots + (shares[0].shape[1] if joined else 0), 128), bf16),
+            ((experts, folded_rows(slots) + (shares[0].shape[1] if joined else 0), 128), bf16),
             ((16, 128), f32, 1), ((col, tok), f32, 1),
         ],
-        scalars, first, far(packed), far(residual_grad_own), *([far(shares[0])] if joined else []),
+        first, far(own_block), far(scale_one), far(residual_grad_own), *([far(shares[0])] if joined else []),
     )
     ret = lax.all_to_all(ret, "expert", split_axis=0, concat_axis=0, tiled=True)
     if joined:

time: 143 us -> 143 us (level)
  no operation moved by 1% of the time
where the time goes in v13:
time: 143 us; the launch traced here: 142 us
  blocking collectives  78.4 us (55%)
  Pallas kernels  31.5 us (22%)
  between operations  14.8 us (10%)
  waiting for transfers between devices  7.6 us (5%)
  starting transfers between devices  6.99 us (5%)
  other arithmetic  1.76 us (1%)
    pallas_call x11, Pallas kernels, call(): pl.pallas_call(body, out_shape=shapes, in_specs=in_specs, compiler_params...  31.5 us
    all_to_all x1, blocking collectives, shards(): ret = lax.all_to_all(ret, 'expert', split_axis=0, concat_axis=0, tiled=True)  20.4 us
    all_to_all x1, blocking collectives, shards(): lax.all_to_all(back, ('expert', 'head'), split_axis=0, concat_axis=0, til...  15.7 us
    all_to_all x1, blocking collectives, shards(): lax.all_to_all(send, 'expert', split_axis=0, concat_axis=0, tiled=True)  13.7 us
    all_gather x1, blocking collectives, shards(): packed = lax.all_gather(own_block, 'head')  8.02 us
    all_to_all x1, blocking collectives, shards(): lax.all_to_all(branch, 'head', split_axis=0, concat_axis=0, tiled=True)  7.69 us
    all_gather x1, blocking collectives, shards(): quarters = lax.all_gather(quarter.reshape(total, 2 * col), 'head')  6.68 us
    all_gather x1, blocking collectives, shards(): expert_grad = lax.all_gather(grad_own, 'head')  6.15 us
  transfers between devices with their start and end apart: 4, of which 2 were waited for; matrix products, arithmetic and copies ran while one was open for 1% of the time, Pallas kernels for 21%

profile of v13, /device:TPU:0, one launch (start us, length us, event | category | flops | bytes accessed | tf_op | source)
XLA Modules:
  0.0 141.7 jit_solution(2654466720427173673)
XLA Ops:
  7.2 0.0 all-gather.9.cloned.1.call-start
  7.2 0.7 all-gather.9.cloned.1.call-update
  7.9 0.0 all-gather.7.cloned.1.call-start
  8.6 0.1 pad.3.clone
  8.7 0.1 pad_add_fusion.scalars
  8.8 0.7 maximum_bitcast_fusion
  9.5 0.9 maximum_maximum_fusion.block
  10.5 0.0 copy-start.2
  10.5 8.0 %all-gather = bf16[1600,128]{1,0:T(8,128)(2,1)S(1)} all-gather(bf16[400,128]{1,0:T(8,128)(2,1)S(1)} %maximum_maximum_fusion.block), channel_id=2, replica_groups=mesh['expert'=8,'head'=4] {'head'}, dimensions={0}, use_global_device_ids=true | all-gather | bytes 512000 | tf_op jit(solution)/shard_map/all_gather | solution.py:536
  18.5 0.0 copy-start
  18.5 3.5 %shard_map.246 = (bf16[3,192,128]{2,1,0:T(8,128)(2,1)}, f32[3,128,128]{2,1,0:T(8,128)}, bf16[192,128]{1,0:T(8,128)(2,1)}, bf16[4,192,128]{2,1,0:T(8,128)(2,1)S(1)}, f32[8,128]{1,0:T(8,128)}) custom-call(s32[3]{0:T(128)S(1)} %pad_add_fusion.scalars, bf16[4,400,128]{2,1,0:T(8,128)(2,1)S(1)} %bitcast.32, bf16[192,768]{1,0:T(8,128)(2,1)} %bitcast.38, ...), custom_call_target="tpu_custom_call" | custom-call | tf_op jit(solution)/shard_map/pallas_call | solution.py:31
  22.0 7.7 %all_to_all.30.came = bf16[4,192,128]{2,1,0:T(8,128)(2,1)S(1)} all-to-all(bf16[4,192,128]{2,1,0:T(8,128)(2,1)S(1)} %get-tuple-element.56), channel_id=1, replica_groups=mesh['expert'=8,'head'=4] {'head'}, dimensions={0} | all-to-all | bytes 393216 | tf_op jit(solution)/shard_map/all_to_all | solution.py:548
  29.7 1.6 %shard_map.247 = (f32[192,128]{1,0:T(8,128)}, bf16[192,128]{1,0:T(8,128)(2,1)}, f32[8,128]{1,0:T(8,128)}, bf16[8,24,384]{2,1,0:T(8,128)(2,1)S(1)}) custom-call(s32[3]{0:T(128)S(1)} %pad_add_fusion.scalars, bf16[4,192,128]{2,1,0:T(8,128)(2,1)S(1)} %all_to_all.30.came, bf16[192,128]{1,0:T(8,128)(2,1)} %bitcast.50, bf16[192,128]{1,0:T(8,128)(2,1)} %bitcast.52, ...), custom_call_target="tpu_custom_call" | custom-call | tf_op jit(solution)/shard_map/pallas_call | solution.py:31
  31.3 13.7 %all_to_all.31 = bf16[8,24,384]{2,1,0:T(8,128)(2,1)S(1)} all-to-all(bf16[8,24,384]{2,1,0:T(8,128)(2,1)S(1)} %get-tuple-element.57), channel_id=1, replica_groups=mesh['expert'=8,'head'=4] {'expert'}, dimensions={0} | all-to-all | bytes 294912 | tf_op jit(solution)/shard_map/all_to_all | solution.py:554
  45.0 6.7 %all_gather.29.quarters = bf16[4,192,384]{2,1,0:T(8,128)(2,1)S(1)} all-gather(bf16[1,192,384]{2,1,0:T(8,128)(2,1)S(1)} %bitcast.47), channel_id=1, replica_groups=mesh['expert'=8,'head'=4] {'head'}, dimensions={0}, use_global_device_ids=true | all-gather | bytes 737280 | tf_op jit(solution)/shard_map/all_gather | solution.py:555
  51.7 0.0 copy-done.2
  51.7 0.0 copy-done
  51.7 4.8 %shard_map.248 = (bf16[32,40,128]{2,1,0:T(8,128)(2,1)S(1)}, bf16[4,288,128]{2,1,0:T(8,128)(2,1)}, bf16[192,768]{1,0:T(8,128)(2,1)}, bf16[192,768]{1,0:T(8,128)(2...) custom-call(s32[3]{0:T(128)S(1)} %pad_add_fusion.scalars, bf16[4,192,384]{2,1,0:T(8,128)(2,1)S(1)} %all_gather.29.quarters, ...), custom_call_target="tpu_custom_call" | custom-call | tf_op jit(solution)/shard_map/pallas_call | solution.py:31
  56.5 15.7 %all_to_all.32.came = bf16[32,40,128]{2,1,0:T(8,128)(2,1)S(1)} all-to-all(bf16[32,40,128]{2,1,0:T(8,128)(2,1)S(1)} %get-tuple-element.58), channel_id=1, replica_groups=mesh['expert'=8,'head'=4] {'expert','head'}, dimensions={0} | all-to-all | bytes 655360 | tf_op jit(solution)/shard_map/all_to_all | solution.py:563
  72.2 1.8 %shard_map.249 = (bf16[384,128]{1,0:T(8,128)(2,1)S(1)}, f32[8,128]{1,0:T(8,128)}, f32[8,128]{1,0:T(8,128)}) custom-call(bf16[32,40,128]{2,1,0:T(8,128)(2,1)S(1)} %all_to_all.32.came, f32[8,128]{1,0:T(8,128)} %get-tuple-element.59.side, bf16[192,128]{1,0:T(8,128)(2,1)} %get-tuple-element.60.low), custom_call_target="tpu_custom_call" | custom-call | tf_op jit(solution)/shard_map/pallas_call | solution.py:31
  74.0 6.1 %all-gather.1 = bf16[1536,128]{1,0:T(8,128)(2,1)S(1)} all-gather(bf16[384,128]{1,0:T(8,128)(2,1)S(1)} %get-tuple-element.61), channel_id=3, replica_groups=mesh['expert'=8,'head'=4] {'head'}, dimensions={0}, use_global_device_ids=true | all-gather | bytes 491520 | tf_op jit(solution)/shard_map/all_gather | solution.py:569
  80.2 5.0 %shard_map.250 = (bf16[576,128]{1,0:T(8,128)(2,1)}, bf16[4,496,128]{2,1,0:T(8,128)(2,1)}, f32[192,128]{1,0:T(8,128)}, f32[8,128]{1,0:T(8,128)}, bf16[8,160,128]{2,1,0:T(8,128)(2,1)}) custom-call(s32[3]{0:T(128)S(1)} %pad_add_fusion.scalars, bf16[4,400,128]{2,1,0:T(8,128)(2,1)} %bitcast.34, bf16[4,384,128]{2,1,0:T(8,128)(2,1)S(1)} %bitcast.36, ...), custom_call_target="tpu_custom_call" | custom-call | tf_op jit(solution)/shard_map/pallas_call | solution.py:31
  85.1 0.0 all-gather.7.cloned.1.call-update
  85.2 3.5 %all-to-all-start.3 = ((bf16[4,496,128]{2,1,0:T(8,128)(2,1)}), bf16[4,496,128]{2,1,0:T(8,128)(2,1)S(1)}, u32[]{:S(2)}, u32[]{:S(2)}) async-start(bf16[4,496,128]{2,1,0:T(8,128)(2,1)} %get-tuple-element.68), calls=%async_computation.3 | async-start | bytes 1015808 | tf_op jit(solution)/shard_map/all_to_all | solution.py:590
  88.7 4.0 %shard_map.251 = (f32[768,768]{1,0:T(8,128)}, f32[768,768]{1,0:T(8,128)}) custom-call(bf16[192,768]{1,0:T(8,128)(2,1)} %get-tuple-element.69.rows_ref, bf16[192,768]{1,0:T(8,128)(2,1)} %get-tuple-element.70.hidden, bf16[192,768]{1,0:T(8,128)(2,1)} %get-tuple-element.71.before, bf16[192,768]{1,0:T(8,128)(2,1)} %get-tuple-element.72.grads), custom_call_target="tpu_custom_call" | custom-call | tf_op jit(solution)/shard_map/pallas_call | solution.py:31
  92.7 4.6 %all-to-all-done.3.came = bf16[4,496,128]{2,1,0:T(8,128)(2,1)S(1)} async-done(((bf16[4,496,128]{2,1,0:T(8,128)(2,1)}), bf16[4,496,128]{2,1,0:T(8,128)(2,1)S(1)}, u32[]{:S(2)}, u32[]{:S(2)}) %all-to-all-start.3) | async-done | bytes 507936 | tf_op jit(solution)/shard_map/all_to_all | solution.py:590
  97.3 2.0 %shard_map.252 = (bf16[8,200,128]{2,1,0:T(8,128)(2,1)S(1)}, f32[16,128]{1,0:T(8,128)}, f32[192,128]{1,0:T(8,128)}) custom-call(bf16[4,496,128]{2,1,0:T(8,128)(2,1)S(1)} %all-to-all-done.3.came, bf16[400,128]{1,0:T(8,128)(2,1)} %copy-done.2, f32[8,128]{1,0:T(8,128)} %get-tuple-element.76.scale_one, f32[192,128]{1,0:T(8,128)} %get-tuple-element.77.own, ...), custom_call_target="tpu_custom_call" | custom-call | tf_op jit(solution)/shard_map/pallas_call | solution.py:31
  99.3 20.4 %all_to_all.33.came = bf16[8,200,128]{2,1,0:T(8,128)(2,1)S(1)} all-to-all(bf16[8,200,128]{2,1,0:T(8,128)(2,1)S(1)} %get-tuple-element.79), channel_id=1, replica_groups=mesh['expert'=8,'head'=4] {'expert'}, dimensions={0} | all-to-all | bytes 819200 | tf_op jit(solution)/shard_map/all_to_all | solution.py:603
  119.8 0.0 copy-start.1
  119.8 0.8 shard_map.253
  120.6 3.4 %all-to-all-start.5 = ((bf16[8,160,128]{2,1,0:T(8,128)(2,1)}), bf16[8,160,128]{2,1,0:T(8,128)(2,1)S(1)}, u32[]{:S(2)}, u32[]{:S(2)}) async-start(bf16[8,160,128]{2,1,0:T(8,128)(2,1)} %shard_map.253), calls=%async_computation.5 | async-start | bytes 655360 | tf_op jit(solution)/shard_map/all_to_all | solution.py:608
  124.1 0.0 copy-done.1
  124.1 1.9 %shard_map.255 = bf16[192,128]{1,0:T(8,128)(2,1)} custom-call(bf16[8,200,128]{2,1,0:T(8,128)(2,1)} %copy-done.1, f32[8,128]{1,0:T(8,128)} %get-tuple-element.59.side, f32[8,128]{1,0:T(8,128)} %get-tuple-element.84.gate, f32[192,128]{1,0:T(8,128)} %get-tuple-element.85.residual), custom_call_target="tpu_custom_call" | custom-call | tf_op jit(solution)/shard_map/pallas_call | solution.py:31
  126.0 0.0 all-gather.9.cloned.1.call-done
  126.0 0.0 all-gather.7.cloned.1.call-done
  126.0 4.4 %shard_map.254 = (f32[192,768]{1,0:T(8,128)}, f32[192,768]{1,0:T(8,128)}, f32[192,768]{1,0:T(8,128)}) custom-call(bf16[8,576,128]{2,1,0:T(8,128)(2,1)} %bitcast.44, bf16[8,4,192,128]{3,2,1,0:T(8,128)(2,1)} %bitcast.37, bf16[4,400,128]{2,1,0:T(8,128)(2,1)} %bitcast.35), custom_call_target="tpu_custom_call" | custom-call | tf_op jit(solution)/shard_map/pallas_call | solution.py:31
  130.4 2.3 %all-to-all-done.5.came = bf16[8,160,128]{2,1,0:T(8,128)(2,1)S(1)} async-done(((bf16[8,160,128]{2,1,0:T(8,128)(2,1)}), bf16[8,160,128]{2,1,0:T(8,128)(2,1)S(1)}, u32[]{:S(2)}, u32[]{:S(2)}) %all-to-all-start.5) | async-done | bytes 327712 | tf_op jit(solution)/shard_map/all_to_all | solution.py:608
  132.7 1.6 %shard_map.256 = (f32[192,768]{1,0:T(8,128)}, f32[8,768]{1,0:T(8,128)}, f32[3,32]{1,0:T(4,128)}, f32[8,256]{1,0:T(8,128)S(1)}, f32[1,1]{1,0:T(1,128)}) custom-call(bf16[8,160,128]{2,1,0:T(8,128)(2,1)S(1)} %all-to-all-done.5.came, s32[1,255]{1,0:T(1,128)} %bitcast.57, f32[8,128]{1,0:T(8,128)} %get-tuple-element.63.stats), custom_call_target="tpu_custom_call" | custom-call | tf_op jit(solution)/shard_map/pallas_call | solution.py:31
  134.3 0.6 fusion
  (1 shorter events, 0.0 us)
Async XLA Ops:
  7.2 118.8 %all-gather.9.cloned.1.call-start = ((), (), s32[]{:S(2)}) async-start(), calls=%async_computation.7 | async-start | bytes 1622016 | tf_op jit(solution)/shard_map/all_gather | solution.py:538
  7.9 118.1 %all-gather.7.cloned.1.call-start = ((), (), s32[]{:S(2)}) async-start(), calls=%async_computation.6 | async-start | bytes 1327104 | tf_op jit(solution)/shard_map/all_gather | solution.py:588
  10.5 41.2 %copy-start.2 = (bf16[400,128]{1,0:T(8,128)(2,1)}, bf16[400,128]{1,0:T(8,128)(2,1)S(1)}, u32[]{:S(2)}) copy-start(bf16[400,128]{1,0:T(8,128)(2,1)S(1)} %maximum_maximum_fusion.block) | copy-start | bytes 307204
  18.5 33.2 %copy-start = (bf16[1600,128]{1,0:T(8,128)(2,1)}, bf16[1600,128]{1,0:T(8,128)(2,1)S(1)}, u32[]{:S(2)}) copy-start(bf16[1600,128]{1,0:T(8,128)(2,1)S(1)} %all-gather) | copy-start | bytes 1228804
  85.2 12.1 %all-to-all-start.3 = ((bf16[4,496,128]{2,1,0:T(8,128)(2,1)}), bf16[4,496,128]{2,1,0:T(8,128)(2,1)S(1)}, u32[]{:S(2)}, u32[]{:S(2)}) async-start(bf16[4,496,128]{2,1,0:T(8,128)(2,1)} %get-tuple-element.68), calls=%async_computation.3 | async-start | bytes 1015808 | tf_op jit(solution)/shard_map/all_to_all | solution.py:590
  119.8 4.3 %copy-start.1 = (bf16[8,200,128]{2,1,0:T(8,128)(2,1)}, bf16[8,200,128]{2,1,0:T(8,128)(2,1)S(1)}, u32[]{:S(2)}) copy-start(bf16[8,200,128]{2,1,0:T(8,128)(2,1)S(1)} %all_to_all.33.came) | copy-start | bytes 1228804
  120.6 12.0 %all-to-all-start.5 = ((bf16[8,160,128]{2,1,0:T(8,128)(2,1)}), bf16[8,160,128]{2,1,0:T(8,128)(2,1)S(1)}, u32[]{:S(2)}, u32[]{:S(2)}) async-start(bf16[8,160,128]{2,1,0:T(8,128)(2,1)} %shard_map.253), calls=%async_computation.5 | async-start | bytes 655360 | tf_op jit(solution)/shard_map/all_to_all | solution.py:608
Sparse Core Ops, SparseCore 0:
  10.9 59.0 all-gather.8
  85.3 40.3 all-gather.6

commit v14 on v13

--- a/solution.py
+++ b/solution.py
@@ -591,7 +591,6 @@
     in_weight_grad, out_weight_grad = call(
         weights_kernel, [((width, width), f32, 1)] * 2, far(rows), far(hidden), far(before_grad), far(back_rows)
     )
-    first, in_weight_grad, out_weight_grad = lax.optimization_barrier((first, in_weight_grad, out_weight_grad))
     ret, gain_one_part, input_grad = call(
         first_kernel,
         [
@@ -601,6 +600,7 @@
         first, far(own_block), far(scale_one), far(residual_grad_own), *([far(shares[0])] if joined else []),
     )
     ret = lax.all_to_all(ret, "expert", split_axis=0, concat_axis=0, tiled=True)
+    ret, in_weight_grad, out_weight_grad = lax.optimization_barrier((ret, in_weight_grad, out_weight_grad))
     if joined:
         share = call(
             functools.partial(share_kernel, slots), [(shares[0].shape, bf16)], ret

time: 143 us -> 142 us (level)
  blocking collectives: 78.4 us -> 69 us
  waiting for transfers between devices: 7.6 us -> 16.8 us
    all_to_all x1, blocking collectives: 20.4 us -> 11.1 us  [shards(): lax.all_to_all(first, 'head', split_axis=0, concat_axis=0, tiled=True)]
    all_to_all x1, waiting for transfers between devices: 4.62 us -> 12.3 us  [shards(): ret = lax.all_to_all(ret, 'expert', split_axis=0, concat_axis=0, tiled=True)]
    all_gather x1, waiting for transfers between devices: 0.01 us -> 2.07 us  [shards(): late_all = lax.all_gather(late, 'expert')]
  transfers between devices with their start and end apart: 4 -> 4, of which waited for: 2 -> 3; matrix products, arithmetic and copies ran while one was open for 1% -> 1% of each run, Pallas kernels for 21% -> 21%
where the time goes in v14:
time: 142 us
  blocking collectives  69 us (49%)
  Pallas kernels  31.5 us (22%)
  waiting for transfers between devices  16.8 us (12%)
  between operations  14.8 us (10%)
  starting transfers between devices  6.97 us (5%)
  other arithmetic  1.76 us (1%)
    pallas_call x11, Pallas kernels, call(): pl.pallas_call(body, out_shape=shapes, in_specs=in_specs, compiler_params...  31.5 us
    all_to_all x1, blocking collectives, shards(): lax.all_to_all(back, ('expert', 'head'), split_axis=0, concat_axis=0, til...  15.7 us
    all_to_all x1, blocking collectives, shards(): lax.all_to_all(send, 'expert', split_axis=0, concat_axis=0, tiled=True)  13.7 us
    all_to_all x1, waiting for transfers between devices, shards(): ret = lax.all_to_all(ret, 'expert', split_axis=0, concat_axis=0, tiled=True)  12.3 us
    all_to_all x1, blocking collectives, shards(): lax.all_to_all(first, 'head', split_axis=0, concat_axis=0, tiled=True)  11.1 us
    all_gather x1, blocking collectives, shards(): packed = lax.all_gather(own_block, 'head')  8.02 us
    all_to_all x1, blocking collectives, shards(): lax.all_to_all(branch, 'head', split_axis=0, concat_axis=0, tiled=True)  7.69 us
    all_gather x1, blocking collectives, shards(): quarters = lax.all_gather(quarter.reshape(total, 2 * col), 'head')  6.68 us
  transfers between devices with their start and end apart: 4, of which 3 were waited for; matrix products, arithmetic and copies ran while one was open for 1% of the time, Pallas kernels for 21%

profile of v14, /device:TPU:0, one launch (start us, length us, event | category | flops | bytes accessed | tf_op | source)
XLA Modules:
  0.0 141.5 jit_solution(14273176821378626119)
XLA Ops:
  7.2 0.0 all-gather.9.cloned.1.call-start
  7.2 0.7 all-gather.9.cloned.1.call-update
  7.9 0.0 all-gather.7.cloned.1.call-start
  8.6 0.1 pad.3.clone
  8.7 0.1 pad_add_fusion.scalars
  8.8 0.7 maximum_bitcast_fusion
  9.5 0.9 maximum_maximum_fusion.block
  10.5 0.0 copy-start.2
  10.5 8.0 %all-gather = bf16[1600,128]{1,0:T(8,128)(2,1)S(1)} all-gather(bf16[400,128]{1,0:T(8,128)(2,1)S(1)} %maximum_maximum_fusion.block), channel_id=2, replica_groups=mesh['expert'=8,'head'=4] {'head'}, dimensions={0}, use_global_device_ids=true | all-gather | bytes 512000 | tf_op jit(solution)/shard_map/all_gather | solution.py:536
  18.5 0.0 copy-start
  18.5 3.5 %shard_map.246 = (bf16[3,192,128]{2,1,0:T(8,128)(2,1)}, f32[3,128,128]{2,1,0:T(8,128)}, bf16[192,128]{1,0:T(8,128)(2,1)}, bf16[4,192,128]{2,1,0:T(8,128)(2,1)S(1)}, f32[8,128]{1,0:T(8,128)}) custom-call(s32[3]{0:T(128)S(1)} %pad_add_fusion.scalars, bf16[4,400,128]{2,1,0:T(8,128)(2,1)S(1)} %bitcast.32, bf16[192,768]{1,0:T(8,128)(2,1)} %bitcast.38, ...), custom_call_target="tpu_custom_call" | custom-call | tf_op jit(solution)/shard_map/pallas_call | solution.py:31
  22.0 7.7 %all_to_all.30.came = bf16[4,192,128]{2,1,0:T(8,128)(2,1)S(1)} all-to-all(bf16[4,192,128]{2,1,0:T(8,128)(2,1)S(1)} %get-tuple-element.56), channel_id=1, replica_groups=mesh['expert'=8,'head'=4] {'head'}, dimensions={0} | all-to-all | bytes 393216 | tf_op jit(solution)/shard_map/all_to_all | solution.py:548
  29.7 1.6 %shard_map.247 = (f32[192,128]{1,0:T(8,128)}, bf16[192,128]{1,0:T(8,128)(2,1)}, f32[8,128]{1,0:T(8,128)}, bf16[8,24,384]{2,1,0:T(8,128)(2,1)S(1)}) custom-call(s32[3]{0:T(128)S(1)} %pad_add_fusion.scalars, bf16[4,192,128]{2,1,0:T(8,128)(2,1)S(1)} %all_to_all.30.came, bf16[192,128]{1,0:T(8,128)(2,1)} %bitcast.50, bf16[192,128]{1,0:T(8,128)(2,1)} %bitcast.52, ...), custom_call_target="tpu_custom_call" | custom-call | tf_op jit(solution)/shard_map/pallas_call | solution.py:31
  31.3 13.7 %all_to_all.31 = bf16[8,24,384]{2,1,0:T(8,128)(2,1)S(1)} all-to-all(bf16[8,24,384]{2,1,0:T(8,128)(2,1)S(1)} %get-tuple-element.57), channel_id=1, replica_groups=mesh['expert'=8,'head'=4] {'expert'}, dimensions={0} | all-to-all | bytes 294912 | tf_op jit(solution)/shard_map/all_to_all | solution.py:554
  45.0 6.7 %all_gather.29.quarters = bf16[4,192,384]{2,1,0:T(8,128)(2,1)S(1)} all-gather(bf16[1,192,384]{2,1,0:T(8,128)(2,1)S(1)} %bitcast.47), channel_id=1, replica_groups=mesh['expert'=8,'head'=4] {'head'}, dimensions={0}, use_global_device_ids=true | all-gather | bytes 737280 | tf_op jit(solution)/shard_map/all_gather | solution.py:555
  51.7 0.0 copy-done.2
  51.7 0.0 copy-done
  51.7 4.8 %shard_map.248 = (bf16[32,40,128]{2,1,0:T(8,128)(2,1)S(1)}, bf16[4,288,128]{2,1,0:T(8,128)(2,1)}, bf16[192,768]{1,0:T(8,128)(2,1)}, bf16[192,768]{1,0:T(8,128)(2...) custom-call(s32[3]{0:T(128)S(1)} %pad_add_fusion.scalars, bf16[4,192,384]{2,1,0:T(8,128)(2,1)S(1)} %all_gather.29.quarters, ...), custom_call_target="tpu_custom_call" | custom-call | tf_op jit(solution)/shard_map/pallas_call | solution.py:31
  56.5 15.7 %all_to_all.32.came = bf16[32,40,128]{2,1,0:T(8,128)(2,1)S(1)} all-to-all(bf16[32,40,128]{2,1,0:T(8,128)(2,1)S(1)} %get-tuple-element.58), channel_id=1, replica_groups=mesh['expert'=8,'head'=4] {'expert','head'}, dimensions={0} | all-to-all | bytes 655360 | tf_op jit(solution)/shard_map/all_to_all | solution.py:563
  72.2 1.8 %shard_map.249 = (bf16[384,128]{1,0:T(8,128)(2,1)S(1)}, f32[8,128]{1,0:T(8,128)}, f32[8,128]{1,0:T(8,128)}) custom-call(bf16[32,40,128]{2,1,0:T(8,128)(2,1)S(1)} %all_to_all.32.came, f32[8,128]{1,0:T(8,128)} %get-tuple-element.59.side, bf16[192,128]{1,0:T(8,128)(2,1)} %get-tuple-element.60.low), custom_call_target="tpu_custom_call" | custom-call | tf_op jit(solution)/shard_map/pallas_call | solution.py:31
  74.0 6.1 %all-gather.1 = bf16[1536,128]{1,0:T(8,128)(2,1)S(1)} all-gather(bf16[384,128]{1,0:T(8,128)(2,1)S(1)} %get-tuple-element.61), channel_id=3, replica_groups=mesh['expert'=8,'head'=4] {'head'}, dimensions={0}, use_global_device_ids=true | all-gather | bytes 491520 | tf_op jit(solution)/shard_map/all_gather | solution.py:569
  80.2 4.8 %shard_map.250 = (bf16[576,128]{1,0:T(8,128)(2,1)}, bf16[4,496,128]{2,1,0:T(8,128)(2,1)S(1)}, f32[192,128]{1,0:T(8,128)}, f32[8,128]{1,0:T(8,128)}, bf16[8,160,128]{2,1,0:T(8,128)(2,1)}) custom-call(s32[3]{0:T(128)S(1)} %pad_add_fusion.scalars, bf16[4,400,128]{2,1,0:T(8,128)(2,1)} %bitcast.34, bf16[4,384,128]{2,1,0:T(8,128)(2,1)S(1)} %bitcast.36, ...), custom_call_target="tpu_custom_call" | custom-call | tf_op jit(solution)/shard_map/pallas_call | solution.py:31
  85.0 0.0 all-gather.7.cloned.1.call-update
  85.0 11.1 %all_to_all.33.came = bf16[4,496,128]{2,1,0:T(8,128)(2,1)S(1)} all-to-all(bf16[4,496,128]{2,1,0:T(8,128)(2,1)S(1)} %get-tuple-element.68), channel_id=1, replica_groups=mesh['expert'=8,'head'=4] {'head'}, dimensions={0} | all-to-all | bytes 1015808 | tf_op jit(solution)/shard_map/all_to_all | solution.py:590
  96.1 2.2 %shard_map.251 = (bf16[8,200,128]{2,1,0:T(8,128)(2,1)}, f32[16,128]{1,0:T(8,128)}, f32[192,128]{1,0:T(8,128)}) custom-call(bf16[4,496,128]{2,1,0:T(8,128)(2,1)S(1)} %all_to_all.33.came, bf16[400,128]{1,0:T(8,128)(2,1)} %copy-done.2, f32[8,128]{1,0:T(8,128)} %get-tuple-element.69.scale_one, f32[192,128]{1,0:T(8,128)} %get-tuple-element.70.own, ...), custom_call_target="tpu_custom_call" | custom-call | tf_op jit(solution)/shard_map/pallas_call | solution.py:31
  98.2 3.5 %all-to-all-start.4 = ((bf16[8,200,128]{2,1,0:T(8,128)(2,1)}), bf16[8,200,128]{2,1,0:T(8,128)(2,1)S(1)}, u32[]{:S(2)}, u32[]{:S(2)}) async-start(bf16[8,200,128]{2,1,0:T(8,128)(2,1)} %get-tuple-element.72), calls=%async_computation.4 | async-start | bytes 819200 | tf_op jit(solution)/shard_map/all_to_all | solution.py:602
  101.7 4.0 %shard_map.252 = (f32[768,768]{1,0:T(8,128)}, f32[768,768]{1,0:T(8,128)}) custom-call(bf16[192,768]{1,0:T(8,128)(2,1)} %get-tuple-element.73.rows_ref, bf16[192,768]{1,0:T(8,128)(2,1)} %get-tuple-element.74.hidden, bf16[192,768]{1,0:T(8,128)(2,1)} %get-tuple-element.75.before, bf16[192,768]{1,0:T(8,128)(2,1)} %get-tuple-element.76.grads), custom_call_target="tpu_custom_call" | custom-call | tf_op jit(solution)/shard_map/pallas_call | solution.py:31
  105.7 12.3 %all-to-all-done.4.came = bf16[8,200,128]{2,1,0:T(8,128)(2,1)S(1)} async-done(((bf16[8,200,128]{2,1,0:T(8,128)(2,1)}), bf16[8,200,128]{2,1,0:T(8,128)(2,1)S(1)}, u32[]{:S(2)}, u32[]{:S(2)}) %all-to-all-start.4) | async-done | bytes 409632 | tf_op jit(solution)/shard_map/all_to_all | solution.py:602
  118.0 0.0 copy-start.1
  118.0 0.8 shard_map.253
  118.9 3.4 %all-to-all-start.5 = ((bf16[8,160,128]{2,1,0:T(8,128)(2,1)}), bf16[8,160,128]{2,1,0:T(8,128)(2,1)S(1)}, u32[]{:S(2)}, u32[]{:S(2)}) async-start(bf16[8,160,128]{2,1,0:T(8,128)(2,1)} %shard_map.253), calls=%async_computation.5 | async-start | bytes 655360 | tf_op jit(solution)/shard_map/all_to_all | solution.py:608
  122.3 0.0 copy-done.1
  122.3 1.9 %shard_map.255 = bf16[192,128]{1,0:T(8,128)(2,1)} custom-call(bf16[8,200,128]{2,1,0:T(8,128)(2,1)} %copy-done.1, f32[8,128]{1,0:T(8,128)} %get-tuple-element.59.side, f32[8,128]{1,0:T(8,128)} %get-tuple-element.84.gate, f32[192,128]{1,0:T(8,128)} %get-tuple-element.85.residual), custom_call_target="tpu_custom_call" | custom-call | tf_op jit(solution)/shard_map/pallas_call | solution.py:31
  124.2 0.0 all-gather.9.cloned.1.call-done
  124.2 2.1 %all-gather.7.cloned.1.call-done = bf16[4608,128]{1,0:T(8,128)(2,1)} async-done(((bf16[576,128]{1,0:T(8,128)(2,1)}), bf16[4608,128]{1,0:T(8,128)(2,1)}) %all-gather.7.cloned.1.call-update) | async-done | bytes 1179664 | tf_op jit(solution)/shard_map/all_gather | solution.py:588
  126.3 4.4 %shard_map.254 = (f32[192,768]{1,0:T(8,128)}, f32[192,768]{1,0:T(8,128)}, f32[192,768]{1,0:T(8,128)}) custom-call(bf16[8,576,128]{2,1,0:T(8,128)(2,1)} %bitcast.44, bf16[8,4,192,128]{3,2,1,0:T(8,128)(2,1)} %bitcast.37, bf16[4,400,128]{2,1,0:T(8,128)(2,1)} %bitcast.35), custom_call_target="tpu_custom_call" | custom-call | tf_op jit(solution)/shard_map/pallas_call | solution.py:31
  130.7 1.8 %all-to-all-done.5.came = bf16[8,160,128]{2,1,0:T(8,128)(2,1)S(1)} async-done(((bf16[8,160,128]{2,1,0:T(8,128)(2,1)}), bf16[8,160,128]{2,1,0:T(8,128)(2,1)S(1)}, u32[]{:S(2)}, u32[]{:S(2)}) %all-to-all-start.5) | async-done | bytes 327712 | tf_op jit(solution)/shard_map/all_to_all | solution.py:608
  132.5 1.6 %shard_map.256 = (f32[192,768]{1,0:T(8,128)}, f32[8,768]{1,0:T(8,128)}, f32[3,32]{1,0:T(4,128)}, f32[8,256]{1,0:T(8,128)S(1)}, f32[1,1]{1,0:T(1,128)}) custom-call(bf16[8,160,128]{2,1,0:T(8,128)(2,1)S(1)} %all-to-all-done.5.came, s32[1,255]{1,0:T(1,128)} %bitcast.57, f32[8,128]{1,0:T(8,128)} %get-tuple-element.63.stats), custom_call_target="tpu_custom_call" | custom-call | tf_op jit(solution)/shard_map/pallas_call | solution.py:31
  134.1 0.6 fusion
  (1 shorter events, 0.0 us)
Async XLA Ops:
  7.2 117.0 %all-gather.9.cloned.1.call-start = ((), (), s32[]{:S(2)}) async-start(), calls=%async_computation.7 | async-start | bytes 1622016 | tf_op jit(solution)/shard_map/all_gather | solution.py:538
  7.9 118.4 %all-gather.7.cloned.1.call-start = ((), (), s32[]{:S(2)}) async-start(), calls=%async_computation.6 | async-start | bytes 1327104 | tf_op jit(solution)/shard_map/all_gather | solution.py:588
  10.5 41.2 %copy-start.2 = (bf16[400,128]{1,0:T(8,128)(2,1)}, bf16[400,128]{1,0:T(8,128)(2,1)S(1)}, u32[]{:S(2)}) copy-start(bf16[400,128]{1,0:T(8,128)(2,1)S(1)} %maximum_maximum_fusion.block) | copy-start | bytes 307204
  18.5 33.2 %copy-start = (bf16[1600,128]{1,0:T(8,128)(2,1)}, bf16[1600,128]{1,0:T(8,128)(2,1)S(1)}, u32[]{:S(2)}) copy-start(bf16[1600,128]{1,0:T(8,128)(2,1)S(1)} %all-gather) | copy-start | bytes 1228804
  98.2 19.8 %all-to-all-start.4 = ((bf16[8,200,128]{2,1,0:T(8,128)(2,1)}), bf16[8,200,128]{2,1,0:T(8,128)(2,1)S(1)}, u32[]{:S(2)}, u32[]{:S(2)}) async-start(bf16[8,200,128]{2,1,0:T(8,128)(2,1)} %get-tuple-element.72), calls=%async_computation.4 | async-start | bytes 819200 | tf_op jit(solution)/shard_map/all_to_all | solution.py:602
  118.0 4.3 %copy-start.1 = (bf16[8,200,128]{2,1,0:T(8,128)(2,1)}, bf16[8,200,128]{2,1,0:T(8,128)(2,1)S(1)}, u32[]{:S(2)}) copy-start(bf16[8,200,128]{2,1,0:T(8,128)(2,1)S(1)} %all-to-all-done.4.came) | copy-start | bytes 1228804
  118.9 13.6 %all-to-all-start.5 = ((bf16[8,160,128]{2,1,0:T(8,128)(2,1)}), bf16[8,160,128]{2,1,0:T(8,128)(2,1)S(1)}, u32[]{:S(2)}, u32[]{:S(2)}) async-start(bf16[8,160,128]{2,1,0:T(8,128)(2,1)} %shard_map.253), calls=%async_computation.5 | async-start | bytes 655360 | tf_op jit(solution)/shard_map/all_to_all | solution.py:608
Sparse Core Ops, SparseCore 0:
  10.9 59.0 all-gather.8
  85.1 41.1 all-gather.6
